TPU v7x, 128 devices: a whole 4x4x4 slice. The times are simulated.
128 devices in a mesh: dp: 32 (over y, x, core), expert: 4 (over z).
Axes of the slice: x: 4, y: 4, z: 4, core: 2. Of those that a mesh axis runs over, the one named last changes fastest.
Arguments:
- tokens: bfloat16 [32768, 1024], P(('dp', 'expert')), may hold values from -6 to 6
- out_grad: bfloat16 [32768, 1024], P(('dp', 'expert')), may hold values from -6 to 6
- gate: float32 [32768], P(('dp', 'expert')), may hold values from 0.2 to 1
- region: int32 [32768, 1], P(('dp', 'expert')), may hold values from 0 to 3; in each aligned block of 256 rows (0 to 255, 256 to 511, ...) at most 128 rows name the same one
- w_in: bfloat16 [4, 4096, 1024], P('expert'), may hold values from -0.1875 to 0.1875
- w_out: bfloat16 [4, 4096, 1024], P('expert'), may hold values from -0.09375 to 0.09375
Outputs:
- token_grad: bfloat16 [32768, 1024], P(('dp', 'expert'))
- w_in_grad: float32 [4, 4096, 1024], P('expert', 'dp')
- w_out_grad: float32 [4, 4096, 1024], P('expert', 'dp')
Inputs may be any that keep to these rules, and one draw needn't show every extreme that they name: `region`: of the 256 rows of one device, at most 128 name the same expert, and in every draw some device has exactly 128 rows for some expert.
All inputs are finite; a program needn't handle non-finite values.
Results may differ from a plain program's by a relative error of at most 0.02.
Values may be sent and summed in bfloat16 or wider, within the bound.
No kernel may reach another device: no remote copies, remote signals or barrier semaphores. Data moves between devices by JAX's collectives and lax.ppermute only.
A program may use at most 128 MiB of HBM per device.

v0:
```python
import math

import jax
import jax.numpy as jnp
from jax import lax
from jax.sharding import PartitionSpec as P


def gelu_parts(pre_act):
    root_two_pi = 0.7978845608028654
    cubic = pre_act * pre_act * pre_act
    tanh_val = jnp.tanh(root_two_pi * (pre_act + 0.044715 * cubic))
    halved = 0.5 * (1.0 + tanh_val)
    gelu_value = pre_act * halved
    gelu_slope = halved + 0.5 * pre_act * (1.0 - tanh_val * tanh_val) * root_two_pi * (
        1.0 + 3.0 * 0.044715 * pre_act * pre_act
    )
    return (gelu_value, gelu_slope)


def expert_rows(inputs_win, grads_win, weight_in, weight_out):
    pre_act = lax.dot_general(
        inputs_win, weight_in, (((1,), (1,)), ((), ())), preferred_element_type=jnp.float32
    )
    gelu_value, gelu_slope = gelu_parts(pre_act)
    activation = gelu_value.astype(jnp.bfloat16)
    act_grad = lax.dot_general(
        grads_win, weight_out, (((1,), (1,)), ((), ())), preferred_element_type=jnp.float32
    )
    pre_grad = (act_grad * gelu_slope).astype(jnp.bfloat16)
    row_grads = jnp.dot(pre_grad, weight_in, preferred_element_type=jnp.float32).astype(
        jnp.bfloat16
    )
    return (activation, pre_grad, row_grads)


def send_back(row_grads):
    return lax.all_to_all(row_grads, "expert", split_axis=0, concat_axis=0, tiled=True)


def local(tokens, out_grad, gate, region, w_in, w_out):
    groups = lax.axis_size("expert")
    dp_count = lax.axis_size("dp")
    token_count = tokens.shape[0]
    model_width = tokens.shape[1]
    capacity = 2 * token_count // groups
    slot_count = groups * capacity
    region_ids = region[:, 0]
    onehot = (region_ids[:, None] == jnp.arange(groups, dtype=jnp.int32)[None, :]).astype(jnp.int32)
    rank_in = jnp.sum(jnp.cumsum(onehot, 0) * onehot, 1) - 1
    slot_ids = region_ids * capacity + rank_in
    scaled = (gate[:, None] * out_grad.astype(jnp.float32)).astype(jnp.bfloat16)
    send_x = jnp.zeros((slot_count, model_width), jnp.bfloat16).at[slot_ids].set(tokens)
    send_d = jnp.zeros((slot_count, model_width), jnp.bfloat16).at[slot_ids].set(scaled)
    recv_x, recv_d = (
        lax.all_to_all(send_x, "expert", split_axis=0, concat_axis=0, tiled=True),
        lax.all_to_all(send_d, "expert", split_axis=0, concat_axis=0, tiled=True),
    )
    weight_in = w_in[0]
    weight_out = w_out[0]
    activation, pre_grad, row_grads = expert_rows(recv_x, recv_d, weight_in, weight_out)
    grad_scale = 1.0 / math.sqrt(float(token_count * dp_count))
    returned = send_back(row_grads)
    summed = lax.psum_scatter(
        jnp.concatenate(
            [
                lax.dot_general(
                    pre_grad, recv_x, (((0,), (0,)), ((), ())), preferred_element_type=jnp.float32
                ),
                lax.dot_general(
                    activation, recv_d, (((0,), (0,)), ((), ())), preferred_element_type=jnp.float32
                ),
            ],
            axis=1,
        ).astype(jnp.bfloat16),
        "dp",
        scatter_dimension=0,
        tiled=True,
    ).astype(jnp.float32)
    grad_in = summed[:, :model_width]
    grad_out = summed[:, model_width:]
    token_grad = returned[slot_ids]
    return (token_grad, (grad_in * grad_scale)[None], (grad_out * grad_scale)[None])


def solution(mesh):
    return jax.shard_map(
        local,
        mesh=mesh,
        in_specs=(
            P(("dp", "expert"), None),
            P(("dp", "expert"), None),
            P(("dp", "expert")),
            P(("dp", "expert"), None),
            P("expert", None, None),
            P("expert", None, None),
        ),
        out_specs=(P(("dp", "expert"), None), P("expert", "dp", None), P("expert", "dp", None)),
        check_vma=False,
    )
```

profile of v0, /device:TPU:0, one launch (start us, length us, event | category | flops | bytes accessed | tf_op | source)
XLA Modules:
  0.0 233.6 jit_solution(9790195171405055864)
XLA Ops:
  7.2 0.7 compare_convert_fusion
  7.8 1.2 reduce-window.6
  9.4 0.7 fusion.32
  10.2 0.7 compare_select_fusion
  10.8 3.2 %scatter_custom_fusion.1 = bf16[512,1024]{1,0:T(8,128)(2,1)} fusion(s32[256]{0:T(256)S(1)} %bitcast.57, bf16[256,1024]{1,0:T(8,128)(2,1)} %param.6, bf16[]{:T(256)} %constant.11.clone.1), kind=kCustom, calls=%fused_computation.37 | custom fusion | bytes 1049088 | tf_op jit(solution)/shard_map/scatter | solution.py:53
  14.0 5.4 %all-to-all-start.1 = ((bf16[4,128,1024]{2,1,0:T(8,128)(2,1)}), bf16[4,128,1024]{2,1,0:T(8,128)(2,1)S(1)}, u32[]{:S(2)}, u32[]{:S(2)}) async-start(bf16[4,128,1024]{2,1,0:T(8,128)(2,1)} %bitcast.9), calls=%async_computation.1 | async-start | bytes 2097152 | tf_op jit(solution)/shard_map/all_to_all | solution.py:56
  19.4 3.3 %scatter_custom_fusion = bf16[512,1024]{1,0:T(8,128)(2,1)} fusion(s32[256]{0:T(256)S(1)} %bitcast.58, bf16[256,1024]{1,0:T(8,128)(2,1)} %param.7, f32[256]{0:T(256)} %param.8, bf16[]{:T(256)} %constant.11.clone.1), kind=kCustom, calls=%fused_computation.31 | custom fusion | flops 786432 | bytes 1573890 | tf_op jit(solution)/shard_map/scatter | solution.py:54
  22.7 11.8 %all-to-all-done.1 = bf16[4,128,1024]{2,1,0:T(8,128)(2,1)S(1)} async-done(((bf16[4,128,1024]{2,1,0:T(8,128)(2,1)}), bf16[4,128,1024]{2,1,0:T(8,128)(2,1)S(1)}, u32[]{:S(2)}, u32[]{:S(2)}) %all-to-all-start.1) | async-done | bytes 1048608 | tf_op jit(solution)/shard_map/all_to_all | solution.py:56
  34.5 3.5 %all-to-all-start = ((bf16[4,128,1024]{2,1,0:T(8,128)(2,1)}), bf16[4,128,1024]{2,1,0:T(8,128)(2,1)S(1)}, u32[]{:S(2)}, u32[]{:S(2)}) async-start(bf16[4,128,1024]{2,1,0:T(8,128)(2,1)} %bitcast.6), calls=%async_computation | async-start | bytes 2097152 | tf_op jit(solution)/shard_map/all_to_all | solution.py:57
  38.2 10.1 %fusion.11 = f32[512,4096]{1,0:T(8,128)} fusion(bf16[512,1024]{1,0:T(8,128)(2,1)S(1)} %bitcast.51, bf16[1,4096,1024]{2,1,0:T(8,128)(2,1)} %param.10), kind=kOutput, calls=%fused_computation.17 | convolution fusion | flops 4294967296 | bytes 17825792 | tf_op jit(solution)/shard_map/dot_general | solution.py:22
  48.4 3.8 %all-to-all-done = bf16[4,128,1024]{2,1,0:T(8,128)(2,1)S(1)} async-done(((bf16[4,128,1024]{2,1,0:T(8,128)(2,1)}), bf16[4,128,1024]{2,1,0:T(8,128)(2,1)S(1)}, u32[]{:S(2)}, u32[]{:S(2)}) %all-to-all-start) | async-done | bytes 1048608 | tf_op jit(solution)/shard_map/all_to_all | solution.py:57
  52.2 7.4 %convolution_convert_fusion = bf16[4096,1024]{0,1:T(8,128)(2,1)S(1)} fusion(bf16[512,1024]{1,0:T(8,128)(2,1)S(1)} %bitcast.53, f32[512,4096]{1,0:T(8,128)} %fusion.11), kind=kOutput, calls=%fused_computation.23 | convolution fusion | flops 4318035968 | bytes 17825792 | tf_op jit(solution)/shard_map/dot_general | solution.py:70
  59.6 12.1 %fusion.8 = bf16[512,4096]{1,0:T(8,128)(2,1)} fusion(f32[512,4096]{1,0:T(8,128)S(1)} %copy-done, bf16[512,1024]{1,0:T(8,128)(2,1)S(1)} %bitcast.54, bf16[1,4096,1024]{2,1,0:T(8,128)(2,1)} %param.11), kind=kOutput, calls=%fused_computation.14 | convolution fusion | flops 4334813184 | bytes 22020096 | tf_op jit(solution)/shard_map/dot_general | solution.py:27
  71.7 7.0 %convolution_convert_fusion.1 = bf16[4096,1024]{0,1:T(8,128)(2,1)S(1)} fusion(bf16[512,4096]{1,0:T(8,128)(2,1)} %fusion.8, bf16[512,1024]{1,0:T(8,128)(2,1)S(1)} %bitcast.52), kind=kOutput, calls=%fused_computation.24 | convolution fusion | flops 4299161600 | bytes 13631488 | tf_op jit(solution)/shard_map/dot_general | solution.py:67
  78.7 7.3 %pad_maximum_fusion = bf16[4096,2048]{0,1:T(8,128)(2,1)} fusion(bf16[4096,1024]{0,1:T(8,128)(2,1)S(1)} %convolution_convert_fusion, bf16[4096,1024]{0,1:T(8,128)(2,1)S(1)} %convolution_convert_fusion.1), kind=kLoop, calls=%fused_computation.3 | loop fusion | flops 33554432 | bytes 33554432 | tf_op jit(solution)/shard_map/concatenate | solution.py:65
  86.0 22.6 %copy.21 = bf16[4096,2048]{1,0:T(8,128)(2,1)} copy(bf16[4096,2048]{0,1:T(8,128)(2,1)} %pad_maximum_fusion) | data formatting | bytes 33554432
  108.6 10.1 %fusion.21 = bf16[512,1024]{1,0:T(8,128)(2,1)} fusion(bf16[512,4096]{1,0:T(8,128)(2,1)} %fusion.8, bf16[1,4096,1024]{2,1,0:T(8,128)(2,1)} %param.10), kind=kOutput, calls=%fused_computation.29 | convolution fusion | flops 4295491584 | bytes 13631488 | tf_op jit(solution)/shard_map/dot_general | solution.py:31
  118.7 3.6 %all-to-all-start.2 = ((bf16[4,128,1024]{2,1,0:T(8,128)(2,1)}), bf16[4,128,1024]{2,1,0:T(8,128)(2,1)S(1)}, u32[]{:S(2)}, u32[]{:S(2)}) async-start(bf16[4,128,1024]{2,1,0:T(8,128)(2,1)} %bitcast.12), calls=%async_computation.2 | async-start | bytes 2097152 | tf_op jit(solution)/shard_map/all_to_all | solution.py:38
  122.3 13.2 %all-to-all-done.2 = bf16[4,128,1024]{2,1,0:T(8,128)(2,1)S(1)} async-done(((bf16[4,128,1024]{2,1,0:T(8,128)(2,1)}), bf16[4,128,1024]{2,1,0:T(8,128)(2,1)S(1)}, u32[]{:S(2)}, u32[]{:S(2)}) %all-to-all-start.2) | async-done | bytes 1048608 | tf_op jit(solution)/shard_map/all_to_all | solution.py:38
  135.5 2.0 gather_fusion
  137.5 85.9 %reduce-scatter.4.cloned.1.call-done = bf16[128,2048]{1,0:T(8,128)(2,1)} async-done(((bf16[4096,2048]{1,0:T(8,128)(2,1)}), bf16[128,2048]{1,0:T(8,128)(2,1)}) %reduce-scatter.4.cloned.1.call-update) | async-done | bytes 524304
  223.3 1.3 copy.22
  224.8 1.0 copy.20
  225.8 1.0 copy.19
  (14 shorter events, 0.8 us)
Async XLA Ops:
  14.0 20.5 %all-to-all-start.1 = ((bf16[4,128,1024]{2,1,0:T(8,128)(2,1)}), bf16[4,128,1024]{2,1,0:T(8,128)(2,1)S(1)}, u32[]{:S(2)}, u32[]{:S(2)}) async-start(bf16[4,128,1024]{2,1,0:T(8,128)(2,1)} %bitcast.9), calls=%async_computation.1 | async-start | bytes 2097152 | tf_op jit(solution)/shard_map/all_to_all | solution.py:56
  34.5 17.7 %all-to-all-start = ((bf16[4,128,1024]{2,1,0:T(8,128)(2,1)}), bf16[4,128,1024]{2,1,0:T(8,128)(2,1)S(1)}, u32[]{:S(2)}, u32[]{:S(2)}) async-start(bf16[4,128,1024]{2,1,0:T(8,128)(2,1)} %bitcast.6), calls=%async_computation | async-start | bytes 2097152 | tf_op jit(solution)/shard_map/all_to_all | solution.py:57
  38.0 185.3 %reduce-scatter.4.cloned.1.call-start = ((), (), s32[]{:S(2)}) async-start(), calls=%async_computation.4 | async-start | bytes 17301504
  52.2 7.4 %copy-start = (f32[512,4096]{1,0:T(8,128)S(1)}, f32[512,4096]{1,0:T(8,128)}, u32[]{:S(2)}) copy-start(f32[512,4096]{1,0:T(8,128)} %fusion.11) | copy-start | bytes 25165828
  118.7 16.8 %all-to-all-start.2 = ((bf16[4,128,1024]{2,1,0:T(8,128)(2,1)}), bf16[4,128,1024]{2,1,0:T(8,128)(2,1)S(1)}, u32[]{:S(2)}, u32[]{:S(2)}) async-start(bf16[4,128,1024]{2,1,0:T(8,128)(2,1)} %bitcast.12), calls=%async_computation.2 | async-start | bytes 2097152 | tf_op jit(solution)/shard_map/all_to_all | solution.py:38
Sparse Core Ops, SparseCore 0:
  108.7 114.5 reduce-scatter.3
where the time goes:
time: 235 us; the launch traced here: 234 us
  waiting for transfers between devices  115 us (49%)
  matrix products  46.8 us (20%)
  local copies, waits for them, and re-layouts  31.3 us (13%)
  other arithmetic  14.2 us (6%)
  between operations  14.1 us (6%)
  starting transfers between devices  12.7 us (5%)
    unnamed x2, waiting for transfers between devices  85.9 us
    unnamed x6, local copies, waits for them, and re-layouts  25.9 us
    all_to_all x1, waiting for transfers between devices, send_back(): lax.all_to_all(row_grads, 'expert', split_axis=0, concat_axis=0, tiled=True)  13.2 us
    dot_general x1, matrix products, expert_rows(): lax.dot_general(grads_win, weight_out, (((1,), (1,)), ((), ())), preferre...  12.1 us
    all_to_all x1, waiting for transfers between devices, local(): lax.all_to_all(send_x, 'expert', split_axis=0, concat_axis=0, tiled=True)  11.8 us
    dot_general x1, matrix products, expert_rows(): jnp.dot(pre_grad, weight_in, preferred_element_type=jnp.float32)  10.1 us
    dot_general x1, matrix products, expert_rows(): lax.dot_general(inputs_win, weight_in, (((1,), (1,)), ((), ())), preferre...  10.1 us
    dot_general x1, matrix products, local(): lax.dot_general(activation, recv_d, (((0,), (0,)), ((), ())), preferred_e...  7.4 us
  transfers between devices with their start and end apart: 4, of which 4 were waited for; matrix products, arithmetic and copies ran while one was open for 11% of the time, Pallas kernels for 0%

commit v1 on v0

v1 whole, which is shorter than its diff:
```python
import math

import jax
import jax.numpy as jnp
from jax import lax
from jax.experimental import pallas as pl
from jax.experimental.pallas import tpu as pltpu
from jax.sharding import Mesh, PartitionSpec as P

BF16 = jnp.bfloat16
F32 = jnp.float32
VMEM_LIMIT = 44 * 1024 * 1024
ORDER = (2, 1, 3, 0)
INVERSE = (3, 1, 0, 2)


def ring(step):
    return [(i, (i + step) % 4) for i in range(4)]


def swap_core(array):
    return lax.ppermute(array, "core", [(0, 1), (1, 0)])


def params():
    return pltpu.CompilerParams(vmem_limit_bytes=VMEM_LIMIT)


def cost(nbytes=1024):
    return pl.CostEstimate(flops=0, bytes_accessed=int(nbytes), transcendentals=0)


def shape(rows, cols, dtype=BF16):
    return jax.ShapeDtypeStruct((rows, cols), dtype)


def dot_nt(a, b):
    return lax.dot_general(a, b, (((1,), (1,)), ((), ())), preferred_element_type=F32)


def dot_nn(a, b):
    return lax.dot_general(a, b, (((1,), (0,)), ((), ())), preferred_element_type=F32)


def dot_tn(a, b):
    return lax.dot_general(a, b, (((0,), (0,)), ((), ())), preferred_element_type=F32)


def gelu_parts(pre_act):
    root_two_pi = 0.7978845608028654
    square = pre_act * pre_act
    inner = pre_act * (root_two_pi + root_two_pi * 0.044715 * square)
    halved = 0.5 + 0.5 * jnp.tanh(inner)
    value = pre_act * halved
    slope_of_inner = 2.0 * root_two_pi + 6.0 * root_two_pi * 0.044715 * square
    return value, halved + value * (1.0 - halved) * slope_of_inner


VMEM = pl.BlockSpec(memory_space=pltpu.VMEM)
ANY = pl.BlockSpec(memory_space=pl.ANY)


def dispatch_tokens(region, tokens):
    n, width = tokens.shape

    def body(region_ref, tok_ref, place_ref, out_ref):
        dest = region_ref[...]
        onehot = (dest == lax.broadcasted_iota(jnp.int32, (8, n), 0)).astype(F32)
        upper = (
            lax.broadcasted_iota(jnp.int32, (n, n), 0) < lax.broadcasted_iota(jnp.int32, (n, n), 1)
        ).astype(F32)
        before = dot_nn(onehot.astype(BF16), upper.astype(BF16))
        rank = jnp.sum(before * onehot, axis=0, keepdims=True).astype(jnp.int32)
        slot = dest * 128 + rank
        place = (slot == lax.broadcasted_iota(jnp.int32, (512, n), 0)).astype(F32).astype(BF16)
        place_ref[...] = place
        out_ref[...] = dot_nn(place, tok_ref[...]).astype(BF16)

    return pl.pallas_call(
        body,
        out_shape=[shape(512, n), shape(512, width)],
        in_specs=[VMEM] * 2,
        out_specs=[VMEM] * 2,
        compiler_params=params(),
        cost_estimate=cost(4 * n * width * 2),
    )(region, tokens)


def dispatch_grads(place, gate, grads):
    n, width = grads.shape

    def body(place_ref, gate_ref, grad_ref, out_ref):
        column = jnp.transpose(jnp.broadcast_to(gate_ref[...], (128, n)))[:, :1]
        scaled = (column * grad_ref[...].astype(F32)).astype(BF16)
        out_ref[...] = dot_nn(place_ref[...], scaled).astype(BF16)

    return pl.pallas_call(
        body,
        out_shape=shape(512, width),
        in_specs=[VMEM] * 3,
        out_specs=VMEM,
        compiler_params=params(),
        cost_estimate=cost(4 * n * width * 2),
    )(place, gate, grads)


HBM = pl.BlockSpec(memory_space=pltpu.HBM)


def weight_scratch(width, count):
    return [pltpu.VMEM((512 * count, width), BF16), pltpu.SemaphoreType.DMA((4 * count,))]


def weight_group(table_ref, weight_ref, w_buf, sems, offset, count):
    step = pl.program_id(0)

    def fetch(k):
        block = pl.multiple_of(table_ref[offset + k] * 128, 128)
        place = pl.multiple_of(k * 128, 128)
        return pltpu.make_async_copy(
            weight_ref.at[pl.ds(block, 128), :], w_buf.at[pl.ds(place, 128), :], sems.at[k]
        )

    @pl.when(step == 0)
    def _():
        for k in range(4 * count):
            fetch(k).start()

    for q in range(4):
        fetch(4 * step + q).wait()
    return w_buf.at[pl.ds(pl.multiple_of(step * 512, 512), 512), :]


def after(array, *others):
    def body(*refs):
        del refs

    return pl.pallas_call(
        body,
        in_specs=[ANY] * (1 + len(others)),
        out_specs=ANY,
        out_shape=jax.ShapeDtypeStruct(array.shape, array.dtype),
        input_output_aliases={0: 0},
        compiler_params=params(),
        cost_estimate=cost(),
    )(array, *others)


def columns(halves, c):
    return halves[c // 2][(c % 2) * 256 : (c % 2 + 1) * 256, :]


def forward(table, halves, weight):
    width = weight.shape[1]
    tok = 1024

    def body(table_ref, own_ref, other_ref, weight_ref, first_ref, act_ref, slope_ref, mark_ref, w_buf, sems):
        mark_ref[...] = jnp.zeros_like(mark_ref)
        w_ref = weight_group(table_ref, weight_ref, w_buf, sems, 0, 4)
        for c in range(4):
            cols = slice(c * 256, (c + 1) * 256)
            act, slope = gelu_parts(dot_nt(w_ref[...], columns((own_ref, other_ref), c)))
            slope_ref[:, cols] = slope.astype(BF16)
            act = act.astype(BF16)

            @pl.when(pl.program_id(0) == 0)
            def _():
                first_ref[:, cols] = act

            @pl.when(pl.program_id(0) > 0)
            def _():
                act_ref[:, cols] = act


    return pl.pallas_call(
        body,
        grid_spec=pltpu.PrefetchScalarGridSpec(
            num_scalar_prefetch=1,
            grid=(4,),
            in_specs=[VMEM] * 2 + [HBM],
            out_specs=[
                pl.BlockSpec((512, tok), lambda i, *_: (0, 0)),
                pl.BlockSpec((512, tok), lambda i, *_: (jnp.maximum(i - 1, 0), 0)),
                pl.BlockSpec((512, tok), lambda i, *_: (i, 0)),
            ]
            + [pl.BlockSpec((8, 128), lambda i, *_: (0, 0))],
            scratch_shapes=weight_scratch(width, 4),
        ),
        out_shape=[shape(512, tok), shape(1536, tok), shape(2048, tok), shape(8, 128, F32)],
        compiler_params=params(),
        cost_estimate=cost(2**24),
    )(table, *halves, weight)


def outer(left, halves):
    return dot_nn(left[:, :512], halves[0][...]) + dot_nn(left[:, 512:], halves[1][...])


def outer_products(act, halves, first, count, deps):
    width = halves[0].shape[1]
    split = act.shape[0] == 512

    def body(act_ref, own_ref, other_ref, *refs):
        outs = refs[len(deps) :]
        span = 512 // len(outs)
        for k, out in enumerate(outs):
            out[...] = outer(act_ref[k * span : (k + 1) * span, :], (own_ref, other_ref)).astype(BF16)

    return pl.pallas_call(
        body,
        grid=(count,),
        in_specs=[pl.BlockSpec((512, 1024), lambda i: (i + first, 0))] + [VMEM] * 2 + [ANY] * len(deps),
        out_specs=[pl.BlockSpec((256, width), lambda i: (0, 0))] * 2
        if split
        else pl.BlockSpec((512, width), lambda i: (i, 0)),
        out_shape=[shape(256, width)] * 2 if split else shape(512 * count, width),
        compiler_params=params(),
        cost_estimate=cost(2**20 * (2 + 2 * count)),
    )(act, *halves, *deps)


def backward(table, grads, rows, slope, weight, groups, deps):
    first, count = groups
    width = weight.shape[1]
    tok = 1024
    split = first == 0

    def body(table_ref, d_own, d_other, x_own, x_other, slope_ref, weight_ref, *refs):
        pre_ref, *outs, w_buf, sems, s_buf = refs[len(deps) :]
        step = pl.program_id(0)
        w_ref = weight_group(table_ref, weight_ref, w_buf, sems, 16 + 4 * first, count)
        for q in range(4):
            block = pl.multiple_of(table_ref[32 + 4 * (step + first) + q] * 128, 128)
            s_buf[q * 128 : (q + 1) * 128, :] = slope_ref[pl.ds(block, 128), :]
        for c in range(4):
            cols = slice(c * 256, (c + 1) * 256)
            act_grad = dot_nt(w_ref[...], columns((d_own, d_other), c))
            pre_ref[:, cols] = (act_grad * s_buf[:, cols].astype(F32)).astype(BF16)
        span = 512 // len(outs)
        for k, out in enumerate(outs):
            out[...] = outer(pre_ref[k * span : (k + 1) * span, :], (x_own, x_other)).astype(BF16)

    return pl.pallas_call(
        body,
        grid_spec=pltpu.PrefetchScalarGridSpec(
            num_scalar_prefetch=1,
            grid=(count,),
            in_specs=[VMEM] * 5 + [HBM] + [ANY] * len(deps),
            out_specs=[pl.BlockSpec((512, tok), lambda i, *_: (i, 0))]
            + (
                [pl.BlockSpec((256, width), lambda i, *_: (0, 0))] * 2
                if split
                else [pl.BlockSpec((512, width), lambda i, *_: (i, 0))]
            ),
            scratch_shapes=weight_scratch(width, count) + [pltpu.VMEM((512, tok), BF16)],
        ),
        out_shape=[shape(512 * count, tok)]
        + ([shape(256, width)] * 2 if split else [shape(512 * count, width)]),
        compiler_params=params(),
        cost_estimate=cost(2**20 * (2 + 4 * count)),
    )(table, *grads, *rows, slope, weight, *deps)


def row_gradients(table, pre, weight, deps):
    width = weight.shape[1]
    rows = 512

    def body(table_ref, a_ref, b_ref, c_ref, weight_ref, *refs):
        out_ref, w_buf, sems, total = refs[len(deps) :]
        step = pl.program_id(0)
        w_ref = weight_group(table_ref, weight_ref, w_buf, sems, 16, 4)

        @pl.when(step == 0)
        def _():
            total[...] = dot_tn(a_ref[...], w_ref[...])

        @pl.when(jnp.logical_and(step > 0, step < 3))
        def _():
            begin = pl.multiple_of((step - 1) * 512, 512)
            total[...] += dot_tn(b_ref[pl.ds(begin, 512), :], w_ref[...])

        @pl.when(step == 3)
        def _():
            final = (total[...] + dot_tn(c_ref[...], w_ref[...])).astype(BF16)
            own = table_ref[48]
            out_ref[pl.ds(pl.multiple_of(own * rows, rows), rows), :] = final[:rows]
            out_ref[pl.ds(pl.multiple_of((1 - own) * rows, rows), rows), :] = final[rows:]

    return pl.pallas_call(
        body,
        grid_spec=pltpu.PrefetchScalarGridSpec(
            num_scalar_prefetch=1,
            grid=(4,),
            in_specs=[VMEM] * 3 + [HBM] + [ANY] * len(deps),
            out_specs=pl.BlockSpec((2 * rows, width), lambda i, *_: (0, 0)),
            scratch_shapes=weight_scratch(width, 4) + [pltpu.VMEM((2 * rows, width), F32)],
        ),
        out_shape=shape(2 * rows, width),
        compiler_params=params(),
        cost_estimate=cost(2**23 + 2**22),
    )(table, *pre, weight, *deps)


def restore_order(place, rows):
    n, width = place.shape[1], rows.shape[1]

    def body(place_ref, rows_ref, out_ref):
        out_ref[...] = dot_tn(place_ref[...], rows_ref[...]).astype(BF16)

    return pl.pallas_call(
        body,
        out_shape=shape(n, width),
        in_specs=[VMEM] * 2,
        out_specs=VMEM,
        compiler_params=params(),
        cost_estimate=cost(2**21),
    )(place, rows)


def add(*terms):
    total = terms[0].astype(F32)
    for term in terms[1:]:
        total = total + term.astype(F32)
    return total


def small(array):
    return array[:8, :128]


def both(pair):
    return pair[0][-8:, :128], pair[1][:8, :128]


def first_hop(low, high, axis):
    return lax.ppermute(low, axis, ring(3)), lax.ppermute(high, axis, ring(1))


def join(arrived, following, previous):
    h = following.shape[0] // 2
    from_next, from_prev = arrived
    up = jnp.concatenate([following[:h], add(following[h:], from_prev).astype(BF16)], axis=0)
    down = jnp.concatenate([add(previous[:h], from_next).astype(BF16), previous[h:]], axis=0)
    return up, down


def second_hop(up, down, axis):
    return lax.ppermute(up, axis, ring(1)), lax.ppermute(down, axis, ring(3))


def within(group, axis):
    n = group.shape[0] // 4
    own, following, opposite, previous = (group[k * n : (k + 1) * n] for k in range(4))
    arrived = first_hop(opposite[: n // 2], opposite[n // 2 :], axis)
    return own, *join(arrived, following, previous)


def sum_cores(terms):
    terms = lax.all_to_all(terms, "core", split_axis=0, concat_axis=0, tiled=True)
    n = terms.shape[0] // 2
    return add(terms[:n], terms[n:]).astype(BF16)


def once(index, work, like):
    trips = 1 + jnp.minimum(index, 0)
    return lax.fori_loop(0, trips, lambda _, start: work(start), jnp.zeros_like(like))


def local(tokens, out_grad, gate, region, w_in, w_out):
    x, y, core = (lax.axis_index(a).astype(jnp.int32) for a in ("x", "y", "core"))
    scale = 1.0 / math.sqrt(float(tokens.shape[0] * lax.axis_size(("y", "x", "core"))))
    order = jnp.array(ORDER, jnp.int32)
    every = jnp.arange(4, dtype=jnp.int32)
    by_x = ((((y + every[None, :]) % 4) * 4 + (x + order[:, None]) % 4) * 2 + core).reshape(16)
    by_y = ((((y + order[:, None]) % 4) * 4 + (x + every[None, :]) % 4) * 2 + core).reshape(16)
    same = jnp.array([INVERSE[q] * 4 + ORDER[p] for p in range(4) for q in range(4)], jnp.int32)
    table = jnp.concatenate([by_x, by_y, same, core[None]])
    weight_in, weight_out = w_in[0], w_out[0]

    def exchange(array):
        return lax.all_to_all(array, "expert", split_axis=0, concat_axis=0, tiled=True)

    place, send_x = dispatch_tokens(region.reshape(1, -1), tokens)
    send_d = dispatch_grads(place, gate.reshape(1, -1), out_grad)
    own_x = exchange(send_x)
    own_d = exchange(send_d)
    rows_x = (own_x, swap_core(own_x))
    act_first, act_rest, slope, mark = forward(table, rows_x, weight_in)
    own_d = after(own_d, mark)
    rows_d = (own_d, swap_core(own_d))

    out_low, out_high = outer_products(act_first, rows_d, 0, 1, ())
    out_hop = first_hop(out_low, out_high, "x")
    pre_a, in_low, in_high = backward(
        table, rows_d, rows_x, slope, weight_out, (0, 1), (small(out_high),)
    )
    in_hop = first_hop(in_low, in_high, "y")
    out_sides = outer_products(act_rest, rows_d, 0, 2, (small(in_high),))
    out_join = join(out_hop, out_sides[:512], out_sides[512:])
    out_parts = second_hop(*out_join, "x")
    pre_b, in_sides = backward(table, rows_d, rows_x, slope, weight_out, (1, 2), both(out_join))
    in_join = join(in_hop, in_sides[:512], in_sides[512:])
    in_parts = second_hop(*in_join, "y")
    pre_c, in_own = backward(table, rows_d, rows_x, slope, weight_out, (3, 1), both(in_join))
    out_own = outer_products(act_rest, rows_d, 2, 1, (small(in_own),))
    own = once(
        x,
        lambda start: sum_cores(
            row_gradients(table, (pre_a, pre_b, pre_c), weight_in, (small(start),))
        ),
        rows_x[0],
    )
    back = exchange(own)

    group = add(after(out_own, small(own)), *out_parts).astype(BF16)
    last = within(group, "y")
    grad_out = add(last[0], *second_hop(*last[1:], "y")) * scale
    group = add(after(in_own, *both(last[1:])), *in_parts).astype(BF16)
    last = within(group, "x")
    grad_in = add(last[0], *second_hop(*last[1:], "x")) * scale
    token_grad = restore_order(place, back)
    return token_grad, grad_in[None], grad_out[None]


def solution(mesh):
    chips = Mesh(mesh.devices.reshape(4, 4, 2, 4), ("y", "x", "core", "expert"))
    rows = ("y", "x", "core", "expert")
    plane = ("y", "x", "core")
    return jax.shard_map(
        local,
        mesh=chips,
        in_specs=(
            P(rows, None),
            P(rows, None),
            P(rows),
            P(rows, None),
            P("expert", None, None),
            P("expert", None, None),
        ),
        out_specs=(P(rows, None), P("expert", plane, None), P("expert", plane, None)),
        check_vma=False,
    )
```

time: 235 us -> 161 us (0.69)
  waiting for transfers between devices: 115 us -> 13.2 us
  Pallas kernels: 0 us -> 53.5 us
  matrix products: 46.8 us -> 0 us
  starting transfers between devices: 12.7 us -> 35.5 us
  blocking collectives: 0 us -> 20.3 us
  local copies, waits for them, and re-layouts: 31.3 us -> 16 us
  between operations: 14.1 us -> 1.04 us
  other arithmetic: 14.2 us -> 20.5 us
    unnamed x2 -> x0, waiting for transfers between devices: 85.9 us -> none
    pallas_call x0 -> x14, Pallas kernels: none -> 53.5 us  [the longest x3 17.4 us: backward(): pl.pallas_call(body, grid_spec=pltpu.PrefetchScalarGridSpec(num_scalar_pr...]
    dot_general x5 -> x0, matrix products: 46.8 us -> none  [the longest x1 12.1 us: expert_rows(): lax.dot_general(grads_win, weight_out, (((1,), (1,)), ((), ())), preferre...]
    all_to_all x3, waiting for transfers between devices: 28.8 us -> 2.99 us  [the longest x1 2.98 us: sum_cores(): lax.all_to_all(terms, 'core', split_axis=0, concat_axis=0, tiled=True)]
    ppermute x0 -> x18, starting transfers between devices: none -> 22.6 us  [the longest x8 11.7 us: second_hop(): return (lax.ppermute(up, axis, ring(1)), lax.ppermute(down, axis, ring(3)))]
    all_to_all x0 -> x1, blocking collectives: none -> 20.3 us  [exchange(): lax.all_to_all(array, 'expert', split_axis=0, concat_axis=0, tiled=True)]
    unnamed x6 -> x42, local copies, waits for them, and re-layouts: 25.9 us -> 11.7 us
    ppermute x0 -> x18, waiting for transfers between devices: none -> 10.2 us  [the longest x8 4.9 us: second_hop(): return (lax.ppermute(up, axis, ring(1)), lax.ppermute(down, axis, ring(3)))]
  transfers between devices with their start and end apart: 4 -> 21, of which waited for: 4 -> 6; matrix products, arithmetic and copies ran while one was open for 11% -> 14% of each run, Pallas kernels for 0% -> 32%
where the time goes in v1:
time: 161 us; the launch traced here: 160 us
  Pallas kernels  53.5 us (33%)
  starting transfers between devices  35.5 us (22%)
  other arithmetic  20.5 us (13%)
  blocking collectives  20.3 us (13%)
  local copies, waits for them, and re-layouts  16 us (10%)
  waiting for transfers between devices  13.2 us (8%)
    all_to_all x1, blocking collectives, exchange(): lax.all_to_all(array, 'expert', split_axis=0, concat_axis=0, tiled=True)  20.3 us
    pallas_call x3, Pallas kernels, backward(): pl.pallas_call(body, grid_spec=pltpu.PrefetchScalarGridSpec(num_scalar_pr...  17.4 us
    pallas_call x1, Pallas kernels, forward(): pl.pallas_call(body, grid_spec=pltpu.PrefetchScalarGridSpec(num_scalar_pr...  17.1 us
    ppermute x8, starting transfers between devices, second_hop(): return (lax.ppermute(up, axis, ring(1)), lax.ppermute(down, axis, ring(3)))  11.7 us
    unnamed x42, local copies, waits for them, and re-layouts  11.7 us
    pallas_call x1, Pallas kernels, row_gradients(): pl.pallas_call(body, grid_spec=pltpu.PrefetchScalarGridSpec(num_scalar_pr...  10.8 us
    ppermute x8, starting transfers between devices, first_hop(): return (lax.ppermute(low, axis, ring(3)), lax.ppermute(high, axis, ring(1)))  10.4 us
    all_to_all x2, starting transfers between devices, exchange(): lax.all_to_all(array, 'expert', split_axis=0, concat_axis=0, tiled=True)  7.99 us
  transfers between devices with their start and end apart: 21, of which 6 were waited for; matrix products, arithmetic and copies ran while one was open for 14% of the time, Pallas kernels for 32%

profile of v1, /device:TPU:0, one launch (start us, length us, event | category | flops | bytes accessed | tf_op | source)
XLA Modules:
  0.0 160.1 jit_solution(2970640043919091931)
XLA Ops:
  3.1 20.3 %all_to_all.42 = bf16[4,128,1024]{2,1,0:T(8,128)(2,1)S(1)} all-to-all(bf16[4,128,1024]{2,1,0:T(8,128)(2,1)S(1)} %bitcast.30), channel_id=1, replica_groups=mesh['y'=4,'x'=4,'core'=2,'expert'=4] {'expert'}, dimensions={0} | all-to-all | bytes 2097152 | tf_op jit(solution)/shard_map/all_to_all | solution.py:381
  24.9 3.5 %all-to-all-start.1 = ((bf16[4,128,1024]{2,1,0:T(8,128)(2,1)}), bf16[4,128,1024]{2,1,0:T(8,128)(2,1)S(1)}, u32[]{:S(2)}, u32[]{:S(2)}) async-start(bf16[4,128,1024]{2,1,0:T(8,128)(2,1)} %bitcast.29), calls=%async_computation.1 | async-start | bytes 2097152 | tf_op jit(solution)/shard_map/all_to_all | solution.py:381
  28.9 17.1 %shard_map.105 = (bf16[512,1024]{1,0:T(8,128)(2,1)S(1)}, bf16[1536,1024]{1,0:T(8,128)(2,1)S(1)}, bf16[2048,1024]{1,0:T(8,128)(2,1)}, f32[8,128]{1,0:T(8,128)S(1)}) custom-call(s32[49]{0:T(128)S(1)} %pad_add_fusion.table_ref, bf16[512,1024]{1,0:T(8,128)(2,1)S(1)} %bitcast.24, bf16[512,1024]{1,0:T(8,128)(2,1)S(1)} %collective-permute-done.other_ref.x_other, ...), custom_call_target="tpu_custom_call" | custom-call | bytes 16777216 | tf_op jit(solution)/shard_map/pallas_call | solution.py:175
  49.1 2.3 %collective-permute-done.1.other_ref.d_other = bf16[512,1024]{1,0:T(8,128)(2,1)S(1)} collective-permute-done((bf16[512,1024]{1,0:T(8,128)(2,1)S(1)}, bf16[512,1024]{1,0:T(8,128)(2,1)S(1)}, u32[]{:S(2)}, u32[]{:S(2)}) %collective-permute-start.1) | collective-permute-done | bytes 1048608 | tf_op jit(solution)/shard_map/ppermute | solution.py:22
  51.4 2.0 %shard_map.107 = (bf16[256,1024]{1,0:T(8,128)(2,1)}, bf16[256,1024]{1,0:T(8,128)(2,1)}) custom-call(bf16[512,1024]{1,0:T(8,128)(2,1)S(1)} %copy-done.12, bf16[512,1024]{1,0:T(8,128)(2,1)S(1)} %shard_map.106.own_ref.d_own, bf16[512,1024]{1,0:T(8,128)(2,1)S(1)} %collective-permute-done.1.other_ref.d_other), custom_call_target="tpu_custom_call" | custom-call | bytes 4194304 | tf_op jit(solution)/shard_map/pallas_call | solution.py:209
  53.5 2.8 %collective-permute-start.3 = (bf16[256,1024]{1,0:T(8,128)(2,1)}, bf16[256,1024]{1,0:T(8,128)(2,1)}, u32[]{:S(2)}, u32[]{:S(2)}) collective-permute-start(bf16[256,1024]{1,0:T(8,128)(2,1)} %get-tuple-element.70), channel_id=1, source_target_pairs={{0,24},{8,0},{16,8},{24,16},{1,25},{9,1},{17,9},{25,17},{2,26},{10... | collective-permute-start | bytes 1572872 | tf_op jit(solution)/shard_map/ppermute | solution.py:336
  57.0 2.2 %copy-done = bf16[2048,1024]{1,0:T(8,128)(2,1)S(1)} copy-done((bf16[2048,1024]{1,0:T(8,128)(2,1)S(1)}, bf16[2048,1024]{1,0:T(8,128)(2,1)}, u32[]{:S(2)}) %copy-start) | copy-done | bytes 4194328
  60.4 4.4 %shard_map.108 = (bf16[512,1024]{1,0:T(8,128)(2,1)}, bf16[256,1024]{1,0:T(8,128)(2,1)S(1)}, bf16[256,1024]{1,0:T(8,128)(2,1)S(1)}) custom-call(s32[49]{0:T(128)S(1)} %pad_add_fusion.table_ref, bf16[512,1024]{1,0:T(8,128)(2,1)S(1)} %shard_map.106.own_ref.d_own, bf16[512,1024]{1,0:T(8,128)(2,1)S(1)} %collective-permute-done.1.other_ref.d_other, ...), custom_call_target="tpu_custom_call" | custom-call | bytes 6291456 | tf_op jit(solution)/shard_map/pallas_call | solution.py:243
  68.1 2.5 %shard_map.109 = bf16[1024,1024]{1,0:T(8,128)(2,1)S(1)} custom-call(bf16[1536,1024]{1,0:T(8,128)(2,1)S(1)} %copy-done.6, bf16[512,1024]{1,0:T(8,128)(2,1)S(1)} %shard_map.106.own_ref.d_own, bf16[512,1024]{1,0:T(8,128)(2,1)S(1)} %collective-permute-done.1.other_ref.d_other, bf16[8,128]{1,0:T(8,128)(2,1)S(1)} %slice.138.refs_0_), custom_call_target="tpu_custom_call" | custom-call | bytes 6291456 | tf_op jit(solution)/shard_map/pallas_call | solution.py:209
  75.4 3.2 %collective-permute-start.7 = (bf16[512,1024]{1,0:T(8,128)(2,1)}, bf16[512,1024]{1,0:T(8,128)(2,1)}, u32[]{:S(2)}, u32[]{:S(2)}) collective-permute-start(bf16[512,1024]{1,0:T(8,128)(2,1)} %pad_maximum_fusion.1), channel_id=1, source_target_pairs={{0,24},{8,0},{16,8},{24,16},{1,25},{9,1},{17,9},{25,17},{2,26},{10... | collective-permute-start | bytes 3145736 | tf_op jit(solution)/shard_map/ppermute | solution.py:348
  78.7 8.8 %shard_map.110 = (bf16[1024,1024]{1,0:T(8,128)(2,1)}, bf16[1024,1024]{1,0:T(8,128)(2,1)S(1)}) custom-call(s32[49]{0:T(128)S(1)} %pad_add_fusion.table_ref, bf16[512,1024]{1,0:T(8,128)(2,1)S(1)} %shard_map.106.own_ref.d_own, bf16[512,1024]{1,0:T(8,128)(2,1)S(1)} %collective-permute-done.1.other_ref.d_other, bf16[512,1024]{1,0:T(8,128)(2,1)S(1)} %bitcast.26, ...), custom_call_target="tpu_custom_call" | custom-call | bytes 10485760 | tf_op jit(solution)/shard_map/pallas_call | solution.py:243
  93.4 4.1 %shard_map.111 = (bf16[512,1024]{1,0:T(8,128)(2,1)}, bf16[512,1024]{1,0:T(8,128)(2,1)S(1)}) custom-call(s32[49]{0:T(128)S(1)} %pad_add_fusion.table_ref, bf16[512,1024]{1,0:T(8,128)(2,1)S(1)} %shard_map.106.own_ref.d_own, bf16[512,1024]{1,0:T(8,128)(2,1)S(1)} %collective-permute-done.1.other_ref.d_other, bf16[512,1024]{1,0:T(8,128)(2,1)S(1)} %bitcast.27, ...), custom_call_target="tpu_custom_call" | custom-call | bytes 6291456 | tf_op jit(solution)/shard_map/pallas_call | solution.py:243
  99.6 22.3 %while.10 = (s32[]{:T(128)}, bf16[512,1024]{1,0:T(8,128)(2,1)}, s32[]{:T(128)}, s32[49]{0:T(128)S(1)}, bf16[512,1024]{1,0:T(8,128)(2,1)}, /*index=5*/bf16[1024,1...) while((s32[]{:T(128)}, bf16[512,1024]{1,0:T(8,128)(2,1)}, s32[]{:T(128)}, ...), condition=%wide.region_1.2_spmd, body=%wide.region_0.1_spmd.sunk | while | flops 2097154 | bytes 22024316 | solution.py:366
  100.4 10.8 %body.1 = bf16[1024,1024]{1,0:T(8,128)(2,1)} custom-call(s32[49]{0:T(128)S(1)} %get-tuple-element.187.table_ref, bf16[512,1024]{1,0:T(8,128)(2,1)} %get-tuple-element.188.a_ref, bf16[1024,1024]{1,0:T(8,128)(2,1)} %get-tuple-element.189.b_ref, bf16[512,1024]{1,0:T(8,128)(2,1)} %get-tuple-element.190.c_ref, bf16[4096,1024]{1,0:T(8,128)(2,1)} %get-tuple-element.191.weight_ref, ...), custom_call_target="tpu_custom_call" | custom-call | bytes 12582912 | tf_op jit(solution)/shard_map/while/body/pallas_call | solution.py:289
  111.1 4.9 %all-to-all-start = ((bf16[2,512,1024]{2,1,0:T(8,128)(2,1)}), bf16[2,512,1024]{2,1,0:T(8,128)(2,1)}, u32[]{:S(2)}, u32[]{:S(2)}) async-start(bf16[2,512,1024]{2,1,0:T(8,128)(2,1)} %bitcast.21), calls=%async_computation | async-start | bytes 4194304 | tf_op jit(solution)/shard_map/while/body/all_to_all | solution.py:359
  116.0 3.0 %all-to-all-done = bf16[2,512,1024]{2,1,0:T(8,128)(2,1)} async-done(((bf16[2,512,1024]{2,1,0:T(8,128)(2,1)}), bf16[2,512,1024]{2,1,0:T(8,128)(2,1)}, u32[]{:S(2)}, u32[]{:S(2)}) %all-to-all-start) | async-done | bytes 2097184 | tf_op jit(solution)/shard_map/while/body/all_to_all | solution.py:359
  119.0 2.9 %fusion.12 = bf16[512,1024]{1,0:T(8,128)(2,1)} fusion(bf16[2,512,1024]{2,1,0:T(8,128)(2,1)} %all-to-all-done), kind=kLoop, calls=%fused_computation.1.clone.1 | loop fusion | flops 2097152 | bytes 3145728 | tf_op jit(solution)/shard_map/while/body/convert_element_type | solution.py:361
  125.7 2.2 %add_convert_fusion.2 = bf16[512,1024]{1,0:T(8,128)(2,1)S(1)} fusion(bf16[512,1024]{1,0:T(8,128)(2,1)} %collective-permute-done.7, bf16[512,1024]{1,0:T(8,128)(2,1)} %collective-permute-done.6, bf16[512,1024]{1,0:T(8,128)(2,1)S(1)} %shard_map.114), kind=kLoop, calls=%fused_computation.3 | loop fusion | flops 3145728 | bytes 4194304 | tf_op jit(solution)/shard_map/convert_element_type | solution.py:415
  130.7 4.5 %all-to-all-start.3 = ((bf16[4,128,1024]{2,1,0:T(8,128)(2,1)}), bf16[4,128,1024]{2,1,0:T(8,128)(2,1)S(1)}, u32[]{:S(2)}, u32[]{:S(2)}) async-start(bf16[4,128,1024]{2,1,0:T(8,128)(2,1)} %bitcast.11), calls=%async_computation.3 | async-start | bytes 2097152 | tf_op jit(solution)/shard_map/all_to_all | solution.py:381
  135.2 2.1 %collective-permute-done.8 = bf16[64,1024]{1,0:T(8,128)(2,1)} collective-permute-done((bf16[64,1024]{1,0:T(8,128)(2,1)}, bf16[64,1024]{1,0:T(8,128)(2,1)}, u32[]{:S(2)}, u32[]{:S(2)}) %collective-permute-start.8) | collective-permute-done | bytes 131104 | tf_op jit(solution)/shard_map/ppermute | solution.py:336
  138.4 2.2 %add_convert_fusion.1 = bf16[512,1024]{1,0:T(8,128)(2,1)S(1)} fusion(bf16[512,1024]{1,0:T(8,128)(2,1)} %collective-permute-done.11, bf16[512,1024]{1,0:T(8,128)(2,1)} %collective-permute-done.10, bf16[512,1024]{1,0:T(8,128)(2,1)S(1)} %shard_map.115), kind=kLoop, calls=%fused_computation.2 | loop fusion | flops 3145728 | bytes 4194304 | tf_op jit(solution)/shard_map/convert_element_type | solution.py:418
  140.9 2.0 %collective-permute-start.12 = (bf16[64,1024]{1,0:T(8,128)(2,1)S(1)}, bf16[64,1024]{1,0:T(8,128)(2,1)S(1)}, u32[]{:S(2)}, u32[]{:S(2)}) collective-permute-start(bf16[64,1024]{1,0:T(8,128)(2,1)S(1)} %get-tuple-element.108), channel_id=1, source_target_pairs={{0,8},{8,16},{16,24},{24,0},{1,9},{9,17},{17,25},{25,1},{2,10},{10... | collective-permute-start | bytes 393224 | tf_op jit(solution)/shard_map/ppermute | solution.py:336
  144.4 3.2 %collective-permute-start.17 = (bf16[128,1024]{1,0:T(8,128)(2,1)}, bf16[128,1024]{1,0:T(8,128)(2,1)S(1)}, u32[]{:S(2)}, u32[]{:S(2)}) collective-permute-start(bf16[128,1024]{1,0:T(8,128)(2,1)} %pad_maximum_fusion.7), channel_id=1, source_target_pairs={{0,96},{32,0},{64,32},{96,64},{1,97},{33,1},{65,33},{97,65},{2,98}... | collective-permute-start | bytes 786440 | tf_op jit(solution)/shard_map/ppermute | solution.py:348
  155.1 3.1 %collective-permute-done.13 = bf16[128,1024]{1,0:T(8,128)(2,1)S(1)} collective-permute-done((bf16[128,1024]{1,0:T(8,128)(2,1)}, bf16[128,1024]{1,0:T(8,128)(2,1)S(1)}, u32[]{:S(2)}, u32[]{:S(2)}) %collective-permute-start.13) | collective-permute-done | bytes 262176 | tf_op jit(solution)/shard_map/ppermute | solution.py:348
  (116 shorter events, 45.0 us)
Async XLA Ops:
  0.6 22.7 %copy-start.13 = (bf16[256,1024]{1,0:T(8,128)(2,1)S(1)}, bf16[256,1024]{1,0:T(8,128)(2,1)}, u32[]{:S(2)}) copy-start(bf16[256,1024]{1,0:T(8,128)(2,1)} %grad_ref.1) | copy-start | bytes 1572868
  2.4 20.9 %copy-start.16 = (f32[256]{0:T(256)S(1)}, f32[256]{0:T(256)}, u32[]{:S(2)}) copy-start(f32[256]{0:T(256)} %param.12) | copy-start | bytes 3076
  23.3 5.6 %collective-permute-start = (bf16[512,1024]{1,0:T(8,128)(2,1)S(1)}, bf16[512,1024]{1,0:T(8,128)(2,1)S(1)}, u32[]{:S(2)}, u32[]{:S(2)}) collective-permute-start(bf16[512,1024]{1,0:T(8,128)(2,1)S(1)} %bitcast.23), channel_id=1, source_target_pairs={{0,4},{4,0},{1,5},{5,1},{2,6},{6,2},{3,7},{7,3},{8,12},{12,8},{9,1... | collective-permute-start | bytes 3145736 | tf_op jit(solution)/shard_map/ppermute | solution.py:22
  24.9 23.7 %all-to-all-start.1 = ((bf16[4,128,1024]{2,1,0:T(8,128)(2,1)}), bf16[4,128,1024]{2,1,0:T(8,128)(2,1)S(1)}, u32[]{:S(2)}, u32[]{:S(2)}) async-start(bf16[4,128,1024]{2,1,0:T(8,128)(2,1)} %bitcast.29), calls=%async_computation.1 | async-start | bytes 2097152 | tf_op jit(solution)/shard_map/all_to_all | solution.py:381
  48.6 2.8 %collective-permute-start.1 = (bf16[512,1024]{1,0:T(8,128)(2,1)S(1)}, bf16[512,1024]{1,0:T(8,128)(2,1)S(1)}, u32[]{:S(2)}, u32[]{:S(2)}) collective-permute-start(bf16[512,1024]{1,0:T(8,128)(2,1)S(1)} %shard_map.106.own_ref.d_own), channel_id=1, source_target_pairs={{0,4},{4,0},{1,5},{5,1},{2,6},{6,2},{3,7},{7,3},{8,12},{12,8},{9,1... | collective-permute-start | bytes 3145736 | tf_op jit(solution)/shard_map/ppermute | solution.py:22
  53.5 17.3 %collective-permute-start.3 = (bf16[256,1024]{1,0:T(8,128)(2,1)}, bf16[256,1024]{1,0:T(8,128)(2,1)}, u32[]{:S(2)}, u32[]{:S(2)}) collective-permute-start(bf16[256,1024]{1,0:T(8,128)(2,1)} %get-tuple-element.70), channel_id=1, source_target_pairs={{0,24},{8,0},{16,8},{24,16},{1,25},{9,1},{17,9},{25,17},{2,26},{10... | collective-permute-start | bytes 1572872 | tf_op jit(solution)/shard_map/ppermute | solution.py:336
  56.2 15.4 %collective-permute-start.2 = (bf16[256,1024]{1,0:T(8,128)(2,1)}, bf16[256,1024]{1,0:T(8,128)(2,1)}, u32[]{:S(2)}, u32[]{:S(2)}) collective-permute-start(bf16[256,1024]{1,0:T(8,128)(2,1)} %get-tuple-element.66), channel_id=1, source_target_pairs={{0,8},{8,16},{16,24},{24,0},{1,9},{9,17},{17,25},{25,1},{2,10},{10... | collective-permute-start | bytes 1572872 | tf_op jit(solution)/shard_map/ppermute | solution.py:336
  64.8 22.8 %collective-permute-start.4 = (bf16[256,1024]{1,0:T(8,128)(2,1)S(1)}, bf16[256,1024]{1,0:T(8,128)(2,1)S(1)}, u32[]{:S(2)}, u32[]{:S(2)}) collective-permute-start(bf16[256,1024]{1,0:T(8,128)(2,1)S(1)} %get-tuple-element.69), channel_id=1, source_target_pairs={{0,32},{32,64},{64,96},{96,0},{1,33},{33,65},{65,97},{97,1},{2,34}... | collective-permute-start | bytes 1572872 | tf_op jit(solution)/shard_map/ppermute | solution.py:336
  66.5 21.1 %collective-permute-start.5 = (bf16[256,1024]{1,0:T(8,128)(2,1)S(1)}, bf16[256,1024]{1,0:T(8,128)(2,1)S(1)}, u32[]{:S(2)}, u32[]{:S(2)}) collective-permute-start(bf16[256,1024]{1,0:T(8,128)(2,1)S(1)} %get-tuple-element.73), channel_id=1, source_target_pairs={{0,96},{32,0},{64,32},{96,64},{1,97},{33,1},{65,33},{97,65},{2,98}... | collective-permute-start | bytes 1572872 | tf_op jit(solution)/shard_map/ppermute | solution.py:336
  74.3 51.4 %collective-permute-start.6 = (bf16[512,1024]{1,0:T(8,128)(2,1)}, bf16[512,1024]{1,0:T(8,128)(2,1)}, u32[]{:S(2)}, u32[]{:S(2)}) collective-permute-start(bf16[512,1024]{1,0:T(8,128)(2,1)} %pad_maximum_fusion), channel_id=1, source_target_pairs={{0,8},{8,16},{16,24},{24,0},{1,9},{9,17},{17,25},{25,1},{2,10},{10... | collective-permute-start | bytes 3145736 | tf_op jit(solution)/shard_map/ppermute | solution.py:348
  75.4 50.3 %collective-permute-start.7 = (bf16[512,1024]{1,0:T(8,128)(2,1)}, bf16[512,1024]{1,0:T(8,128)(2,1)}, u32[]{:S(2)}, u32[]{:S(2)}) collective-permute-start(bf16[512,1024]{1,0:T(8,128)(2,1)} %pad_maximum_fusion.1), channel_id=1, source_target_pairs={{0,24},{8,0},{16,8},{24,16},{1,25},{9,1},{17,9},{25,17},{2,26},{10... | collective-permute-start | bytes 3145736 | tf_op jit(solution)/shard_map/ppermute | solution.py:348
  90.1 48.2 %collective-permute-start.10 = (bf16[512,1024]{1,0:T(8,128)(2,1)}, bf16[512,1024]{1,0:T(8,128)(2,1)}, u32[]{:S(2)}, u32[]{:S(2)}) collective-permute-start(bf16[512,1024]{1,0:T(8,128)(2,1)} %pad_maximum_fusion.2), channel_id=1, source_target_pairs={{0,32},{32,64},{64,96},{96,0},{1,33},{33,65},{65,97},{97,1},{2,34}... | collective-permute-start | bytes 3145736 | tf_op jit(solution)/shard_map/ppermute | solution.py:348
  91.7 46.7 %collective-permute-start.11 = (bf16[512,1024]{1,0:T(8,128)(2,1)}, bf16[512,1024]{1,0:T(8,128)(2,1)}, u32[]{:S(2)}, u32[]{:S(2)}) collective-permute-start(bf16[512,1024]{1,0:T(8,128)(2,1)} %pad_maximum_fusion.3), channel_id=1, source_target_pairs={{0,96},{32,0},{64,32},{96,64},{1,97},{33,1},{65,33},{97,65},{2,98}... | collective-permute-start | bytes 3145736 | tf_op jit(solution)/shard_map/ppermute | solution.py:348
  99.6 23.0 %copy-start.9 = (bf16[512,1024]{1,0:T(8,128)(2,1)S(1)}, bf16[512,1024]{1,0:T(8,128)(2,1)}, u32[]{:S(2)}) copy-start(bf16[512,1024]{1,0:T(8,128)(2,1)} %copy-done.8) | copy-start | bytes 3145732
  111.1 7.8 %all-to-all-start = ((bf16[2,512,1024]{2,1,0:T(8,128)(2,1)}), bf16[2,512,1024]{2,1,0:T(8,128)(2,1)}, u32[]{:S(2)}, u32[]{:S(2)}) async-start(bf16[2,512,1024]{2,1,0:T(8,128)(2,1)} %bitcast.21), calls=%async_computation | async-start | bytes 4194304 | tf_op jit(solution)/shard_map/while/body/all_to_all | solution.py:359
  128.7 6.5 %collective-permute-start.9 = (bf16[64,1024]{1,0:T(8,128)(2,1)}, bf16[64,1024]{1,0:T(8,128)(2,1)}, u32[]{:S(2)}, u32[]{:S(2)}) collective-permute-start(bf16[64,1024]{1,0:T(8,128)(2,1)} %get-tuple-element.103), channel_id=1, source_target_pairs={{0,96},{32,0},{64,32},{96,64},{1,97},{33,1},{65,33},{97,65},{2,98}... | collective-permute-start | bytes 393224 | tf_op jit(solution)/shard_map/ppermute | solution.py:336
  130.5 6.8 %collective-permute-start.8 = (bf16[64,1024]{1,0:T(8,128)(2,1)}, bf16[64,1024]{1,0:T(8,128)(2,1)}, u32[]{:S(2)}, u32[]{:S(2)}) collective-permute-start(bf16[64,1024]{1,0:T(8,128)(2,1)} %get-tuple-element.104), channel_id=1, source_target_pairs={{0,32},{32,64},{64,96},{96,0},{1,33},{33,65},{65,97},{97,1},{2,34}... | collective-permute-start | bytes 393224 | tf_op jit(solution)/shard_map/ppermute | solution.py:336
  130.7 20.4 %all-to-all-start.3 = ((bf16[4,128,1024]{2,1,0:T(8,128)(2,1)}), bf16[4,128,1024]{2,1,0:T(8,128)(2,1)S(1)}, u32[]{:S(2)}, u32[]{:S(2)}) async-start(bf16[4,128,1024]{2,1,0:T(8,128)(2,1)} %bitcast.11), calls=%async_computation.3 | async-start | bytes 2097152 | tf_op jit(solution)/shard_map/all_to_all | solution.py:381
  140.6 7.0 %collective-permute-start.14 = (bf16[64,1024]{1,0:T(8,128)(2,1)S(1)}, bf16[64,1024]{1,0:T(8,128)(2,1)S(1)}, u32[]{:S(2)}, u32[]{:S(2)}) collective-permute-start(bf16[64,1024]{1,0:T(8,128)(2,1)S(1)} %get-tuple-element.107), channel_id=1, source_target_pairs={{0,24},{8,0},{16,8},{24,16},{1,25},{9,1},{17,9},{25,17},{2,26},{10... | collective-permute-start | bytes 393224 | tf_op jit(solution)/shard_map/ppermute | solution.py:336
  140.9 6.7 %collective-permute-start.12 = (bf16[64,1024]{1,0:T(8,128)(2,1)S(1)}, bf16[64,1024]{1,0:T(8,128)(2,1)S(1)}, u32[]{:S(2)}, u32[]{:S(2)}) collective-permute-start(bf16[64,1024]{1,0:T(8,128)(2,1)S(1)} %get-tuple-element.108), channel_id=1, source_target_pairs={{0,8},{8,16},{16,24},{24,0},{1,9},{9,17},{17,25},{25,1},{2,10},{10... | collective-permute-start | bytes 393224 | tf_op jit(solution)/shard_map/ppermute | solution.py:336
  143.6 8.8 %collective-permute-start.16 = (bf16[128,1024]{1,0:T(8,128)(2,1)}, bf16[128,1024]{1,0:T(8,128)(2,1)S(1)}, u32[]{:S(2)}, u32[]{:S(2)}) collective-permute-start(bf16[128,1024]{1,0:T(8,128)(2,1)} %pad_maximum_fusion.6), channel_id=1, source_target_pairs={{0,32},{32,64},{64,96},{96,0},{1,33},{33,65},{65,97},{97,1},{2,34}... | collective-permute-start | bytes 786440 | tf_op jit(solution)/shard_map/ppermute | solution.py:348
  144.4 8.0 %collective-permute-start.17 = (bf16[128,1024]{1,0:T(8,128)(2,1)}, bf16[128,1024]{1,0:T(8,128)(2,1)S(1)}, u32[]{:S(2)}, u32[]{:S(2)}) collective-permute-start(bf16[128,1024]{1,0:T(8,128)(2,1)} %pad_maximum_fusion.7), channel_id=1, source_target_pairs={{0,96},{32,0},{64,32},{96,64},{1,97},{33,1},{65,33},{97,65},{2,98}... | collective-permute-start | bytes 786440 | tf_op jit(solution)/shard_map/ppermute | solution.py:348
  148.4 6.7 %collective-permute-start.15 = (bf16[128,1024]{1,0:T(8,128)(2,1)}, bf16[128,1024]{1,0:T(8,128)(2,1)}, u32[]{:S(2)}, u32[]{:S(2)}) collective-permute-start(bf16[128,1024]{1,0:T(8,128)(2,1)} %pad_maximum_fusion.5), channel_id=1, source_target_pairs={{0,24},{8,0},{16,8},{24,16},{1,25},{9,1},{17,9},{25,17},{2,26},{10... | collective-permute-start | bytes 786440 | tf_op jit(solution)/shard_map/ppermute | solution.py:348
  150.4 7.8 %collective-permute-start.13 = (bf16[128,1024]{1,0:T(8,128)(2,1)}, bf16[128,1024]{1,0:T(8,128)(2,1)S(1)}, u32[]{:S(2)}, u32[]{:S(2)}) collective-permute-start(bf16[128,1024]{1,0:T(8,128)(2,1)} %pad_maximum_fusion.4), channel_id=1, source_target_pairs={{0,8},{8,16},{16,24},{24,0},{1,9},{9,17},{17,25},{25,1},{2,10},{10... | collective-permute-start | bytes 786440 | tf_op jit(solution)/shard_map/ppermute | solution.py:348
  (18 other events, 75.1 us)

commit v2 on v1

v2 whole, which is shorter than its diff:
```python
import math

import jax
import jax.numpy as jnp
from jax import lax
from jax.experimental import pallas as pl
from jax.experimental.pallas import tpu as pltpu
from jax.sharding import Mesh, PartitionSpec as P

BF16 = jnp.bfloat16
F32 = jnp.float32
VMEM_LIMIT = 28 * 1024 * 1024
ORDER = (2, 1, 3, 0)
INVERSE = (3, 1, 0, 2)


def ring(step):
    return [(i, (i + step) % 4) for i in range(4)]


def swap_core(array):
    return lax.ppermute(array, "core", [(0, 1), (1, 0)])


def params():
    return pltpu.CompilerParams(vmem_limit_bytes=VMEM_LIMIT)


def cost(nbytes=1024):
    return pl.CostEstimate(flops=0, bytes_accessed=int(nbytes), transcendentals=0)


def shape(rows, cols, dtype=BF16):
    return jax.ShapeDtypeStruct((rows, cols), dtype)


def dot_nt(a, b):
    return lax.dot_general(a, b, (((1,), (1,)), ((), ())), preferred_element_type=F32)


def dot_nn(a, b):
    return lax.dot_general(a, b, (((1,), (0,)), ((), ())), preferred_element_type=F32)


def dot_tn(a, b):
    return lax.dot_general(a, b, (((0,), (0,)), ((), ())), preferred_element_type=F32)


def gelu_parts(pre_act):
    root_two_pi = 0.7978845608028654
    square = pre_act * pre_act
    inner = pre_act * (root_two_pi + root_two_pi * 0.044715 * square)
    halved = 0.5 + 0.5 * jnp.tanh(inner)
    value = pre_act * halved
    slope_of_inner = 2.0 * root_two_pi + 6.0 * root_two_pi * 0.044715 * square
    return value, halved + value * (1.0 - halved) * slope_of_inner


VMEM = pl.BlockSpec(memory_space=pltpu.VMEM)
ANY = pl.BlockSpec(memory_space=pl.ANY)


def dispatch_tokens(where, region, tokens):
    n, width = tokens.shape

    def body(where_ref, region_ref, tok_ref, place_ref, *outs):
        dest = jnp.bitwise_and(region_ref[...] - where_ref[0] + 4, 3)
        onehot = (dest == lax.broadcasted_iota(jnp.int32, (8, n), 0)).astype(F32)
        upper = (
            lax.broadcasted_iota(jnp.int32, (n, n), 0) < lax.broadcasted_iota(jnp.int32, (n, n), 1)
        ).astype(F32)
        before = dot_nn(onehot.astype(BF16), upper.astype(BF16))
        rank = jnp.sum(before * onehot, axis=0, keepdims=True).astype(jnp.int32)
        slot = dest * 128 + rank
        place = (slot == lax.broadcasted_iota(jnp.int32, (512, n), 0)).astype(F32).astype(BF16)
        place_ref[...] = place
        for r, out in enumerate(outs):
            out[...] = dot_nn(place[r * 128 : (r + 1) * 128], tok_ref[...]).astype(BF16)

    return pl.pallas_call(
        body,
        out_shape=[shape(512, n)] + [shape(128, width)] * 4,
        in_specs=[pl.BlockSpec(memory_space=pltpu.SMEM)] + [VMEM] * 2,
        out_specs=[VMEM] * 5,
        compiler_params=params(),
        cost_estimate=cost(4 * n * width * 2),
    )(where, region, tokens)


def dispatch_grads(place, gate, grads):
    n, width = grads.shape

    def body(place_ref, gate_ref, grad_ref, *outs):
        column = jnp.transpose(jnp.broadcast_to(gate_ref[...], (128, n)))[:, :1]
        scaled = (column * grad_ref[...].astype(F32)).astype(BF16)
        for r, out in enumerate(outs):
            out[...] = dot_nn(place_ref[r * 128 : (r + 1) * 128, :], scaled).astype(BF16)

    return pl.pallas_call(
        body,
        out_shape=[shape(128, width)] * 4,
        in_specs=[VMEM] * 3,
        out_specs=[VMEM] * 4,
        compiler_params=params(),
        cost_estimate=cost(4 * n * width * 2),
    )(place, gate, grads)


HBM = pl.BlockSpec(memory_space=pltpu.HBM)


def block_scratch(width, count):
    return [pltpu.VMEM((512 * count, width), BF16), pltpu.SemaphoreType.DMA((4 * count,))]


def block_group(table_ref, weight_ref, w_buf, sems, offset, count):
    step = pl.program_id(0)

    def fetch(k):
        block = pl.multiple_of(table_ref[offset + k] * 128, 128)
        place = pl.multiple_of(k * 128, 128)
        return pltpu.make_async_copy(
            weight_ref.at[pl.ds(block, 128), :], w_buf.at[pl.ds(place, 128), :], sems.at[k]
        )

    @pl.when(step == 0)
    def _():
        for k in range(4 * count):
            fetch(k).start()

    for q in range(4):
        fetch(4 * step + q).wait()
    return w_buf.at[pl.ds(pl.multiple_of(step * 512, 512), 512), :]


def after(array, *others):
    def body(*refs):
        del refs

    return pl.pallas_call(
        body,
        in_specs=[ANY] * (1 + len(others)),
        out_specs=ANY,
        out_shape=jax.ShapeDtypeStruct(array.shape, array.dtype),
        input_output_aliases={0: 0},
        compiler_params=params(),
        cost_estimate=cost(),
    )(array, *others)


MARK = jax.ShapeDtypeStruct((8, 128), F32)
MARK_SPEC = pl.BlockSpec((8, 128), lambda i, *_: (0, 0))


def fixed(rows, cols):
    return pl.BlockSpec((rows, cols), lambda i, *_: (0, 0))


def merge(table_ref, part_refs, all_ref):
    for k, ref in enumerate(part_refs):
        begin = pl.multiple_of(k // 4 * 512 + table_ref[48 + k % 4] * 128, 128)
        all_ref[pl.ds(begin, 128), :] = ref[...]


def forward(table, parts, weight):
    width = weight.shape[1]
    tok = 128 * len(parts)

    def body(table_ref, *refs):
        part_refs, weight_ref = refs[: len(parts)], refs[len(parts)]
        act_ref, slope_ref, all_ref, mark_ref, w_buf, sems = refs[len(parts) + 1 :]

        @pl.when(pl.program_id(0) == 0)
        def _():
            mark_ref[...] = jnp.zeros_like(mark_ref)
            merge(table_ref, part_refs, all_ref)

        w_ref = block_group(table_ref, weight_ref, w_buf, sems, 0, 4)
        for c in range(tok // 256):
            cols = slice(c * 256, (c + 1) * 256)
            act, slope = gelu_parts(dot_nt(w_ref[...], all_ref[cols, :]))
            act_ref[:, cols] = act.astype(BF16)
            slope_ref[:, cols] = slope.astype(BF16)

    return pl.pallas_call(
        body,
        grid_spec=pltpu.PrefetchScalarGridSpec(
            num_scalar_prefetch=1,
            grid=(4,),
            in_specs=[VMEM] * len(parts) + [HBM],
            out_specs=[pl.BlockSpec((512, tok), lambda i, *_: (i, 0))] * 2
            + [fixed(tok, width), MARK_SPEC],
            scratch_shapes=block_scratch(width, 4),
        ),
        out_shape=[pltpu.HBM((2048, tok), BF16)] * 2 + [shape(tok, width), MARK],
        compiler_params=params(),
        cost_estimate=cost(2**24),
    )(table, *parts, weight)


def outer_first(table, act, parts):
    width = parts[0].shape[1]
    tok = 128 * len(parts)

    def body(table_ref, act_ref, *refs):
        part_refs, (low_ref, high_ref, all_ref, mark_ref) = refs[: len(parts)], refs[len(parts) :]
        mark_ref[...] = jnp.zeros_like(mark_ref)
        merge(table_ref, part_refs, all_ref)
        low_ref[...] = dot_nn(act_ref[:256, :], all_ref[...]).astype(BF16)
        high_ref[...] = dot_nn(act_ref[256:, :], all_ref[...]).astype(BF16)

    return pl.pallas_call(
        body,
        grid_spec=pltpu.PrefetchScalarGridSpec(
            num_scalar_prefetch=1,
            grid=(1,),
            in_specs=[fixed(512, tok)] + [VMEM] * len(parts),
            out_specs=[fixed(256, width)] * 2 + [fixed(tok, width), MARK_SPEC],
        ),
        out_shape=[shape(256, width)] * 2 + [shape(tok, width), MARK],
        compiler_params=params(),
        cost_estimate=cost(2**22),
    )(table, act, *parts)


def outer_rest(act, rows, first, count, deps):
    tok, width = rows.shape

    def body(act_ref, rows_ref, *refs):
        out_ref = refs[len(deps)]
        out_ref[...] = dot_nn(act_ref[...], rows_ref[...]).astype(BF16)

    return pl.pallas_call(
        body,
        grid=(count,),
        in_specs=[pl.BlockSpec((512, tok), lambda i: (i + first, 0)), VMEM] + [ANY] * len(deps),
        out_specs=pl.BlockSpec((512, width), lambda i: (i, 0)),
        out_shape=shape(512 * count, width),
        compiler_params=params(),
        cost_estimate=cost(2**20 * (2 + 2 * count)),
    )(act, rows, *deps)


def backward(table, grads, rows, slope, weight, first, count, deps):
    tok, width = rows.shape
    split = first == 0

    def body(table_ref, grads_ref, rows_ref, slope_ref, weight_ref, *refs):
        pre_ref, *outs, mark_ref, w_buf, w_sems, s_buf, s_sems = refs[len(deps) :]
        mark_ref[...] = jnp.zeros_like(mark_ref)
        w_ref = block_group(table_ref, weight_ref, w_buf, w_sems, 16 + 4 * first, count)
        s_ref = block_group(table_ref, slope_ref, s_buf, s_sems, 32 + 4 * first, count)
        for c in range(tok // 256):
            cols = slice(c * 256, (c + 1) * 256)
            act_grad = dot_nt(w_ref[...], grads_ref[cols, :])
            pre_ref[:, cols] = (act_grad * s_ref[:, cols].astype(F32)).astype(BF16)
        span = 512 // len(outs)
        for k, out in enumerate(outs):
            out[...] = dot_nn(pre_ref[k * span : (k + 1) * span, :], rows_ref[...]).astype(BF16)

    def groups(cols):
        return pl.BlockSpec((512, cols), lambda i, *_: (i, 0))

    return pl.pallas_call(
        body,
        grid_spec=pltpu.PrefetchScalarGridSpec(
            num_scalar_prefetch=1,
            grid=(count,),
            in_specs=[VMEM] * 2 + [HBM] * 2 + [ANY] * len(deps),
            out_specs=[groups(tok)]
            + ([fixed(256, width)] * 2 if split else [groups(width)])
            + [MARK_SPEC],
            scratch_shapes=block_scratch(width, count) + block_scratch(tok, count),
        ),
        out_shape=[shape(512 * count, tok)]
        + ([shape(256, width)] * 2 if split else [shape(512 * count, width)])
        + [MARK],
        compiler_params=params(),
        cost_estimate=cost(2**20 * (2 + 4 * count)),
    )(table, grads, rows, slope, weight, *deps)


def row_gradients(table, pre, weight, deps):
    width = weight.shape[1]
    rows = 512

    def body(table_ref, a_ref, b_ref, c_ref, weight_ref, *refs):
        own_ref, other_ref, w_buf, sems, total = refs[len(deps) :]
        step = pl.program_id(0)
        w_ref = block_group(table_ref, weight_ref, w_buf, sems, 16, 4)

        @pl.when(step == 0)
        def _():
            total[...] = dot_tn(a_ref[...], w_ref[...])

        @pl.when(jnp.logical_and(step > 0, step < 3))
        def _():
            begin = pl.multiple_of((step - 1) * 512, 512)
            total[...] += dot_tn(b_ref[pl.ds(begin, 512), :], w_ref[...])

        @pl.when(step == 3)
        def _():
            final = (total[...] + dot_tn(c_ref[...], w_ref[...])).astype(BF16)
            own_ref[...] = final[:rows]
            other_ref[...] = final[rows:]

    return pl.pallas_call(
        body,
        grid_spec=pltpu.PrefetchScalarGridSpec(
            num_scalar_prefetch=1,
            grid=(4,),
            in_specs=[VMEM] * 3 + [HBM] + [ANY] * len(deps),
            out_specs=[fixed(rows, width)] * 2,
            scratch_shapes=block_scratch(width, 4) + [pltpu.VMEM((2 * rows, width), F32)],
        ),
        out_shape=[shape(rows, width)] * 2,
        compiler_params=params(),
        cost_estimate=cost(2**23 + 2**22),
    )(table, *pre, weight, *deps)


def join(sides, arrived):
    n, width = sides.shape
    h = n // 4

    def body(sides_ref, from_next, from_prev, up_ref, down_ref, mark_ref):
        mark_ref[...] = jnp.zeros_like(mark_ref)
        up_ref[:h, :] = sides_ref[:h, :]
        up_ref[h:, :] = add(sides_ref[h : 2 * h, :], from_prev[...]).astype(BF16)
        down_ref[:h, :] = add(sides_ref[2 * h : 3 * h, :], from_next[...]).astype(BF16)
        down_ref[h:, :] = sides_ref[3 * h :, :]

    return pl.pallas_call(
        body,
        out_shape=[shape(2 * h, width)] * 2 + [MARK],
        in_specs=[VMEM] * 3,
        out_specs=[VMEM] * 3,
        compiler_params=params(),
        cost_estimate=cost(4 * n * width),
    )(sides, *arrived)


def restore_order(where, place, rows):
    n, width = place.shape[1], rows.shape[1]

    def body(where_ref, place_ref, rows_ref, out_ref):
        total = jnp.zeros((n, width), F32)
        for e in range(4):
            bucket = pl.multiple_of(jnp.bitwise_and(e - where_ref[0] + 4, 3) * 128, 128)
            total += dot_tn(place_ref[pl.ds(bucket, 128), :], rows_ref[e * 128 : (e + 1) * 128, :])
        out_ref[...] = total.astype(BF16)

    return pl.pallas_call(
        body,
        out_shape=shape(n, width),
        in_specs=[pl.BlockSpec(memory_space=pltpu.SMEM)] + [VMEM] * 2,
        out_specs=VMEM,
        compiler_params=params(),
        cost_estimate=cost(2**21),
    )(where, place, rows)


def add(*terms):
    total = terms[0].astype(F32)
    for term in terms[1:]:
        total = total + term.astype(F32)
    return total


def first_hop(low, high, axis):
    return lax.ppermute(low, axis, ring(3)), lax.ppermute(high, axis, ring(1))


def second_hop(up, down, axis):
    return lax.ppermute(up, axis, ring(1)), lax.ppermute(down, axis, ring(3))


def combine(own, received):
    n, width = own.shape
    q = n // 4

    def body(own_ref, left, right, keep_ref, sides_ref, low_ref, high_ref, mark_ref):
        mark_ref[...] = jnp.zeros_like(mark_ref)

        def total(begin, end):
            span = slice(begin, end)
            return add(own_ref[span, :], left[span, :], right[span, :]).astype(BF16)

        low_ref[...] = total(2 * q, 2 * q + q // 2)
        high_ref[...] = total(2 * q + q // 2, 3 * q)
        keep_ref[...] = total(0, q)
        sides_ref[:q, :] = total(q, 2 * q)
        sides_ref[q:, :] = total(3 * q, n)

    return pl.pallas_call(
        body,
        out_shape=[shape(q, width), shape(2 * q, width), shape(q // 2, width), shape(q // 2, width), MARK],
        in_specs=[VMEM] * 3,
        out_specs=[VMEM] * 5,
        compiler_params=params(),
        cost_estimate=cost(8 * n * width),
    )(own, *received)


def in_hbm(array):
    return pltpu.with_memory_space_constraint(array, pltpu.HBM)


def sum_cores(own, other):
    return add(own, swap_core(other)).astype(BF16)


def once(index, work, start):
    trips = 1 + jnp.minimum(index, 0)
    return lax.fori_loop(0, trips, lambda _, array: work(array), start)


def local(tokens, out_grad, gate, region, w_in, w_out):
    expert = lax.axis_index("expert").astype(jnp.int32)
    x, y, core = (lax.axis_index(a).astype(jnp.int32) for a in ("x", "y", "core"))
    scale = 1.0 / math.sqrt(float(tokens.shape[0] * lax.axis_size(("y", "x", "core"))))
    order = jnp.array(ORDER, jnp.int32)
    every = jnp.arange(4, dtype=jnp.int32)
    by_x = ((((y + every[None, :]) % 4) * 4 + (x + order[:, None]) % 4) * 2 + core).reshape(16)
    by_y = ((((y + order[:, None]) % 4) * 4 + (x + every[None, :]) % 4) * 2 + core).reshape(16)
    same = jnp.array([INVERSE[q] * 4 + ORDER[p] for p in range(4) for q in range(4)], jnp.int32)
    table = jnp.concatenate([by_x, by_y, same, (expert - every) % 4])
    weight_in, weight_out = in_hbm(w_in[0]), in_hbm(w_out[0])

    place, *send_x = dispatch_tokens(expert[None], region.reshape(1, -1), tokens)
    send_d = dispatch_grads(place, gate.reshape(1, -1), out_grad)

    def to_owner(parts):
        return [parts[0]] + [lax.ppermute(parts[r], "expert", ring(r)) for r in (1, 2, 3)]

    own_x = to_owner(send_x)
    both_x = own_x + [swap_core(p) for p in own_x]
    own_d = to_owner(send_d)
    act, slope, rows_x, mark = forward(table, both_x, weight_in)
    act, slope = in_hbm(act), in_hbm(slope)
    own_d = [after(part, mark) for part in own_d]
    both_d = own_d + [swap_core(p) for p in own_d]

    out_low, out_high, rows_d, mark = outer_first(table, act, both_d)
    hop = first_hop(out_low, out_high, "x")
    pre_a, in_low, in_high, mark = backward(
        table, rows_d, rows_x, slope, weight_out, 0, 1, (mark,)
    )
    out_sides = outer_rest(act, rows_d, 1, 2, (mark,))
    *pair, mark = join(out_sides, hop)
    out_parts = second_hop(*pair, "x")
    hop = first_hop(in_low, in_high, "y")
    pre_b, in_sides, mark = backward(table, rows_d, rows_x, slope, weight_out, 1, 2, (mark,))
    *pair, mark = join(in_sides, hop)
    in_parts = second_hop(*pair, "y")
    pre_c, in_own, mark = backward(table, rows_d, rows_x, slope, weight_out, 3, 1, (mark,))
    out_own = outer_rest(act, rows_d, 3, 1, (mark,))
    own = once(
        x,
        lambda start: sum_cores(
            *row_gradients(table, (pre_a, pre_b, pre_c), weight_in, (start,))
        ),
        out_own,
    )
    back = lax.all_to_all(own, "expert", split_axis=0, concat_axis=0, tiled=True)

    keep, sides, low, high, mark = combine(out_own, out_parts)
    *pair, mark = join(sides, first_hop(low, high, "y"))
    grad_out = add(keep, *second_hop(*pair, "y")) * scale
    keep, sides, low, high, _ = combine(after(in_own, mark), in_parts)
    *pair, _ = join(sides, first_hop(low, high, "x"))
    grad_in = add(keep, *second_hop(*pair, "x")) * scale
    token_grad = restore_order(expert[None], place, back)
    return token_grad, grad_in[None], grad_out[None]


def solution(mesh):
    chips = Mesh(mesh.devices.reshape(4, 4, 2, 4), ("y", "x", "core", "expert"))
    rows = ("y", "x", "core", "expert")
    plane = ("y", "x", "core")
    return jax.shard_map(
        local,
        mesh=chips,
        in_specs=(
            P(rows, None),
            P(rows, None),
            P(rows),
            P(rows, None),
            P("expert", None, None),
            P("expert", None, None),
        ),
        out_specs=(P(rows, None), P("expert", plane, None), P("expert", plane, None)),
        check_vma=False,
    )
```

time: 161 us -> 148 us (0.919)
  blocking collectives: 20.3 us -> 0 us
  other arithmetic: 20.5 us -> 7.97 us
  waiting for transfers between devices: 13.2 us -> 24.9 us
  Pallas kernels: 53.5 us -> 64.8 us
  local copies, waits for them, and re-layouts: 16 us -> 5.29 us
  starting transfers between devices: 35.5 us -> 43 us
    all_to_all x1 -> x0, blocking collectives: 20.3 us -> none  [exchange(): lax.all_to_all(array, 'expert', split_axis=0, concat_axis=0, tiled=True)]
    pallas_call x6 -> x12, Pallas kernels: 8.29 us -> 23.1 us  [the longest x2 6.61 us: outer_rest(): pl.pallas_call(body, grid=(count,), in_specs=[pl.BlockSpec((512, tok), la...]
    ppermute x0 -> x6, starting transfers between devices: none -> 14.6 us  [to_owner(): lax.ppermute(parts[r], 'expert', ring(r))]
    ppermute x8, waiting for transfers between devices: 3.03 us -> 15.1 us  [first_hop(): return (lax.ppermute(low, axis, ring(3)), lax.ppermute(high, axis, ring(1)))]
    all_to_all x3 -> x1, starting transfers between devices: 12.8 us -> 3.51 us  [local(): lax.all_to_all(own, 'expert', split_axis=0, concat_axis=0, tiled=True)]
    convert_element_type x7 -> x1, other arithmetic: 10.4 us -> 2.6 us  [sum_cores(): return add(own, swap_core(other)).astype(BF16)]
    unnamed x42 -> x21, local copies, waits for them, and re-layouts: 11.7 us -> 5.13 us
    concatenate x9 -> x1, other arithmetic: 7.15 us -> 0.73 us  [local(): table = jnp.concatenate([by_x, by_y, same, (expert - every) % 4])]
  transfers between devices with their start and end apart: 21 -> 32, of which waited for: 6 -> 14; matrix products, arithmetic and copies ran while one was open for 14% -> 5% of each run, Pallas kernels for 32% -> 34%
where the time goes in v2:
time: 148 us; the launch traced here: 147 us
  Pallas kernels  64.8 us (44%)
  starting transfers between devices  43 us (29%)
  waiting for transfers between devices  24.9 us (17%)
  other arithmetic  7.97 us (5%)
  local copies, waits for them, and re-layouts  5.29 us (4%)
    pallas_call x3, Pallas kernels, backward(): pl.pallas_call(body, grid_spec=pltpu.PrefetchScalarGridSpec(num_scalar_pr...  19.6 us
    ppermute x8, waiting for transfers between devices, first_hop(): return (lax.ppermute(low, axis, ring(3)), lax.ppermute(high, axis, ring(1)))  15.1 us
    ppermute x6, starting transfers between devices, to_owner(): lax.ppermute(parts[r], 'expert', ring(r))  14.6 us
    ppermute x8, starting transfers between devices, second_hop(): return (lax.ppermute(up, axis, ring(1)), lax.ppermute(down, axis, ring(3)))  13.1 us
    pallas_call x1, Pallas kernels, forward(): pl.pallas_call(body, grid_spec=pltpu.PrefetchScalarGridSpec(num_scalar_pr...  11.8 us
    pallas_call x1, Pallas kernels, row_gradients(): pl.pallas_call(body, grid_spec=pltpu.PrefetchScalarGridSpec(num_scalar_pr...  10.4 us
    ppermute x8, starting transfers between devices, first_hop(): return (lax.ppermute(low, axis, ring(3)), lax.ppermute(high, axis, ring(1)))  10.2 us
    pallas_call x2, Pallas kernels, outer_rest(): pl.pallas_call(body, grid=(count,), in_specs=[pl.BlockSpec((512, tok), la...  6.61 us
  transfers between devices with their start and end apart: 32, of which 14 were waited for; matrix products, arithmetic and copies ran while one was open for 5% of the time, Pallas kernels for 34%

profile of v2, /device:TPU:0, one launch (start us, length us, event | category | flops | bytes accessed | tf_op | source)
XLA Modules:
  0.0 146.9 jit_solution(8919995245288487487)
XLA Ops:
  5.1 3.6 %collective-permute-start.2 = (bf16[128,1024]{1,0:T(8,128)(2,1)S(1)}, bf16[128,1024]{1,0:T(8,128)(2,1)S(1)}, u32[]{:S(2)}, u32[]{:S(2)}) collective-permute-start(bf16[128,1024]{1,0:T(8,128)(2,1)S(1)} %get-tuple-element.96), channel_id=1, source_target_pairs={{0,2},{1,3},{2,0},{3,1},{4,6},{5,7},{6,4},{7,5},{8,10},{9,11},{10,... | collective-permute-start | bytes 786440 | tf_op jit(solution)/shard_map/ppermute | solution.py:434
  10.3 3.2 %collective-permute-done.1.refs_1_ = bf16[128,1024]{1,0:T(8,128)(2,1)S(1)} collective-permute-done((bf16[128,1024]{1,0:T(8,128)(2,1)S(1)}, bf16[128,1024]{1,0:T(8,128)(2,1)S(1)}, u32[]{:S(2)}, u32[]{:S(2)}) %collective-permute-start.1) | collective-permute-done | bytes 262176 | tf_op jit(solution)/shard_map/ppermute | solution.py:434
  16.7 2.9 %collective-permute-start.10 = (bf16[128,1024]{1,0:T(8,128)(2,1)}, bf16[128,1024]{1,0:T(8,128)(2,1)S(1)}, u32[]{:S(2)}, u32[]{:S(2)}) collective-permute-start(bf16[128,1024]{1,0:T(8,128)(2,1)} %get-tuple-element.103), channel_id=1, source_target_pairs={{0,3},{1,0},{2,1},{3,2},{4,7},{5,4},{6,5},{7,6},{8,11},{9,8},{10,9... | collective-permute-start | bytes 786440 | tf_op jit(solution)/shard_map/ppermute | solution.py:434
  20.3 3.6 %collective-permute-start.9 = (bf16[128,1024]{1,0:T(8,128)(2,1)}, bf16[128,1024]{1,0:T(8,128)(2,1)S(1)}, u32[]{:S(2)}, u32[]{:S(2)}) collective-permute-start(bf16[128,1024]{1,0:T(8,128)(2,1)} %get-tuple-element.102), channel_id=1, source_target_pairs={{0,2},{1,3},{2,0},{3,1},{4,6},{5,7},{6,4},{7,5},{8,10},{9,11},{10,... | collective-permute-start | bytes 786440 | tf_op jit(solution)/shard_map/ppermute | solution.py:434
  27.2 11.8 %shard_map.104 = (bf16[2048,1024]{1,0:T(8,128)(2,1)}, bf16[2048,1024]{1,0:T(8,128)(2,1)}, bf16[1024,1024]{1,0:T(8,128)(2,1)S(1)}, f32[8,128]{1,0:T(8,128)S(1)}) custom-call(s32[52]{0:T(128)S(1)} %pad_add_fusion.table_ref, bf16[128,1024]{1,0:T(8,128)(2,1)S(1)} %get-tuple-element.94.refs_0_, bf16[128,1024]{1,0:T(8,128)(2,1)S(1)} %collective-permute-done.1.refs_1_, ...), custom_call_target="tpu_custom_call" | custom-call | bytes 16777216 | tf_op jit(solution)/shard_map/pallas_call | solution.py:185
  41.7 4.0 %shard_map.110 = (bf16[256,1024]{1,0:T(8,128)(2,1)}, bf16[256,1024]{1,0:T(8,128)(2,1)}, bf16[1024,1024]{1,0:T(8,128)(2,1)S(1)}, f32[8,128]{1,0:T(8,128)S(1)}) custom-call(s32[52]{0:T(128)S(1)} %pad_add_fusion.table_ref, bf16[2048,1024]{1,0:T(8,128)(2,1)} %get-tuple-element.98.act_ref, bf16[128,1024]{1,0:T(8,128)(2,1)S(1)} %shard_map.106.refs_0_, ...), custom_call_target="tpu_custom_call" | custom-call | bytes 4194304 | tf_op jit(solution)/shard_map/pallas_call | solution.py:212
  45.7 2.8 %collective-permute-start.15 = (bf16[256,1024]{1,0:T(8,128)(2,1)}, bf16[256,1024]{1,0:T(8,128)(2,1)}, u32[]{:S(2)}, u32[]{:S(2)}) collective-permute-start(bf16[256,1024]{1,0:T(8,128)(2,1)} %get-tuple-element.109), channel_id=1, source_target_pairs={{0,24},{8,0},{16,8},{24,16},{1,25},{9,1},{17,9},{25,17},{2,26},{10... | collective-permute-start | bytes 1572872 | tf_op jit(solution)/shard_map/ppermute | solution.py:371
  48.4 6.2 %shard_map.111 = (bf16[512,1024]{1,0:T(8,128)(2,1)}, bf16[256,1024]{1,0:T(8,128)(2,1)}, bf16[256,1024]{1,0:T(8,128)(2,1)}, f32[8,128]{1,0:T(8,128)S(1)}) custom-call(s32[52]{0:T(128)S(1)} %pad_add_fusion.table_ref, bf16[1024,1024]{1,0:T(8,128)(2,1)S(1)} %get-tuple-element.104.grads_ref.rows_ref, bf16[1024,1024]{1,0:T(8,128)(2,1)S(1)} %get-tuple-element.105.rows_ref, ...), custom_call_target="tpu_custom_call" | custom-call | bytes 6291456 | tf_op jit(solution)/shard_map/pallas_call | solution.py:264
  54.6 3.1 %collective-permute-start.17 = (bf16[256,1024]{1,0:T(8,128)(2,1)}, bf16[256,1024]{1,0:T(8,128)(2,1)S(1)}, u32[]{:S(2)}, u32[]{:S(2)}) collective-permute-start(bf16[256,1024]{1,0:T(8,128)(2,1)} %get-tuple-element.113), channel_id=1, source_target_pairs={{0,96},{32,0},{64,32},{96,64},{1,97},{33,1},{65,33},{97,65},{2,98}... | collective-permute-start | bytes 1572872 | tf_op jit(solution)/shard_map/ppermute | solution.py:371
  57.7 3.8 %shard_map.112.sides_ref = bf16[1024,1024]{1,0:T(8,128)(2,1)S(1)} custom-call(bf16[2048,1024]{1,0:T(8,128)(2,1)} %get-tuple-element.98.act_ref, bf16[1024,1024]{1,0:T(8,128)(2,1)S(1)} %get-tuple-element.104.grads_ref.rows_ref, f32[8,128]{1,0:T(8,128)S(1)} %get-tuple-element.108.refs_0_), custom_call_target="tpu_custom_call" | custom-call | bytes 6291456 | tf_op jit(solution)/shard_map/pallas_call | solution.py:233
  63.7 2.8 %shard_map.113 = (bf16[512,1024]{1,0:T(8,128)(2,1)}, bf16[512,1024]{1,0:T(8,128)(2,1)}, f32[8,128]{1,0:T(8,128)S(1)}) custom-call(bf16[1024,1024]{1,0:T(8,128)(2,1)S(1)} %shard_map.112.sides_ref, bf16[256,1024]{1,0:T(8,128)(2,1)} %collective-permute-done.15.from_next, bf16[256,1024]{1,0:T(8,128)(2,1)} %collective-permute-done.16.from_prev), custom_call_target="tpu_custom_call" | custom-call | bytes 4194304 | tf_op jit(solution)/shard_map/pallas_call | solution.py:333
  66.4 8.0 %shard_map.114 = (bf16[1024,1024]{1,0:T(8,128)(2,1)}, bf16[1024,1024]{1,0:T(8,128)(2,1)S(1)}, f32[8,128]{1,0:T(8,128)}) custom-call(s32[52]{0:T(128)S(1)} %pad_add_fusion.table_ref, bf16[1024,1024]{1,0:T(8,128)(2,1)S(1)} %get-tuple-element.104.grads_ref.rows_ref, bf16[1024,1024]{1,0:T(8,128)(2,1)S(1)} %copy-done.1, ...), custom_call_target="tpu_custom_call" | custom-call | bytes 10485760 | tf_op jit(solution)/shard_map/pallas_call | solution.py:264
  76.0 5.4 %shard_map.116 = (bf16[512,1024]{1,0:T(8,128)(2,1)}, bf16[512,1024]{1,0:T(8,128)(2,1)S(1)}, f32[8,128]{1,0:T(8,128)S(1)}) custom-call(s32[52]{0:T(128)S(1)} %pad_add_fusion.table_ref, bf16[1024,1024]{1,0:T(8,128)(2,1)S(1)} %get-tuple-element.104.grads_ref.rows_ref, bf16[1024,1024]{1,0:T(8,128)(2,1)S(1)} %copy-done.1, ...), custom_call_target="tpu_custom_call" | custom-call | bytes 6291456 | tf_op jit(solution)/shard_map/pallas_call | solution.py:264
  81.4 2.9 %shard_map.117.own_ref = bf16[512,1024]{1,0:T(8,128)(2,1)S(1)} custom-call(bf16[2048,1024]{1,0:T(8,128)(2,1)} %get-tuple-element.98.act_ref, bf16[1024,1024]{1,0:T(8,128)(2,1)S(1)} %get-tuple-element.104.grads_ref.rows_ref, f32[8,128]{1,0:T(8,128)S(1)} %get-tuple-element.116.refs_0_), custom_call_target="tpu_custom_call" | custom-call | bytes 4194304 | tf_op jit(solution)/shard_map/pallas_call | solution.py:233
  84.4 3.2 %collective-permute-start.20 = (bf16[512,1024]{1,0:T(8,128)(2,1)}, bf16[512,1024]{1,0:T(8,128)(2,1)}, u32[]{:S(2)}, u32[]{:S(2)}) collective-permute-start(bf16[512,1024]{1,0:T(8,128)(2,1)} %get-tuple-element.123), channel_id=1, source_target_pairs={{0,24},{8,0},{16,8},{24,16},{1,25},{9,1},{17,9},{25,17},{2,26},{10... | collective-permute-start | bytes 3145736 | tf_op jit(solution)/shard_map/ppermute | solution.py:375
  91.8 16.0 %while.10 = (s32[]{:T(128)}, bf16[512,1024]{1,0:T(8,128)(2,1)}, s32[]{:T(128)}, s32[52]{0:T(128)S(1)}, bf16[512,1024]{1,0:T(8,128)(2,1)}, /*index=5*/bf16[1024,1...) while((s32[]{:T(128)}, bf16[512,1024]{1,0:T(8,128)(2,1)}, s32[]{:T(128)}, ...), condition=%wide.region_1.2_spmd, body=%wide.region_0.1_spmd.sunk | while | flops 2097154 | bytes 19923076 | solution.py:415
  91.8 10.4 %body.1 = (bf16[512,1024]{1,0:T(8,128)(2,1)S(1)}, bf16[512,1024]{1,0:T(8,128)(2,1)}) custom-call(s32[52]{0:T(128)S(1)} %get-tuple-element.233.table_ref, bf16[512,1024]{1,0:T(8,128)(2,1)} %get-tuple-element.234.a_ref, bf16[1024,1024]{1,0:T(8,128)(2,1)} %get-tuple-element.235.b_ref, bf16[512,1024]{1,0:T(8,128)(2,1)} %get-tuple-element.236.c_ref, ...), custom_call_target="tpu_custom_call" | custom-call | bytes 12582912 | tf_op jit(solution)/shard_map/while/body/pallas_call | solution.py:307
  102.3 3.0 %collective-permute-done = bf16[512,1024]{1,0:T(8,128)(2,1)} collective-permute-done((bf16[512,1024]{1,0:T(8,128)(2,1)}, bf16[512,1024]{1,0:T(8,128)(2,1)}, u32[]{:S(2)}, u32[]{:S(2)}) %collective-permute-start) | collective-permute-done | bytes 1048608 | tf_op jit(solution)/shard_map/while/body/ppermute | solution.py:22
  107.9 3.5 %all-to-all-start = ((bf16[4,128,1024]{2,1,0:T(8,128)(2,1)}), bf16[4,128,1024]{2,1,0:T(8,128)(2,1)S(1)}, u32[]{:S(2)}, u32[]{:S(2)}) async-start(bf16[4,128,1024]{2,1,0:T(8,128)(2,1)} %bitcast.19), calls=%async_computation | async-start | bytes 2097152 | tf_op jit(solution)/shard_map/all_to_all | solution.py:465
  116.4 3.5 %collective-permute-done.21.from_next = bf16[64,1024]{1,0:T(8,128)(2,1)S(1)} collective-permute-done((bf16[64,1024]{1,0:T(8,128)(2,1)S(1)}, bf16[64,1024]{1,0:T(8,128)(2,1)S(1)}, u32[]{:S(2)}, u32[]{:S(2)}) %collective-permute-start.21) | collective-permute-done | bytes 131104 | tf_op jit(solution)/shard_map/ppermute | solution.py:371
  119.9 2.7 %collective-permute-done.22.from_prev = bf16[64,1024]{1,0:T(8,128)(2,1)S(1)} collective-permute-done((bf16[64,1024]{1,0:T(8,128)(2,1)S(1)}, bf16[64,1024]{1,0:T(8,128)(2,1)S(1)}, u32[]{:S(2)}, u32[]{:S(2)}) %collective-permute-start.22) | collective-permute-done | bytes 131104 | tf_op jit(solution)/shard_map/ppermute | solution.py:371
  122.8 3.2 %collective-permute-start.30 = (bf16[128,1024]{1,0:T(8,128)(2,1)S(1)}, bf16[128,1024]{1,0:T(8,128)(2,1)}, u32[]{:S(2)}, u32[]{:S(2)}) collective-permute-start(bf16[128,1024]{1,0:T(8,128)(2,1)S(1)} %get-tuple-element.138), channel_id=1, source_target_pairs={{0,96},{32,0},{64,32},{96,64},{1,97},{33,1},{65,33},{97,65},{2,98}... | collective-permute-start | bytes 786440 | tf_op jit(solution)/shard_map/ppermute | solution.py:375
  132.8 4.1 %collective-permute-done.26.from_prev = bf16[64,1024]{1,0:T(8,128)(2,1)S(1)} collective-permute-done((bf16[64,1024]{1,0:T(8,128)(2,1)S(1)}, bf16[64,1024]{1,0:T(8,128)(2,1)S(1)}, u32[]{:S(2)}, u32[]{:S(2)}) %collective-permute-start.26) | collective-permute-done | bytes 131104 | tf_op jit(solution)/shard_map/ppermute | solution.py:371
  137.5 3.2 %collective-permute-start.28 = (bf16[128,1024]{1,0:T(8,128)(2,1)S(1)}, bf16[128,1024]{1,0:T(8,128)(2,1)}, u32[]{:S(2)}, u32[]{:S(2)}) collective-permute-start(bf16[128,1024]{1,0:T(8,128)(2,1)S(1)} %get-tuple-element.135), channel_id=1, source_target_pairs={{0,24},{8,0},{16,8},{24,16},{1,25},{9,1},{17,9},{25,17},{2,26},{10... | collective-permute-start | bytes 786440 | tf_op jit(solution)/shard_map/ppermute | solution.py:375
  (95 shorter events, 45.4 us)
Async XLA Ops:
  3.0 10.5 %collective-permute-start.1 = (bf16[128,1024]{1,0:T(8,128)(2,1)S(1)}, bf16[128,1024]{1,0:T(8,128)(2,1)S(1)}, u32[]{:S(2)}, u32[]{:S(2)}) collective-permute-start(bf16[128,1024]{1,0:T(8,128)(2,1)S(1)} %get-tuple-element.95), channel_id=1, source_target_pairs={{0,1},{1,2},{2,3},{3,0},{4,5},{5,6},{6,7},{7,4},{8,9},{9,10},{10,1... | collective-permute-start | bytes 786440 | tf_op jit(solution)/shard_map/ppermute | solution.py:434
  5.1 15.2 %collective-permute-start.2 = (bf16[128,1024]{1,0:T(8,128)(2,1)S(1)}, bf16[128,1024]{1,0:T(8,128)(2,1)S(1)}, u32[]{:S(2)}, u32[]{:S(2)}) collective-permute-start(bf16[128,1024]{1,0:T(8,128)(2,1)S(1)} %get-tuple-element.96), channel_id=1, source_target_pairs={{0,2},{1,3},{2,0},{3,1},{4,6},{5,7},{6,4},{7,5},{8,10},{9,11},{10,... | collective-permute-start | bytes 786440 | tf_op jit(solution)/shard_map/ppermute | solution.py:434
  8.6 15.3 %collective-permute-start.3 = (bf16[128,1024]{1,0:T(8,128)(2,1)S(1)}, bf16[128,1024]{1,0:T(8,128)(2,1)S(1)}, u32[]{:S(2)}, u32[]{:S(2)}) collective-permute-start(bf16[128,1024]{1,0:T(8,128)(2,1)S(1)} %get-tuple-element.97), channel_id=1, source_target_pairs={{0,3},{1,0},{2,1},{3,2},{4,7},{5,4},{6,5},{7,6},{8,11},{9,8},{10,9... | collective-permute-start | bytes 786440 | tf_op jit(solution)/shard_map/ppermute | solution.py:434
  9.7 15.6 %collective-permute-start.4 = (bf16[128,1024]{1,0:T(8,128)(2,1)S(1)}, bf16[128,1024]{1,0:T(8,128)(2,1)S(1)}, u32[]{:S(2)}, u32[]{:S(2)}) collective-permute-start(bf16[128,1024]{1,0:T(8,128)(2,1)S(1)} %get-tuple-element.94.refs_0_), channel_id=1, source_target_pairs={{0,4},{4,0},{1,5},{5,1},{2,6},{6,2},{3,7},{7,3},{8,12},{12,8},{9,1... | collective-permute-start | bytes 786440 | tf_op jit(solution)/shard_map/ppermute | solution.py:22
  13.5 11.8 %collective-permute-start.5 = (bf16[128,1024]{1,0:T(8,128)(2,1)S(1)}, bf16[128,1024]{1,0:T(8,128)(2,1)S(1)}, u32[]{:S(2)}, u32[]{:S(2)}) collective-permute-start(bf16[128,1024]{1,0:T(8,128)(2,1)S(1)} %collective-permute-done.1.refs_1_), channel_id=1, source_target_pairs={{0,4},{4,0},{1,5},{5,1},{2,6},{6,2},{3,7},{7,3},{8,12},{12,8},{9,1... | collective-permute-start | bytes 786440 | tf_op jit(solution)/shard_map/ppermute | solution.py:22
  16.7 22.3 %collective-permute-start.10 = (bf16[128,1024]{1,0:T(8,128)(2,1)}, bf16[128,1024]{1,0:T(8,128)(2,1)S(1)}, u32[]{:S(2)}, u32[]{:S(2)}) collective-permute-start(bf16[128,1024]{1,0:T(8,128)(2,1)} %get-tuple-element.103), channel_id=1, source_target_pairs={{0,3},{1,0},{2,1},{3,2},{4,7},{5,4},{6,5},{7,6},{8,11},{9,8},{10,9... | collective-permute-start | bytes 786440 | tf_op jit(solution)/shard_map/ppermute | solution.py:434
  20.3 18.9 %collective-permute-start.9 = (bf16[128,1024]{1,0:T(8,128)(2,1)}, bf16[128,1024]{1,0:T(8,128)(2,1)S(1)}, u32[]{:S(2)}, u32[]{:S(2)}) collective-permute-start(bf16[128,1024]{1,0:T(8,128)(2,1)} %get-tuple-element.102), channel_id=1, source_target_pairs={{0,2},{1,3},{2,0},{3,1},{4,6},{5,7},{6,4},{7,5},{8,10},{9,11},{10,... | collective-permute-start | bytes 786440 | tf_op jit(solution)/shard_map/ppermute | solution.py:434
  23.9 15.7 %collective-permute-start.8 = (bf16[128,1024]{1,0:T(8,128)(2,1)}, bf16[128,1024]{1,0:T(8,128)(2,1)S(1)}, u32[]{:S(2)}, u32[]{:S(2)}) collective-permute-start(bf16[128,1024]{1,0:T(8,128)(2,1)} %get-tuple-element.101), channel_id=1, source_target_pairs={{0,1},{1,2},{2,3},{3,0},{4,5},{5,6},{6,7},{7,4},{8,9},{9,10},{10,1... | collective-permute-start | bytes 786440 | tf_op jit(solution)/shard_map/ppermute | solution.py:434
  45.7 15.8 %collective-permute-start.15 = (bf16[256,1024]{1,0:T(8,128)(2,1)}, bf16[256,1024]{1,0:T(8,128)(2,1)}, u32[]{:S(2)}, u32[]{:S(2)}) collective-permute-start(bf16[256,1024]{1,0:T(8,128)(2,1)} %get-tuple-element.109), channel_id=1, source_target_pairs={{0,24},{8,0},{16,8},{24,16},{1,25},{9,1},{17,9},{25,17},{2,26},{10... | collective-permute-start | bytes 1572872 | tf_op jit(solution)/shard_map/ppermute | solution.py:371
  48.4 15.2 %collective-permute-start.16 = (bf16[256,1024]{1,0:T(8,128)(2,1)}, bf16[256,1024]{1,0:T(8,128)(2,1)}, u32[]{:S(2)}, u32[]{:S(2)}) collective-permute-start(bf16[256,1024]{1,0:T(8,128)(2,1)} %get-tuple-element.110), channel_id=1, source_target_pairs={{0,8},{8,16},{16,24},{24,0},{1,9},{9,17},{17,25},{25,1},{2,10},{10... | collective-permute-start | bytes 1572872 | tf_op jit(solution)/shard_map/ppermute | solution.py:371
  54.6 19.8 %collective-permute-start.17 = (bf16[256,1024]{1,0:T(8,128)(2,1)}, bf16[256,1024]{1,0:T(8,128)(2,1)S(1)}, u32[]{:S(2)}, u32[]{:S(2)}) collective-permute-start(bf16[256,1024]{1,0:T(8,128)(2,1)} %get-tuple-element.113), channel_id=1, source_target_pairs={{0,96},{32,0},{64,32},{96,64},{1,97},{33,1},{65,33},{97,65},{2,98}... | collective-permute-start | bytes 1572872 | tf_op jit(solution)/shard_map/ppermute | solution.py:371
  57.7 16.8 %collective-permute-start.18 = (bf16[256,1024]{1,0:T(8,128)(2,1)}, bf16[256,1024]{1,0:T(8,128)(2,1)S(1)}, u32[]{:S(2)}, u32[]{:S(2)}) collective-permute-start(bf16[256,1024]{1,0:T(8,128)(2,1)} %get-tuple-element.114), channel_id=1, source_target_pairs={{0,32},{32,64},{64,96},{96,0},{1,33},{33,65},{65,97},{97,1},{2,34}... | collective-permute-start | bytes 1572872 | tf_op jit(solution)/shard_map/ppermute | solution.py:371
  84.3 27.1 %collective-permute-start.19 = (bf16[512,1024]{1,0:T(8,128)(2,1)}, bf16[512,1024]{1,0:T(8,128)(2,1)}, u32[]{:S(2)}, u32[]{:S(2)}) collective-permute-start(bf16[512,1024]{1,0:T(8,128)(2,1)} %get-tuple-element.122), channel_id=1, source_target_pairs={{0,8},{8,16},{16,24},{24,0},{1,9},{9,17},{17,25},{25,1},{2,10},{10... | collective-permute-start | bytes 3145736 | tf_op jit(solution)/shard_map/ppermute | solution.py:375
  84.4 27.0 %collective-permute-start.20 = (bf16[512,1024]{1,0:T(8,128)(2,1)}, bf16[512,1024]{1,0:T(8,128)(2,1)}, u32[]{:S(2)}, u32[]{:S(2)}) collective-permute-start(bf16[512,1024]{1,0:T(8,128)(2,1)} %get-tuple-element.123), channel_id=1, source_target_pairs={{0,24},{8,0},{16,8},{24,16},{1,25},{9,1},{17,9},{25,17},{2,26},{10... | collective-permute-start | bytes 3145736 | tf_op jit(solution)/shard_map/ppermute | solution.py:375
  87.6 38.4 %collective-permute-start.23 = (bf16[512,1024]{1,0:T(8,128)(2,1)}, bf16[512,1024]{1,0:T(8,128)(2,1)S(1)}, u32[]{:S(2)}, u32[]{:S(2)}) collective-permute-start(bf16[512,1024]{1,0:T(8,128)(2,1)} %get-tuple-element.128), channel_id=1, source_target_pairs={{0,32},{32,64},{64,96},{96,0},{1,33},{33,65},{65,97},{97,1},{2,34}... | collective-permute-start | bytes 3145736 | tf_op jit(solution)/shard_map/ppermute | solution.py:375
  89.2 36.8 %collective-permute-start.24 = (bf16[512,1024]{1,0:T(8,128)(2,1)}, bf16[512,1024]{1,0:T(8,128)(2,1)}, u32[]{:S(2)}, u32[]{:S(2)}) collective-permute-start(bf16[512,1024]{1,0:T(8,128)(2,1)} %get-tuple-element.129), channel_id=1, source_target_pairs={{0,96},{32,0},{64,32},{96,64},{1,97},{33,1},{65,33},{97,65},{2,98}... | collective-permute-start | bytes 3145736 | tf_op jit(solution)/shard_map/ppermute | solution.py:375
  107.9 32.9 %all-to-all-start = ((bf16[4,128,1024]{2,1,0:T(8,128)(2,1)}), bf16[4,128,1024]{2,1,0:T(8,128)(2,1)S(1)}, u32[]{:S(2)}, u32[]{:S(2)}) async-start(bf16[4,128,1024]{2,1,0:T(8,128)(2,1)} %bitcast.19), calls=%async_computation | async-start | bytes 2097152 | tf_op jit(solution)/shard_map/all_to_all | solution.py:465
  114.3 5.5 %collective-permute-start.21 = (bf16[64,1024]{1,0:T(8,128)(2,1)S(1)}, bf16[64,1024]{1,0:T(8,128)(2,1)S(1)}, u32[]{:S(2)}, u32[]{:S(2)}) collective-permute-start(bf16[64,1024]{1,0:T(8,128)(2,1)S(1)} %get-tuple-element.125), channel_id=1, source_target_pairs={{0,96},{32,0},{64,32},{96,64},{1,97},{33,1},{65,33},{97,65},{2,98}... | collective-permute-start | bytes 393224 | tf_op jit(solution)/shard_map/ppermute | solution.py:371
  116.1 6.5 %collective-permute-start.22 = (bf16[64,1024]{1,0:T(8,128)(2,1)S(1)}, bf16[64,1024]{1,0:T(8,128)(2,1)S(1)}, u32[]{:S(2)}, u32[]{:S(2)}) collective-permute-start(bf16[64,1024]{1,0:T(8,128)(2,1)S(1)} %get-tuple-element.126), channel_id=1, source_target_pairs={{0,32},{32,64},{64,96},{96,0},{1,33},{33,65},{65,97},{97,1},{2,34}... | collective-permute-start | bytes 393224 | tf_op jit(solution)/shard_map/ppermute | solution.py:371
  122.7 19.6 %collective-permute-start.29 = (bf16[128,1024]{1,0:T(8,128)(2,1)S(1)}, bf16[128,1024]{1,0:T(8,128)(2,1)}, u32[]{:S(2)}, u32[]{:S(2)}) collective-permute-start(bf16[128,1024]{1,0:T(8,128)(2,1)S(1)} %get-tuple-element.137), channel_id=1, source_target_pairs={{0,32},{32,64},{64,96},{96,0},{1,33},{33,65},{65,97},{97,1},{2,34}... | collective-permute-start | bytes 786440 | tf_op jit(solution)/shard_map/ppermute | solution.py:375
  122.8 19.5 %collective-permute-start.30 = (bf16[128,1024]{1,0:T(8,128)(2,1)S(1)}, bf16[128,1024]{1,0:T(8,128)(2,1)}, u32[]{:S(2)}, u32[]{:S(2)}) collective-permute-start(bf16[128,1024]{1,0:T(8,128)(2,1)S(1)} %get-tuple-element.138), channel_id=1, source_target_pairs={{0,96},{32,0},{64,32},{96,64},{1,97},{33,1},{65,33},{97,65},{2,98}... | collective-permute-start | bytes 786440 | tf_op jit(solution)/shard_map/ppermute | solution.py:375
  130.2 6.7 %collective-permute-start.26 = (bf16[64,1024]{1,0:T(8,128)(2,1)S(1)}, bf16[64,1024]{1,0:T(8,128)(2,1)S(1)}, u32[]{:S(2)}, u32[]{:S(2)}) collective-permute-start(bf16[64,1024]{1,0:T(8,128)(2,1)S(1)} %get-tuple-element.133), channel_id=1, source_target_pairs={{0,8},{8,16},{16,24},{24,0},{1,9},{9,17},{17,25},{25,1},{2,10},{10... | collective-permute-start | bytes 393224 | tf_op jit(solution)/shard_map/ppermute | solution.py:371
  137.5 7.6 %collective-permute-start.27 = (bf16[128,1024]{1,0:T(8,128)(2,1)S(1)}, bf16[128,1024]{1,0:T(8,128)(2,1)S(1)}, u32[]{:S(2)}, u32[]{:S(2)}) collective-permute-start(bf16[128,1024]{1,0:T(8,128)(2,1)S(1)} %get-tuple-element.134), channel_id=1, source_target_pairs={{0,8},{8,16},{16,24},{24,0},{1,9},{9,17},{17,25},{25,1},{2,10},{10... | collective-permute-start | bytes 786440 | tf_op jit(solution)/shard_map/ppermute | solution.py:375
  137.5 7.6 %collective-permute-start.28 = (bf16[128,1024]{1,0:T(8,128)(2,1)S(1)}, bf16[128,1024]{1,0:T(8,128)(2,1)}, u32[]{:S(2)}, u32[]{:S(2)}) collective-permute-start(bf16[128,1024]{1,0:T(8,128)(2,1)S(1)} %get-tuple-element.135), channel_id=1, source_target_pairs={{0,24},{8,0},{16,8},{24,16},{1,25},{9,1},{17,9},{25,17},{2,26},{10... | collective-permute-start | bytes 786440 | tf_op jit(solution)/shard_map/ppermute | solution.py:375
  (18 other events, 69.1 us)

commit v3 on v2

--- a/solution.py
+++ b/solution.py
@@ -285,7 +285,7 @@
     rows = 512
 
     def body(table_ref, a_ref, b_ref, c_ref, weight_ref, *refs):
-        own_ref, other_ref, w_buf, sems, total = refs[len(deps) :]
+        out_ref, w_buf, sems, total = refs[len(deps) :]
         step = pl.program_id(0)
         w_ref = block_group(table_ref, weight_ref, w_buf, sems, 16, 4)
 
@@ -301,8 +301,9 @@
         @pl.when(step == 3)
         def _():
             final = (total[...] + dot_tn(c_ref[...], w_ref[...])).astype(BF16)
-            own_ref[...] = final[:rows]
-            other_ref[...] = final[rows:]
+            own = table_ref[52]
+            out_ref[pl.ds(pl.multiple_of(own * rows, rows), rows), :] = final[:rows]
+            out_ref[pl.ds(pl.multiple_of((1 - own) * rows, rows), rows), :] = final[rows:]
 
     return pl.pallas_call(
         body,
@@ -310,10 +311,10 @@
             num_scalar_prefetch=1,
             grid=(4,),
             in_specs=[VMEM] * 3 + [HBM] + [ANY] * len(deps),
-            out_specs=[fixed(rows, width)] * 2,
+            out_specs=fixed(2 * rows, width),
             scratch_shapes=block_scratch(width, 4) + [pltpu.VMEM((2 * rows, width), F32)],
         ),
-        out_shape=[shape(rows, width)] * 2,
+        out_shape=shape(2 * rows, width),
         compiler_params=params(),
         cost_estimate=cost(2**23 + 2**22),
     )(table, *pre, weight, *deps)
@@ -406,13 +407,10 @@
     return pltpu.with_memory_space_constraint(array, pltpu.HBM)
 
 
-def sum_cores(own, other):
-    return add(own, swap_core(other)).astype(BF16)
-
-
-def once(index, work, start):
-    trips = 1 + jnp.minimum(index, 0)
-    return lax.fori_loop(0, trips, lambda _, array: work(array), start)
+def sum_cores(terms):
+    terms = lax.all_to_all(terms, "core", split_axis=0, concat_axis=0, tiled=True)
+    n = terms.shape[0] // 2
+    return add(terms[:n], terms[n:]).astype(BF16)
 
 
 def local(tokens, out_grad, gate, region, w_in, w_out):
@@ -424,7 +422,7 @@
     by_x = ((((y + every[None, :]) % 4) * 4 + (x + order[:, None]) % 4) * 2 + core).reshape(16)
     by_y = ((((y + order[:, None]) % 4) * 4 + (x + every[None, :]) % 4) * 2 + core).reshape(16)
     same = jnp.array([INVERSE[q] * 4 + ORDER[p] for p in range(4) for q in range(4)], jnp.int32)
-    table = jnp.concatenate([by_x, by_y, same, (expert - every) % 4])
+    table = jnp.concatenate([by_x, by_y, same, (expert - every) % 4, core[None]])
     weight_in, weight_out = in_hbm(w_in[0]), in_hbm(w_out[0])
 
     place, *send_x = dispatch_tokens(expert[None], region.reshape(1, -1), tokens)
@@ -455,13 +453,7 @@
     in_parts = second_hop(*pair, "y")
     pre_c, in_own, mark = backward(table, rows_d, rows_x, slope, weight_out, 3, 1, (mark,))
     out_own = outer_rest(act, rows_d, 3, 1, (mark,))
-    own = once(
-        x,
-        lambda start: sum_cores(
-            *row_gradients(table, (pre_a, pre_b, pre_c), weight_in, (start,))
-        ),
-        out_own,
-    )
+    own = sum_cores(row_gradients(table, (pre_a, pre_b, pre_c), weight_in, ()))
     back = lax.all_to_all(own, "expert", split_axis=0, concat_axis=0, tiled=True)
 
     keep, sides, low, high, mark = combine(out_own, out_parts)

time: 148 us -> 137 us (0.926)
  blocking collectives: 0 us -> 5.42 us
  starting transfers between devices: 43 us -> 37.8 us
  Pallas kernels: 64.8 us -> 60.5 us
  waiting for transfers between devices: 24.9 us -> 21.8 us
  other arithmetic: 7.97 us -> 4.95 us
    ppermute x6, starting transfers between devices: 14.6 us -> 8.26 us  [to_owner(): lax.ppermute(parts[r], 'expert', ring(r))]
    all_to_all x0 -> x1, blocking collectives: none -> 5.42 us  [sum_cores(): lax.all_to_all(terms, 'core', split_axis=0, concat_axis=0, tiled=True)]
    pallas_call x1, Pallas kernels: 10.4 us -> 7.24 us  [row_gradients(): pl.pallas_call(body, grid_spec=pltpu.PrefetchScalarGridSpec(num_scalar_pr...]
    ppermute x6, waiting for transfers between devices: 3.9 us -> 6.93 us  [to_owner(): lax.ppermute(parts[r], 'expert', ring(r))]
    ppermute x9 -> x8, waiting for transfers between devices: 5.03 us -> 2.04 us  [swap_core(): return lax.ppermute(array, 'core', [(0, 1), (1, 0)])]
    ppermute x8, waiting for transfers between devices: 15.1 us -> 12.8 us  [first_hop(): return (lax.ppermute(low, axis, ring(3)), lax.ppermute(high, axis, ring(1)))]
    unnamed x21 -> x8, local copies, waits for them, and re-layouts: 5.13 us -> 3.43 us
  transfers between devices with their start and end apart: 32 -> 31, of which waited for: 14 -> 11; matrix products, arithmetic and copies ran while one was open for 5% -> 4% of each run, Pallas kernels for 34% -> 41%
where the time goes in v3:
time: 137 us; the launch traced here: 136 us
  Pallas kernels  60.5 us (44%)
  starting transfers between devices  37.8 us (28%)
  waiting for transfers between devices  21.8 us (16%)
  blocking collectives  5.42 us (4%)
  other arithmetic  4.95 us (4%)
  local copies, waits for them, and re-layouts  4.33 us (3%)
    pallas_call x3, Pallas kernels, backward(): pl.pallas_call(body, grid_spec=pltpu.PrefetchScalarGridSpec(num_scalar_pr...  18.8 us
    ppermute x8, starting transfers between devices, second_hop(): return (lax.ppermute(up, axis, ring(1)), lax.ppermute(down, axis, ring(3)))  13 us
    ppermute x8, waiting for transfers between devices, first_hop(): return (lax.ppermute(low, axis, ring(3)), lax.ppermute(high, axis, ring(1)))  12.8 us
    pallas_call x1, Pallas kernels, forward(): pl.pallas_call(body, grid_spec=pltpu.PrefetchScalarGridSpec(num_scalar_pr...  11.7 us
    ppermute x8, starting transfers between devices, first_hop(): return (lax.ppermute(low, axis, ring(3)), lax.ppermute(high, axis, ring(1)))  9.96 us
    ppermute x6, starting transfers between devices, to_owner(): lax.ppermute(parts[r], 'expert', ring(r))  8.26 us
    pallas_call x1, Pallas kernels, row_gradients(): pl.pallas_call(body, grid_spec=pltpu.PrefetchScalarGridSpec(num_scalar_pr...  7.24 us
    ppermute x6, waiting for transfers between devices, to_owner(): lax.ppermute(parts[r], 'expert', ring(r))  6.93 us
  transfers between devices with their start and end apart: 31, of which 11 were waited for; matrix products, arithmetic and copies ran while one was open for 4% of the time, Pallas kernels for 41%

profile of v3, /device:TPU:0, one launch (start us, length us, event | category | flops | bytes accessed | tf_op | source)
XLA Modules:
  0.0 135.6 jit_solution(8700028949384313423)
XLA Ops:
  5.5 3.6 %collective-permute-start.1 = (bf16[128,1024]{1,0:T(8,128)(2,1)S(1)}, bf16[128,1024]{1,0:T(8,128)(2,1)S(1)}, u32[]{:S(2)}, u32[]{:S(2)}) collective-permute-start(bf16[128,1024]{1,0:T(8,128)(2,1)S(1)} %get-tuple-element.51), channel_id=1, source_target_pairs={{0,2},{1,3},{2,0},{3,1},{4,6},{5,7},{6,4},{7,5},{8,10},{9,11},{10,... | collective-permute-start | bytes 786440 | tf_op jit(solution)/shard_map/ppermute | solution.py:432
  15.3 6.9 %collective-permute-done.1.refs_2_ = bf16[128,1024]{1,0:T(8,128)(2,1)S(1)} collective-permute-done((bf16[128,1024]{1,0:T(8,128)(2,1)S(1)}, bf16[128,1024]{1,0:T(8,128)(2,1)S(1)}, u32[]{:S(2)}, u32[]{:S(2)}) %collective-permute-start.1) | collective-permute-done | bytes 262176 | tf_op jit(solution)/shard_map/ppermute | solution.py:432
  24.7 11.7 %shard_map.104 = (bf16[2048,1024]{1,0:T(8,128)(2,1)}, bf16[2048,1024]{1,0:T(8,128)(2,1)}, bf16[1024,1024]{1,0:T(8,128)(2,1)S(1)}, f32[8,128]{1,0:T(8,128)S(1)}) custom-call(s32[53]{0:T(128)S(1)} %concatenate.3.table_ref, bf16[128,1024]{1,0:T(8,128)(2,1)S(1)} %get-tuple-element.49.refs_0_, bf16[128,1024]{1,0:T(8,128)(2,1)S(1)} %collective-permute-done.refs_1_, ...), custom_call_target="tpu_custom_call" | custom-call | bytes 16777216 | tf_op jit(solution)/shard_map/pallas_call | solution.py:185
  39.2 3.1 %shard_map.110 = (bf16[256,1024]{1,0:T(8,128)(2,1)S(1)}, bf16[256,1024]{1,0:T(8,128)(2,1)S(1)}, bf16[1024,1024]{1,0:T(8,128)(2,1)S(1)}, f32[8,128]{1,0:T(8,128)S(1)}) custom-call(s32[53]{0:T(128)S(1)} %concatenate.3.table_ref, bf16[2048,1024]{1,0:T(8,128)(2,1)} %get-tuple-element.53.act_ref, bf16[128,1024]{1,0:T(8,128)(2,1)S(1)} %shard_map.106.refs_0_, ...), custom_call_target="tpu_custom_call" | custom-call | bytes 4194304 | tf_op jit(solution)/shard_map/pallas_call | solution.py:212
  42.4 2.8 %collective-permute-start.14 = (bf16[256,1024]{1,0:T(8,128)(2,1)S(1)}, bf16[256,1024]{1,0:T(8,128)(2,1)S(1)}, u32[]{:S(2)}, u32[]{:S(2)}) collective-permute-start(bf16[256,1024]{1,0:T(8,128)(2,1)S(1)} %get-tuple-element.65), channel_id=1, source_target_pairs={{0,24},{8,0},{16,8},{24,16},{1,25},{9,1},{17,9},{25,17},{2,26},{10... | collective-permute-start | bytes 1572872 | tf_op jit(solution)/shard_map/ppermute | solution.py:372
  45.2 5.4 %shard_map.111 = (bf16[512,1024]{1,0:T(8,128)(2,1)S(1)}, bf16[256,1024]{1,0:T(8,128)(2,1)S(1)}, bf16[256,1024]{1,0:T(8,128)(2,1)S(1)}, f32[8,128]{1,0:T(8,128)S(1)}) custom-call(s32[53]{0:T(128)S(1)} %concatenate.3.table_ref, bf16[1024,1024]{1,0:T(8,128)(2,1)S(1)} %get-tuple-element.59.grads_ref.rows_ref, bf16[1024,1024]{1,0:T(8,128)(2,1)S(1)} %get-tuple-element.60.rows_ref, ...), custom_call_target="tpu_custom_call" | custom-call | bytes 6291456 | tf_op jit(solution)/shard_map/pallas_call | solution.py:264
  50.6 3.1 %collective-permute-start.16 = (bf16[256,1024]{1,0:T(8,128)(2,1)S(1)}, bf16[256,1024]{1,0:T(8,128)(2,1)S(1)}, u32[]{:S(2)}, u32[]{:S(2)}) collective-permute-start(bf16[256,1024]{1,0:T(8,128)(2,1)S(1)} %get-tuple-element.70), channel_id=1, source_target_pairs={{0,96},{32,0},{64,32},{96,64},{1,97},{33,1},{65,33},{97,65},{2,98}... | collective-permute-start | bytes 1572872 | tf_op jit(solution)/shard_map/ppermute | solution.py:372
  53.7 3.8 %shard_map.112.sides_ref = bf16[1024,1024]{1,0:T(8,128)(2,1)S(1)} custom-call(bf16[2048,1024]{1,0:T(8,128)(2,1)} %get-tuple-element.53.act_ref, bf16[1024,1024]{1,0:T(8,128)(2,1)S(1)} %get-tuple-element.59.grads_ref.rows_ref, f32[8,128]{1,0:T(8,128)S(1)} %get-tuple-element.64.refs_0_), custom_call_target="tpu_custom_call" | custom-call | bytes 6291456 | tf_op jit(solution)/shard_map/pallas_call | solution.py:233
  57.5 2.7 %collective-permute-done.15.from_prev = bf16[256,1024]{1,0:T(8,128)(2,1)S(1)} collective-permute-done((bf16[256,1024]{1,0:T(8,128)(2,1)S(1)}, bf16[256,1024]{1,0:T(8,128)(2,1)S(1)}, u32[]{:S(2)}, u32[]{:S(2)}) %collective-permute-start.15) | collective-permute-done | bytes 524320 | tf_op jit(solution)/shard_map/ppermute | solution.py:372
  61.7 3.2 %collective-permute-start.19 = (bf16[512,1024]{1,0:T(8,128)(2,1)}, bf16[512,1024]{1,0:T(8,128)(2,1)}, u32[]{:S(2)}, u32[]{:S(2)}) collective-permute-start(bf16[512,1024]{1,0:T(8,128)(2,1)} %get-tuple-element.77), channel_id=1, source_target_pairs={{0,24},{8,0},{16,8},{24,16},{1,25},{9,1},{17,9},{25,17},{2,26},{10... | collective-permute-start | bytes 3145736 | tf_op jit(solution)/shard_map/ppermute | solution.py:376
  64.9 8.0 %shard_map.114 = (bf16[1024,1024]{1,0:T(8,128)(2,1)S(1)}, bf16[1024,1024]{1,0:T(8,128)(2,1)S(1)}, f32[8,128]{1,0:T(8,128)}) custom-call(s32[53]{0:T(128)S(1)} %concatenate.3.table_ref, bf16[1024,1024]{1,0:T(8,128)(2,1)S(1)} %get-tuple-element.59.grads_ref.rows_ref, bf16[1024,1024]{1,0:T(8,128)(2,1)S(1)} %get-tuple-element.60.rows_ref, ...), custom_call_target="tpu_custom_call" | custom-call | bytes 10485760 | tf_op jit(solution)/shard_map/pallas_call | solution.py:264
  77.8 5.4 %shard_map.116 = (bf16[512,1024]{1,0:T(8,128)(2,1)S(1)}, bf16[512,1024]{1,0:T(8,128)(2,1)S(1)}, f32[8,128]{1,0:T(8,128)S(1)}) custom-call(s32[53]{0:T(128)S(1)} %concatenate.3.table_ref, bf16[1024,1024]{1,0:T(8,128)(2,1)S(1)} %get-tuple-element.59.grads_ref.rows_ref, bf16[1024,1024]{1,0:T(8,128)(2,1)S(1)} %get-tuple-element.60.rows_ref, ...), custom_call_target="tpu_custom_call" | custom-call | bytes 6291456 | tf_op jit(solution)/shard_map/pallas_call | solution.py:264
  83.1 7.2 %shard_map.117 = bf16[1024,1024]{1,0:T(8,128)(2,1)S(1)} custom-call(s32[53]{0:T(128)S(1)} %concatenate.3.table_ref, bf16[512,1024]{1,0:T(8,128)(2,1)S(1)} %get-tuple-element.63.a_ref, bf16[1024,1024]{1,0:T(8,128)(2,1)S(1)} %get-tuple-element.68.b_ref, bf16[512,1024]{1,0:T(8,128)(2,1)S(1)} %get-tuple-element.73.c_ref, bf16[4096,1024]{1,0:T(8,128)(2,1)} %bitcast.20), custom_call_target="tpu_custom_call" | custom-call | bytes 12582912 | tf_op jit(solution)/shard_map/pallas_call | solution.py:308
  90.4 5.4 %all_to_all.17 = bf16[2,512,1024]{2,1,0:T(8,128)(2,1)S(1)} all-to-all(bf16[2,512,1024]{2,1,0:T(8,128)(2,1)S(1)} %bitcast.13), channel_id=1, replica_groups=mesh['y'=4,'x'=4,'core'=2,'expert'=4] {'core'}, dimensions={0} | all-to-all | bytes 4194304 | tf_op jit(solution)/shard_map/all_to_all | solution.py:411
  97.2 4.7 %all-to-all-start.1 = ((bf16[4,128,1024]{2,1,0:T(8,128)(2,1)}), bf16[4,128,1024]{2,1,0:T(8,128)(2,1)}, u32[]{:S(2)}, u32[]{:S(2)}) async-start(bf16[4,128,1024]{2,1,0:T(8,128)(2,1)} %bitcast.21), calls=%async_computation.1 | async-start | bytes 2097152 | tf_op jit(solution)/shard_map/all_to_all | solution.py:457
  101.9 2.5 %shard_map.119.own_ref = bf16[512,1024]{1,0:T(8,128)(2,1)S(1)} custom-call(bf16[2048,1024]{1,0:T(8,128)(2,1)} %get-tuple-element.53.act_ref, bf16[1024,1024]{1,0:T(8,128)(2,1)S(1)} %get-tuple-element.59.grads_ref.rows_ref, f32[8,128]{1,0:T(8,128)S(1)} %get-tuple-element.75.refs_0_), custom_call_target="tpu_custom_call" | custom-call | bytes 4194304 | tf_op jit(solution)/shard_map/pallas_call | solution.py:233
  104.4 2.1 %shard_map.120 = (bf16[128,1024]{1,0:T(8,128)(2,1)S(1)}, bf16[256,1024]{1,0:T(8,128)(2,1)S(1)}, bf16[64,1024]{1,0:T(8,128)(2,1)S(1)}, bf16[64,1024]{1,0:T(8,128)(2,1)S(1)}, f32[8,128]{1,0:T(8,128)}) custom-call(bf16[512,1024]{1,0:T(8,128)(2,1)S(1)} %shard_map.119.own_ref, bf16[512,1024]{1,0:T(8,128)(2,1)} %collective-permute-done.18.left, ...), custom_call_target="tpu_custom_call" | custom-call | bytes 4194304 | tf_op jit(solution)/shard_map/pallas_call | solution.py:396
  108.6 3.2 %collective-permute-done.20.from_next = bf16[64,1024]{1,0:T(8,128)(2,1)S(1)} collective-permute-done((bf16[64,1024]{1,0:T(8,128)(2,1)S(1)}, bf16[64,1024]{1,0:T(8,128)(2,1)S(1)}, u32[]{:S(2)}, u32[]{:S(2)}) %collective-permute-start.20) | collective-permute-done | bytes 131104 | tf_op jit(solution)/shard_map/ppermute | solution.py:372
  111.8 2.7 %collective-permute-done.21.from_prev = bf16[64,1024]{1,0:T(8,128)(2,1)S(1)} collective-permute-done((bf16[64,1024]{1,0:T(8,128)(2,1)S(1)}, bf16[64,1024]{1,0:T(8,128)(2,1)S(1)}, u32[]{:S(2)}, u32[]{:S(2)}) %collective-permute-start.21) | collective-permute-done | bytes 131104 | tf_op jit(solution)/shard_map/ppermute | solution.py:372
  114.7 3.2 %collective-permute-start.29 = (bf16[128,1024]{1,0:T(8,128)(2,1)S(1)}, bf16[128,1024]{1,0:T(8,128)(2,1)}, u32[]{:S(2)}, u32[]{:S(2)}) collective-permute-start(bf16[128,1024]{1,0:T(8,128)(2,1)S(1)} %get-tuple-element.92), channel_id=1, source_target_pairs={{0,96},{32,0},{64,32},{96,64},{1,97},{33,1},{65,33},{97,65},{2,98}... | collective-permute-start | bytes 786440 | tf_op jit(solution)/shard_map/ppermute | solution.py:376
  117.9 2.1 %shard_map.123 = (bf16[128,1024]{1,0:T(8,128)(2,1)S(1)}, bf16[256,1024]{1,0:T(8,128)(2,1)S(1)}, bf16[64,1024]{1,0:T(8,128)(2,1)S(1)}, bf16[64,1024]{1,0:T(8,128)(2,1)S(1)}, f32[8,128]{1,0:T(8,128)}) custom-call(bf16[512,1024]{1,0:T(8,128)(2,1)S(1)} %shard_map.122.own_ref, bf16[512,1024]{1,0:T(8,128)(2,1)} %collective-permute-done.22.left, ...), custom_call_target="tpu_custom_call" | custom-call | bytes 4194304 | tf_op jit(solution)/shard_map/pallas_call | solution.py:396
  122.1 2.9 %collective-permute-done.24.from_next = bf16[64,1024]{1,0:T(8,128)(2,1)S(1)} collective-permute-done((bf16[64,1024]{1,0:T(8,128)(2,1)S(1)}, bf16[64,1024]{1,0:T(8,128)(2,1)S(1)}, u32[]{:S(2)}, u32[]{:S(2)}) %collective-permute-start.24) | collective-permute-done | bytes 131104 | tf_op jit(solution)/shard_map/ppermute | solution.py:372
  127.7 2.4 %collective-permute-start.27 = (bf16[128,1024]{1,0:T(8,128)(2,1)S(1)}, bf16[128,1024]{1,0:T(8,128)(2,1)S(1)}, u32[]{:S(2)}, u32[]{:S(2)}) collective-permute-start(bf16[128,1024]{1,0:T(8,128)(2,1)S(1)} %get-tuple-element.89), channel_id=1, source_target_pairs={{0,24},{8,0},{16,8},{24,16},{1,25},{9,1},{17,9},{25,17},{2,26},{10... | collective-permute-start | bytes 786440 | tf_op jit(solution)/shard_map/ppermute | solution.py:376
  130.1 2.7 %shard_map.118 = bf16[256,1024]{1,0:T(8,128)(2,1)} custom-call(s32[1]{0:T(128)} %bitcast.where_ref, bf16[512,256]{1,0:T(8,128)(2,1)S(1)} %get-tuple-element.48.place_ref, bf16[512,1024]{1,0:T(8,128)(2,1)} %bitcast.8.rows_ref), custom_call_target="tpu_custom_call" | custom-call | bytes 2097152 | tf_op jit(solution)/shard_map/pallas_call | solution.py:354
  (80 shorter events, 33.8 us)
Async XLA Ops:
  3.5 10.7 %collective-permute-start = (bf16[128,1024]{1,0:T(8,128)(2,1)}, bf16[128,1024]{1,0:T(8,128)(2,1)S(1)}, u32[]{:S(2)}, u32[]{:S(2)}) collective-permute-start(bf16[128,1024]{1,0:T(8,128)(2,1)} %get-tuple-element.50), channel_id=1, source_target_pairs={{0,1},{1,2},{2,3},{3,0},{4,5},{5,6},{6,7},{7,4},{8,9},{9,10},{10,1... | collective-permute-start | bytes 786440 | tf_op jit(solution)/shard_map/ppermute | solution.py:432
  5.5 16.6 %collective-permute-start.1 = (bf16[128,1024]{1,0:T(8,128)(2,1)S(1)}, bf16[128,1024]{1,0:T(8,128)(2,1)S(1)}, u32[]{:S(2)}, u32[]{:S(2)}) collective-permute-start(bf16[128,1024]{1,0:T(8,128)(2,1)S(1)} %get-tuple-element.51), channel_id=1, source_target_pairs={{0,2},{1,3},{2,0},{3,1},{4,6},{5,7},{6,4},{7,5},{8,10},{9,11},{10,... | collective-permute-start | bytes 786440 | tf_op jit(solution)/shard_map/ppermute | solution.py:432
  9.1 13.0 %collective-permute-start.2 = (bf16[128,1024]{1,0:T(8,128)(2,1)S(1)}, bf16[128,1024]{1,0:T(8,128)(2,1)S(1)}, u32[]{:S(2)}, u32[]{:S(2)}) collective-permute-start(bf16[128,1024]{1,0:T(8,128)(2,1)S(1)} %get-tuple-element.52), channel_id=1, source_target_pairs={{0,3},{1,0},{2,1},{3,2},{4,7},{5,4},{6,5},{7,6},{8,11},{9,8},{10,9... | collective-permute-start | bytes 786440 | tf_op jit(solution)/shard_map/ppermute | solution.py:432
  10.1 12.7 %collective-permute-start.3 = (bf16[128,1024]{1,0:T(8,128)(2,1)S(1)}, bf16[128,1024]{1,0:T(8,128)(2,1)S(1)}, u32[]{:S(2)}, u32[]{:S(2)}) collective-permute-start(bf16[128,1024]{1,0:T(8,128)(2,1)S(1)} %get-tuple-element.49.refs_0_), channel_id=1, source_target_pairs={{0,4},{4,0},{1,5},{5,1},{2,6},{6,2},{3,7},{7,3},{8,12},{12,8},{9,1... | collective-permute-start | bytes 786440 | tf_op jit(solution)/shard_map/ppermute | solution.py:22
  13.2 23.5 %collective-permute-start.7 = (bf16[128,1024]{1,0:T(8,128)(2,1)}, bf16[128,1024]{1,0:T(8,128)(2,1)S(1)}, u32[]{:S(2)}, u32[]{:S(2)}) collective-permute-start(bf16[128,1024]{1,0:T(8,128)(2,1)} %get-tuple-element.56), channel_id=1, source_target_pairs={{0,1},{1,2},{2,3},{3,0},{4,5},{5,6},{6,7},{7,4},{8,9},{9,10},{10,1... | collective-permute-start | bytes 786440 | tf_op jit(solution)/shard_map/ppermute | solution.py:432
  14.3 8.6 %collective-permute-start.4 = (bf16[128,1024]{1,0:T(8,128)(2,1)S(1)}, bf16[128,1024]{1,0:T(8,128)(2,1)S(1)}, u32[]{:S(2)}, u32[]{:S(2)}) collective-permute-start(bf16[128,1024]{1,0:T(8,128)(2,1)S(1)} %collective-permute-done.refs_1_), channel_id=1, source_target_pairs={{0,4},{4,0},{1,5},{5,1},{2,6},{6,2},{3,7},{7,3},{8,12},{12,8},{9,1... | collective-permute-start | bytes 786440 | tf_op jit(solution)/shard_map/ppermute | solution.py:22
  22.2 14.9 %collective-permute-start.8 = (bf16[128,1024]{1,0:T(8,128)(2,1)}, bf16[128,1024]{1,0:T(8,128)(2,1)S(1)}, u32[]{:S(2)}, u32[]{:S(2)}) collective-permute-start(bf16[128,1024]{1,0:T(8,128)(2,1)} %get-tuple-element.57), channel_id=1, source_target_pairs={{0,2},{1,3},{2,0},{3,1},{4,6},{5,7},{6,4},{7,5},{8,10},{9,11},{10,... | collective-permute-start | bytes 786440 | tf_op jit(solution)/shard_map/ppermute | solution.py:432
  22.2 15.1 %collective-permute-start.9 = (bf16[128,1024]{1,0:T(8,128)(2,1)}, bf16[128,1024]{1,0:T(8,128)(2,1)S(1)}, u32[]{:S(2)}, u32[]{:S(2)}) collective-permute-start(bf16[128,1024]{1,0:T(8,128)(2,1)} %get-tuple-element.58), channel_id=1, source_target_pairs={{0,3},{1,0},{2,1},{3,2},{4,7},{5,4},{6,5},{7,6},{8,11},{9,8},{10,9... | collective-permute-start | bytes 786440 | tf_op jit(solution)/shard_map/ppermute | solution.py:432
  42.4 15.1 %collective-permute-start.14 = (bf16[256,1024]{1,0:T(8,128)(2,1)S(1)}, bf16[256,1024]{1,0:T(8,128)(2,1)S(1)}, u32[]{:S(2)}, u32[]{:S(2)}) collective-permute-start(bf16[256,1024]{1,0:T(8,128)(2,1)S(1)} %get-tuple-element.65), channel_id=1, source_target_pairs={{0,24},{8,0},{16,8},{24,16},{1,25},{9,1},{17,9},{25,17},{2,26},{10... | collective-permute-start | bytes 1572872 | tf_op jit(solution)/shard_map/ppermute | solution.py:372
  45.2 14.9 %collective-permute-start.15 = (bf16[256,1024]{1,0:T(8,128)(2,1)S(1)}, bf16[256,1024]{1,0:T(8,128)(2,1)S(1)}, u32[]{:S(2)}, u32[]{:S(2)}) collective-permute-start(bf16[256,1024]{1,0:T(8,128)(2,1)S(1)} %get-tuple-element.66), channel_id=1, source_target_pairs={{0,8},{8,16},{16,24},{24,0},{1,9},{9,17},{17,25},{25,1},{2,10},{10... | collective-permute-start | bytes 1572872 | tf_op jit(solution)/shard_map/ppermute | solution.py:372
  50.6 22.3 %collective-permute-start.16 = (bf16[256,1024]{1,0:T(8,128)(2,1)S(1)}, bf16[256,1024]{1,0:T(8,128)(2,1)S(1)}, u32[]{:S(2)}, u32[]{:S(2)}) collective-permute-start(bf16[256,1024]{1,0:T(8,128)(2,1)S(1)} %get-tuple-element.70), channel_id=1, source_target_pairs={{0,96},{32,0},{64,32},{96,64},{1,97},{33,1},{65,33},{97,65},{2,98}... | collective-permute-start | bytes 1572872 | tf_op jit(solution)/shard_map/ppermute | solution.py:372
  53.7 19.3 %collective-permute-start.17 = (bf16[256,1024]{1,0:T(8,128)(2,1)S(1)}, bf16[256,1024]{1,0:T(8,128)(2,1)S(1)}, u32[]{:S(2)}, u32[]{:S(2)}) collective-permute-start(bf16[256,1024]{1,0:T(8,128)(2,1)S(1)} %get-tuple-element.71), channel_id=1, source_target_pairs={{0,32},{32,64},{64,96},{96,0},{1,33},{33,65},{65,97},{97,1},{2,34}... | collective-permute-start | bytes 1572872 | tf_op jit(solution)/shard_map/ppermute | solution.py:372
  61.7 42.7 %collective-permute-start.18 = (bf16[512,1024]{1,0:T(8,128)(2,1)}, bf16[512,1024]{1,0:T(8,128)(2,1)}, u32[]{:S(2)}, u32[]{:S(2)}) collective-permute-start(bf16[512,1024]{1,0:T(8,128)(2,1)} %get-tuple-element.76), channel_id=1, source_target_pairs={{0,8},{8,16},{16,24},{24,0},{1,9},{9,17},{17,25},{25,1},{2,10},{10... | collective-permute-start | bytes 3145736 | tf_op jit(solution)/shard_map/ppermute | solution.py:376
  61.7 42.7 %collective-permute-start.19 = (bf16[512,1024]{1,0:T(8,128)(2,1)}, bf16[512,1024]{1,0:T(8,128)(2,1)}, u32[]{:S(2)}, u32[]{:S(2)}) collective-permute-start(bf16[512,1024]{1,0:T(8,128)(2,1)} %get-tuple-element.77), channel_id=1, source_target_pairs={{0,24},{8,0},{16,8},{24,16},{1,25},{9,1},{17,9},{25,17},{2,26},{10... | collective-permute-start | bytes 3145736 | tf_op jit(solution)/shard_map/ppermute | solution.py:376
  74.5 43.4 %collective-permute-start.22 = (bf16[512,1024]{1,0:T(8,128)(2,1)}, bf16[512,1024]{1,0:T(8,128)(2,1)}, u32[]{:S(2)}, u32[]{:S(2)}) collective-permute-start(bf16[512,1024]{1,0:T(8,128)(2,1)} %get-tuple-element.82), channel_id=1, source_target_pairs={{0,32},{32,64},{64,96},{96,0},{1,33},{33,65},{65,97},{97,1},{2,34}... | collective-permute-start | bytes 3145736 | tf_op jit(solution)/shard_map/ppermute | solution.py:376
  76.1 41.8 %collective-permute-start.23 = (bf16[512,1024]{1,0:T(8,128)(2,1)}, bf16[512,1024]{1,0:T(8,128)(2,1)}, u32[]{:S(2)}, u32[]{:S(2)}) collective-permute-start(bf16[512,1024]{1,0:T(8,128)(2,1)} %get-tuple-element.83), channel_id=1, source_target_pairs={{0,96},{32,0},{64,32},{96,64},{1,97},{33,1},{65,33},{97,65},{2,98}... | collective-permute-start | bytes 3145736 | tf_op jit(solution)/shard_map/ppermute | solution.py:376
  97.2 32.9 %all-to-all-start.1 = ((bf16[4,128,1024]{2,1,0:T(8,128)(2,1)}), bf16[4,128,1024]{2,1,0:T(8,128)(2,1)}, u32[]{:S(2)}, u32[]{:S(2)}) async-start(bf16[4,128,1024]{2,1,0:T(8,128)(2,1)} %bitcast.21), calls=%async_computation.1 | async-start | bytes 2097152 | tf_op jit(solution)/shard_map/all_to_all | solution.py:457
  106.5 5.3 %collective-permute-start.20 = (bf16[64,1024]{1,0:T(8,128)(2,1)S(1)}, bf16[64,1024]{1,0:T(8,128)(2,1)S(1)}, u32[]{:S(2)}, u32[]{:S(2)}) collective-permute-start(bf16[64,1024]{1,0:T(8,128)(2,1)S(1)} %get-tuple-element.79), channel_id=1, source_target_pairs={{0,96},{32,0},{64,32},{96,64},{1,97},{33,1},{65,33},{97,65},{2,98}... | collective-permute-start | bytes 393224 | tf_op jit(solution)/shard_map/ppermute | solution.py:372
  108.3 6.2 %collective-permute-start.21 = (bf16[64,1024]{1,0:T(8,128)(2,1)S(1)}, bf16[64,1024]{1,0:T(8,128)(2,1)S(1)}, u32[]{:S(2)}, u32[]{:S(2)}) collective-permute-start(bf16[64,1024]{1,0:T(8,128)(2,1)S(1)} %get-tuple-element.80), channel_id=1, source_target_pairs={{0,32},{32,64},{64,96},{96,0},{1,33},{33,65},{65,97},{97,1},{2,34}... | collective-permute-start | bytes 393224 | tf_op jit(solution)/shard_map/ppermute | solution.py:372
  114.6 18.3 %collective-permute-start.28 = (bf16[128,1024]{1,0:T(8,128)(2,1)S(1)}, bf16[128,1024]{1,0:T(8,128)(2,1)S(1)}, u32[]{:S(2)}, u32[]{:S(2)}) collective-permute-start(bf16[128,1024]{1,0:T(8,128)(2,1)S(1)} %get-tuple-element.91), channel_id=1, source_target_pairs={{0,32},{32,64},{64,96},{96,0},{1,33},{33,65},{65,97},{97,1},{2,34}... | collective-permute-start | bytes 786440 | tf_op jit(solution)/shard_map/ppermute | solution.py:376
  114.7 18.2 %collective-permute-start.29 = (bf16[128,1024]{1,0:T(8,128)(2,1)S(1)}, bf16[128,1024]{1,0:T(8,128)(2,1)}, u32[]{:S(2)}, u32[]{:S(2)}) collective-permute-start(bf16[128,1024]{1,0:T(8,128)(2,1)S(1)} %get-tuple-element.92), channel_id=1, source_target_pairs={{0,96},{32,0},{64,32},{96,64},{1,97},{33,1},{65,33},{97,65},{2,98}... | collective-permute-start | bytes 786440 | tf_op jit(solution)/shard_map/ppermute | solution.py:376
  120.1 6.2 %collective-permute-start.25 = (bf16[64,1024]{1,0:T(8,128)(2,1)S(1)}, bf16[64,1024]{1,0:T(8,128)(2,1)S(1)}, u32[]{:S(2)}, u32[]{:S(2)}) collective-permute-start(bf16[64,1024]{1,0:T(8,128)(2,1)S(1)} %get-tuple-element.87), channel_id=1, source_target_pairs={{0,8},{8,16},{16,24},{24,0},{1,9},{9,17},{17,25},{25,1},{2,10},{10... | collective-permute-start | bytes 393224 | tf_op jit(solution)/shard_map/ppermute | solution.py:372
  126.9 7.9 %collective-permute-start.26 = (bf16[128,1024]{1,0:T(8,128)(2,1)S(1)}, bf16[128,1024]{1,0:T(8,128)(2,1)S(1)}, u32[]{:S(2)}, u32[]{:S(2)}) collective-permute-start(bf16[128,1024]{1,0:T(8,128)(2,1)S(1)} %get-tuple-element.88), channel_id=1, source_target_pairs={{0,8},{8,16},{16,24},{24,0},{1,9},{9,17},{17,25},{25,1},{2,10},{10... | collective-permute-start | bytes 786440 | tf_op jit(solution)/shard_map/ppermute | solution.py:376
  127.7 7.0 %collective-permute-start.27 = (bf16[128,1024]{1,0:T(8,128)(2,1)S(1)}, bf16[128,1024]{1,0:T(8,128)(2,1)S(1)}, u32[]{:S(2)}, u32[]{:S(2)}) collective-permute-start(bf16[128,1024]{1,0:T(8,128)(2,1)S(1)} %get-tuple-element.89), channel_id=1, source_target_pairs={{0,24},{8,0},{16,8},{24,16},{1,25},{9,1},{17,9},{25,17},{2,26},{10... | collective-permute-start | bytes 786440 | tf_op jit(solution)/shard_map/ppermute | solution.py:376
  (11 other events, 19.0 us)

commit v4 on v3

--- a/solution.py
+++ b/solution.py
@@ -60,50 +60,68 @@
 ANY = pl.BlockSpec(memory_space=pl.ANY)
 
 
+def bucket(where_ref, r):
+    return pl.ds(pl.multiple_of(jnp.bitwise_and(where_ref[0] + r, 3) * 128, 128), 128)
+
+
 def dispatch_tokens(where, region, tokens):
     n, width = tokens.shape
 
-    def body(where_ref, region_ref, tok_ref, place_ref, *outs):
-        dest = jnp.bitwise_and(region_ref[...] - where_ref[0] + 4, 3)
-        onehot = (dest == lax.broadcasted_iota(jnp.int32, (8, n), 0)).astype(F32)
+    def body(where_ref, region_hbm, tok_hbm, place_ref, *refs):
+        outs, (region_ref, tok_ref, sems) = refs[:4], refs[4:]
+        copies = [
+            pltpu.make_async_copy(region_hbm, region_ref, sems.at[0]),
+            pltpu.make_async_copy(tok_hbm, tok_ref, sems.at[1]),
+        ]
+        for copy in copies:
+            copy.start()
         upper = (
             lax.broadcasted_iota(jnp.int32, (n, n), 0) < lax.broadcasted_iota(jnp.int32, (n, n), 1)
         ).astype(F32)
+        copies[0].wait()
+        dest = region_ref[...]
+        onehot = (dest == lax.broadcasted_iota(jnp.int32, (8, n), 0)).astype(F32)
         before = dot_nn(onehot.astype(BF16), upper.astype(BF16))
         rank = jnp.sum(before * onehot, axis=0, keepdims=True).astype(jnp.int32)
         slot = dest * 128 + rank
         place = (slot == lax.broadcasted_iota(jnp.int32, (512, n), 0)).astype(F32).astype(BF16)
         place_ref[...] = place
+        copies[1].wait()
         for r, out in enumerate(outs):
-            out[...] = dot_nn(place[r * 128 : (r + 1) * 128], tok_ref[...]).astype(BF16)
+            out[...] = dot_nn(place_ref[bucket(where_ref, r), :], tok_ref[...]).astype(BF16)
 
     return pl.pallas_call(
         body,
         out_shape=[shape(512, n)] + [shape(128, width)] * 4,
-        in_specs=[pl.BlockSpec(memory_space=pltpu.SMEM)] + [VMEM] * 2,
+        in_specs=[pl.BlockSpec(memory_space=pltpu.SMEM)] + [HBM] * 2,
         out_specs=[VMEM] * 5,
+        scratch_shapes=[
+            pltpu.VMEM((1, n), jnp.int32),
+            pltpu.VMEM((n, width), BF16),
+            pltpu.SemaphoreType.DMA((2,)),
+        ],
         compiler_params=params(),
         cost_estimate=cost(4 * n * width * 2),
     )(where, region, tokens)
 
 
-def dispatch_grads(place, gate, grads):
+def dispatch_grads(where, place, gate, grads):
     n, width = grads.shape
 
-    def body(place_ref, gate_ref, grad_ref, *outs):
+    def body(where_ref, place_ref, gate_ref, grad_ref, *outs):
         column = jnp.transpose(jnp.broadcast_to(gate_ref[...], (128, n)))[:, :1]
         scaled = (column * grad_ref[...].astype(F32)).astype(BF16)
         for r, out in enumerate(outs):
-            out[...] = dot_nn(place_ref[r * 128 : (r + 1) * 128, :], scaled).astype(BF16)
+            out[...] = dot_nn(place_ref[bucket(where_ref, r), :], scaled).astype(BF16)
 
     return pl.pallas_call(
         body,
         out_shape=[shape(128, width)] * 4,
-        in_specs=[VMEM] * 3,
+        in_specs=[pl.BlockSpec(memory_space=pltpu.SMEM)] + [VMEM] * 3,
         out_specs=[VMEM] * 4,
         compiler_params=params(),
         cost_estimate=cost(4 * n * width * 2),
-    )(place, gate, grads)
+    )(where, place, gate, grads)
 
 
 HBM = pl.BlockSpec(memory_space=pltpu.HBM)
@@ -341,24 +359,20 @@
     )(sides, *arrived)
 
 
-def restore_order(where, place, rows):
+def restore_order(place, rows):
     n, width = place.shape[1], rows.shape[1]
 
-    def body(where_ref, place_ref, rows_ref, out_ref):
-        total = jnp.zeros((n, width), F32)
-        for e in range(4):
-            bucket = pl.multiple_of(jnp.bitwise_and(e - where_ref[0] + 4, 3) * 128, 128)
-            total += dot_tn(place_ref[pl.ds(bucket, 128), :], rows_ref[e * 128 : (e + 1) * 128, :])
-        out_ref[...] = total.astype(BF16)
+    def body(place_ref, rows_ref, out_ref):
+        out_ref[...] = dot_tn(place_ref[...], rows_ref[...]).astype(BF16)
 
     return pl.pallas_call(
         body,
         out_shape=shape(n, width),
-        in_specs=[pl.BlockSpec(memory_space=pltpu.SMEM)] + [VMEM] * 2,
+        in_specs=[VMEM] * 2,
         out_specs=VMEM,
         compiler_params=params(),
         cost_estimate=cost(2**21),
-    )(where, place, rows)
+    )(place, rows)
 
 
 def add(*terms):
@@ -376,31 +390,55 @@
     return lax.ppermute(up, axis, ring(1)), lax.ppermute(down, axis, ring(3))
 
 
+def cut(total, refs):
+    keep_ref, sides_ref, low_ref, high_ref, mark_ref = refs
+    n = total.shape[0]
+    q = n // 4
+    mark_ref[...] = jnp.zeros_like(mark_ref)
+    total = total.astype(BF16)
+    keep_ref[...] = total[:q]
+    sides_ref[:q, :] = total[q : 2 * q]
+    low_ref[...] = total[2 * q : 2 * q + q // 2]
+    high_ref[...] = total[2 * q + q // 2 : 3 * q]
+    sides_ref[q:, :] = total[3 * q :]
+
+
+def cut_shapes(n, width):
+    return [shape(n // k, width) for k in (4, 2, 8, 8)] + [MARK]
+
+
 def combine(own, received):
     n, width = own.shape
-    q = n // 4
-
-    def body(own_ref, left, right, keep_ref, sides_ref, low_ref, high_ref, mark_ref):
-        mark_ref[...] = jnp.zeros_like(mark_ref)
-
-        def total(begin, end):
-            span = slice(begin, end)
-            return add(own_ref[span, :], left[span, :], right[span, :]).astype(BF16)
-
-        low_ref[...] = total(2 * q, 2 * q + q // 2)
-        high_ref[...] = total(2 * q + q // 2, 3 * q)
-        keep_ref[...] = total(0, q)
-        sides_ref[:q, :] = total(q, 2 * q)
-        sides_ref[q:, :] = total(3 * q, n)
-
-    return pl.pallas_call(
-        body,
-        out_shape=[shape(q, width), shape(2 * q, width), shape(q // 2, width), shape(q // 2, width), MARK],
+
+    def body(own_ref, left, right, *refs):
+        cut(add(own_ref[...], left[...], right[...]), refs)
+
+    return pl.pallas_call(
+        body,
+        out_shape=cut_shapes(n, width),
         in_specs=[VMEM] * 3,
         out_specs=[VMEM] * 5,
         compiler_params=params(),
         cost_estimate=cost(8 * n * width),
     )(own, *received)
+
+
+def combine_product(act, rows, group, received):
+    tok, width = rows.shape
+
+    def body(act_ref, rows_ref, left, right, *refs):
+        cut(dot_nn(act_ref[...], rows_ref[...]) + add(left[...], right[...]), refs)
+
+    shapes = cut_shapes(512, width)
+    return pl.pallas_call(
+        body,
+        grid=(1,),
+        in_specs=[pl.BlockSpec((512, tok), lambda i: (group, 0))] + [VMEM] * 3,
+        out_specs=[fixed(*out.shape) for out in shapes],
+        out_shape=shapes,
+        compiler_params=params(),
+        cost_estimate=cost(10 * 512 * width),
+    )(act, rows, *received)
 
 
 def in_hbm(array):
@@ -425,8 +463,10 @@
     table = jnp.concatenate([by_x, by_y, same, (expert - every) % 4, core[None]])
     weight_in, weight_out = in_hbm(w_in[0]), in_hbm(w_out[0])
 
-    place, *send_x = dispatch_tokens(expert[None], region.reshape(1, -1), tokens)
-    send_d = dispatch_grads(place, gate.reshape(1, -1), out_grad)
+    place, *send_x = dispatch_tokens(
+        expert[None], in_hbm(region.reshape(1, -1)), in_hbm(tokens)
+    )
+    send_d = dispatch_grads(expert[None], place, gate.reshape(1, -1), out_grad)
 
     def to_owner(parts):
         return [parts[0]] + [lax.ppermute(parts[r], "expert", ring(r)) for r in (1, 2, 3)]
@@ -452,17 +492,20 @@
     *pair, mark = join(in_sides, hop)
     in_parts = second_hop(*pair, "y")
     pre_c, in_own, mark = backward(table, rows_d, rows_x, slope, weight_out, 3, 1, (mark,))
-    out_own = outer_rest(act, rows_d, 3, 1, (mark,))
     own = sum_cores(row_gradients(table, (pre_a, pre_b, pre_c), weight_in, ()))
     back = lax.all_to_all(own, "expert", split_axis=0, concat_axis=0, tiled=True)
 
-    keep, sides, low, high, mark = combine(out_own, out_parts)
-    *pair, mark = join(sides, first_hop(low, high, "y"))
-    grad_out = add(keep, *second_hop(*pair, "y")) * scale
-    keep, sides, low, high, _ = combine(after(in_own, mark), in_parts)
-    *pair, _ = join(sides, first_hop(low, high, "x"))
-    grad_in = add(keep, *second_hop(*pair, "x")) * scale
-    token_grad = restore_order(expert[None], place, back)
+    out_keep, out_sides, low, high, mark = combine_product(act, rows_d, 3, out_parts)
+    out_hop = first_hop(low, high, "y")
+    in_keep, in_sides, low, high, mark = combine(after(in_own, mark), in_parts)
+    in_hop = first_hop(low, high, "x")
+    *pair, mark = join(after(out_sides, mark), out_hop)
+    out_parts = second_hop(*pair, "y")
+    *pair, _ = join(after(in_sides, mark), in_hop)
+    in_parts = second_hop(*pair, "x")
+    grad_out = add(out_keep, *out_parts) * scale
+    grad_in = add(in_keep, *in_parts) * scale
+    token_grad = restore_order(place, back)
     return token_grad, grad_in[None], grad_out[None]
 
 

time: 137 us -> 132 us (0.964)
  local copies, waits for them, and re-layouts: 4.33 us -> 2.63 us
    pallas_call x2 -> x1, Pallas kernels: 6.23 us -> 3.76 us  [outer_rest(): pl.pallas_call(body, grid=(count,), in_specs=[pl.BlockSpec((512, tok), la...]
    ppermute x8, waiting for transfers between devices: 12.8 us -> 10.8 us  [first_hop(): return (lax.ppermute(low, axis, ring(3)), lax.ppermute(high, axis, ring(1)))]
    unnamed x8, local copies, waits for them, and re-layouts: 3.43 us -> 1.73 us
  transfers between devices with their start and end apart: 31 -> 31, of which waited for: 11 -> 12; matrix products, arithmetic and copies ran while one was open for 4% -> 3% of each run, Pallas kernels for 41% -> 41%
where the time goes in v4:
time: 132 us; the launch traced here: 131 us
  Pallas kernels  59.4 us (45%)
  starting transfers between devices  38 us (29%)
  waiting for transfers between devices  20.8 us (16%)
  blocking collectives  5.42 us (4%)
  other arithmetic  4 us (3%)
  local copies, waits for them, and re-layouts  2.63 us (2%)
    pallas_call x3, Pallas kernels, backward(): pl.pallas_call(body, grid_spec=pltpu.PrefetchScalarGridSpec(num_scalar_pr...  18.8 us
    ppermute x8, starting transfers between devices, second_hop(): return (lax.ppermute(up, axis, ring(1)), lax.ppermute(down, axis, ring(3)))  13 us
    pallas_call x1, Pallas kernels, forward(): pl.pallas_call(body, grid_spec=pltpu.PrefetchScalarGridSpec(num_scalar_pr...  11.7 us
    ppermute x8, waiting for transfers between devices, first_hop(): return (lax.ppermute(low, axis, ring(3)), lax.ppermute(high, axis, ring(1)))  10.8 us
    ppermute x8, starting transfers between devices, first_hop(): return (lax.ppermute(low, axis, ring(3)), lax.ppermute(high, axis, ring(1)))  10 us
    ppermute x6, starting transfers between devices, to_owner(): lax.ppermute(parts[r], 'expert', ring(r))  8.43 us
    pallas_call x1, Pallas kernels, row_gradients(): pl.pallas_call(body, grid_spec=pltpu.PrefetchScalarGridSpec(num_scalar_pr...  7.24 us
    ppermute x6, waiting for transfers between devices, to_owner(): lax.ppermute(parts[r], 'expert', ring(r))  6.93 us
  transfers between devices with their start and end apart: 31, of which 12 were waited for; matrix products, arithmetic and copies ran while one was open for 3% of the time, Pallas kernels for 41%

profile of v4, /device:TPU:0, one launch (start us, length us, event | category | flops | bytes accessed | tf_op | source)
XLA Modules:
  0.0 131.1 jit_solution(18294929827257164455)
XLA Ops:
  0.6 2.1 %shard_map.103 = (bf16[512,256]{1,0:T(8,128)(2,1)S(1)}, bf16[128,1024]{1,0:T(8,128)(2,1)S(1)}, bf16[128,1024]{1,0:T(8,128)(2,1)}, bf16[128,1024]{1,0:T(8,128)(2,1)S(1)}, bf16[128,1024]{1,0:T(8,128)(2,1)S(1)}) custom-call(s32[1]{0:T(128)} %bitcast.where_ref, s32[1,256]{1,0:T(1,128)} %bitcast.21, bf16[256,1024]{1,0:T(8,128)(2,1)} %tok_hbm.1), custom_call_target="tpu_custom_call" | custom-call | bytes 2097152 | tf_op jit(solution)/shard_map/pallas_call | solution.py:93
  2.7 2.1 %collective-permute-start = (bf16[128,1024]{1,0:T(8,128)(2,1)}, bf16[128,1024]{1,0:T(8,128)(2,1)S(1)}, u32[]{:S(2)}, u32[]{:S(2)}) collective-permute-start(bf16[128,1024]{1,0:T(8,128)(2,1)} %get-tuple-element.51), channel_id=1, source_target_pairs={{0,1},{1,2},{2,3},{3,0},{4,5},{5,6},{6,7},{7,4},{8,9},{9,10},{10,1... | collective-permute-start | bytes 786440 | tf_op jit(solution)/shard_map/ppermute | solution.py:472
  4.8 3.6 %collective-permute-start.1 = (bf16[128,1024]{1,0:T(8,128)(2,1)S(1)}, bf16[128,1024]{1,0:T(8,128)(2,1)S(1)}, u32[]{:S(2)}, u32[]{:S(2)}) collective-permute-start(bf16[128,1024]{1,0:T(8,128)(2,1)S(1)} %get-tuple-element.52), channel_id=1, source_target_pairs={{0,2},{1,3},{2,0},{3,1},{4,6},{5,7},{6,4},{7,5},{8,10},{9,11},{10,... | collective-permute-start | bytes 786440 | tf_op jit(solution)/shard_map/ppermute | solution.py:472
  14.5 6.9 %collective-permute-done.1.refs_2_ = bf16[128,1024]{1,0:T(8,128)(2,1)S(1)} collective-permute-done((bf16[128,1024]{1,0:T(8,128)(2,1)S(1)}, bf16[128,1024]{1,0:T(8,128)(2,1)S(1)}, u32[]{:S(2)}, u32[]{:S(2)}) %collective-permute-start.1) | collective-permute-done | bytes 262176 | tf_op jit(solution)/shard_map/ppermute | solution.py:472
  24.1 11.7 %shard_map.104 = (bf16[2048,1024]{1,0:T(8,128)(2,1)}, bf16[2048,1024]{1,0:T(8,128)(2,1)}, bf16[1024,1024]{1,0:T(8,128)(2,1)S(1)}, f32[8,128]{1,0:T(8,128)S(1)}) custom-call(s32[53]{0:T(128)S(1)} %concatenate.3.table_ref, bf16[128,1024]{1,0:T(8,128)(2,1)S(1)} %get-tuple-element.50.refs_0_, bf16[128,1024]{1,0:T(8,128)(2,1)S(1)} %collective-permute-done.refs_1_, ...), custom_call_target="tpu_custom_call" | custom-call | bytes 16777216 | tf_op jit(solution)/shard_map/pallas_call | solution.py:203
  38.6 3.1 %shard_map.110 = (bf16[256,1024]{1,0:T(8,128)(2,1)S(1)}, bf16[256,1024]{1,0:T(8,128)(2,1)S(1)}, bf16[1024,1024]{1,0:T(8,128)(2,1)S(1)}, f32[8,128]{1,0:T(8,128)S(1)}) custom-call(s32[53]{0:T(128)S(1)} %concatenate.3.table_ref, bf16[2048,1024]{1,0:T(8,128)(2,1)} %get-tuple-element.54.act_ref, bf16[128,1024]{1,0:T(8,128)(2,1)S(1)} %shard_map.106.refs_0_, ...), custom_call_target="tpu_custom_call" | custom-call | bytes 4194304 | tf_op jit(solution)/shard_map/pallas_call | solution.py:230
  41.7 2.8 %collective-permute-start.14 = (bf16[256,1024]{1,0:T(8,128)(2,1)S(1)}, bf16[256,1024]{1,0:T(8,128)(2,1)S(1)}, u32[]{:S(2)}, u32[]{:S(2)}) collective-permute-start(bf16[256,1024]{1,0:T(8,128)(2,1)S(1)} %get-tuple-element.66), channel_id=1, source_target_pairs={{0,24},{8,0},{16,8},{24,16},{1,25},{9,1},{17,9},{25,17},{2,26},{10... | collective-permute-start | bytes 1572872 | tf_op jit(solution)/shard_map/ppermute | solution.py:386
  44.6 5.4 %shard_map.111 = (bf16[512,1024]{1,0:T(8,128)(2,1)S(1)}, bf16[256,1024]{1,0:T(8,128)(2,1)S(1)}, bf16[256,1024]{1,0:T(8,128)(2,1)S(1)}, f32[8,128]{1,0:T(8,128)S(1)}) custom-call(s32[53]{0:T(128)S(1)} %concatenate.3.table_ref, bf16[1024,1024]{1,0:T(8,128)(2,1)S(1)} %get-tuple-element.60.grads_ref.rows_ref, bf16[1024,1024]{1,0:T(8,128)(2,1)S(1)} %get-tuple-element.61.rows_ref, ...), custom_call_target="tpu_custom_call" | custom-call | bytes 6291456 | tf_op jit(solution)/shard_map/pallas_call | solution.py:282
  50.0 3.1 %collective-permute-start.16 = (bf16[256,1024]{1,0:T(8,128)(2,1)S(1)}, bf16[256,1024]{1,0:T(8,128)(2,1)S(1)}, u32[]{:S(2)}, u32[]{:S(2)}) collective-permute-start(bf16[256,1024]{1,0:T(8,128)(2,1)S(1)} %get-tuple-element.71), channel_id=1, source_target_pairs={{0,96},{32,0},{64,32},{96,64},{1,97},{33,1},{65,33},{97,65},{2,98}... | collective-permute-start | bytes 1572872 | tf_op jit(solution)/shard_map/ppermute | solution.py:386
  53.0 3.8 %shard_map.112.sides_ref = bf16[1024,1024]{1,0:T(8,128)(2,1)S(1)} custom-call(bf16[2048,1024]{1,0:T(8,128)(2,1)} %get-tuple-element.54.act_ref, bf16[1024,1024]{1,0:T(8,128)(2,1)S(1)} %get-tuple-element.60.grads_ref.rows_ref, f32[8,128]{1,0:T(8,128)S(1)} %get-tuple-element.65.refs_0_), custom_call_target="tpu_custom_call" | custom-call | bytes 6291456 | tf_op jit(solution)/shard_map/pallas_call | solution.py:251
  56.8 2.6 %collective-permute-done.15.from_prev = bf16[256,1024]{1,0:T(8,128)(2,1)S(1)} collective-permute-done((bf16[256,1024]{1,0:T(8,128)(2,1)S(1)}, bf16[256,1024]{1,0:T(8,128)(2,1)S(1)}, u32[]{:S(2)}, u32[]{:S(2)}) %collective-permute-start.15) | collective-permute-done | bytes 524320 | tf_op jit(solution)/shard_map/ppermute | solution.py:386
  61.0 3.2 %collective-permute-start.19 = (bf16[512,1024]{1,0:T(8,128)(2,1)}, bf16[512,1024]{1,0:T(8,128)(2,1)}, u32[]{:S(2)}, u32[]{:S(2)}) collective-permute-start(bf16[512,1024]{1,0:T(8,128)(2,1)} %get-tuple-element.77), channel_id=1, source_target_pairs={{0,24},{8,0},{16,8},{24,16},{1,25},{9,1},{17,9},{25,17},{2,26},{10... | collective-permute-start | bytes 3145736 | tf_op jit(solution)/shard_map/ppermute | solution.py:390
  64.3 8.0 %shard_map.114 = (bf16[1024,1024]{1,0:T(8,128)(2,1)S(1)}, bf16[1024,1024]{1,0:T(8,128)(2,1)S(1)}, f32[8,128]{1,0:T(8,128)}) custom-call(s32[53]{0:T(128)S(1)} %concatenate.3.table_ref, bf16[1024,1024]{1,0:T(8,128)(2,1)S(1)} %get-tuple-element.60.grads_ref.rows_ref, bf16[1024,1024]{1,0:T(8,128)(2,1)S(1)} %get-tuple-element.61.rows_ref, ...), custom_call_target="tpu_custom_call" | custom-call | bytes 10485760 | tf_op jit(solution)/shard_map/pallas_call | solution.py:282
  77.1 5.4 %shard_map.116 = (bf16[512,1024]{1,0:T(8,128)(2,1)S(1)}, bf16[512,1024]{1,0:T(8,128)(2,1)S(1)}, f32[8,128]{1,0:T(8,128)}) custom-call(s32[53]{0:T(128)S(1)} %concatenate.3.table_ref, bf16[1024,1024]{1,0:T(8,128)(2,1)S(1)} %get-tuple-element.60.grads_ref.rows_ref, bf16[1024,1024]{1,0:T(8,128)(2,1)S(1)} %get-tuple-element.61.rows_ref, ...), custom_call_target="tpu_custom_call" | custom-call | bytes 6291456 | tf_op jit(solution)/shard_map/pallas_call | solution.py:282
  82.5 7.2 %shard_map.117 = bf16[1024,1024]{1,0:T(8,128)(2,1)S(1)} custom-call(s32[53]{0:T(128)S(1)} %concatenate.3.table_ref, bf16[512,1024]{1,0:T(8,128)(2,1)S(1)} %get-tuple-element.64.a_ref, bf16[1024,1024]{1,0:T(8,128)(2,1)S(1)} %get-tuple-element.69.b_ref, bf16[512,1024]{1,0:T(8,128)(2,1)S(1)} %get-tuple-element.74.c_ref, bf16[4096,1024]{1,0:T(8,128)(2,1)} %bitcast.19), custom_call_target="tpu_custom_call" | custom-call | bytes 12582912 | tf_op jit(solution)/shard_map/pallas_call | solution.py:326
  89.7 5.4 %all_to_all.17 = bf16[2,512,1024]{2,1,0:T(8,128)(2,1)S(1)} all-to-all(bf16[2,512,1024]{2,1,0:T(8,128)(2,1)S(1)} %bitcast.13), channel_id=1, replica_groups=mesh['y'=4,'x'=4,'core'=2,'expert'=4] {'core'}, dimensions={0} | all-to-all | bytes 4194304 | tf_op jit(solution)/shard_map/all_to_all | solution.py:449
  96.5 4.6 %all-to-all-start.1 = ((bf16[4,128,1024]{2,1,0:T(8,128)(2,1)}), bf16[4,128,1024]{2,1,0:T(8,128)(2,1)}, u32[]{:S(2)}, u32[]{:S(2)}) async-start(bf16[4,128,1024]{2,1,0:T(8,128)(2,1)} %bitcast.20), calls=%async_computation.1 | async-start | bytes 2097152 | tf_op jit(solution)/shard_map/all_to_all | solution.py:496
  101.2 3.1 %shard_map.119 = (bf16[128,1024]{1,0:T(8,128)(2,1)S(1)}, bf16[256,1024]{1,0:T(8,128)(2,1)S(1)}, bf16[64,1024]{1,0:T(8,128)(2,1)S(1)}, bf16[64,1024]{1,0:T(8,128)(2,1)S(1)}, f32[8,128]{1,0:T(8,128)S(1)}) custom-call(bf16[2048,1024]{1,0:T(8,128)(2,1)} %get-tuple-element.54.act_ref, bf16[1024,1024]{1,0:T(8,128)(2,1)S(1)} %get-tuple-element.60.grads_ref.rows_ref, ...), custom_call_target="tpu_custom_call" | custom-call | bytes 5242880 | tf_op jit(solution)/shard_map/pallas_call | solution.py:433
  109.6 2.7 %collective-permute-done.23.from_prev = bf16[64,1024]{1,0:T(8,128)(2,1)S(1)} collective-permute-done((bf16[64,1024]{1,0:T(8,128)(2,1)S(1)}, bf16[64,1024]{1,0:T(8,128)(2,1)S(1)}, u32[]{:S(2)}, u32[]{:S(2)}) %collective-permute-start.23) | collective-permute-done | bytes 131104 | tf_op jit(solution)/shard_map/ppermute | solution.py:386
  112.5 3.2 %collective-permute-start.29 = (bf16[128,1024]{1,0:T(8,128)(2,1)S(1)}, bf16[128,1024]{1,0:T(8,128)(2,1)S(1)}, u32[]{:S(2)}, u32[]{:S(2)}) collective-permute-start(bf16[128,1024]{1,0:T(8,128)(2,1)S(1)} %get-tuple-element.94), channel_id=1, source_target_pairs={{0,96},{32,0},{64,32},{96,64},{1,97},{33,1},{65,33},{97,65},{2,98}... | collective-permute-start | bytes 786440 | tf_op jit(solution)/shard_map/ppermute | solution.py:390
  115.8 2.0 %collective-permute-start.25 = (bf16[64,1024]{1,0:T(8,128)(2,1)S(1)}, bf16[64,1024]{1,0:T(8,128)(2,1)S(1)}, u32[]{:S(2)}, u32[]{:S(2)}) collective-permute-start(bf16[64,1024]{1,0:T(8,128)(2,1)S(1)} %get-tuple-element.89), channel_id=1, source_target_pairs={{0,8},{8,16},{16,24},{24,0},{1,9},{9,17},{17,25},{25,1},{2,10},{10... | collective-permute-start | bytes 393224 | tf_op jit(solution)/shard_map/ppermute | solution.py:386
  117.8 2.9 %collective-permute-done.24.from_next = bf16[64,1024]{1,0:T(8,128)(2,1)S(1)} collective-permute-done((bf16[64,1024]{1,0:T(8,128)(2,1)S(1)}, bf16[64,1024]{1,0:T(8,128)(2,1)S(1)}, u32[]{:S(2)}, u32[]{:S(2)}) %collective-permute-start.24) | collective-permute-done | bytes 131104 | tf_op jit(solution)/shard_map/ppermute | solution.py:386
  123.4 2.4 %collective-permute-start.27 = (bf16[128,1024]{1,0:T(8,128)(2,1)S(1)}, bf16[128,1024]{1,0:T(8,128)(2,1)S(1)}, u32[]{:S(2)}, u32[]{:S(2)}) collective-permute-start(bf16[128,1024]{1,0:T(8,128)(2,1)S(1)} %get-tuple-element.91), channel_id=1, source_target_pairs={{0,24},{8,0},{16,8},{24,16},{1,25},{9,1},{17,9},{25,17},{2,26},{10... | collective-permute-start | bytes 786440 | tf_op jit(solution)/shard_map/ppermute | solution.py:390
  125.8 2.5 %shard_map.118 = bf16[256,1024]{1,0:T(8,128)(2,1)} custom-call(bf16[512,256]{1,0:T(8,128)(2,1)S(1)} %get-tuple-element.49.place_ref, bf16[512,1024]{1,0:T(8,128)(2,1)} %bitcast.8.rows_ref), custom_call_target="tpu_custom_call" | custom-call | bytes 2097152 | tf_op jit(solution)/shard_map/pallas_call | solution.py:368
  (81 shorter events, 30.2 us)
Async XLA Ops:
  2.7 10.8 %collective-permute-start = (bf16[128,1024]{1,0:T(8,128)(2,1)}, bf16[128,1024]{1,0:T(8,128)(2,1)S(1)}, u32[]{:S(2)}, u32[]{:S(2)}) collective-permute-start(bf16[128,1024]{1,0:T(8,128)(2,1)} %get-tuple-element.51), channel_id=1, source_target_pairs={{0,1},{1,2},{2,3},{3,0},{4,5},{5,6},{6,7},{7,4},{8,9},{9,10},{10,1... | collective-permute-start | bytes 786440 | tf_op jit(solution)/shard_map/ppermute | solution.py:472
  4.8 16.6 %collective-permute-start.1 = (bf16[128,1024]{1,0:T(8,128)(2,1)S(1)}, bf16[128,1024]{1,0:T(8,128)(2,1)S(1)}, u32[]{:S(2)}, u32[]{:S(2)}) collective-permute-start(bf16[128,1024]{1,0:T(8,128)(2,1)S(1)} %get-tuple-element.52), channel_id=1, source_target_pairs={{0,2},{1,3},{2,0},{3,1},{4,6},{5,7},{6,4},{7,5},{8,10},{9,11},{10,... | collective-permute-start | bytes 786440 | tf_op jit(solution)/shard_map/ppermute | solution.py:472
  8.4 13.0 %collective-permute-start.2 = (bf16[128,1024]{1,0:T(8,128)(2,1)S(1)}, bf16[128,1024]{1,0:T(8,128)(2,1)S(1)}, u32[]{:S(2)}, u32[]{:S(2)}) collective-permute-start(bf16[128,1024]{1,0:T(8,128)(2,1)S(1)} %get-tuple-element.53), channel_id=1, source_target_pairs={{0,3},{1,0},{2,1},{3,2},{4,7},{5,4},{6,5},{7,6},{8,11},{9,8},{10,9... | collective-permute-start | bytes 786440 | tf_op jit(solution)/shard_map/ppermute | solution.py:472
  9.4 12.8 %collective-permute-start.3 = (bf16[128,1024]{1,0:T(8,128)(2,1)S(1)}, bf16[128,1024]{1,0:T(8,128)(2,1)S(1)}, u32[]{:S(2)}, u32[]{:S(2)}) collective-permute-start(bf16[128,1024]{1,0:T(8,128)(2,1)S(1)} %get-tuple-element.50.refs_0_), channel_id=1, source_target_pairs={{0,4},{4,0},{1,5},{5,1},{2,6},{6,2},{3,7},{7,3},{8,12},{12,8},{9,1... | collective-permute-start | bytes 786440 | tf_op jit(solution)/shard_map/ppermute | solution.py:22
  12.5 23.6 %collective-permute-start.7 = (bf16[128,1024]{1,0:T(8,128)(2,1)}, bf16[128,1024]{1,0:T(8,128)(2,1)S(1)}, u32[]{:S(2)}, u32[]{:S(2)}) collective-permute-start(bf16[128,1024]{1,0:T(8,128)(2,1)} %get-tuple-element.57), channel_id=1, source_target_pairs={{0,1},{1,2},{2,3},{3,0},{4,5},{5,6},{6,7},{7,4},{8,9},{9,10},{10,1... | collective-permute-start | bytes 786440 | tf_op jit(solution)/shard_map/ppermute | solution.py:472
  13.5 8.7 %collective-permute-start.4 = (bf16[128,1024]{1,0:T(8,128)(2,1)S(1)}, bf16[128,1024]{1,0:T(8,128)(2,1)S(1)}, u32[]{:S(2)}, u32[]{:S(2)}) collective-permute-start(bf16[128,1024]{1,0:T(8,128)(2,1)S(1)} %collective-permute-done.refs_1_), channel_id=1, source_target_pairs={{0,4},{4,0},{1,5},{5,1},{2,6},{6,2},{3,7},{7,3},{8,12},{12,8},{9,1... | collective-permute-start | bytes 786440 | tf_op jit(solution)/shard_map/ppermute | solution.py:22
  21.4 15.0 %collective-permute-start.8 = (bf16[128,1024]{1,0:T(8,128)(2,1)}, bf16[128,1024]{1,0:T(8,128)(2,1)S(1)}, u32[]{:S(2)}, u32[]{:S(2)}) collective-permute-start(bf16[128,1024]{1,0:T(8,128)(2,1)} %get-tuple-element.58), channel_id=1, source_target_pairs={{0,2},{1,3},{2,0},{3,1},{4,6},{5,7},{6,4},{7,5},{8,10},{9,11},{10,... | collective-permute-start | bytes 786440 | tf_op jit(solution)/shard_map/ppermute | solution.py:472
  21.4 15.2 %collective-permute-start.9 = (bf16[128,1024]{1,0:T(8,128)(2,1)}, bf16[128,1024]{1,0:T(8,128)(2,1)S(1)}, u32[]{:S(2)}, u32[]{:S(2)}) collective-permute-start(bf16[128,1024]{1,0:T(8,128)(2,1)} %get-tuple-element.59), channel_id=1, source_target_pairs={{0,3},{1,0},{2,1},{3,2},{4,7},{5,4},{6,5},{7,6},{8,11},{9,8},{10,9... | collective-permute-start | bytes 786440 | tf_op jit(solution)/shard_map/ppermute | solution.py:472
  41.7 15.1 %collective-permute-start.14 = (bf16[256,1024]{1,0:T(8,128)(2,1)S(1)}, bf16[256,1024]{1,0:T(8,128)(2,1)S(1)}, u32[]{:S(2)}, u32[]{:S(2)}) collective-permute-start(bf16[256,1024]{1,0:T(8,128)(2,1)S(1)} %get-tuple-element.66), channel_id=1, source_target_pairs={{0,24},{8,0},{16,8},{24,16},{1,25},{9,1},{17,9},{25,17},{2,26},{10... | collective-permute-start | bytes 1572872 | tf_op jit(solution)/shard_map/ppermute | solution.py:386
  44.6 14.9 %collective-permute-start.15 = (bf16[256,1024]{1,0:T(8,128)(2,1)S(1)}, bf16[256,1024]{1,0:T(8,128)(2,1)S(1)}, u32[]{:S(2)}, u32[]{:S(2)}) collective-permute-start(bf16[256,1024]{1,0:T(8,128)(2,1)S(1)} %get-tuple-element.67), channel_id=1, source_target_pairs={{0,8},{8,16},{16,24},{24,0},{1,9},{9,17},{17,25},{25,1},{2,10},{10... | collective-permute-start | bytes 1572872 | tf_op jit(solution)/shard_map/ppermute | solution.py:386
  50.0 22.3 %collective-permute-start.16 = (bf16[256,1024]{1,0:T(8,128)(2,1)S(1)}, bf16[256,1024]{1,0:T(8,128)(2,1)S(1)}, u32[]{:S(2)}, u32[]{:S(2)}) collective-permute-start(bf16[256,1024]{1,0:T(8,128)(2,1)S(1)} %get-tuple-element.71), channel_id=1, source_target_pairs={{0,96},{32,0},{64,32},{96,64},{1,97},{33,1},{65,33},{97,65},{2,98}... | collective-permute-start | bytes 1572872 | tf_op jit(solution)/shard_map/ppermute | solution.py:386
  53.0 19.2 %collective-permute-start.17 = (bf16[256,1024]{1,0:T(8,128)(2,1)S(1)}, bf16[256,1024]{1,0:T(8,128)(2,1)S(1)}, u32[]{:S(2)}, u32[]{:S(2)}) collective-permute-start(bf16[256,1024]{1,0:T(8,128)(2,1)S(1)} %get-tuple-element.72), channel_id=1, source_target_pairs={{0,32},{32,64},{64,96},{96,0},{1,33},{33,65},{65,97},{97,1},{2,34}... | collective-permute-start | bytes 1572872 | tf_op jit(solution)/shard_map/ppermute | solution.py:386
  61.0 40.1 %collective-permute-start.18 = (bf16[512,1024]{1,0:T(8,128)(2,1)}, bf16[512,1024]{1,0:T(8,128)(2,1)}, u32[]{:S(2)}, u32[]{:S(2)}) collective-permute-start(bf16[512,1024]{1,0:T(8,128)(2,1)} %get-tuple-element.76), channel_id=1, source_target_pairs={{0,8},{8,16},{16,24},{24,0},{1,9},{9,17},{17,25},{25,1},{2,10},{10... | collective-permute-start | bytes 3145736 | tf_op jit(solution)/shard_map/ppermute | solution.py:390
  61.0 40.1 %collective-permute-start.19 = (bf16[512,1024]{1,0:T(8,128)(2,1)}, bf16[512,1024]{1,0:T(8,128)(2,1)}, u32[]{:S(2)}, u32[]{:S(2)}) collective-permute-start(bf16[512,1024]{1,0:T(8,128)(2,1)} %get-tuple-element.77), channel_id=1, source_target_pairs={{0,24},{8,0},{16,8},{24,16},{1,25},{9,1},{17,9},{25,17},{2,26},{10... | collective-permute-start | bytes 3145736 | tf_op jit(solution)/shard_map/ppermute | solution.py:390
  73.9 32.5 %collective-permute-start.20 = (bf16[512,1024]{1,0:T(8,128)(2,1)}, bf16[512,1024]{1,0:T(8,128)(2,1)}, u32[]{:S(2)}, u32[]{:S(2)}) collective-permute-start(bf16[512,1024]{1,0:T(8,128)(2,1)} %get-tuple-element.79), channel_id=1, source_target_pairs={{0,32},{32,64},{64,96},{96,0},{1,33},{33,65},{65,97},{97,1},{2,34}... | collective-permute-start | bytes 3145736 | tf_op jit(solution)/shard_map/ppermute | solution.py:390
  75.4 31.0 %collective-permute-start.21 = (bf16[512,1024]{1,0:T(8,128)(2,1)}, bf16[512,1024]{1,0:T(8,128)(2,1)}, u32[]{:S(2)}, u32[]{:S(2)}) collective-permute-start(bf16[512,1024]{1,0:T(8,128)(2,1)} %get-tuple-element.80), channel_id=1, source_target_pairs={{0,96},{32,0},{64,32},{96,64},{1,97},{33,1},{65,33},{97,65},{2,98}... | collective-permute-start | bytes 3145736 | tf_op jit(solution)/shard_map/ppermute | solution.py:390
  96.5 29.3 %all-to-all-start.1 = ((bf16[4,128,1024]{2,1,0:T(8,128)(2,1)}), bf16[4,128,1024]{2,1,0:T(8,128)(2,1)}, u32[]{:S(2)}, u32[]{:S(2)}) async-start(bf16[4,128,1024]{2,1,0:T(8,128)(2,1)} %bitcast.20), calls=%async_computation.1 | async-start | bytes 2097152 | tf_op jit(solution)/shard_map/all_to_all | solution.py:496
  104.3 5.3 %collective-permute-start.22 = (bf16[64,1024]{1,0:T(8,128)(2,1)S(1)}, bf16[64,1024]{1,0:T(8,128)(2,1)S(1)}, u32[]{:S(2)}, u32[]{:S(2)}) collective-permute-start(bf16[64,1024]{1,0:T(8,128)(2,1)S(1)} %get-tuple-element.85), channel_id=1, source_target_pairs={{0,96},{32,0},{64,32},{96,64},{1,97},{33,1},{65,33},{97,65},{2,98}... | collective-permute-start | bytes 393224 | tf_op jit(solution)/shard_map/ppermute | solution.py:386
  106.2 6.2 %collective-permute-start.23 = (bf16[64,1024]{1,0:T(8,128)(2,1)S(1)}, bf16[64,1024]{1,0:T(8,128)(2,1)S(1)}, u32[]{:S(2)}, u32[]{:S(2)}) collective-permute-start(bf16[64,1024]{1,0:T(8,128)(2,1)S(1)} %get-tuple-element.86), channel_id=1, source_target_pairs={{0,32},{32,64},{64,96},{96,0},{1,33},{33,65},{65,97},{97,1},{2,34}... | collective-permute-start | bytes 393224 | tf_op jit(solution)/shard_map/ppermute | solution.py:386
  112.4 15.8 %collective-permute-start.28 = (bf16[128,1024]{1,0:T(8,128)(2,1)S(1)}, bf16[128,1024]{1,0:T(8,128)(2,1)S(1)}, u32[]{:S(2)}, u32[]{:S(2)}) collective-permute-start(bf16[128,1024]{1,0:T(8,128)(2,1)S(1)} %get-tuple-element.93), channel_id=1, source_target_pairs={{0,32},{32,64},{64,96},{96,0},{1,33},{33,65},{65,97},{97,1},{2,34}... | collective-permute-start | bytes 786440 | tf_op jit(solution)/shard_map/ppermute | solution.py:390
  112.5 15.8 %collective-permute-start.29 = (bf16[128,1024]{1,0:T(8,128)(2,1)S(1)}, bf16[128,1024]{1,0:T(8,128)(2,1)S(1)}, u32[]{:S(2)}, u32[]{:S(2)}) collective-permute-start(bf16[128,1024]{1,0:T(8,128)(2,1)S(1)} %get-tuple-element.94), channel_id=1, source_target_pairs={{0,96},{32,0},{64,32},{96,64},{1,97},{33,1},{65,33},{97,65},{2,98}... | collective-permute-start | bytes 786440 | tf_op jit(solution)/shard_map/ppermute | solution.py:390
  115.8 6.2 %collective-permute-start.25 = (bf16[64,1024]{1,0:T(8,128)(2,1)S(1)}, bf16[64,1024]{1,0:T(8,128)(2,1)S(1)}, u32[]{:S(2)}, u32[]{:S(2)}) collective-permute-start(bf16[64,1024]{1,0:T(8,128)(2,1)S(1)} %get-tuple-element.89), channel_id=1, source_target_pairs={{0,8},{8,16},{16,24},{24,0},{1,9},{9,17},{17,25},{25,1},{2,10},{10... | collective-permute-start | bytes 393224 | tf_op jit(solution)/shard_map/ppermute | solution.py:386
  122.6 7.6 %collective-permute-start.26 = (bf16[128,1024]{1,0:T(8,128)(2,1)S(1)}, bf16[128,1024]{1,0:T(8,128)(2,1)S(1)}, u32[]{:S(2)}, u32[]{:S(2)}) collective-permute-start(bf16[128,1024]{1,0:T(8,128)(2,1)S(1)} %get-tuple-element.90), channel_id=1, source_target_pairs={{0,8},{8,16},{16,24},{24,0},{1,9},{9,17},{17,25},{25,1},{2,10},{10... | collective-permute-start | bytes 786440 | tf_op jit(solution)/shard_map/ppermute | solution.py:390
  123.4 6.8 %collective-permute-start.27 = (bf16[128,1024]{1,0:T(8,128)(2,1)S(1)}, bf16[128,1024]{1,0:T(8,128)(2,1)S(1)}, u32[]{:S(2)}, u32[]{:S(2)}) collective-permute-start(bf16[128,1024]{1,0:T(8,128)(2,1)S(1)} %get-tuple-element.91), channel_id=1, source_target_pairs={{0,24},{8,0},{16,8},{24,16},{1,25},{9,1},{17,9},{25,17},{2,26},{10... | collective-permute-start | bytes 786440 | tf_op jit(solution)/shard_map/ppermute | solution.py:390
  (11 other events, 39.3 us)

commit v5 on v4

--- a/solution.py
+++ b/solution.py
@@ -194,11 +194,15 @@
             merge(table_ref, part_refs, all_ref)
 
         w_ref = block_group(table_ref, weight_ref, w_buf, sems, 0, 4)
-        for c in range(tok // 256):
-            cols = slice(c * 256, (c + 1) * 256)
-            act, slope = gelu_parts(dot_nt(w_ref[...], all_ref[cols, :]))
+        pre_act = dot_nt(w_ref[...], all_ref[:256, :])
+        for begin in range(0, tok, 256):
+            cols = slice(begin, begin + 256)
+            if begin + 256 < tok:
+                following = dot_nt(w_ref[...], all_ref[begin + 256 : begin + 512, :])
+            act, slope = gelu_parts(pre_act)
             act_ref[:, cols] = act.astype(BF16)
             slope_ref[:, cols] = slope.astype(BF16)
+            pre_act = following
 
     return pl.pallas_call(
         body,
@@ -268,10 +272,13 @@
         mark_ref[...] = jnp.zeros_like(mark_ref)
         w_ref = block_group(table_ref, weight_ref, w_buf, w_sems, 16 + 4 * first, count)
         s_ref = block_group(table_ref, slope_ref, s_buf, s_sems, 32 + 4 * first, count)
-        for c in range(tok // 256):
-            cols = slice(c * 256, (c + 1) * 256)
-            act_grad = dot_nt(w_ref[...], grads_ref[cols, :])
+        act_grad = dot_nt(w_ref[...], grads_ref[:256, :])
+        for begin in range(0, tok, 256):
+            cols = slice(begin, begin + 256)
+            if begin + 256 < tok:
+                following = dot_nt(w_ref[...], grads_ref[begin + 256 : begin + 512, :])
             pre_ref[:, cols] = (act_grad * s_ref[:, cols].astype(F32)).astype(BF16)
+            act_grad = following
         span = 512 // len(outs)
         for k, out in enumerate(outs):
             out[...] = dot_nn(pre_ref[k * span : (k + 1) * span, :], rows_ref[...]).astype(BF16)
@@ -338,25 +345,29 @@
     )(table, *pre, weight, *deps)
 
 
-def join(sides, arrived):
-    n, width = sides.shape
+def join(*sums):
+    n, width = sums[0][0].shape
     h = n // 4
 
-    def body(sides_ref, from_next, from_prev, up_ref, down_ref, mark_ref):
-        mark_ref[...] = jnp.zeros_like(mark_ref)
-        up_ref[:h, :] = sides_ref[:h, :]
-        up_ref[h:, :] = add(sides_ref[h : 2 * h, :], from_prev[...]).astype(BF16)
-        down_ref[:h, :] = add(sides_ref[2 * h : 3 * h, :], from_next[...]).astype(BF16)
-        down_ref[h:, :] = sides_ref[3 * h :, :]
-
-    return pl.pallas_call(
-        body,
-        out_shape=[shape(2 * h, width)] * 2 + [MARK],
-        in_specs=[VMEM] * 3,
-        out_specs=[VMEM] * 3,
+    def body(*refs):
+        ins, outs = refs[: 3 * len(sums)], refs[3 * len(sums) :]
+        outs[-1][...] = jnp.zeros_like(outs[-1])
+        for k in range(len(sums)):
+            sides_ref, from_next, from_prev = ins[3 * k : 3 * k + 3]
+            up_ref, down_ref = outs[2 * k : 2 * k + 2]
+            up_ref[:h, :] = sides_ref[:h, :]
+            up_ref[h:, :] = add(sides_ref[h : 2 * h, :], from_prev[...]).astype(BF16)
+            down_ref[:h, :] = add(sides_ref[2 * h : 3 * h, :], from_next[...]).astype(BF16)
+            down_ref[h:, :] = sides_ref[3 * h :, :]
+
+    return pl.pallas_call(
+        body,
+        out_shape=[shape(2 * h, width)] * (2 * len(sums)) + [MARK],
+        in_specs=[VMEM] * (3 * len(sums)),
+        out_specs=[VMEM] * (2 * len(sums) + 1),
         compiler_params=params(),
         cost_estimate=cost(4 * n * width),
-    )(sides, *arrived)
+    )(*[array for sides, arrived in sums for array in (sides, *arrived)])
 
 
 def restore_order(place, rows):
@@ -485,11 +496,11 @@
         table, rows_d, rows_x, slope, weight_out, 0, 1, (mark,)
     )
     out_sides = outer_rest(act, rows_d, 1, 2, (mark,))
-    *pair, mark = join(out_sides, hop)
+    *pair, mark = join((out_sides, hop))
     out_parts = second_hop(*pair, "x")
     hop = first_hop(in_low, in_high, "y")
     pre_b, in_sides, mark = backward(table, rows_d, rows_x, slope, weight_out, 1, 2, (mark,))
-    *pair, mark = join(in_sides, hop)
+    *pair, mark = join((in_sides, hop))
     in_parts = second_hop(*pair, "y")
     pre_c, in_own, mark = backward(table, rows_d, rows_x, slope, weight_out, 3, 1, (mark,))
     own = sum_cores(row_gradients(table, (pre_a, pre_b, pre_c), weight_in, ()))
@@ -499,10 +510,9 @@
     out_hop = first_hop(low, high, "y")
     in_keep, in_sides, low, high, mark = combine(after(in_own, mark), in_parts)
     in_hop = first_hop(low, high, "x")
-    *pair, mark = join(after(out_sides, mark), out_hop)
-    out_parts = second_hop(*pair, "y")
-    *pair, _ = join(after(in_sides, mark), in_hop)
-    in_parts = second_hop(*pair, "x")
+    *pairs, _ = join((out_sides, out_hop), (in_sides, in_hop))
+    out_parts = second_hop(*pairs[:2], "y")
+    in_parts = second_hop(*pairs[2:], "x")
     grad_out = add(out_keep, *out_parts) * scale
     grad_in = add(in_keep, *in_parts) * scale
     token_grad = restore_order(place, back)

time: 132 us -> 128 us (0.970)
  waiting for transfers between devices: 20.8 us -> 16.7 us
    ppermute x8, waiting for transfers between devices: 10.8 us -> 6.8 us  [first_hop(): return (lax.ppermute(low, axis, ring(3)), lax.ppermute(high, axis, ring(1)))]
    pallas_call x4 -> x3, Pallas kernels: 3.82 us -> 3.79 us  [join(): pl.pallas_call(body, out_shape=[shape(2 * h, width)] * (2 * len(sums)) +...]
  transfers between devices with their start and end apart: 31 -> 31, of which waited for: 12 -> 11; matrix products, arithmetic and copies ran while one was open for 3% -> 3% of each run, Pallas kernels for 41% -> 43%
where the time goes in v5:
time: 128 us; the launch traced here: 127 us
  Pallas kernels  59.8 us (47%)
  starting transfers between devices  37.9 us (30%)
  waiting for transfers between devices  16.7 us (13%)
  blocking collectives  5.42 us (4%)
  other arithmetic  3.99 us (3%)
  local copies, waits for them, and re-layouts  2.63 us (2%)
    pallas_call x3, Pallas kernels, backward(): pl.pallas_call(body, grid_spec=pltpu.PrefetchScalarGridSpec(num_scalar_pr...  18.8 us
    ppermute x8, starting transfers between devices, second_hop(): return (lax.ppermute(up, axis, ring(1)), lax.ppermute(down, axis, ring(3)))  12.9 us
    pallas_call x1, Pallas kernels, forward(): pl.pallas_call(body, grid_spec=pltpu.PrefetchScalarGridSpec(num_scalar_pr...  11.7 us
    ppermute x8, starting transfers between devices, first_hop(): return (lax.ppermute(low, axis, ring(3)), lax.ppermute(high, axis, ring(1)))  10 us
    ppermute x6, starting transfers between devices, to_owner(): lax.ppermute(parts[r], 'expert', ring(r))  8.43 us
    pallas_call x1, Pallas kernels, row_gradients(): pl.pallas_call(body, grid_spec=pltpu.PrefetchScalarGridSpec(num_scalar_pr...  7.24 us
    ppermute x6, waiting for transfers between devices, to_owner(): lax.ppermute(parts[r], 'expert', ring(r))  6.94 us
    ppermute x8, waiting for transfers between devices, first_hop(): return (lax.ppermute(low, axis, ring(3)), lax.ppermute(high, axis, ring(1)))  6.8 us
  transfers between devices with their start and end apart: 31, of which 11 were waited for; matrix products, arithmetic and copies ran while one was open for 3% of the time, Pallas kernels for 43%

profile of v5, /device:TPU:0, one launch (start us, length us, event | category | flops | bytes accessed | tf_op | source)
XLA Modules:
  0.0 127.4 jit_solution(1169728997327371994)
XLA Ops:
  0.6 2.1 %shard_map.103 = (bf16[512,256]{1,0:T(8,128)(2,1)S(1)}, bf16[128,1024]{1,0:T(8,128)(2,1)S(1)}, bf16[128,1024]{1,0:T(8,128)(2,1)}, bf16[128,1024]{1,0:T(8,128)(2,1)S(1)}, bf16[128,1024]{1,0:T(8,128)(2,1)S(1)}) custom-call(s32[1]{0:T(128)} %bitcast.where_ref, s32[1,256]{1,0:T(1,128)} %bitcast.21, bf16[256,1024]{1,0:T(8,128)(2,1)} %tok_hbm.1), custom_call_target="tpu_custom_call" | custom-call | bytes 2097152 | tf_op jit(solution)/shard_map/pallas_call | solution.py:93
  2.7 2.1 %collective-permute-start = (bf16[128,1024]{1,0:T(8,128)(2,1)}, bf16[128,1024]{1,0:T(8,128)(2,1)S(1)}, u32[]{:S(2)}, u32[]{:S(2)}) collective-permute-start(bf16[128,1024]{1,0:T(8,128)(2,1)} %get-tuple-element.49), channel_id=1, source_target_pairs={{0,1},{1,2},{2,3},{3,0},{4,5},{5,6},{6,7},{7,4},{8,9},{9,10},{10,1... | collective-permute-start | bytes 786440 | tf_op jit(solution)/shard_map/ppermute | solution.py:483
  4.8 3.6 %collective-permute-start.1 = (bf16[128,1024]{1,0:T(8,128)(2,1)S(1)}, bf16[128,1024]{1,0:T(8,128)(2,1)S(1)}, u32[]{:S(2)}, u32[]{:S(2)}) collective-permute-start(bf16[128,1024]{1,0:T(8,128)(2,1)S(1)} %get-tuple-element.50), channel_id=1, source_target_pairs={{0,2},{1,3},{2,0},{3,1},{4,6},{5,7},{6,4},{7,5},{8,10},{9,11},{10,... | collective-permute-start | bytes 786440 | tf_op jit(solution)/shard_map/ppermute | solution.py:483
  14.5 6.9 %collective-permute-done.1.refs_2_ = bf16[128,1024]{1,0:T(8,128)(2,1)S(1)} collective-permute-done((bf16[128,1024]{1,0:T(8,128)(2,1)S(1)}, bf16[128,1024]{1,0:T(8,128)(2,1)S(1)}, u32[]{:S(2)}, u32[]{:S(2)}) %collective-permute-start.1) | collective-permute-done | bytes 262176 | tf_op jit(solution)/shard_map/ppermute | solution.py:483
  24.1 11.7 %shard_map.104 = (bf16[2048,1024]{1,0:T(8,128)(2,1)}, bf16[2048,1024]{1,0:T(8,128)(2,1)}, bf16[1024,1024]{1,0:T(8,128)(2,1)S(1)}, f32[8,128]{1,0:T(8,128)S(1)}) custom-call(s32[53]{0:T(128)S(1)} %concatenate.3.table_ref, bf16[128,1024]{1,0:T(8,128)(2,1)S(1)} %get-tuple-element.48.refs_0_, bf16[128,1024]{1,0:T(8,128)(2,1)S(1)} %collective-permute-done.refs_1_, ...), custom_call_target="tpu_custom_call" | custom-call | bytes 16777216 | tf_op jit(solution)/shard_map/pallas_call | solution.py:207
  38.6 3.1 %shard_map.110 = (bf16[256,1024]{1,0:T(8,128)(2,1)S(1)}, bf16[256,1024]{1,0:T(8,128)(2,1)S(1)}, bf16[1024,1024]{1,0:T(8,128)(2,1)S(1)}, f32[8,128]{1,0:T(8,128)S(1)}) custom-call(s32[53]{0:T(128)S(1)} %concatenate.3.table_ref, bf16[2048,1024]{1,0:T(8,128)(2,1)} %get-tuple-element.52.act_ref, bf16[128,1024]{1,0:T(8,128)(2,1)S(1)} %shard_map.106.refs_0_, ...), custom_call_target="tpu_custom_call" | custom-call | bytes 4194304 | tf_op jit(solution)/shard_map/pallas_call | solution.py:234
  41.7 2.8 %collective-permute-start.14 = (bf16[256,1024]{1,0:T(8,128)(2,1)S(1)}, bf16[256,1024]{1,0:T(8,128)(2,1)S(1)}, u32[]{:S(2)}, u32[]{:S(2)}) collective-permute-start(bf16[256,1024]{1,0:T(8,128)(2,1)S(1)} %get-tuple-element.64), channel_id=1, source_target_pairs={{0,24},{8,0},{16,8},{24,16},{1,25},{9,1},{17,9},{25,17},{2,26},{10... | collective-permute-start | bytes 1572872 | tf_op jit(solution)/shard_map/ppermute | solution.py:397
  44.6 5.4 %shard_map.111 = (bf16[512,1024]{1,0:T(8,128)(2,1)S(1)}, bf16[256,1024]{1,0:T(8,128)(2,1)S(1)}, bf16[256,1024]{1,0:T(8,128)(2,1)S(1)}, f32[8,128]{1,0:T(8,128)S(1)}) custom-call(s32[53]{0:T(128)S(1)} %concatenate.3.table_ref, bf16[1024,1024]{1,0:T(8,128)(2,1)S(1)} %get-tuple-element.58.grads_ref.rows_ref, bf16[1024,1024]{1,0:T(8,128)(2,1)S(1)} %get-tuple-element.59.rows_ref, ...), custom_call_target="tpu_custom_call" | custom-call | bytes 6291456 | tf_op jit(solution)/shard_map/pallas_call | solution.py:289
  50.0 3.1 %collective-permute-start.16 = (bf16[256,1024]{1,0:T(8,128)(2,1)S(1)}, bf16[256,1024]{1,0:T(8,128)(2,1)S(1)}, u32[]{:S(2)}, u32[]{:S(2)}) collective-permute-start(bf16[256,1024]{1,0:T(8,128)(2,1)S(1)} %get-tuple-element.69), channel_id=1, source_target_pairs={{0,96},{32,0},{64,32},{96,64},{1,97},{33,1},{65,33},{97,65},{2,98}... | collective-permute-start | bytes 1572872 | tf_op jit(solution)/shard_map/ppermute | solution.py:397
  53.1 3.8 %shard_map.112.refs_0_ = bf16[1024,1024]{1,0:T(8,128)(2,1)S(1)} custom-call(bf16[2048,1024]{1,0:T(8,128)(2,1)} %get-tuple-element.52.act_ref, bf16[1024,1024]{1,0:T(8,128)(2,1)S(1)} %get-tuple-element.58.grads_ref.rows_ref, f32[8,128]{1,0:T(8,128)S(1)} %get-tuple-element.63.refs_0_), custom_call_target="tpu_custom_call" | custom-call | bytes 6291456 | tf_op jit(solution)/shard_map/pallas_call | solution.py:255
  56.8 2.6 %collective-permute-done.15.refs_2_ = bf16[256,1024]{1,0:T(8,128)(2,1)S(1)} collective-permute-done((bf16[256,1024]{1,0:T(8,128)(2,1)S(1)}, bf16[256,1024]{1,0:T(8,128)(2,1)S(1)}, u32[]{:S(2)}, u32[]{:S(2)}) %collective-permute-start.15) | collective-permute-done | bytes 524320 | tf_op jit(solution)/shard_map/ppermute | solution.py:397
  61.0 3.2 %collective-permute-start.19 = (bf16[512,1024]{1,0:T(8,128)(2,1)}, bf16[512,1024]{1,0:T(8,128)(2,1)}, u32[]{:S(2)}, u32[]{:S(2)}) collective-permute-start(bf16[512,1024]{1,0:T(8,128)(2,1)} %get-tuple-element.75), channel_id=1, source_target_pairs={{0,24},{8,0},{16,8},{24,16},{1,25},{9,1},{17,9},{25,17},{2,26},{10... | collective-permute-start | bytes 3145736 | tf_op jit(solution)/shard_map/ppermute | solution.py:401
  64.3 8.0 %shard_map.114 = (bf16[1024,1024]{1,0:T(8,128)(2,1)S(1)}, bf16[1024,1024]{1,0:T(8,128)(2,1)S(1)}, f32[8,128]{1,0:T(8,128)}) custom-call(s32[53]{0:T(128)S(1)} %concatenate.3.table_ref, bf16[1024,1024]{1,0:T(8,128)(2,1)S(1)} %get-tuple-element.58.grads_ref.rows_ref, bf16[1024,1024]{1,0:T(8,128)(2,1)S(1)} %get-tuple-element.59.rows_ref, ...), custom_call_target="tpu_custom_call" | custom-call | bytes 10485760 | tf_op jit(solution)/shard_map/pallas_call | solution.py:289
  77.1 5.4 %shard_map.116 = (bf16[512,1024]{1,0:T(8,128)(2,1)S(1)}, bf16[512,1024]{1,0:T(8,128)(2,1)S(1)}, f32[8,128]{1,0:T(8,128)}) custom-call(s32[53]{0:T(128)S(1)} %concatenate.3.table_ref, bf16[1024,1024]{1,0:T(8,128)(2,1)S(1)} %get-tuple-element.58.grads_ref.rows_ref, bf16[1024,1024]{1,0:T(8,128)(2,1)S(1)} %get-tuple-element.59.rows_ref, ...), custom_call_target="tpu_custom_call" | custom-call | bytes 6291456 | tf_op jit(solution)/shard_map/pallas_call | solution.py:289
  82.5 7.2 %shard_map.117 = bf16[1024,1024]{1,0:T(8,128)(2,1)S(1)} custom-call(s32[53]{0:T(128)S(1)} %concatenate.3.table_ref, bf16[512,1024]{1,0:T(8,128)(2,1)S(1)} %get-tuple-element.62.a_ref, bf16[1024,1024]{1,0:T(8,128)(2,1)S(1)} %get-tuple-element.67.b_ref, bf16[512,1024]{1,0:T(8,128)(2,1)S(1)} %get-tuple-element.72.c_ref, bf16[4096,1024]{1,0:T(8,128)(2,1)} %bitcast.19), custom_call_target="tpu_custom_call" | custom-call | bytes 12582912 | tf_op jit(solution)/shard_map/pallas_call | solution.py:333
  89.7 5.4 %all_to_all.17 = bf16[2,512,1024]{2,1,0:T(8,128)(2,1)S(1)} all-to-all(bf16[2,512,1024]{2,1,0:T(8,128)(2,1)S(1)} %bitcast.13), channel_id=1, replica_groups=mesh['y'=4,'x'=4,'core'=2,'expert'=4] {'core'}, dimensions={0} | all-to-all | bytes 4194304 | tf_op jit(solution)/shard_map/all_to_all | solution.py:460
  96.5 4.6 %all-to-all-start.1 = ((bf16[4,128,1024]{2,1,0:T(8,128)(2,1)}), bf16[4,128,1024]{2,1,0:T(8,128)(2,1)}, u32[]{:S(2)}, u32[]{:S(2)}) async-start(bf16[4,128,1024]{2,1,0:T(8,128)(2,1)} %bitcast.20), calls=%async_computation.1 | async-start | bytes 2097152 | tf_op jit(solution)/shard_map/all_to_all | solution.py:507
  101.2 3.1 %shard_map.119 = (bf16[128,1024]{1,0:T(8,128)(2,1)S(1)}, bf16[256,1024]{1,0:T(8,128)(2,1)S(1)}, bf16[64,1024]{1,0:T(8,128)(2,1)S(1)}, bf16[64,1024]{1,0:T(8,128)(2,1)S(1)}, f32[8,128]{1,0:T(8,128)S(1)}) custom-call(bf16[2048,1024]{1,0:T(8,128)(2,1)} %get-tuple-element.52.act_ref, bf16[1024,1024]{1,0:T(8,128)(2,1)S(1)} %get-tuple-element.58.grads_ref.rows_ref, ...), custom_call_target="tpu_custom_call" | custom-call | bytes 5242880 | tf_op jit(solution)/shard_map/pallas_call | solution.py:444
  104.3 1.9 %collective-permute-start.22 = (bf16[64,1024]{1,0:T(8,128)(2,1)S(1)}, bf16[64,1024]{1,0:T(8,128)(2,1)S(1)}, u32[]{:S(2)}, u32[]{:S(2)}) collective-permute-start(bf16[64,1024]{1,0:T(8,128)(2,1)S(1)} %get-tuple-element.81), channel_id=1, source_target_pairs={{0,96},{32,0},{64,32},{96,64},{1,97},{33,1},{65,33},{97,65},{2,98}... | collective-permute-start | bytes 393224 | tf_op jit(solution)/shard_map/ppermute | solution.py:397
  106.4 2.4 %shard_map.121 = (bf16[128,1024]{1,0:T(8,128)(2,1)S(1)}, bf16[256,1024]{1,0:T(8,128)(2,1)S(1)}, bf16[64,1024]{1,0:T(8,128)(2,1)S(1)}, bf16[64,1024]{1,0:T(8,128)(2,1)S(1)}, f32[8,128]{1,0:T(8,128)}) custom-call(bf16[512,1024]{1,0:T(8,128)(2,1)S(1)} %shard_map.120.own_ref, bf16[512,1024]{1,0:T(8,128)(2,1)} %collective-permute-done.20.left, ...), custom_call_target="tpu_custom_call" | custom-call | bytes 4194304 | tf_op jit(solution)/shard_map/pallas_call | solution.py:427
  108.8 2.0 %collective-permute-start.25 = (bf16[64,1024]{1,0:T(8,128)(2,1)S(1)}, bf16[64,1024]{1,0:T(8,128)(2,1)S(1)}, u32[]{:S(2)}, u32[]{:S(2)}) collective-permute-start(bf16[64,1024]{1,0:T(8,128)(2,1)S(1)} %get-tuple-element.85), channel_id=1, source_target_pairs={{0,8},{8,16},{16,24},{24,0},{1,9},{9,17},{17,25},{25,1},{2,10},{10... | collective-permute-start | bytes 393224 | tf_op jit(solution)/shard_map/ppermute | solution.py:397
  116.4 2.4 %collective-permute-start.27 = (bf16[128,1024]{1,0:T(8,128)(2,1)S(1)}, bf16[128,1024]{1,0:T(8,128)(2,1)S(1)}, u32[]{:S(2)}, u32[]{:S(2)}) collective-permute-start(bf16[128,1024]{1,0:T(8,128)(2,1)S(1)} %get-tuple-element.87), channel_id=1, source_target_pairs={{0,24},{8,0},{16,8},{24,16},{1,25},{9,1},{17,9},{25,17},{2,26},{10... | collective-permute-start | bytes 786440 | tf_op jit(solution)/shard_map/ppermute | solution.py:401
  119.2 2.9 %collective-permute-start.29 = (bf16[128,1024]{1,0:T(8,128)(2,1)S(1)}, bf16[128,1024]{1,0:T(8,128)(2,1)S(1)}, u32[]{:S(2)}, u32[]{:S(2)}) collective-permute-start(bf16[128,1024]{1,0:T(8,128)(2,1)S(1)} %get-tuple-element.90), channel_id=1, source_target_pairs={{0,96},{32,0},{64,32},{96,64},{1,97},{33,1},{65,33},{97,65},{2,98}... | collective-permute-start | bytes 786440 | tf_op jit(solution)/shard_map/ppermute | solution.py:401
  122.1 2.5 %shard_map.118 = bf16[256,1024]{1,0:T(8,128)(2,1)} custom-call(bf16[512,256]{1,0:T(8,128)(2,1)S(1)} %get-tuple-element.47.place_ref, bf16[512,1024]{1,0:T(8,128)(2,1)} %bitcast.8.rows_ref), custom_call_target="tpu_custom_call" | custom-call | bytes 2097152 | tf_op jit(solution)/shard_map/pallas_call | solution.py:379
  (78 shorter events, 28.3 us)
Async XLA Ops:
  2.7 10.8 %collective-permute-start = (bf16[128,1024]{1,0:T(8,128)(2,1)}, bf16[128,1024]{1,0:T(8,128)(2,1)S(1)}, u32[]{:S(2)}, u32[]{:S(2)}) collective-permute-start(bf16[128,1024]{1,0:T(8,128)(2,1)} %get-tuple-element.49), channel_id=1, source_target_pairs={{0,1},{1,2},{2,3},{3,0},{4,5},{5,6},{6,7},{7,4},{8,9},{9,10},{10,1... | collective-permute-start | bytes 786440 | tf_op jit(solution)/shard_map/ppermute | solution.py:483
  4.8 16.6 %collective-permute-start.1 = (bf16[128,1024]{1,0:T(8,128)(2,1)S(1)}, bf16[128,1024]{1,0:T(8,128)(2,1)S(1)}, u32[]{:S(2)}, u32[]{:S(2)}) collective-permute-start(bf16[128,1024]{1,0:T(8,128)(2,1)S(1)} %get-tuple-element.50), channel_id=1, source_target_pairs={{0,2},{1,3},{2,0},{3,1},{4,6},{5,7},{6,4},{7,5},{8,10},{9,11},{10,... | collective-permute-start | bytes 786440 | tf_op jit(solution)/shard_map/ppermute | solution.py:483
  8.4 13.0 %collective-permute-start.2 = (bf16[128,1024]{1,0:T(8,128)(2,1)S(1)}, bf16[128,1024]{1,0:T(8,128)(2,1)S(1)}, u32[]{:S(2)}, u32[]{:S(2)}) collective-permute-start(bf16[128,1024]{1,0:T(8,128)(2,1)S(1)} %get-tuple-element.51), channel_id=1, source_target_pairs={{0,3},{1,0},{2,1},{3,2},{4,7},{5,4},{6,5},{7,6},{8,11},{9,8},{10,9... | collective-permute-start | bytes 786440 | tf_op jit(solution)/shard_map/ppermute | solution.py:483
  9.4 12.8 %collective-permute-start.3 = (bf16[128,1024]{1,0:T(8,128)(2,1)S(1)}, bf16[128,1024]{1,0:T(8,128)(2,1)S(1)}, u32[]{:S(2)}, u32[]{:S(2)}) collective-permute-start(bf16[128,1024]{1,0:T(8,128)(2,1)S(1)} %get-tuple-element.48.refs_0_), channel_id=1, source_target_pairs={{0,4},{4,0},{1,5},{5,1},{2,6},{6,2},{3,7},{7,3},{8,12},{12,8},{9,1... | collective-permute-start | bytes 786440 | tf_op jit(solution)/shard_map/ppermute | solution.py:22
  12.5 23.6 %collective-permute-start.7 = (bf16[128,1024]{1,0:T(8,128)(2,1)}, bf16[128,1024]{1,0:T(8,128)(2,1)S(1)}, u32[]{:S(2)}, u32[]{:S(2)}) collective-permute-start(bf16[128,1024]{1,0:T(8,128)(2,1)} %get-tuple-element.55), channel_id=1, source_target_pairs={{0,1},{1,2},{2,3},{3,0},{4,5},{5,6},{6,7},{7,4},{8,9},{9,10},{10,1... | collective-permute-start | bytes 786440 | tf_op jit(solution)/shard_map/ppermute | solution.py:483
  13.5 8.7 %collective-permute-start.4 = (bf16[128,1024]{1,0:T(8,128)(2,1)S(1)}, bf16[128,1024]{1,0:T(8,128)(2,1)S(1)}, u32[]{:S(2)}, u32[]{:S(2)}) collective-permute-start(bf16[128,1024]{1,0:T(8,128)(2,1)S(1)} %collective-permute-done.refs_1_), channel_id=1, source_target_pairs={{0,4},{4,0},{1,5},{5,1},{2,6},{6,2},{3,7},{7,3},{8,12},{12,8},{9,1... | collective-permute-start | bytes 786440 | tf_op jit(solution)/shard_map/ppermute | solution.py:22
  21.4 15.0 %collective-permute-start.8 = (bf16[128,1024]{1,0:T(8,128)(2,1)}, bf16[128,1024]{1,0:T(8,128)(2,1)S(1)}, u32[]{:S(2)}, u32[]{:S(2)}) collective-permute-start(bf16[128,1024]{1,0:T(8,128)(2,1)} %get-tuple-element.56), channel_id=1, source_target_pairs={{0,2},{1,3},{2,0},{3,1},{4,6},{5,7},{6,4},{7,5},{8,10},{9,11},{10,... | collective-permute-start | bytes 786440 | tf_op jit(solution)/shard_map/ppermute | solution.py:483
  21.4 15.2 %collective-permute-start.9 = (bf16[128,1024]{1,0:T(8,128)(2,1)}, bf16[128,1024]{1,0:T(8,128)(2,1)S(1)}, u32[]{:S(2)}, u32[]{:S(2)}) collective-permute-start(bf16[128,1024]{1,0:T(8,128)(2,1)} %get-tuple-element.57), channel_id=1, source_target_pairs={{0,3},{1,0},{2,1},{3,2},{4,7},{5,4},{6,5},{7,6},{8,11},{9,8},{10,9... | collective-permute-start | bytes 786440 | tf_op jit(solution)/shard_map/ppermute | solution.py:483
  41.7 15.1 %collective-permute-start.14 = (bf16[256,1024]{1,0:T(8,128)(2,1)S(1)}, bf16[256,1024]{1,0:T(8,128)(2,1)S(1)}, u32[]{:S(2)}, u32[]{:S(2)}) collective-permute-start(bf16[256,1024]{1,0:T(8,128)(2,1)S(1)} %get-tuple-element.64), channel_id=1, source_target_pairs={{0,24},{8,0},{16,8},{24,16},{1,25},{9,1},{17,9},{25,17},{2,26},{10... | collective-permute-start | bytes 1572872 | tf_op jit(solution)/shard_map/ppermute | solution.py:397
  44.6 14.9 %collective-permute-start.15 = (bf16[256,1024]{1,0:T(8,128)(2,1)S(1)}, bf16[256,1024]{1,0:T(8,128)(2,1)S(1)}, u32[]{:S(2)}, u32[]{:S(2)}) collective-permute-start(bf16[256,1024]{1,0:T(8,128)(2,1)S(1)} %get-tuple-element.65), channel_id=1, source_target_pairs={{0,8},{8,16},{16,24},{24,0},{1,9},{9,17},{17,25},{25,1},{2,10},{10... | collective-permute-start | bytes 1572872 | tf_op jit(solution)/shard_map/ppermute | solution.py:397
  50.0 22.3 %collective-permute-start.16 = (bf16[256,1024]{1,0:T(8,128)(2,1)S(1)}, bf16[256,1024]{1,0:T(8,128)(2,1)S(1)}, u32[]{:S(2)}, u32[]{:S(2)}) collective-permute-start(bf16[256,1024]{1,0:T(8,128)(2,1)S(1)} %get-tuple-element.69), channel_id=1, source_target_pairs={{0,96},{32,0},{64,32},{96,64},{1,97},{33,1},{65,33},{97,65},{2,98}... | collective-permute-start | bytes 1572872 | tf_op jit(solution)/shard_map/ppermute | solution.py:397
  53.1 19.2 %collective-permute-start.17 = (bf16[256,1024]{1,0:T(8,128)(2,1)S(1)}, bf16[256,1024]{1,0:T(8,128)(2,1)S(1)}, u32[]{:S(2)}, u32[]{:S(2)}) collective-permute-start(bf16[256,1024]{1,0:T(8,128)(2,1)S(1)} %get-tuple-element.70), channel_id=1, source_target_pairs={{0,32},{32,64},{64,96},{96,0},{1,33},{33,65},{65,97},{97,1},{2,34}... | collective-permute-start | bytes 1572872 | tf_op jit(solution)/shard_map/ppermute | solution.py:397
  61.0 40.1 %collective-permute-start.18 = (bf16[512,1024]{1,0:T(8,128)(2,1)}, bf16[512,1024]{1,0:T(8,128)(2,1)}, u32[]{:S(2)}, u32[]{:S(2)}) collective-permute-start(bf16[512,1024]{1,0:T(8,128)(2,1)} %get-tuple-element.74), channel_id=1, source_target_pairs={{0,8},{8,16},{16,24},{24,0},{1,9},{9,17},{17,25},{25,1},{2,10},{10... | collective-permute-start | bytes 3145736 | tf_op jit(solution)/shard_map/ppermute | solution.py:401
  61.0 40.1 %collective-permute-start.19 = (bf16[512,1024]{1,0:T(8,128)(2,1)}, bf16[512,1024]{1,0:T(8,128)(2,1)}, u32[]{:S(2)}, u32[]{:S(2)}) collective-permute-start(bf16[512,1024]{1,0:T(8,128)(2,1)} %get-tuple-element.75), channel_id=1, source_target_pairs={{0,24},{8,0},{16,8},{24,16},{1,25},{9,1},{17,9},{25,17},{2,26},{10... | collective-permute-start | bytes 3145736 | tf_op jit(solution)/shard_map/ppermute | solution.py:401
  73.9 32.5 %collective-permute-start.20 = (bf16[512,1024]{1,0:T(8,128)(2,1)}, bf16[512,1024]{1,0:T(8,128)(2,1)}, u32[]{:S(2)}, u32[]{:S(2)}) collective-permute-start(bf16[512,1024]{1,0:T(8,128)(2,1)} %get-tuple-element.77), channel_id=1, source_target_pairs={{0,32},{32,64},{64,96},{96,0},{1,33},{33,65},{65,97},{97,1},{2,34}... | collective-permute-start | bytes 3145736 | tf_op jit(solution)/shard_map/ppermute | solution.py:401
  75.5 30.9 %collective-permute-start.21 = (bf16[512,1024]{1,0:T(8,128)(2,1)}, bf16[512,1024]{1,0:T(8,128)(2,1)}, u32[]{:S(2)}, u32[]{:S(2)}) collective-permute-start(bf16[512,1024]{1,0:T(8,128)(2,1)} %get-tuple-element.78), channel_id=1, source_target_pairs={{0,96},{32,0},{64,32},{96,64},{1,97},{33,1},{65,33},{97,65},{2,98}... | collective-permute-start | bytes 3145736 | tf_op jit(solution)/shard_map/ppermute | solution.py:401
  96.5 25.6 %all-to-all-start.1 = ((bf16[4,128,1024]{2,1,0:T(8,128)(2,1)}), bf16[4,128,1024]{2,1,0:T(8,128)(2,1)}, u32[]{:S(2)}, u32[]{:S(2)}) async-start(bf16[4,128,1024]{2,1,0:T(8,128)(2,1)} %bitcast.20), calls=%async_computation.1 | async-start | bytes 2097152 | tf_op jit(solution)/shard_map/all_to_all | solution.py:507
  104.3 6.5 %collective-permute-start.22 = (bf16[64,1024]{1,0:T(8,128)(2,1)S(1)}, bf16[64,1024]{1,0:T(8,128)(2,1)S(1)}, u32[]{:S(2)}, u32[]{:S(2)}) collective-permute-start(bf16[64,1024]{1,0:T(8,128)(2,1)S(1)} %get-tuple-element.81), channel_id=1, source_target_pairs={{0,96},{32,0},{64,32},{96,64},{1,97},{33,1},{65,33},{97,65},{2,98}... | collective-permute-start | bytes 393224 | tf_op jit(solution)/shard_map/ppermute | solution.py:397
  106.2 6.2 %collective-permute-start.23 = (bf16[64,1024]{1,0:T(8,128)(2,1)S(1)}, bf16[64,1024]{1,0:T(8,128)(2,1)S(1)}, u32[]{:S(2)}, u32[]{:S(2)}) collective-permute-start(bf16[64,1024]{1,0:T(8,128)(2,1)S(1)} %get-tuple-element.82), channel_id=1, source_target_pairs={{0,32},{32,64},{64,96},{96,0},{1,33},{33,65},{65,97},{97,1},{2,34}... | collective-permute-start | bytes 393224 | tf_op jit(solution)/shard_map/ppermute | solution.py:397
  108.8 6.2 %collective-permute-start.25 = (bf16[64,1024]{1,0:T(8,128)(2,1)S(1)}, bf16[64,1024]{1,0:T(8,128)(2,1)S(1)}, u32[]{:S(2)}, u32[]{:S(2)}) collective-permute-start(bf16[64,1024]{1,0:T(8,128)(2,1)S(1)} %get-tuple-element.85), channel_id=1, source_target_pairs={{0,8},{8,16},{16,24},{24,0},{1,9},{9,17},{17,25},{25,1},{2,10},{10... | collective-permute-start | bytes 393224 | tf_op jit(solution)/shard_map/ppermute | solution.py:397
  115.6 9.0 %collective-permute-start.26 = (bf16[128,1024]{1,0:T(8,128)(2,1)S(1)}, bf16[128,1024]{1,0:T(8,128)(2,1)S(1)}, u32[]{:S(2)}, u32[]{:S(2)}) collective-permute-start(bf16[128,1024]{1,0:T(8,128)(2,1)S(1)} %get-tuple-element.86), channel_id=1, source_target_pairs={{0,8},{8,16},{16,24},{24,0},{1,9},{9,17},{17,25},{25,1},{2,10},{10... | collective-permute-start | bytes 786440 | tf_op jit(solution)/shard_map/ppermute | solution.py:401
  116.4 8.2 %collective-permute-start.27 = (bf16[128,1024]{1,0:T(8,128)(2,1)S(1)}, bf16[128,1024]{1,0:T(8,128)(2,1)S(1)}, u32[]{:S(2)}, u32[]{:S(2)}) collective-permute-start(bf16[128,1024]{1,0:T(8,128)(2,1)S(1)} %get-tuple-element.87), channel_id=1, source_target_pairs={{0,24},{8,0},{16,8},{24,16},{1,25},{9,1},{17,9},{25,17},{2,26},{10... | collective-permute-start | bytes 786440 | tf_op jit(solution)/shard_map/ppermute | solution.py:401
  118.9 7.6 %collective-permute-start.28 = (bf16[128,1024]{1,0:T(8,128)(2,1)S(1)}, bf16[128,1024]{1,0:T(8,128)(2,1)S(1)}, u32[]{:S(2)}, u32[]{:S(2)}) collective-permute-start(bf16[128,1024]{1,0:T(8,128)(2,1)S(1)} %get-tuple-element.89), channel_id=1, source_target_pairs={{0,32},{32,64},{64,96},{96,0},{1,33},{33,65},{65,97},{97,1},{2,34}... | collective-permute-start | bytes 786440 | tf_op jit(solution)/shard_map/ppermute | solution.py:401
  119.2 7.2 %collective-permute-start.29 = (bf16[128,1024]{1,0:T(8,128)(2,1)S(1)}, bf16[128,1024]{1,0:T(8,128)(2,1)S(1)}, u32[]{:S(2)}, u32[]{:S(2)}) collective-permute-start(bf16[128,1024]{1,0:T(8,128)(2,1)S(1)} %get-tuple-element.90), channel_id=1, source_target_pairs={{0,96},{32,0},{64,32},{96,64},{1,97},{33,1},{65,33},{97,65},{2,98}... | collective-permute-start | bytes 786440 | tf_op jit(solution)/shard_map/ppermute | solution.py:401
  (11 other events, 30.9 us)

commit v6 on v5

--- a/solution.py
+++ b/solution.py
@@ -9,7 +9,7 @@
 
 BF16 = jnp.bfloat16
 F32 = jnp.float32
-VMEM_LIMIT = 28 * 1024 * 1024
+VMEM_LIMIT = 18 * 1024 * 1024
 ORDER = (2, 1, 3, 0)
 INVERSE = (3, 1, 0, 2)
 
@@ -57,6 +57,7 @@
 
 
 VMEM = pl.BlockSpec(memory_space=pltpu.VMEM)
+SMEM = pl.BlockSpec(memory_space=pltpu.SMEM)
 ANY = pl.BlockSpec(memory_space=pl.ANY)
 
 
@@ -93,7 +94,7 @@
     return pl.pallas_call(
         body,
         out_shape=[shape(512, n)] + [shape(128, width)] * 4,
-        in_specs=[pl.BlockSpec(memory_space=pltpu.SMEM)] + [HBM] * 2,
+        in_specs=[SMEM] + [HBM] * 2,
         out_specs=[VMEM] * 5,
         scratch_shapes=[
             pltpu.VMEM((1, n), jnp.int32),
@@ -105,10 +106,11 @@
     )(where, region, tokens)
 
 
-def dispatch_grads(where, place, gate, grads):
+def dispatch_grads(where, place, gate, grads, deps):
     n, width = grads.shape
 
-    def body(where_ref, place_ref, gate_ref, grad_ref, *outs):
+    def body(where_ref, place_ref, gate_ref, grad_ref, *refs):
+        outs = refs[len(deps) :]
         column = jnp.transpose(jnp.broadcast_to(gate_ref[...], (128, n)))[:, :1]
         scaled = (column * grad_ref[...].astype(F32)).astype(BF16)
         for r, out in enumerate(outs):
@@ -117,38 +119,50 @@
     return pl.pallas_call(
         body,
         out_shape=[shape(128, width)] * 4,
-        in_specs=[pl.BlockSpec(memory_space=pltpu.SMEM)] + [VMEM] * 3,
+        in_specs=[SMEM] + [VMEM] * 3 + [ANY] * len(deps),
         out_specs=[VMEM] * 4,
         compiler_params=params(),
         cost_estimate=cost(4 * n * width * 2),
-    )(where, place, gate, grads)
+    )(where, place, gate, grads, *deps)
 
 
 HBM = pl.BlockSpec(memory_space=pltpu.HBM)
 
 
-def block_scratch(width, count):
-    return [pltpu.VMEM((512 * count, width), BF16), pltpu.SemaphoreType.DMA((4 * count,))]
-
-
-def block_group(table_ref, weight_ref, w_buf, sems, offset, count):
-    step = pl.program_id(0)
-
-    def fetch(k):
-        block = pl.multiple_of(table_ref[offset + k] * 128, 128)
-        place = pl.multiple_of(k * 128, 128)
-        return pltpu.make_async_copy(
-            weight_ref.at[pl.ds(block, 128), :], w_buf.at[pl.ds(place, 128), :], sems.at[k]
-        )
-
-    @pl.when(step == 0)
-    def _():
-        for k in range(4 * count):
-            fetch(k).start()
-
-    for q in range(4):
-        fetch(4 * step + q).wait()
-    return w_buf.at[pl.ds(pl.multiple_of(step * 512, 512), 512), :]
+def fetch_weights(table, w_in, w_out):
+    count, width = 16, w_in.shape[1]
+
+    def body(table_ref, in_hbm_ref, out_hbm_ref, in_ref, out_ref, mark_ref, sems):
+        mark_ref[...] = jnp.zeros_like(mark_ref)
+        copies = []
+        for k in range(count):
+            for side, (source, target) in enumerate(((in_hbm_ref, in_ref), (out_hbm_ref, out_ref))):
+                block = pl.multiple_of(table_ref[count * side + k] * 128, 128)
+                copies.append(
+                    pltpu.make_async_copy(
+                        source.at[pl.ds(block, 128), :],
+                        target.at[pl.ds(k * 128, 128), :],
+                        sems.at[side, k],
+                    )
+                )
+        for copy in copies:
+            copy.start()
+        for copy in copies:
+            copy.wait()
+
+    return pl.pallas_call(
+        body,
+        out_shape=[pltpu.VMEM((count * 128, width), BF16)] * 2 + [MARK],
+        in_specs=[SMEM] + [HBM] * 2,
+        out_specs=[VMEM] * 3,
+        scratch_shapes=[pltpu.SemaphoreType.DMA((2, count))],
+        compiler_params=params(),
+        cost_estimate=cost(2**24),
+    )(table, w_in, w_out)
+
+
+def group_rows(index):
+    return pl.ds(pl.multiple_of(index * 512, 512), 512)
 
 
 def after(array, *others):
@@ -167,11 +181,6 @@
 
 
 MARK = jax.ShapeDtypeStruct((8, 128), F32)
-MARK_SPEC = pl.BlockSpec((8, 128), lambda i, *_: (0, 0))
-
-
-def fixed(rows, cols):
-    return pl.BlockSpec((rows, cols), lambda i, *_: (0, 0))
 
 
 def merge(table_ref, part_refs, all_ref):
@@ -186,35 +195,27 @@
 
     def body(table_ref, *refs):
         part_refs, weight_ref = refs[: len(parts)], refs[len(parts)]
-        act_ref, slope_ref, all_ref, mark_ref, w_buf, sems = refs[len(parts) + 1 :]
-
-        @pl.when(pl.program_id(0) == 0)
+        act_ref, slope_ref, all_ref, mark_ref = refs[len(parts) + 1 :]
+        step = pl.program_id(0)
+
+        @pl.when(step == 0)
         def _():
             mark_ref[...] = jnp.zeros_like(mark_ref)
             merge(table_ref, part_refs, all_ref)
 
-        w_ref = block_group(table_ref, weight_ref, w_buf, sems, 0, 4)
-        pre_act = dot_nt(w_ref[...], all_ref[:256, :])
+        group = group_rows(step)
         for begin in range(0, tok, 256):
             cols = slice(begin, begin + 256)
-            if begin + 256 < tok:
-                following = dot_nt(w_ref[...], all_ref[begin + 256 : begin + 512, :])
-            act, slope = gelu_parts(pre_act)
-            act_ref[:, cols] = act.astype(BF16)
-            slope_ref[:, cols] = slope.astype(BF16)
-            pre_act = following
-
-    return pl.pallas_call(
-        body,
-        grid_spec=pltpu.PrefetchScalarGridSpec(
-            num_scalar_prefetch=1,
-            grid=(4,),
-            in_specs=[VMEM] * len(parts) + [HBM],
-            out_specs=[pl.BlockSpec((512, tok), lambda i, *_: (i, 0))] * 2
-            + [fixed(tok, width), MARK_SPEC],
-            scratch_shapes=block_scratch(width, 4),
-        ),
-        out_shape=[pltpu.HBM((2048, tok), BF16)] * 2 + [shape(tok, width), MARK],
+            act, slope = gelu_parts(dot_nt(weight_ref[group, :], all_ref[cols, :]))
+            act_ref[group, cols] = act.astype(BF16)
+            slope_ref[group, cols] = slope.astype(BF16)
+
+    return pl.pallas_call(
+        body,
+        grid=(4,),
+        in_specs=[SMEM] + [VMEM] * (len(parts) + 1),
+        out_specs=[VMEM] * 4,
+        out_shape=[pltpu.VMEM((2048, tok), BF16)] * 2 + [shape(tok, width), MARK],
         compiler_params=params(),
         cost_estimate=cost(2**24),
     )(table, *parts, weight)
@@ -229,16 +230,12 @@
         mark_ref[...] = jnp.zeros_like(mark_ref)
         merge(table_ref, part_refs, all_ref)
         low_ref[...] = dot_nn(act_ref[:256, :], all_ref[...]).astype(BF16)
-        high_ref[...] = dot_nn(act_ref[256:, :], all_ref[...]).astype(BF16)
-
-    return pl.pallas_call(
-        body,
-        grid_spec=pltpu.PrefetchScalarGridSpec(
-            num_scalar_prefetch=1,
-            grid=(1,),
-            in_specs=[fixed(512, tok)] + [VMEM] * len(parts),
-            out_specs=[fixed(256, width)] * 2 + [fixed(tok, width), MARK_SPEC],
-        ),
+        high_ref[...] = dot_nn(act_ref[256:512, :], all_ref[...]).astype(BF16)
+
+    return pl.pallas_call(
+        body,
+        in_specs=[SMEM] + [VMEM] * (len(parts) + 1),
+        out_specs=[VMEM] * 4,
         out_shape=[shape(256, width)] * 2 + [shape(tok, width), MARK],
         compiler_params=params(),
         cost_estimate=cost(2**22),
@@ -246,17 +243,18 @@
 
 
 def outer_rest(act, rows, first, count, deps):
-    tok, width = rows.shape
+    width = rows.shape[1]
 
     def body(act_ref, rows_ref, *refs):
-        out_ref = refs[len(deps)]
-        out_ref[...] = dot_nn(act_ref[...], rows_ref[...]).astype(BF16)
+        step = pl.program_id(0)
+        product = dot_nn(act_ref[group_rows(step + first), :], rows_ref[...])
+        refs[len(deps)][group_rows(step), :] = product.astype(BF16)
 
     return pl.pallas_call(
         body,
         grid=(count,),
-        in_specs=[pl.BlockSpec((512, tok), lambda i: (i + first, 0)), VMEM] + [ANY] * len(deps),
-        out_specs=pl.BlockSpec((512, width), lambda i: (i, 0)),
+        in_specs=[VMEM] * 2 + [ANY] * len(deps),
+        out_specs=VMEM,
         out_shape=shape(512 * count, width),
         compiler_params=params(),
         cost_estimate=cost(2**20 * (2 + 2 * count)),
@@ -268,35 +266,30 @@
     split = first == 0
 
     def body(table_ref, grads_ref, rows_ref, slope_ref, weight_ref, *refs):
-        pre_ref, *outs, mark_ref, w_buf, w_sems, s_buf, s_sems = refs[len(deps) :]
+        pre_ref, *outs, mark_ref = refs[len(deps) :]
         mark_ref[...] = jnp.zeros_like(mark_ref)
-        w_ref = block_group(table_ref, weight_ref, w_buf, w_sems, 16 + 4 * first, count)
-        s_ref = block_group(table_ref, slope_ref, s_buf, s_sems, 32 + 4 * first, count)
-        act_grad = dot_nt(w_ref[...], grads_ref[:256, :])
+        step = pl.program_id(0)
+        group = group_rows(step + first)
         for begin in range(0, tok, 256):
             cols = slice(begin, begin + 256)
-            if begin + 256 < tok:
-                following = dot_nt(w_ref[...], grads_ref[begin + 256 : begin + 512, :])
-            pre_ref[:, cols] = (act_grad * s_ref[:, cols].astype(F32)).astype(BF16)
-            act_grad = following
-        span = 512 // len(outs)
-        for k, out in enumerate(outs):
-            out[...] = dot_nn(pre_ref[k * span : (k + 1) * span, :], rows_ref[...]).astype(BF16)
-
-    def groups(cols):
-        return pl.BlockSpec((512, cols), lambda i, *_: (i, 0))
-
-    return pl.pallas_call(
-        body,
-        grid_spec=pltpu.PrefetchScalarGridSpec(
-            num_scalar_prefetch=1,
-            grid=(count,),
-            in_specs=[VMEM] * 2 + [HBM] * 2 + [ANY] * len(deps),
-            out_specs=[groups(tok)]
-            + ([fixed(256, width)] * 2 if split else [groups(width)])
-            + [MARK_SPEC],
-            scratch_shapes=block_scratch(width, count) + block_scratch(tok, count),
-        ),
+            act_grad = dot_nt(weight_ref[group, :], grads_ref[cols, :])
+            for q in range(4):
+                block = pl.multiple_of(table_ref[32 + 4 * (step + first) + q] * 128, 128)
+                place = pl.multiple_of(step * 512 + q * 128, 128)
+                part = act_grad[q * 128 : (q + 1) * 128] * slope_ref[pl.ds(block, 128), cols].astype(F32)
+                pre_ref[pl.ds(place, 128), cols] = part.astype(BF16)
+        if split:
+            for k, out in enumerate(outs):
+                out[...] = dot_nn(pre_ref[k * 256 : (k + 1) * 256, :], rows_ref[...]).astype(BF16)
+        else:
+            product = dot_nn(pre_ref[group_rows(step), :], rows_ref[...])
+            outs[0][group_rows(step), :] = product.astype(BF16)
+
+    return pl.pallas_call(
+        body,
+        grid=(count,),
+        in_specs=[SMEM] + [VMEM] * 4 + [ANY] * len(deps),
+        out_specs=[VMEM] * (4 if split else 3),
         out_shape=[shape(512 * count, tok)]
         + ([shape(256, width)] * 2 if split else [shape(512 * count, width)])
         + [MARK],
@@ -305,14 +298,15 @@
     )(table, grads, rows, slope, weight, *deps)
 
 
-def row_gradients(table, pre, weight, deps):
+def row_gradients(table, pre, weight):
     width = weight.shape[1]
     rows = 512
 
-    def body(table_ref, a_ref, b_ref, c_ref, weight_ref, *refs):
-        out_ref, w_buf, sems, total = refs[len(deps) :]
+    def body(table_ref, a_ref, b_ref, c_ref, weight_ref, out_ref, w_ref, total):
         step = pl.program_id(0)
-        w_ref = block_group(table_ref, weight_ref, w_buf, sems, 16, 4)
+        for q in range(4):
+            block = pl.multiple_of(table_ref[32 + 4 * step + q] * 128, 128)
+            w_ref[q * 128 : (q + 1) * 128, :] = weight_ref[pl.ds(block, 128), :]
 
         @pl.when(step == 0)
         def _():
@@ -320,29 +314,25 @@
 
         @pl.when(jnp.logical_and(step > 0, step < 3))
         def _():
-            begin = pl.multiple_of((step - 1) * 512, 512)
-            total[...] += dot_tn(b_ref[pl.ds(begin, 512), :], w_ref[...])
+            total[...] += dot_tn(b_ref[group_rows(step - 1), :], w_ref[...])
 
         @pl.when(step == 3)
         def _():
             final = (total[...] + dot_tn(c_ref[...], w_ref[...])).astype(BF16)
             own = table_ref[52]
-            out_ref[pl.ds(pl.multiple_of(own * rows, rows), rows), :] = final[:rows]
-            out_ref[pl.ds(pl.multiple_of((1 - own) * rows, rows), rows), :] = final[rows:]
-
-    return pl.pallas_call(
-        body,
-        grid_spec=pltpu.PrefetchScalarGridSpec(
-            num_scalar_prefetch=1,
-            grid=(4,),
-            in_specs=[VMEM] * 3 + [HBM] + [ANY] * len(deps),
-            out_specs=fixed(2 * rows, width),
-            scratch_shapes=block_scratch(width, 4) + [pltpu.VMEM((2 * rows, width), F32)],
-        ),
+            out_ref[group_rows(own), :] = final[:rows]
+            out_ref[group_rows(1 - own), :] = final[rows:]
+
+    return pl.pallas_call(
+        body,
+        grid=(4,),
+        in_specs=[SMEM] + [VMEM] * 4,
+        out_specs=VMEM,
         out_shape=shape(2 * rows, width),
+        scratch_shapes=[pltpu.VMEM((512, width), BF16), pltpu.VMEM((2 * rows, width), F32)],
         compiler_params=params(),
         cost_estimate=cost(2**23 + 2**22),
-    )(table, *pre, weight, *deps)
+    )(table, *pre, weight)
 
 
 def join(*sums):
@@ -438,15 +428,14 @@
     tok, width = rows.shape
 
     def body(act_ref, rows_ref, left, right, *refs):
-        cut(dot_nn(act_ref[...], rows_ref[...]) + add(left[...], right[...]), refs)
-
-    shapes = cut_shapes(512, width)
-    return pl.pallas_call(
-        body,
-        grid=(1,),
-        in_specs=[pl.BlockSpec((512, tok), lambda i: (group, 0))] + [VMEM] * 3,
-        out_specs=[fixed(*out.shape) for out in shapes],
-        out_shape=shapes,
+        act_part = act_ref[group * 512 : (group + 1) * 512, :]
+        cut(dot_nn(act_part, rows_ref[...]) + add(left[...], right[...]), refs)
+
+    return pl.pallas_call(
+        body,
+        in_specs=[VMEM] * 4,
+        out_specs=[VMEM] * 5,
+        out_shape=cut_shapes(512, width),
         compiler_params=params(),
         cost_estimate=cost(10 * 512 * width),
     )(act, rows, *received)
@@ -472,21 +461,22 @@
     by_y = ((((y + order[:, None]) % 4) * 4 + (x + every[None, :]) % 4) * 2 + core).reshape(16)
     same = jnp.array([INVERSE[q] * 4 + ORDER[p] for p in range(4) for q in range(4)], jnp.int32)
     table = jnp.concatenate([by_x, by_y, same, (expert - every) % 4, core[None]])
-    weight_in, weight_out = in_hbm(w_in[0]), in_hbm(w_out[0])
+    weight_in, weight_out, mark = fetch_weights(table, in_hbm(w_in[0]), in_hbm(w_out[0]))
 
     place, *send_x = dispatch_tokens(
         expert[None], in_hbm(region.reshape(1, -1)), in_hbm(tokens)
     )
-    send_d = dispatch_grads(expert[None], place, gate.reshape(1, -1), out_grad)
+    send_d = dispatch_grads(expert[None], place, gate.reshape(1, -1), out_grad, ())
 
     def to_owner(parts):
         return [parts[0]] + [lax.ppermute(parts[r], "expert", ring(r)) for r in (1, 2, 3)]
 
     own_x = to_owner(send_x)
+    own_d = to_owner(send_d)
+    own_x[0] = after(own_x[0], mark, send_d[0])
+    own_x[2] = after(own_x[2], own_d[1])
     both_x = own_x + [swap_core(p) for p in own_x]
-    own_d = to_owner(send_d)
     act, slope, rows_x, mark = forward(table, both_x, weight_in)
-    act, slope = in_hbm(act), in_hbm(slope)
     own_d = [after(part, mark) for part in own_d]
     both_d = own_d + [swap_core(p) for p in own_d]
 
@@ -503,7 +493,7 @@
     *pair, mark = join((in_sides, hop))
     in_parts = second_hop(*pair, "y")
     pre_c, in_own, mark = backward(table, rows_d, rows_x, slope, weight_out, 3, 1, (mark,))
-    own = sum_cores(row_gradients(table, (pre_a, pre_b, pre_c), weight_in, ()))
+    own = sum_cores(row_gradients(table, (pre_a, pre_b, pre_c), weight_in))
     back = lax.all_to_all(own, "expert", split_axis=0, concat_axis=0, tiled=True)
 
     out_keep, out_sides, low, high, mark = combine_product(act, rows_d, 3, out_parts)

time: 128 us -> 126 us (0.984)
  Pallas kernels: 59.8 us -> 50.1 us
  waiting for transfers between devices: 16.7 us -> 21.4 us
  local copies, waits for them, and re-layouts: 2.63 us -> 5.52 us
    pallas_call x9 -> x10, Pallas kernels: 49.1 us -> 39.9 us  [the longest x3 12.6 us: backward(): pl.pallas_call(body, grid=(count,), in_specs=[SMEM] + [VMEM] * 4 + [ANY]...]
    ppermute x8, waiting for transfers between devices: 6.8 us -> 10.5 us  [first_hop(): return (lax.ppermute(low, axis, ring(3)), lax.ppermute(high, axis, ring(1)))]
    unnamed x8 -> x16, local copies, waits for them, and re-layouts: 1.73 us -> 4.62 us
  transfers between devices with their start and end apart: 31 -> 31, of which waited for: 11 -> 11; matrix products, arithmetic and copies ran while one was open for 3% -> 3% of each run, Pallas kernels for 43% -> 37%
where the time goes in v6:
time: 126 us; the launch traced here: 125 us
  Pallas kernels  50.1 us (40%)
  starting transfers between devices  37.7 us (30%)
  waiting for transfers between devices  21.4 us (17%)
  local copies, waits for them, and re-layouts  5.52 us (4%)
  blocking collectives  5.42 us (4%)
  other arithmetic  4.05 us (3%)
    ppermute x8, starting transfers between devices, second_hop(): return (lax.ppermute(up, axis, ring(1)), lax.ppermute(down, axis, ring(3)))  12.9 us
    pallas_call x3, Pallas kernels, backward(): pl.pallas_call(body, grid=(count,), in_specs=[SMEM] + [VMEM] * 4 + [ANY]...  12.6 us
    ppermute x8, waiting for transfers between devices, first_hop(): return (lax.ppermute(low, axis, ring(3)), lax.ppermute(high, axis, ring(1)))  10.5 us
    ppermute x8, starting transfers between devices, first_hop(): return (lax.ppermute(low, axis, ring(3)), lax.ppermute(high, axis, ring(1)))  10 us
    pallas_call x1, Pallas kernels, forward(): pl.pallas_call(body, grid=(4,), in_specs=[SMEM] + [VMEM] * (len(parts) +...  9.06 us
    ppermute x6, starting transfers between devices, to_owner(): lax.ppermute(parts[r], 'expert', ring(r))  9 us
    ppermute x6, waiting for transfers between devices, to_owner(): lax.ppermute(parts[r], 'expert', ring(r))  8.05 us
    pallas_call x1, Pallas kernels, row_gradients(): pl.pallas_call(body, grid=(4,), in_specs=[SMEM] + [VMEM] * 4, out_specs=V...  6.18 us
  transfers between devices with their start and end apart: 31, of which 11 were waited for; matrix products, arithmetic and copies ran while one was open for 3% of the time, Pallas kernels for 37%

profile of v6, /device:TPU:0, one launch (start us, length us, event | category | flops | bytes accessed | tf_op | source)
XLA Modules:
  0.0 125.1 jit_solution(2081359755373321243)
XLA Ops:
  2.2 2.1 %collective-permute-start = (bf16[128,1024]{1,0:T(8,128)(2,1)S(1)}, bf16[128,1024]{1,0:T(8,128)(2,1)S(1)}, u32[]{:S(2)}, u32[]{:S(2)}) collective-permute-start(bf16[128,1024]{1,0:T(8,128)(2,1)S(1)} %get-tuple-element.54), channel_id=1, source_target_pairs={{0,1},{1,2},{2,3},{3,0},{4,5},{5,6},{6,7},{7,4},{8,9},{9,10},{10,1... | collective-permute-start | bytes 786440 | tf_op jit(solution)/shard_map/ppermute | solution.py:472
  4.3 3.6 %collective-permute-start.1 = (bf16[128,1024]{1,0:T(8,128)(2,1)S(1)}, bf16[128,1024]{1,0:T(8,128)(2,1)S(1)}, u32[]{:S(2)}, u32[]{:S(2)}) collective-permute-start(bf16[128,1024]{1,0:T(8,128)(2,1)S(1)} %get-tuple-element.55), channel_id=1, source_target_pairs={{0,2},{1,3},{2,0},{3,1},{4,6},{5,7},{6,4},{7,5},{8,10},{9,11},{10,... | collective-permute-start | bytes 786440 | tf_op jit(solution)/shard_map/ppermute | solution.py:472
  14.6 4.2 %shard_map.104 = (bf16[2048,1024]{1,0:T(8,128)(2,1)S(1)}, bf16[2048,1024]{1,0:T(8,128)(2,1)S(1)}, f32[8,128]{1,0:T(8,128)S(1)}) custom-call(s32[53]{0:T(128)S(1)} %concatenate.3.table_ref, bf16[4096,1024]{1,0:T(8,128)(2,1)} %bitcast.15, bf16[4096,1024]{1,0:T(8,128)(2,1)} %bitcast.16), custom_call_target="tpu_custom_call" | custom-call | bytes 16777216 | tf_op jit(solution)/shard_map/pallas_call | solution.py:153
  20.7 4.3 %collective-permute-done.2.refs_1_.refs_0_ = bf16[128,1024]{1,0:T(8,128)(2,1)S(1)} collective-permute-done((bf16[128,1024]{1,0:T(8,128)(2,1)S(1)}, bf16[128,1024]{1,0:T(8,128)(2,1)S(1)}, u32[]{:S(2)}, u32[]{:S(2)}) %collective-permute-start.2) | collective-permute-done | bytes 262176 | tf_op jit(solution)/shard_map/ppermute | solution.py:472
  26.5 9.1 %shard_map.108 = (bf16[2048,1024]{1,0:T(8,128)(2,1)S(1)}, bf16[2048,1024]{1,0:T(8,128)(2,1)S(1)}, bf16[1024,1024]{1,0:T(8,128)(2,1)S(1)}, f32[8,128]{1,0:T(8,128)S(1)}) custom-call(s32[53]{0:T(128)S(1)} %concatenate.3.table_ref, bf16[128,1024]{1,0:T(8,128)(2,1)S(1)} %shard_map.106.refs_0_, bf16[128,1024]{1,0:T(8,128)(2,1)S(1)} %collective-permute-done.refs_1_, ...), custom_call_target="tpu_custom_call" | custom-call | bytes 16777216 | tf_op jit(solution)/shard_map/pallas_call | solution.py:213
  36.3 2.6 %collective-permute-done.9.refs_0_ = bf16[128,1024]{1,0:T(8,128)(2,1)S(1)} collective-permute-done((bf16[128,1024]{1,0:T(8,128)(2,1)S(1)}, bf16[128,1024]{1,0:T(8,128)(2,1)S(1)}, u32[]{:S(2)}, u32[]{:S(2)}) %collective-permute-start.9) | collective-permute-done | bytes 262176 | tf_op jit(solution)/shard_map/ppermute | solution.py:472
  42.4 2.8 %collective-permute-start.14 = (bf16[256,1024]{1,0:T(8,128)(2,1)S(1)}, bf16[256,1024]{1,0:T(8,128)(2,1)S(1)}, u32[]{:S(2)}, u32[]{:S(2)}) collective-permute-start(bf16[256,1024]{1,0:T(8,128)(2,1)S(1)} %get-tuple-element.70), channel_id=1, source_target_pairs={{0,24},{8,0},{16,8},{24,16},{1,25},{9,1},{17,9},{25,17},{2,26},{10... | collective-permute-start | bytes 1572872 | tf_op jit(solution)/shard_map/ppermute | solution.py:387
  45.3 2.9 %shard_map.114 = (bf16[512,1024]{1,0:T(8,128)(2,1)S(1)}, bf16[256,1024]{1,0:T(8,128)(2,1)S(1)}, bf16[256,1024]{1,0:T(8,128)(2,1)S(1)}, f32[8,128]{1,0:T(8,128)S(1)}) custom-call(s32[53]{0:T(128)S(1)} %concatenate.3.table_ref, bf16[1024,1024]{1,0:T(8,128)(2,1)S(1)} %get-tuple-element.63.grads_ref.rows_ref, bf16[1024,1024]{1,0:T(8,128)(2,1)S(1)} %get-tuple-element.64.rows_ref, ...), custom_call_target="tpu_custom_call" | custom-call | bytes 6291456 | tf_op jit(solution)/shard_map/pallas_call | solution.py:288
  48.2 3.1 %collective-permute-start.16 = (bf16[256,1024]{1,0:T(8,128)(2,1)S(1)}, bf16[256,1024]{1,0:T(8,128)(2,1)S(1)}, u32[]{:S(2)}, u32[]{:S(2)}) collective-permute-start(bf16[256,1024]{1,0:T(8,128)(2,1)S(1)} %get-tuple-element.75), channel_id=1, source_target_pairs={{0,96},{32,0},{64,32},{96,64},{1,97},{33,1},{65,33},{97,65},{2,98}... | collective-permute-start | bytes 1572872 | tf_op jit(solution)/shard_map/ppermute | solution.py:387
  51.3 2.5 %shard_map.115.refs_0_ = bf16[1024,1024]{1,0:T(8,128)(2,1)S(1)} custom-call(bf16[2048,1024]{1,0:T(8,128)(2,1)S(1)} %get-tuple-element.59.act_ref, bf16[1024,1024]{1,0:T(8,128)(2,1)S(1)} %get-tuple-element.63.grads_ref.rows_ref, f32[8,128]{1,0:T(8,128)S(1)} %get-tuple-element.69.refs_0_), custom_call_target="tpu_custom_call" | custom-call | bytes 6291456 | tf_op jit(solution)/shard_map/pallas_call | solution.py:253
  53.8 2.9 %collective-permute-done.14.refs_1_ = bf16[256,1024]{1,0:T(8,128)(2,1)S(1)} collective-permute-done((bf16[256,1024]{1,0:T(8,128)(2,1)S(1)}, bf16[256,1024]{1,0:T(8,128)(2,1)S(1)}, u32[]{:S(2)}, u32[]{:S(2)}) %collective-permute-start.14) | collective-permute-done | bytes 524320 | tf_op jit(solution)/shard_map/ppermute | solution.py:387
  56.7 3.4 %collective-permute-done.15.refs_2_ = bf16[256,1024]{1,0:T(8,128)(2,1)S(1)} collective-permute-done((bf16[256,1024]{1,0:T(8,128)(2,1)S(1)}, bf16[256,1024]{1,0:T(8,128)(2,1)S(1)}, u32[]{:S(2)}, u32[]{:S(2)}) %collective-permute-start.15) | collective-permute-done | bytes 524320 | tf_op jit(solution)/shard_map/ppermute | solution.py:387
  61.7 3.2 %collective-permute-start.19 = (bf16[512,1024]{1,0:T(8,128)(2,1)}, bf16[512,1024]{1,0:T(8,128)(2,1)}, u32[]{:S(2)}, u32[]{:S(2)}) collective-permute-start(bf16[512,1024]{1,0:T(8,128)(2,1)} %get-tuple-element.81), channel_id=1, source_target_pairs={{0,24},{8,0},{16,8},{24,16},{1,25},{9,1},{17,9},{25,17},{2,26},{10... | collective-permute-start | bytes 3145736 | tf_op jit(solution)/shard_map/ppermute | solution.py:391
  64.9 6.3 %shard_map.117 = (bf16[1024,1024]{1,0:T(8,128)(2,1)S(1)}, bf16[1024,1024]{1,0:T(8,128)(2,1)S(1)}, f32[8,128]{1,0:T(8,128)}) custom-call(s32[53]{0:T(128)S(1)} %concatenate.3.table_ref, bf16[1024,1024]{1,0:T(8,128)(2,1)S(1)} %get-tuple-element.63.grads_ref.rows_ref, bf16[1024,1024]{1,0:T(8,128)(2,1)S(1)} %get-tuple-element.64.rows_ref, ...), custom_call_target="tpu_custom_call" | custom-call | bytes 10485760 | tf_op jit(solution)/shard_map/pallas_call | solution.py:288
  76.0 3.4 %shard_map.119 = (bf16[512,1024]{1,0:T(8,128)(2,1)S(1)}, bf16[512,1024]{1,0:T(8,128)(2,1)S(1)}, f32[8,128]{1,0:T(8,128)}) custom-call(s32[53]{0:T(128)S(1)} %concatenate.3.table_ref, bf16[1024,1024]{1,0:T(8,128)(2,1)S(1)} %get-tuple-element.63.grads_ref.rows_ref, bf16[1024,1024]{1,0:T(8,128)(2,1)S(1)} %get-tuple-element.64.rows_ref, ...), custom_call_target="tpu_custom_call" | custom-call | bytes 6291456 | tf_op jit(solution)/shard_map/pallas_call | solution.py:288
  79.4 6.2 %shard_map.120 = bf16[1024,1024]{1,0:T(8,128)(2,1)S(1)} custom-call(s32[53]{0:T(128)S(1)} %concatenate.3.table_ref, bf16[512,1024]{1,0:T(8,128)(2,1)S(1)} %get-tuple-element.68.a_ref, bf16[1024,1024]{1,0:T(8,128)(2,1)S(1)} %get-tuple-element.73.b_ref, bf16[512,1024]{1,0:T(8,128)(2,1)S(1)} %get-tuple-element.78.c_ref, ...), custom_call_target="tpu_custom_call" | custom-call | bytes 12582912 | tf_op jit(solution)/shard_map/pallas_call | solution.py:326
  85.6 5.4 %all_to_all.17 = bf16[2,512,1024]{2,1,0:T(8,128)(2,1)S(1)} all-to-all(bf16[2,512,1024]{2,1,0:T(8,128)(2,1)S(1)} %bitcast.13), channel_id=1, replica_groups=mesh['y'=4,'x'=4,'core'=2,'expert'=4] {'core'}, dimensions={0} | all-to-all | bytes 4194304 | tf_op jit(solution)/shard_map/all_to_all | solution.py:449
  92.5 4.3 %all-to-all-start.1 = ((bf16[4,128,1024]{2,1,0:T(8,128)(2,1)}), bf16[4,128,1024]{2,1,0:T(8,128)(2,1)}, u32[]{:S(2)}, u32[]{:S(2)}) async-start(bf16[4,128,1024]{2,1,0:T(8,128)(2,1)} %bitcast.17), calls=%async_computation.1 | async-start | bytes 2097152 | tf_op jit(solution)/shard_map/all_to_all | solution.py:497
  96.8 2.2 %copy-done.1 = bf16[2048,1024]{1,0:T(8,128)(2,1)S(1)} copy-done((bf16[2048,1024]{1,0:T(8,128)(2,1)S(1)}, bf16[2048,1024]{1,0:T(8,128)(2,1)}, u32[]{:S(2)}) %copy-start.1) | copy-done | bytes 4194328
  99.0 2.8 %shard_map.122 = (bf16[128,1024]{1,0:T(8,128)(2,1)S(1)}, bf16[256,1024]{1,0:T(8,128)(2,1)S(1)}, bf16[64,1024]{1,0:T(8,128)(2,1)S(1)}, bf16[64,1024]{1,0:T(8,128)(2,1)S(1)}, f32[8,128]{1,0:T(8,128)S(1)}) custom-call(bf16[2048,1024]{1,0:T(8,128)(2,1)S(1)} %copy-done.1, bf16[1024,1024]{1,0:T(8,128)(2,1)S(1)} %get-tuple-element.63.grads_ref.rows_ref, ...), custom_call_target="tpu_custom_call" | custom-call | bytes 5242880 | tf_op jit(solution)/shard_map/pallas_call | solution.py:434
  103.9 2.4 %shard_map.124 = (bf16[128,1024]{1,0:T(8,128)(2,1)S(1)}, bf16[256,1024]{1,0:T(8,128)(2,1)S(1)}, bf16[64,1024]{1,0:T(8,128)(2,1)S(1)}, bf16[64,1024]{1,0:T(8,128)(2,1)S(1)}, f32[8,128]{1,0:T(8,128)}) custom-call(bf16[512,1024]{1,0:T(8,128)(2,1)S(1)} %shard_map.123.own_ref, bf16[512,1024]{1,0:T(8,128)(2,1)} %collective-permute-done.20.left, ...), custom_call_target="tpu_custom_call" | custom-call | bytes 4194304 | tf_op jit(solution)/shard_map/pallas_call | solution.py:417
  113.9 2.5 %collective-permute-start.27 = (bf16[128,1024]{1,0:T(8,128)(2,1)S(1)}, bf16[128,1024]{1,0:T(8,128)(2,1)S(1)}, u32[]{:S(2)}, u32[]{:S(2)}) collective-permute-start(bf16[128,1024]{1,0:T(8,128)(2,1)S(1)} %get-tuple-element.93), channel_id=1, source_target_pairs={{0,24},{8,0},{16,8},{24,16},{1,25},{9,1},{17,9},{25,17},{2,26},{10... | collective-permute-start | bytes 786440 | tf_op jit(solution)/shard_map/ppermute | solution.py:391
  116.9 2.8 %collective-permute-start.29 = (bf16[128,1024]{1,0:T(8,128)(2,1)S(1)}, bf16[128,1024]{1,0:T(8,128)(2,1)S(1)}, u32[]{:S(2)}, u32[]{:S(2)}) collective-permute-start(bf16[128,1024]{1,0:T(8,128)(2,1)S(1)} %get-tuple-element.96), channel_id=1, source_target_pairs={{0,96},{32,0},{64,32},{96,64},{1,97},{33,1},{65,33},{97,65},{2,98}... | collective-permute-start | bytes 786440 | tf_op jit(solution)/shard_map/ppermute | solution.py:391
  119.7 2.5 %shard_map.121 = bf16[256,1024]{1,0:T(8,128)(2,1)} custom-call(bf16[512,256]{1,0:T(8,128)(2,1)S(1)} %get-tuple-element.50.place_ref, bf16[512,1024]{1,0:T(8,128)(2,1)} %bitcast.8.rows_ref), custom_call_target="tpu_custom_call" | custom-call | bytes 2097152 | tf_op jit(solution)/shard_map/pallas_call | solution.py:369
  (89 shorter events, 36.8 us)
Async XLA Ops:
  2.2 16.7 %collective-permute-start = (bf16[128,1024]{1,0:T(8,128)(2,1)S(1)}, bf16[128,1024]{1,0:T(8,128)(2,1)S(1)}, u32[]{:S(2)}, u32[]{:S(2)}) collective-permute-start(bf16[128,1024]{1,0:T(8,128)(2,1)S(1)} %get-tuple-element.54), channel_id=1, source_target_pairs={{0,1},{1,2},{2,3},{3,0},{4,5},{5,6},{6,7},{7,4},{8,9},{9,10},{10,1... | collective-permute-start | bytes 786440 | tf_op jit(solution)/shard_map/ppermute | solution.py:472
  4.3 16.4 %collective-permute-start.1 = (bf16[128,1024]{1,0:T(8,128)(2,1)S(1)}, bf16[128,1024]{1,0:T(8,128)(2,1)S(1)}, u32[]{:S(2)}, u32[]{:S(2)}) collective-permute-start(bf16[128,1024]{1,0:T(8,128)(2,1)S(1)} %get-tuple-element.55), channel_id=1, source_target_pairs={{0,2},{1,3},{2,0},{3,1},{4,6},{5,7},{6,4},{7,5},{8,10},{9,11},{10,... | collective-permute-start | bytes 786440 | tf_op jit(solution)/shard_map/ppermute | solution.py:472
  7.8 11.6 %collective-permute-start.3 = (bf16[128,1024]{1,0:T(8,128)(2,1)S(1)}, bf16[128,1024]{1,0:T(8,128)(2,1)S(1)}, u32[]{:S(2)}, u32[]{:S(2)}) collective-permute-start(bf16[128,1024]{1,0:T(8,128)(2,1)S(1)} %get-tuple-element.57), channel_id=1, source_target_pairs={{0,3},{1,0},{2,1},{3,2},{4,7},{5,4},{6,5},{7,6},{8,11},{9,8},{10,9... | collective-permute-start | bytes 786440 | tf_op jit(solution)/shard_map/ppermute | solution.py:472
  11.9 13.0 %collective-permute-start.2 = (bf16[128,1024]{1,0:T(8,128)(2,1)S(1)}, bf16[128,1024]{1,0:T(8,128)(2,1)S(1)}, u32[]{:S(2)}, u32[]{:S(2)}) collective-permute-start(bf16[128,1024]{1,0:T(8,128)(2,1)S(1)} %get-tuple-element.56), channel_id=1, source_target_pairs={{0,1},{1,2},{2,3},{3,0},{4,5},{5,6},{6,7},{7,4},{8,9},{9,10},{10,1... | collective-permute-start | bytes 786440 | tf_op jit(solution)/shard_map/ppermute | solution.py:472
  18.8 6.7 %collective-permute-start.4 = (bf16[128,1024]{1,0:T(8,128)(2,1)S(1)}, bf16[128,1024]{1,0:T(8,128)(2,1)S(1)}, u32[]{:S(2)}, u32[]{:S(2)}) collective-permute-start(bf16[128,1024]{1,0:T(8,128)(2,1)S(1)} %shard_map.106.refs_0_), channel_id=1, source_target_pairs={{0,4},{4,0},{1,5},{5,1},{2,6},{6,2},{3,7},{7,3},{8,12},{12,8},{9,1... | collective-permute-start | bytes 786440 | tf_op jit(solution)/shard_map/ppermute | solution.py:22
  18.9 7.4 %collective-permute-start.5 = (bf16[128,1024]{1,0:T(8,128)(2,1)S(1)}, bf16[128,1024]{1,0:T(8,128)(2,1)S(1)}, u32[]{:S(2)}, u32[]{:S(2)}) collective-permute-start(bf16[128,1024]{1,0:T(8,128)(2,1)S(1)} %collective-permute-done.refs_1_), channel_id=1, source_target_pairs={{0,4},{4,0},{1,5},{5,1},{2,6},{6,2},{3,7},{7,3},{8,12},{12,8},{9,1... | collective-permute-start | bytes 786440 | tf_op jit(solution)/shard_map/ppermute | solution.py:22
  19.4 6.9 %collective-permute-start.7 = (bf16[128,1024]{1,0:T(8,128)(2,1)S(1)}, bf16[128,1024]{1,0:T(8,128)(2,1)S(1)}, u32[]{:S(2)}, u32[]{:S(2)}) collective-permute-start(bf16[128,1024]{1,0:T(8,128)(2,1)S(1)} %collective-permute-done.3.refs_3_), channel_id=1, source_target_pairs={{0,4},{4,0},{1,5},{5,1},{2,6},{6,2},{3,7},{7,3},{8,12},{12,8},{9,1... | collective-permute-start | bytes 786440 | tf_op jit(solution)/shard_map/ppermute | solution.py:22
  24.9 11.2 %collective-permute-start.8 = (bf16[128,1024]{1,0:T(8,128)(2,1)S(1)}, bf16[128,1024]{1,0:T(8,128)(2,1)S(1)}, u32[]{:S(2)}, u32[]{:S(2)}) collective-permute-start(bf16[128,1024]{1,0:T(8,128)(2,1)S(1)} %copy-done.7), channel_id=1, source_target_pairs={{0,2},{1,3},{2,0},{3,1},{4,6},{5,7},{6,4},{7,5},{8,10},{9,11},{10,... | collective-permute-start | bytes 786440 | tf_op jit(solution)/shard_map/ppermute | solution.py:472
  25.5 13.4 %collective-permute-start.9 = (bf16[128,1024]{1,0:T(8,128)(2,1)S(1)}, bf16[128,1024]{1,0:T(8,128)(2,1)S(1)}, u32[]{:S(2)}, u32[]{:S(2)}) collective-permute-start(bf16[128,1024]{1,0:T(8,128)(2,1)S(1)} %get-tuple-element.62), channel_id=1, source_target_pairs={{0,3},{1,0},{2,1},{3,2},{4,7},{5,4},{6,5},{7,6},{8,11},{9,8},{10,9... | collective-permute-start | bytes 786440 | tf_op jit(solution)/shard_map/ppermute | solution.py:472
  42.4 14.3 %collective-permute-start.14 = (bf16[256,1024]{1,0:T(8,128)(2,1)S(1)}, bf16[256,1024]{1,0:T(8,128)(2,1)S(1)}, u32[]{:S(2)}, u32[]{:S(2)}) collective-permute-start(bf16[256,1024]{1,0:T(8,128)(2,1)S(1)} %get-tuple-element.70), channel_id=1, source_target_pairs={{0,24},{8,0},{16,8},{24,16},{1,25},{9,1},{17,9},{25,17},{2,26},{10... | collective-permute-start | bytes 1572872 | tf_op jit(solution)/shard_map/ppermute | solution.py:387
  45.2 14.9 %collective-permute-start.15 = (bf16[256,1024]{1,0:T(8,128)(2,1)S(1)}, bf16[256,1024]{1,0:T(8,128)(2,1)S(1)}, u32[]{:S(2)}, u32[]{:S(2)}) collective-permute-start(bf16[256,1024]{1,0:T(8,128)(2,1)S(1)} %get-tuple-element.71), channel_id=1, source_target_pairs={{0,8},{8,16},{16,24},{24,0},{1,9},{9,17},{17,25},{25,1},{2,10},{10... | collective-permute-start | bytes 1572872 | tf_op jit(solution)/shard_map/ppermute | solution.py:387
  48.2 23.0 %collective-permute-start.16 = (bf16[256,1024]{1,0:T(8,128)(2,1)S(1)}, bf16[256,1024]{1,0:T(8,128)(2,1)S(1)}, u32[]{:S(2)}, u32[]{:S(2)}) collective-permute-start(bf16[256,1024]{1,0:T(8,128)(2,1)S(1)} %get-tuple-element.75), channel_id=1, source_target_pairs={{0,96},{32,0},{64,32},{96,64},{1,97},{33,1},{65,33},{97,65},{2,98}... | collective-permute-start | bytes 1572872 | tf_op jit(solution)/shard_map/ppermute | solution.py:387
  51.3 19.9 %collective-permute-start.17 = (bf16[256,1024]{1,0:T(8,128)(2,1)S(1)}, bf16[256,1024]{1,0:T(8,128)(2,1)S(1)}, u32[]{:S(2)}, u32[]{:S(2)}) collective-permute-start(bf16[256,1024]{1,0:T(8,128)(2,1)S(1)} %get-tuple-element.76), channel_id=1, source_target_pairs={{0,32},{32,64},{64,96},{96,0},{1,33},{33,65},{65,97},{97,1},{2,34}... | collective-permute-start | bytes 1572872 | tf_op jit(solution)/shard_map/ppermute | solution.py:387
  61.7 35.1 %collective-permute-start.18 = (bf16[512,1024]{1,0:T(8,128)(2,1)}, bf16[512,1024]{1,0:T(8,128)(2,1)}, u32[]{:S(2)}, u32[]{:S(2)}) collective-permute-start(bf16[512,1024]{1,0:T(8,128)(2,1)} %get-tuple-element.80), channel_id=1, source_target_pairs={{0,8},{8,16},{16,24},{24,0},{1,9},{9,17},{17,25},{25,1},{2,10},{10... | collective-permute-start | bytes 3145736 | tf_op jit(solution)/shard_map/ppermute | solution.py:391
  61.7 35.1 %collective-permute-start.19 = (bf16[512,1024]{1,0:T(8,128)(2,1)}, bf16[512,1024]{1,0:T(8,128)(2,1)}, u32[]{:S(2)}, u32[]{:S(2)}) collective-permute-start(bf16[512,1024]{1,0:T(8,128)(2,1)} %get-tuple-element.81), channel_id=1, source_target_pairs={{0,24},{8,0},{16,8},{24,16},{1,25},{9,1},{17,9},{25,17},{2,26},{10... | collective-permute-start | bytes 3145736 | tf_op jit(solution)/shard_map/ppermute | solution.py:391
  72.8 31.1 %collective-permute-start.20 = (bf16[512,1024]{1,0:T(8,128)(2,1)}, bf16[512,1024]{1,0:T(8,128)(2,1)}, u32[]{:S(2)}, u32[]{:S(2)}) collective-permute-start(bf16[512,1024]{1,0:T(8,128)(2,1)} %get-tuple-element.83), channel_id=1, source_target_pairs={{0,32},{32,64},{64,96},{96,0},{1,33},{33,65},{65,97},{97,1},{2,34}... | collective-permute-start | bytes 3145736 | tf_op jit(solution)/shard_map/ppermute | solution.py:391
  74.4 29.5 %collective-permute-start.21 = (bf16[512,1024]{1,0:T(8,128)(2,1)}, bf16[512,1024]{1,0:T(8,128)(2,1)}, u32[]{:S(2)}, u32[]{:S(2)}) collective-permute-start(bf16[512,1024]{1,0:T(8,128)(2,1)} %get-tuple-element.84), channel_id=1, source_target_pairs={{0,96},{32,0},{64,32},{96,64},{1,97},{33,1},{65,33},{97,65},{2,98}... | collective-permute-start | bytes 3145736 | tf_op jit(solution)/shard_map/ppermute | solution.py:391
  92.5 27.2 %all-to-all-start.1 = ((bf16[4,128,1024]{2,1,0:T(8,128)(2,1)}), bf16[4,128,1024]{2,1,0:T(8,128)(2,1)}, u32[]{:S(2)}, u32[]{:S(2)}) async-start(bf16[4,128,1024]{2,1,0:T(8,128)(2,1)} %bitcast.17), calls=%async_computation.1 | async-start | bytes 2097152 | tf_op jit(solution)/shard_map/all_to_all | solution.py:497
  101.8 6.5 %collective-permute-start.22 = (bf16[64,1024]{1,0:T(8,128)(2,1)S(1)}, bf16[64,1024]{1,0:T(8,128)(2,1)S(1)}, u32[]{:S(2)}, u32[]{:S(2)}) collective-permute-start(bf16[64,1024]{1,0:T(8,128)(2,1)S(1)} %get-tuple-element.87), channel_id=1, source_target_pairs={{0,96},{32,0},{64,32},{96,64},{1,97},{33,1},{65,33},{97,65},{2,98}... | collective-permute-start | bytes 393224 | tf_op jit(solution)/shard_map/ppermute | solution.py:387
  103.7 6.5 %collective-permute-start.23 = (bf16[64,1024]{1,0:T(8,128)(2,1)S(1)}, bf16[64,1024]{1,0:T(8,128)(2,1)S(1)}, u32[]{:S(2)}, u32[]{:S(2)}) collective-permute-start(bf16[64,1024]{1,0:T(8,128)(2,1)S(1)} %get-tuple-element.88), channel_id=1, source_target_pairs={{0,32},{32,64},{64,96},{96,0},{1,33},{33,65},{65,97},{97,1},{2,34}... | collective-permute-start | bytes 393224 | tf_op jit(solution)/shard_map/ppermute | solution.py:387
  113.2 9.0 %collective-permute-start.26 = (bf16[128,1024]{1,0:T(8,128)(2,1)S(1)}, bf16[128,1024]{1,0:T(8,128)(2,1)S(1)}, u32[]{:S(2)}, u32[]{:S(2)}) collective-permute-start(bf16[128,1024]{1,0:T(8,128)(2,1)S(1)} %get-tuple-element.92), channel_id=1, source_target_pairs={{0,8},{8,16},{16,24},{24,0},{1,9},{9,17},{17,25},{25,1},{2,10},{10... | collective-permute-start | bytes 786440 | tf_op jit(solution)/shard_map/ppermute | solution.py:391
  113.9 8.2 %collective-permute-start.27 = (bf16[128,1024]{1,0:T(8,128)(2,1)S(1)}, bf16[128,1024]{1,0:T(8,128)(2,1)S(1)}, u32[]{:S(2)}, u32[]{:S(2)}) collective-permute-start(bf16[128,1024]{1,0:T(8,128)(2,1)S(1)} %get-tuple-element.93), channel_id=1, source_target_pairs={{0,24},{8,0},{16,8},{24,16},{1,25},{9,1},{17,9},{25,17},{2,26},{10... | collective-permute-start | bytes 786440 | tf_op jit(solution)/shard_map/ppermute | solution.py:391
  116.4 7.7 %collective-permute-start.28 = (bf16[128,1024]{1,0:T(8,128)(2,1)S(1)}, bf16[128,1024]{1,0:T(8,128)(2,1)S(1)}, u32[]{:S(2)}, u32[]{:S(2)}) collective-permute-start(bf16[128,1024]{1,0:T(8,128)(2,1)S(1)} %get-tuple-element.95), channel_id=1, source_target_pairs={{0,32},{32,64},{64,96},{96,0},{1,33},{33,65},{65,97},{97,1},{2,34}... | collective-permute-start | bytes 786440 | tf_op jit(solution)/shard_map/ppermute | solution.py:391
  116.9 7.3 %collective-permute-start.29 = (bf16[128,1024]{1,0:T(8,128)(2,1)S(1)}, bf16[128,1024]{1,0:T(8,128)(2,1)S(1)}, u32[]{:S(2)}, u32[]{:S(2)}) collective-permute-start(bf16[128,1024]{1,0:T(8,128)(2,1)S(1)} %get-tuple-element.96), channel_id=1, source_target_pairs={{0,96},{32,0},{64,32},{96,64},{1,97},{33,1},{65,33},{97,65},{2,98}... | collective-permute-start | bytes 786440 | tf_op jit(solution)/shard_map/ppermute | solution.py:391
  (15 other events, 70.5 us)

commit v7 on v6

--- a/solution.py
+++ b/solution.py
@@ -242,22 +242,23 @@
     )(table, act, *parts)
 
 
-def outer_rest(act, rows, first, count, deps):
+def outer_rest(act, rows, deps):
     width = rows.shape[1]
 
     def body(act_ref, rows_ref, *refs):
-        step = pl.program_id(0)
-        product = dot_nn(act_ref[group_rows(step + first), :], rows_ref[...])
-        refs[len(deps)][group_rows(step), :] = product.astype(BF16)
-
-    return pl.pallas_call(
-        body,
-        grid=(count,),
+        sides_ref, own_ref, mark_ref = refs[len(deps) :]
+        mark_ref[...] = jnp.zeros_like(mark_ref)
+        for k, out in enumerate((sides_ref.at[:512], sides_ref.at[512:], own_ref)):
+            group = act_ref[(k + 1) * 512 : (k + 2) * 512, :]
+            out[...] = dot_nn(group, rows_ref[...]).astype(BF16)
+
+    return pl.pallas_call(
+        body,
         in_specs=[VMEM] * 2 + [ANY] * len(deps),
-        out_specs=VMEM,
-        out_shape=shape(512 * count, width),
-        compiler_params=params(),
-        cost_estimate=cost(2**20 * (2 + 2 * count)),
+        out_specs=[VMEM] * 3,
+        out_shape=[shape(1024, width), shape(512, width), MARK],
+        compiler_params=params(),
+        cost_estimate=cost(2**23),
     )(act, rows, *deps)
 
 
@@ -424,23 +425,6 @@
     )(own, *received)
 
 
-def combine_product(act, rows, group, received):
-    tok, width = rows.shape
-
-    def body(act_ref, rows_ref, left, right, *refs):
-        act_part = act_ref[group * 512 : (group + 1) * 512, :]
-        cut(dot_nn(act_part, rows_ref[...]) + add(left[...], right[...]), refs)
-
-    return pl.pallas_call(
-        body,
-        in_specs=[VMEM] * 4,
-        out_specs=[VMEM] * 5,
-        out_shape=cut_shapes(512, width),
-        compiler_params=params(),
-        cost_estimate=cost(10 * 512 * width),
-    )(act, rows, *received)
-
-
 def in_hbm(array):
     return pltpu.with_memory_space_constraint(array, pltpu.HBM)
 
@@ -485,18 +469,18 @@
     pre_a, in_low, in_high, mark = backward(
         table, rows_d, rows_x, slope, weight_out, 0, 1, (mark,)
     )
-    out_sides = outer_rest(act, rows_d, 1, 2, (mark,))
-    *pair, mark = join((out_sides, hop))
+    out_sides, out_own, mark = outer_rest(act, rows_d, (mark,))
+    in_hop = first_hop(in_low, in_high, "y")
+    pre_b, in_sides, mark = backward(table, rows_d, rows_x, slope, weight_out, 1, 2, (mark,))
+    *pair, mark = join((after(out_sides, mark), hop))
     out_parts = second_hop(*pair, "x")
-    hop = first_hop(in_low, in_high, "y")
-    pre_b, in_sides, mark = backward(table, rows_d, rows_x, slope, weight_out, 1, 2, (mark,))
-    *pair, mark = join((in_sides, hop))
+    *pair, mark = join((after(in_sides, mark), in_hop))
     in_parts = second_hop(*pair, "y")
     pre_c, in_own, mark = backward(table, rows_d, rows_x, slope, weight_out, 3, 1, (mark,))
     own = sum_cores(row_gradients(table, (pre_a, pre_b, pre_c), weight_in))
     back = lax.all_to_all(own, "expert", split_axis=0, concat_axis=0, tiled=True)
 
-    out_keep, out_sides, low, high, mark = combine_product(act, rows_d, 3, out_parts)
+    out_keep, out_sides, low, high, mark = combine(out_own, out_parts)
     out_hop = first_hop(low, high, "y")
     in_keep, in_sides, low, high, mark = combine(after(in_own, mark), in_parts)
     in_hop = first_hop(low, high, "x")

time: 126 us -> 122 us (0.968)
  waiting for transfers between devices: 21.4 us -> 18.3 us
  local copies, waits for them, and re-layouts: 5.52 us -> 2.63 us
  other arithmetic: 4.05 us -> 5.98 us
    ppermute x8, waiting for transfers between devices: 10.5 us -> 6.78 us  [first_hop(): return (lax.ppermute(low, axis, ring(3)), lax.ppermute(high, axis, ring(1)))]
    unnamed x16 -> x8, local copies, waits for them, and re-layouts: 4.62 us -> 1.73 us
    broadcast_in_dim x2, other arithmetic: 1.83 us -> 3.8 us  [local(): return (token_grad, grad_in[None], grad_out[None])]
    pallas_call x1 -> x2, Pallas kernels: 2.37 us -> 4.29 us  [combine(): pl.pallas_call(body, out_shape=cut_shapes(n, width), in_specs=[VMEM] * 3,...]
    pallas_call x2 -> x1, Pallas kernels: 5.33 us -> 3.42 us  [outer_rest(): pl.pallas_call(body, in_specs=[VMEM] * 2 + [ANY] * len(deps), out_specs=[...]
  transfers between devices with their start and end apart: 31 -> 31, of which waited for: 11 -> 10; matrix products, arithmetic and copies ran while one was open for 3% -> 4% of each run, Pallas kernels for 37% -> 37%
where the time goes in v7:
time: 122 us; the launch traced here: 121 us
  Pallas kernels  48.9 us (40%)
  starting transfers between devices  38.8 us (32%)
  waiting for transfers between devices  18.3 us (15%)
  other arithmetic  5.98 us (5%)
  blocking collectives  5.42 us (4%)
  local copies, waits for them, and re-layouts  2.63 us (2%)
    ppermute x8, starting transfers between devices, second_hop(): return (lax.ppermute(up, axis, ring(1)), lax.ppermute(down, axis, ring(3)))  13 us
    pallas_call x3, Pallas kernels, backward(): pl.pallas_call(body, grid=(count,), in_specs=[SMEM] + [VMEM] * 4 + [ANY]...  12.1 us
    ppermute x8, starting transfers between devices, first_hop(): return (lax.ppermute(low, axis, ring(3)), lax.ppermute(high, axis, ring(1)))  11.2 us
    ppermute x6, starting transfers between devices, to_owner(): lax.ppermute(parts[r], 'expert', ring(r))  9.48 us
    pallas_call x1, Pallas kernels, forward(): pl.pallas_call(body, grid=(4,), in_specs=[SMEM] + [VMEM] * (len(parts) +...  9.1 us
    ppermute x6, waiting for transfers between devices, to_owner(): lax.ppermute(parts[r], 'expert', ring(r))  8.79 us
    ppermute x8, waiting for transfers between devices, first_hop(): return (lax.ppermute(low, axis, ring(3)), lax.ppermute(high, axis, ring(1)))  6.78 us
    pallas_call x1, Pallas kernels, row_gradients(): pl.pallas_call(body, grid=(4,), in_specs=[SMEM] + [VMEM] * 4, out_specs=V...  6.14 us
  transfers between devices with their start and end apart: 31, of which 10 were waited for; matrix products, arithmetic and copies ran while one was open for 4% of the time, Pallas kernels for 37%

profile of v7, /device:TPU:0, one launch (start us, length us, event | category | flops | bytes accessed | tf_op | source)
XLA Modules:
  0.0 120.8 jit_solution(955523960203665520)
XLA Ops:
  0.6 2.1 %shard_map.103 = (bf16[512,256]{1,0:T(8,128)(2,1)S(1)}, bf16[128,1024]{1,0:T(8,128)(2,1)S(1)}, bf16[128,1024]{1,0:T(8,128)(2,1)}, bf16[128,1024]{1,0:T(8,128)(2,1)S(1)}, bf16[128,1024]{1,0:T(8,128)(2,1)S(1)}) custom-call(s32[1]{0:T(128)} %bitcast.where_ref, s32[1,256]{1,0:T(1,128)} %bitcast.19, bf16[256,1024]{1,0:T(8,128)(2,1)} %tok_hbm.1), custom_call_target="tpu_custom_call" | custom-call | bytes 2097152 | tf_op jit(solution)/shard_map/pallas_call | solution.py:94
  2.7 2.1 %collective-permute-start = (bf16[128,1024]{1,0:T(8,128)(2,1)}, bf16[128,1024]{1,0:T(8,128)(2,1)S(1)}, u32[]{:S(2)}, u32[]{:S(2)}) collective-permute-start(bf16[128,1024]{1,0:T(8,128)(2,1)} %get-tuple-element.58), channel_id=1, source_target_pairs={{0,1},{1,2},{2,3},{3,0},{4,5},{5,6},{6,7},{7,4},{8,9},{9,10},{10,1... | collective-permute-start | bytes 786440 | tf_op jit(solution)/shard_map/ppermute | solution.py:456
  4.8 3.6 %collective-permute-start.1 = (bf16[128,1024]{1,0:T(8,128)(2,1)S(1)}, bf16[128,1024]{1,0:T(8,128)(2,1)S(1)}, u32[]{:S(2)}, u32[]{:S(2)}) collective-permute-start(bf16[128,1024]{1,0:T(8,128)(2,1)S(1)} %get-tuple-element.59), channel_id=1, source_target_pairs={{0,2},{1,3},{2,0},{3,1},{4,6},{5,7},{6,4},{7,5},{8,10},{9,11},{10,... | collective-permute-start | bytes 786440 | tf_op jit(solution)/shard_map/ppermute | solution.py:456
  14.5 4.2 %shard_map.104 = (bf16[2048,1024]{1,0:T(8,128)(2,1)S(1)}, bf16[2048,1024]{1,0:T(8,128)(2,1)S(1)}, f32[8,128]{1,0:T(8,128)S(1)}) custom-call(s32[53]{0:T(128)S(1)} %concatenate.3.table_ref, bf16[4096,1024]{1,0:T(8,128)(2,1)} %bitcast.16, bf16[4096,1024]{1,0:T(8,128)(2,1)} %bitcast.17), custom_call_target="tpu_custom_call" | custom-call | bytes 16777216 | tf_op jit(solution)/shard_map/pallas_call | solution.py:153
  21.4 3.8 %collective-permute-done.2.refs_1_.refs_0_ = bf16[128,1024]{1,0:T(8,128)(2,1)S(1)} collective-permute-done((bf16[128,1024]{1,0:T(8,128)(2,1)S(1)}, bf16[128,1024]{1,0:T(8,128)(2,1)S(1)}, u32[]{:S(2)}, u32[]{:S(2)}) %collective-permute-start.2) | collective-permute-done | bytes 262176 | tf_op jit(solution)/shard_map/ppermute | solution.py:456
  27.0 9.1 %shard_map.108 = (bf16[2048,1024]{1,0:T(8,128)(2,1)S(1)}, bf16[2048,1024]{1,0:T(8,128)(2,1)S(1)}, bf16[1024,1024]{1,0:T(8,128)(2,1)S(1)}, f32[8,128]{1,0:T(8,128)S(1)}) custom-call(s32[53]{0:T(128)S(1)} %concatenate.3.table_ref, bf16[128,1024]{1,0:T(8,128)(2,1)S(1)} %shard_map.106.refs_0_, bf16[128,1024]{1,0:T(8,128)(2,1)S(1)} %collective-permute-done.refs_1_, ...), custom_call_target="tpu_custom_call" | custom-call | bytes 16777216 | tf_op jit(solution)/shard_map/pallas_call | solution.py:213
  36.8 2.8 %collective-permute-done.9.refs_0_ = bf16[128,1024]{1,0:T(8,128)(2,1)S(1)} collective-permute-done((bf16[128,1024]{1,0:T(8,128)(2,1)S(1)}, bf16[128,1024]{1,0:T(8,128)(2,1)S(1)}, u32[]{:S(2)}, u32[]{:S(2)}) %collective-permute-start.9) | collective-permute-done | bytes 262176 | tf_op jit(solution)/shard_map/ppermute | solution.py:456
  43.1 2.8 %collective-permute-start.14 = (bf16[256,1024]{1,0:T(8,128)(2,1)S(1)}, bf16[256,1024]{1,0:T(8,128)(2,1)S(1)}, u32[]{:S(2)}, u32[]{:S(2)}) collective-permute-start(bf16[256,1024]{1,0:T(8,128)(2,1)S(1)} %get-tuple-element.79), channel_id=1, source_target_pairs={{0,24},{8,0},{16,8},{24,16},{1,25},{9,1},{17,9},{25,17},{2,26},{10... | collective-permute-start | bytes 1572872 | tf_op jit(solution)/shard_map/ppermute | solution.py:388
  46.0 2.9 %shard_map.114 = (bf16[512,1024]{1,0:T(8,128)(2,1)S(1)}, bf16[256,1024]{1,0:T(8,128)(2,1)S(1)}, bf16[256,1024]{1,0:T(8,128)(2,1)S(1)}, f32[8,128]{1,0:T(8,128)S(1)}) custom-call(s32[53]{0:T(128)S(1)} %concatenate.3.table_ref, bf16[1024,1024]{1,0:T(8,128)(2,1)S(1)} %get-tuple-element.67.grads_ref.rows_ref, bf16[1024,1024]{1,0:T(8,128)(2,1)S(1)} %get-tuple-element.68.rows_ref, ...), custom_call_target="tpu_custom_call" | custom-call | bytes 6291456 | tf_op jit(solution)/shard_map/pallas_call | solution.py:289
  48.9 3.1 %collective-permute-start.16 = (bf16[256,1024]{1,0:T(8,128)(2,1)S(1)}, bf16[256,1024]{1,0:T(8,128)(2,1)S(1)}, u32[]{:S(2)}, u32[]{:S(2)}) collective-permute-start(bf16[256,1024]{1,0:T(8,128)(2,1)S(1)} %get-tuple-element.82), channel_id=1, source_target_pairs={{0,96},{32,0},{64,32},{96,64},{1,97},{33,1},{65,33},{97,65},{2,98}... | collective-permute-start | bytes 1572872 | tf_op jit(solution)/shard_map/ppermute | solution.py:388
  52.0 3.4 %shard_map.115 = (bf16[1024,1024]{1,0:T(8,128)(2,1)S(1)}, bf16[512,1024]{1,0:T(8,128)(2,1)S(1)}, f32[8,128]{1,0:T(8,128)S(1)}) custom-call(bf16[2048,1024]{1,0:T(8,128)(2,1)S(1)} %get-tuple-element.63.act_ref, bf16[1024,1024]{1,0:T(8,128)(2,1)S(1)} %get-tuple-element.67.grads_ref.rows_ref, f32[8,128]{1,0:T(8,128)S(1)} %get-tuple-element.73.refs_0_), custom_call_target="tpu_custom_call" | custom-call | bytes 8388608 | tf_op jit(solution)/shard_map/pallas_call | solution.py:255
  55.4 5.8 %shard_map.116 = (bf16[1024,1024]{1,0:T(8,128)(2,1)S(1)}, bf16[1024,1024]{1,0:T(8,128)(2,1)S(1)}, f32[8,128]{1,0:T(8,128)S(1)}) custom-call(s32[53]{0:T(128)S(1)} %concatenate.3.table_ref, bf16[1024,1024]{1,0:T(8,128)(2,1)S(1)} %get-tuple-element.67.grads_ref.rows_ref, bf16[1024,1024]{1,0:T(8,128)(2,1)S(1)} %get-tuple-element.68.rows_ref, ...), custom_call_target="tpu_custom_call" | custom-call | bytes 10485760 | tf_op jit(solution)/shard_map/pallas_call | solution.py:289
  63.5 2.5 %collective-permute-start.19 = (bf16[512,1024]{1,0:T(8,128)(2,1)}, bf16[512,1024]{1,0:T(8,128)(2,1)}, u32[]{:S(2)}, u32[]{:S(2)}) collective-permute-start(bf16[512,1024]{1,0:T(8,128)(2,1)} %get-tuple-element.89), channel_id=1, source_target_pairs={{0,24},{8,0},{16,8},{24,16},{1,25},{9,1},{17,9},{25,17},{2,26},{10... | collective-permute-start | bytes 3145736 | tf_op jit(solution)/shard_map/ppermute | solution.py:392
  68.8 2.6 %collective-permute-start.21 = (bf16[512,1024]{1,0:T(8,128)(2,1)}, bf16[512,1024]{1,0:T(8,128)(2,1)}, u32[]{:S(2)}, u32[]{:S(2)}) collective-permute-start(bf16[512,1024]{1,0:T(8,128)(2,1)} %get-tuple-element.92), channel_id=1, source_target_pairs={{0,96},{32,0},{64,32},{96,64},{1,97},{33,1},{65,33},{97,65},{2,98}... | collective-permute-start | bytes 3145736 | tf_op jit(solution)/shard_map/ppermute | solution.py:392
  71.4 3.4 %shard_map.121 = (bf16[512,1024]{1,0:T(8,128)(2,1)S(1)}, bf16[512,1024]{1,0:T(8,128)(2,1)S(1)}, f32[8,128]{1,0:T(8,128)}) custom-call(s32[53]{0:T(128)S(1)} %concatenate.3.table_ref, bf16[1024,1024]{1,0:T(8,128)(2,1)S(1)} %get-tuple-element.67.grads_ref.rows_ref, bf16[1024,1024]{1,0:T(8,128)(2,1)S(1)} %get-tuple-element.68.rows_ref, ...), custom_call_target="tpu_custom_call" | custom-call | bytes 6291456 | tf_op jit(solution)/shard_map/pallas_call | solution.py:289
  74.9 6.1 %shard_map.122 = bf16[1024,1024]{1,0:T(8,128)(2,1)S(1)} custom-call(s32[53]{0:T(128)S(1)} %concatenate.3.table_ref, bf16[512,1024]{1,0:T(8,128)(2,1)S(1)} %get-tuple-element.72.a_ref, bf16[1024,1024]{1,0:T(8,128)(2,1)S(1)} %get-tuple-element.75.b_ref, bf16[512,1024]{1,0:T(8,128)(2,1)S(1)} %get-tuple-element.85.c_ref, ...), custom_call_target="tpu_custom_call" | custom-call | bytes 12582912 | tf_op jit(solution)/shard_map/pallas_call | solution.py:327
  81.0 5.4 %all_to_all.17 = bf16[2,512,1024]{2,1,0:T(8,128)(2,1)S(1)} all-to-all(bf16[2,512,1024]{2,1,0:T(8,128)(2,1)S(1)} %bitcast.13), channel_id=1, replica_groups=mesh['y'=4,'x'=4,'core'=2,'expert'=4] {'core'}, dimensions={0} | all-to-all | bytes 4194304 | tf_op jit(solution)/shard_map/all_to_all | solution.py:433
  87.8 3.9 %all-to-all-start.1 = ((bf16[4,128,1024]{2,1,0:T(8,128)(2,1)}), bf16[4,128,1024]{2,1,0:T(8,128)(2,1)S(1)}, u32[]{:S(2)}, u32[]{:S(2)}) async-start(bf16[4,128,1024]{2,1,0:T(8,128)(2,1)} %bitcast.18), calls=%async_computation.1 | async-start | bytes 2097152 | tf_op jit(solution)/shard_map/all_to_all | solution.py:481
  96.0 2.4 %shard_map.126 = (bf16[128,1024]{1,0:T(8,128)(2,1)S(1)}, bf16[256,1024]{1,0:T(8,128)(2,1)S(1)}, bf16[64,1024]{1,0:T(8,128)(2,1)S(1)}, bf16[64,1024]{1,0:T(8,128)(2,1)S(1)}, f32[8,128]{1,0:T(8,128)}) custom-call(bf16[512,1024]{1,0:T(8,128)(2,1)S(1)} %shard_map.125.own_ref, bf16[512,1024]{1,0:T(8,128)(2,1)} %collective-permute-done.20.left, ...), custom_call_target="tpu_custom_call" | custom-call | bytes 4194304 | tf_op jit(solution)/shard_map/pallas_call | solution.py:418
  98.3 3.0 %collective-permute-start.24 = (bf16[64,1024]{1,0:T(8,128)(2,1)S(1)}, bf16[64,1024]{1,0:T(8,128)(2,1)S(1)}, u32[]{:S(2)}, u32[]{:S(2)}) collective-permute-start(bf16[64,1024]{1,0:T(8,128)(2,1)S(1)} %get-tuple-element.98), channel_id=1, source_target_pairs={{0,24},{8,0},{16,8},{24,16},{1,25},{9,1},{17,9},{25,17},{2,26},{10... | collective-permute-start | bytes 393224 | tf_op jit(solution)/shard_map/ppermute | solution.py:388
  101.6 2.3 %collective-permute-done.24.refs_4_ = bf16[64,1024]{1,0:T(8,128)(2,1)S(1)} collective-permute-done((bf16[64,1024]{1,0:T(8,128)(2,1)S(1)}, bf16[64,1024]{1,0:T(8,128)(2,1)S(1)}, u32[]{:S(2)}, u32[]{:S(2)}) %collective-permute-start.24) | collective-permute-done | bytes 131104 | tf_op jit(solution)/shard_map/ppermute | solution.py:388
  103.8 3.7 %collective-permute-done.25.refs_5_ = bf16[64,1024]{1,0:T(8,128)(2,1)S(1)} collective-permute-done((bf16[64,1024]{1,0:T(8,128)(2,1)S(1)}, bf16[64,1024]{1,0:T(8,128)(2,1)S(1)}, u32[]{:S(2)}, u32[]{:S(2)}) %collective-permute-start.25) | collective-permute-done | bytes 131104 | tf_op jit(solution)/shard_map/ppermute | solution.py:388
  108.2 3.2 %collective-permute-start.27 = (bf16[128,1024]{1,0:T(8,128)(2,1)S(1)}, bf16[128,1024]{1,0:T(8,128)(2,1)}, u32[]{:S(2)}, u32[]{:S(2)}) collective-permute-start(bf16[128,1024]{1,0:T(8,128)(2,1)S(1)} %get-tuple-element.101), channel_id=1, source_target_pairs={{0,24},{8,0},{16,8},{24,16},{1,25},{9,1},{17,9},{25,17},{2,26},{10... | collective-permute-start | bytes 786440 | tf_op jit(solution)/shard_map/ppermute | solution.py:392
  111.4 3.2 %collective-permute-start.29 = (bf16[128,1024]{1,0:T(8,128)(2,1)S(1)}, bf16[128,1024]{1,0:T(8,128)(2,1)}, u32[]{:S(2)}, u32[]{:S(2)}) collective-permute-start(bf16[128,1024]{1,0:T(8,128)(2,1)S(1)} %get-tuple-element.104), channel_id=1, source_target_pairs={{0,96},{32,0},{64,32},{96,64},{1,97},{33,1},{65,33},{97,65},{2,98}... | collective-permute-start | bytes 786440 | tf_op jit(solution)/shard_map/ppermute | solution.py:392
  (83 shorter events, 32.6 us)
Async XLA Ops:
  2.7 16.1 %collective-permute-start = (bf16[128,1024]{1,0:T(8,128)(2,1)}, bf16[128,1024]{1,0:T(8,128)(2,1)S(1)}, u32[]{:S(2)}, u32[]{:S(2)}) collective-permute-start(bf16[128,1024]{1,0:T(8,128)(2,1)} %get-tuple-element.58), channel_id=1, source_target_pairs={{0,1},{1,2},{2,3},{3,0},{4,5},{5,6},{6,7},{7,4},{8,9},{9,10},{10,1... | collective-permute-start | bytes 786440 | tf_op jit(solution)/shard_map/ppermute | solution.py:456
  4.8 16.6 %collective-permute-start.1 = (bf16[128,1024]{1,0:T(8,128)(2,1)S(1)}, bf16[128,1024]{1,0:T(8,128)(2,1)S(1)}, u32[]{:S(2)}, u32[]{:S(2)}) collective-permute-start(bf16[128,1024]{1,0:T(8,128)(2,1)S(1)} %get-tuple-element.59), channel_id=1, source_target_pairs={{0,2},{1,3},{2,0},{3,1},{4,6},{5,7},{6,4},{7,5},{8,10},{9,11},{10,... | collective-permute-start | bytes 786440 | tf_op jit(solution)/shard_map/ppermute | solution.py:456
  8.4 11.2 %collective-permute-start.3 = (bf16[128,1024]{1,0:T(8,128)(2,1)S(1)}, bf16[128,1024]{1,0:T(8,128)(2,1)S(1)}, u32[]{:S(2)}, u32[]{:S(2)}) collective-permute-start(bf16[128,1024]{1,0:T(8,128)(2,1)S(1)} %get-tuple-element.61), channel_id=1, source_target_pairs={{0,3},{1,0},{2,1},{3,2},{4,7},{5,4},{6,5},{7,6},{8,11},{9,8},{10,9... | collective-permute-start | bytes 786440 | tf_op jit(solution)/shard_map/ppermute | solution.py:456
  11.7 13.5 %collective-permute-start.2 = (bf16[128,1024]{1,0:T(8,128)(2,1)S(1)}, bf16[128,1024]{1,0:T(8,128)(2,1)S(1)}, u32[]{:S(2)}, u32[]{:S(2)}) collective-permute-start(bf16[128,1024]{1,0:T(8,128)(2,1)S(1)} %get-tuple-element.60), channel_id=1, source_target_pairs={{0,1},{1,2},{2,3},{3,0},{4,5},{5,6},{6,7},{7,4},{8,9},{9,10},{10,1... | collective-permute-start | bytes 786440 | tf_op jit(solution)/shard_map/ppermute | solution.py:456
  18.7 7.6 %collective-permute-start.4 = (bf16[128,1024]{1,0:T(8,128)(2,1)S(1)}, bf16[128,1024]{1,0:T(8,128)(2,1)S(1)}, u32[]{:S(2)}, u32[]{:S(2)}) collective-permute-start(bf16[128,1024]{1,0:T(8,128)(2,1)S(1)} %shard_map.106.refs_0_), channel_id=1, source_target_pairs={{0,4},{4,0},{1,5},{5,1},{2,6},{6,2},{3,7},{7,3},{8,12},{12,8},{9,1... | collective-permute-start | bytes 786440 | tf_op jit(solution)/shard_map/ppermute | solution.py:22
  18.8 8.2 %collective-permute-start.5 = (bf16[128,1024]{1,0:T(8,128)(2,1)S(1)}, bf16[128,1024]{1,0:T(8,128)(2,1)S(1)}, u32[]{:S(2)}, u32[]{:S(2)}) collective-permute-start(bf16[128,1024]{1,0:T(8,128)(2,1)S(1)} %collective-permute-done.refs_1_), channel_id=1, source_target_pairs={{0,4},{4,0},{1,5},{5,1},{2,6},{6,2},{3,7},{7,3},{8,12},{12,8},{9,1... | collective-permute-start | bytes 786440 | tf_op jit(solution)/shard_map/ppermute | solution.py:22
  19.6 7.5 %collective-permute-start.7 = (bf16[128,1024]{1,0:T(8,128)(2,1)S(1)}, bf16[128,1024]{1,0:T(8,128)(2,1)S(1)}, u32[]{:S(2)}, u32[]{:S(2)}) collective-permute-start(bf16[128,1024]{1,0:T(8,128)(2,1)S(1)} %collective-permute-done.3.refs_3_), channel_id=1, source_target_pairs={{0,4},{4,0},{1,5},{5,1},{2,6},{6,2},{3,7},{7,3},{8,12},{12,8},{9,1... | collective-permute-start | bytes 786440 | tf_op jit(solution)/shard_map/ppermute | solution.py:22
  25.3 11.5 %collective-permute-start.8 = (bf16[128,1024]{1,0:T(8,128)(2,1)S(1)}, bf16[128,1024]{1,0:T(8,128)(2,1)S(1)}, u32[]{:S(2)}, u32[]{:S(2)}) collective-permute-start(bf16[128,1024]{1,0:T(8,128)(2,1)S(1)} %get-tuple-element.65), channel_id=1, source_target_pairs={{0,2},{1,3},{2,0},{3,1},{4,6},{5,7},{6,4},{7,5},{8,10},{9,11},{10,... | collective-permute-start | bytes 786440 | tf_op jit(solution)/shard_map/ppermute | solution.py:456
  26.3 13.4 %collective-permute-start.9 = (bf16[128,1024]{1,0:T(8,128)(2,1)S(1)}, bf16[128,1024]{1,0:T(8,128)(2,1)S(1)}, u32[]{:S(2)}, u32[]{:S(2)}) collective-permute-start(bf16[128,1024]{1,0:T(8,128)(2,1)S(1)} %get-tuple-element.66), channel_id=1, source_target_pairs={{0,3},{1,0},{2,1},{3,2},{4,7},{5,4},{6,5},{7,6},{8,11},{9,8},{10,9... | collective-permute-start | bytes 786440 | tf_op jit(solution)/shard_map/ppermute | solution.py:456
  43.1 18.0 %collective-permute-start.14 = (bf16[256,1024]{1,0:T(8,128)(2,1)S(1)}, bf16[256,1024]{1,0:T(8,128)(2,1)S(1)}, u32[]{:S(2)}, u32[]{:S(2)}) collective-permute-start(bf16[256,1024]{1,0:T(8,128)(2,1)S(1)} %get-tuple-element.79), channel_id=1, source_target_pairs={{0,24},{8,0},{16,8},{24,16},{1,25},{9,1},{17,9},{25,17},{2,26},{10... | collective-permute-start | bytes 1572872 | tf_op jit(solution)/shard_map/ppermute | solution.py:388
  46.0 15.2 %collective-permute-start.15 = (bf16[256,1024]{1,0:T(8,128)(2,1)S(1)}, bf16[256,1024]{1,0:T(8,128)(2,1)S(1)}, u32[]{:S(2)}, u32[]{:S(2)}) collective-permute-start(bf16[256,1024]{1,0:T(8,128)(2,1)S(1)} %get-tuple-element.80), channel_id=1, source_target_pairs={{0,8},{8,16},{16,24},{24,0},{1,9},{9,17},{17,25},{25,1},{2,10},{10... | collective-permute-start | bytes 1572872 | tf_op jit(solution)/shard_map/ppermute | solution.py:388
  48.9 17.1 %collective-permute-start.16 = (bf16[256,1024]{1,0:T(8,128)(2,1)S(1)}, bf16[256,1024]{1,0:T(8,128)(2,1)S(1)}, u32[]{:S(2)}, u32[]{:S(2)}) collective-permute-start(bf16[256,1024]{1,0:T(8,128)(2,1)S(1)} %get-tuple-element.82), channel_id=1, source_target_pairs={{0,96},{32,0},{64,32},{96,64},{1,97},{33,1},{65,33},{97,65},{2,98}... | collective-permute-start | bytes 1572872 | tf_op jit(solution)/shard_map/ppermute | solution.py:388
  52.0 14.6 %collective-permute-start.17 = (bf16[256,1024]{1,0:T(8,128)(2,1)S(1)}, bf16[256,1024]{1,0:T(8,128)(2,1)S(1)}, u32[]{:S(2)}, u32[]{:S(2)}) collective-permute-start(bf16[256,1024]{1,0:T(8,128)(2,1)S(1)} %get-tuple-element.83), channel_id=1, source_target_pairs={{0,32},{32,64},{64,96},{96,0},{1,33},{33,65},{65,97},{97,1},{2,34}... | collective-permute-start | bytes 1572872 | tf_op jit(solution)/shard_map/ppermute | solution.py:388
  62.8 28.9 %collective-permute-start.18 = (bf16[512,1024]{1,0:T(8,128)(2,1)}, bf16[512,1024]{1,0:T(8,128)(2,1)}, u32[]{:S(2)}, u32[]{:S(2)}) collective-permute-start(bf16[512,1024]{1,0:T(8,128)(2,1)} %get-tuple-element.88), channel_id=1, source_target_pairs={{0,8},{8,16},{16,24},{24,0},{1,9},{9,17},{17,25},{25,1},{2,10},{10... | collective-permute-start | bytes 3145736 | tf_op jit(solution)/shard_map/ppermute | solution.py:392
  63.5 28.2 %collective-permute-start.19 = (bf16[512,1024]{1,0:T(8,128)(2,1)}, bf16[512,1024]{1,0:T(8,128)(2,1)}, u32[]{:S(2)}, u32[]{:S(2)}) collective-permute-start(bf16[512,1024]{1,0:T(8,128)(2,1)} %get-tuple-element.89), channel_id=1, source_target_pairs={{0,24},{8,0},{16,8},{24,16},{1,25},{9,1},{17,9},{25,17},{2,26},{10... | collective-permute-start | bytes 3145736 | tf_op jit(solution)/shard_map/ppermute | solution.py:392
  68.2 27.8 %collective-permute-start.20 = (bf16[512,1024]{1,0:T(8,128)(2,1)}, bf16[512,1024]{1,0:T(8,128)(2,1)}, u32[]{:S(2)}, u32[]{:S(2)}) collective-permute-start(bf16[512,1024]{1,0:T(8,128)(2,1)} %get-tuple-element.91), channel_id=1, source_target_pairs={{0,32},{32,64},{64,96},{96,0},{1,33},{33,65},{65,97},{97,1},{2,34}... | collective-permute-start | bytes 3145736 | tf_op jit(solution)/shard_map/ppermute | solution.py:392
  68.8 27.1 %collective-permute-start.21 = (bf16[512,1024]{1,0:T(8,128)(2,1)}, bf16[512,1024]{1,0:T(8,128)(2,1)}, u32[]{:S(2)}, u32[]{:S(2)}) collective-permute-start(bf16[512,1024]{1,0:T(8,128)(2,1)} %get-tuple-element.92), channel_id=1, source_target_pairs={{0,96},{32,0},{64,32},{96,64},{1,97},{33,1},{65,33},{97,65},{2,98}... | collective-permute-start | bytes 3145736 | tf_op jit(solution)/shard_map/ppermute | solution.py:392
  87.8 26.8 %all-to-all-start.1 = ((bf16[4,128,1024]{2,1,0:T(8,128)(2,1)}), bf16[4,128,1024]{2,1,0:T(8,128)(2,1)S(1)}, u32[]{:S(2)}, u32[]{:S(2)}) async-start(bf16[4,128,1024]{2,1,0:T(8,128)(2,1)} %bitcast.18), calls=%async_computation.1 | async-start | bytes 2097152 | tf_op jit(solution)/shard_map/all_to_all | solution.py:481
  93.6 7.7 %collective-permute-start.22 = (bf16[64,1024]{1,0:T(8,128)(2,1)S(1)}, bf16[64,1024]{1,0:T(8,128)(2,1)S(1)}, u32[]{:S(2)}, u32[]{:S(2)}) collective-permute-start(bf16[64,1024]{1,0:T(8,128)(2,1)S(1)} %get-tuple-element.95), channel_id=1, source_target_pairs={{0,96},{32,0},{64,32},{96,64},{1,97},{33,1},{65,33},{97,65},{2,98}... | collective-permute-start | bytes 393224 | tf_op jit(solution)/shard_map/ppermute | solution.py:388
  95.4 6.2 %collective-permute-start.23 = (bf16[64,1024]{1,0:T(8,128)(2,1)S(1)}, bf16[64,1024]{1,0:T(8,128)(2,1)S(1)}, u32[]{:S(2)}, u32[]{:S(2)}) collective-permute-start(bf16[64,1024]{1,0:T(8,128)(2,1)S(1)} %get-tuple-element.96), channel_id=1, source_target_pairs={{0,32},{32,64},{64,96},{96,0},{1,33},{33,65},{65,97},{97,1},{2,34}... | collective-permute-start | bytes 393224 | tf_op jit(solution)/shard_map/ppermute | solution.py:388
  108.1 7.7 %collective-permute-start.26 = (bf16[128,1024]{1,0:T(8,128)(2,1)S(1)}, bf16[128,1024]{1,0:T(8,128)(2,1)}, u32[]{:S(2)}, u32[]{:S(2)}) collective-permute-start(bf16[128,1024]{1,0:T(8,128)(2,1)S(1)} %get-tuple-element.100), channel_id=1, source_target_pairs={{0,8},{8,16},{16,24},{24,0},{1,9},{9,17},{17,25},{25,1},{2,10},{10... | collective-permute-start | bytes 786440 | tf_op jit(solution)/shard_map/ppermute | solution.py:392
  108.2 7.7 %collective-permute-start.27 = (bf16[128,1024]{1,0:T(8,128)(2,1)S(1)}, bf16[128,1024]{1,0:T(8,128)(2,1)}, u32[]{:S(2)}, u32[]{:S(2)}) collective-permute-start(bf16[128,1024]{1,0:T(8,128)(2,1)S(1)} %get-tuple-element.101), channel_id=1, source_target_pairs={{0,24},{8,0},{16,8},{24,16},{1,25},{9,1},{17,9},{25,17},{2,26},{10... | collective-permute-start | bytes 786440 | tf_op jit(solution)/shard_map/ppermute | solution.py:392
  111.4 7.6 %collective-permute-start.28 = (bf16[128,1024]{1,0:T(8,128)(2,1)S(1)}, bf16[128,1024]{1,0:T(8,128)(2,1)S(1)}, u32[]{:S(2)}, u32[]{:S(2)}) collective-permute-start(bf16[128,1024]{1,0:T(8,128)(2,1)S(1)} %get-tuple-element.103), channel_id=1, source_target_pairs={{0,32},{32,64},{64,96},{96,0},{1,33},{33,65},{65,97},{97,1},{2,34}... | collective-permute-start | bytes 786440 | tf_op jit(solution)/shard_map/ppermute | solution.py:392
  111.4 7.6 %collective-permute-start.29 = (bf16[128,1024]{1,0:T(8,128)(2,1)S(1)}, bf16[128,1024]{1,0:T(8,128)(2,1)}, u32[]{:S(2)}, u32[]{:S(2)}) collective-permute-start(bf16[128,1024]{1,0:T(8,128)(2,1)S(1)} %get-tuple-element.104), channel_id=1, source_target_pairs={{0,96},{32,0},{64,32},{96,64},{1,97},{33,1},{65,33},{97,65},{2,98}... | collective-permute-start | bytes 786440 | tf_op jit(solution)/shard_map/ppermute | solution.py:392
  (11 other events, 40.4 us)

commit v8 on v7

--- a/solution.py
+++ b/solution.py
@@ -458,7 +458,7 @@
     own_x = to_owner(send_x)
     own_d = to_owner(send_d)
     own_x[0] = after(own_x[0], mark, send_d[0])
-    own_x[2] = after(own_x[2], own_d[1])
+    own_x[2] = after(own_x[2], own_d[2])
     both_x = own_x + [swap_core(p) for p in own_x]
     act, slope, rows_x, mark = forward(table, both_x, weight_in)
     own_d = [after(part, mark) for part in own_d]
@@ -478,10 +478,9 @@
     in_parts = second_hop(*pair, "y")
     pre_c, in_own, mark = backward(table, rows_d, rows_x, slope, weight_out, 3, 1, (mark,))
     own = sum_cores(row_gradients(table, (pre_a, pre_b, pre_c), weight_in))
-    back = lax.all_to_all(own, "expert", split_axis=0, concat_axis=0, tiled=True)
-
     out_keep, out_sides, low, high, mark = combine(out_own, out_parts)
     out_hop = first_hop(low, high, "y")
+    back = lax.all_to_all(after(own, mark), "expert", split_axis=0, concat_axis=0, tiled=True)
     in_keep, in_sides, low, high, mark = combine(after(in_own, mark), in_parts)
     in_hop = first_hop(low, high, "x")
     *pairs, _ = join((out_sides, out_hop), (in_sides, in_hop))

time: 122 us -> 120 us (0.984)
  starting transfers between devices: 38.8 us -> 45.6 us
  blocking collectives: 5.42 us -> 0 us
  waiting for transfers between devices: 18.3 us -> 14.9 us
  Pallas kernels: 48.9 us -> 50.4 us
    ppermute x8, waiting for transfers between devices: 6.78 us -> 0.5 us  [first_hop(): return (lax.ppermute(low, axis, ring(3)), lax.ppermute(high, axis, ring(1)))]
    all_to_all x1 -> x0, blocking collectives: 5.42 us -> none  [sum_cores(): lax.all_to_all(terms, 'core', split_axis=0, concat_axis=0, tiled=True)]
    all_to_all x1 -> x2, starting transfers between devices: 3.87 us -> 8.48 us  [the longest x1 4.84 us: sum_cores(): lax.all_to_all(terms, 'core', split_axis=0, concat_axis=0, tiled=True)]
    ppermute x8, waiting for transfers between devices: 1.15 us -> 5.17 us  [second_hop(): return (lax.ppermute(up, axis, ring(1)), lax.ppermute(down, axis, ring(3)))]
    broadcast_in_dim x2, other arithmetic: 3.8 us -> 1.82 us  [local(): return (token_grad, grad_in[None], grad_out[None])]
    ppermute x6, waiting for transfers between devices: 8.79 us -> 7 us  [to_owner(): lax.ppermute(parts[r], 'expert', ring(r))]
    convert_element_type x1, other arithmetic: 1.4 us -> 2.92 us  [sum_cores(): return add(terms[:n], terms[n:]).astype(BF16)]
    pallas_call x1, Pallas kernels: 6.14 us -> 7.53 us  [row_gradients(): pl.pallas_call(body, grid=(4,), in_specs=[SMEM] + [VMEM] * 4, out_specs=V...]
  transfers between devices with their start and end apart: 31 -> 32, of which waited for: 10 -> 12; matrix products, arithmetic and copies ran while one was open for 4% -> 5% of each run, Pallas kernels for 37% -> 38%
where the time goes in v8:
time: 120 us
  Pallas kernels  50.4 us (42%)
  starting transfers between devices  45.6 us (38%)
  waiting for transfers between devices  14.9 us (12%)
  other arithmetic  5.52 us (5%)
  local copies, waits for them, and re-layouts  2.63 us (2%)
    ppermute x8, starting transfers between devices, second_hop(): return (lax.ppermute(up, axis, ring(1)), lax.ppermute(down, axis, ring(3)))  12.9 us
    pallas_call x3, Pallas kernels, backward(): pl.pallas_call(body, grid=(count,), in_specs=[SMEM] + [VMEM] * 4 + [ANY]...  12.2 us
    ppermute x8, starting transfers between devices, first_hop(): return (lax.ppermute(low, axis, ring(3)), lax.ppermute(high, axis, ring(1)))  12 us
    ppermute x6, starting transfers between devices, to_owner(): lax.ppermute(parts[r], 'expert', ring(r))  10.5 us
    pallas_call x1, Pallas kernels, forward(): pl.pallas_call(body, grid=(4,), in_specs=[SMEM] + [VMEM] * (len(parts) +...  9.08 us
    pallas_call x1, Pallas kernels, row_gradients(): pl.pallas_call(body, grid=(4,), in_specs=[SMEM] + [VMEM] * 4, out_specs=V...  7.53 us
    ppermute x6, waiting for transfers between devices, to_owner(): lax.ppermute(parts[r], 'expert', ring(r))  7 us
    ppermute x8, waiting for transfers between devices, second_hop(): return (lax.ppermute(up, axis, ring(1)), lax.ppermute(down, axis, ring(3)))  5.17 us
  transfers between devices with their start and end apart: 32, of which 12 were waited for; matrix products, arithmetic and copies ran while one was open for 5% of the time, Pallas kernels for 38%

profile of v8, /device:TPU:0, one launch (start us, length us, event | category | flops | bytes accessed | tf_op | source)
XLA Modules:
  0.0 119.9 jit_solution(11529020388571288320)
XLA Ops:
  0.6 2.1 %shard_map.103 = (bf16[512,256]{1,0:T(8,128)(2,1)S(1)}, bf16[128,1024]{1,0:T(8,128)(2,1)S(1)}, bf16[128,1024]{1,0:T(8,128)(2,1)}, bf16[128,1024]{1,0:T(8,128)(2,1)S(1)}, bf16[128,1024]{1,0:T(8,128)(2,1)S(1)}) custom-call(s32[1]{0:T(128)} %bitcast.where_ref, s32[1,256]{1,0:T(1,128)} %bitcast.19, bf16[256,1024]{1,0:T(8,128)(2,1)} %tok_hbm.1), custom_call_target="tpu_custom_call" | custom-call | bytes 2097152 | tf_op jit(solution)/shard_map/pallas_call | solution.py:94
  2.7 2.1 %collective-permute-start = (bf16[128,1024]{1,0:T(8,128)(2,1)}, bf16[128,1024]{1,0:T(8,128)(2,1)S(1)}, u32[]{:S(2)}, u32[]{:S(2)}) collective-permute-start(bf16[128,1024]{1,0:T(8,128)(2,1)} %get-tuple-element.58), channel_id=1, source_target_pairs={{0,1},{1,2},{2,3},{3,0},{4,5},{5,6},{6,7},{7,4},{8,9},{9,10},{10,1... | collective-permute-start | bytes 786440 | tf_op jit(solution)/shard_map/ppermute | solution.py:456
  4.8 3.6 %collective-permute-start.1 = (bf16[128,1024]{1,0:T(8,128)(2,1)S(1)}, bf16[128,1024]{1,0:T(8,128)(2,1)S(1)}, u32[]{:S(2)}, u32[]{:S(2)}) collective-permute-start(bf16[128,1024]{1,0:T(8,128)(2,1)S(1)} %get-tuple-element.59), channel_id=1, source_target_pairs={{0,2},{1,3},{2,0},{3,1},{4,6},{5,7},{6,4},{7,5},{8,10},{9,11},{10,... | collective-permute-start | bytes 786440 | tf_op jit(solution)/shard_map/ppermute | solution.py:456
  14.0 4.2 %shard_map.104 = (bf16[2048,1024]{1,0:T(8,128)(2,1)S(1)}, bf16[2048,1024]{1,0:T(8,128)(2,1)S(1)}, f32[8,128]{1,0:T(8,128)S(1)}) custom-call(s32[53]{0:T(128)S(1)} %concatenate.3.table_ref, bf16[4096,1024]{1,0:T(8,128)(2,1)} %bitcast.17, bf16[4096,1024]{1,0:T(8,128)(2,1)} %bitcast.18), custom_call_target="tpu_custom_call" | custom-call | bytes 16777216 | tf_op jit(solution)/shard_map/pallas_call | solution.py:153
  21.4 4.5 %collective-permute-done.2.refs_1_.refs_0_ = bf16[128,1024]{1,0:T(8,128)(2,1)S(1)} collective-permute-done((bf16[128,1024]{1,0:T(8,128)(2,1)S(1)}, bf16[128,1024]{1,0:T(8,128)(2,1)S(1)}, u32[]{:S(2)}, u32[]{:S(2)}) %collective-permute-start.2) | collective-permute-done | bytes 262176 | tf_op jit(solution)/shard_map/ppermute | solution.py:456
  29.1 9.1 %shard_map.108 = (bf16[2048,1024]{1,0:T(8,128)(2,1)S(1)}, bf16[2048,1024]{1,0:T(8,128)(2,1)S(1)}, bf16[1024,1024]{1,0:T(8,128)(2,1)S(1)}, f32[8,128]{1,0:T(8,128)S(1)}) custom-call(s32[53]{0:T(128)S(1)} %concatenate.3.table_ref, bf16[128,1024]{1,0:T(8,128)(2,1)S(1)} %shard_map.106.refs_0_, bf16[128,1024]{1,0:T(8,128)(2,1)S(1)} %collective-permute-done.refs_1_, ...), custom_call_target="tpu_custom_call" | custom-call | bytes 16777216 | tf_op jit(solution)/shard_map/pallas_call | solution.py:213
  42.9 2.8 %collective-permute-start.14 = (bf16[256,1024]{1,0:T(8,128)(2,1)S(1)}, bf16[256,1024]{1,0:T(8,128)(2,1)S(1)}, u32[]{:S(2)}, u32[]{:S(2)}) collective-permute-start(bf16[256,1024]{1,0:T(8,128)(2,1)S(1)} %get-tuple-element.79), channel_id=1, source_target_pairs={{0,24},{8,0},{16,8},{24,16},{1,25},{9,1},{17,9},{25,17},{2,26},{10... | collective-permute-start | bytes 1572872 | tf_op jit(solution)/shard_map/ppermute | solution.py:388
  45.7 2.9 %shard_map.114 = (bf16[512,1024]{1,0:T(8,128)(2,1)S(1)}, bf16[256,1024]{1,0:T(8,128)(2,1)S(1)}, bf16[256,1024]{1,0:T(8,128)(2,1)S(1)}, f32[8,128]{1,0:T(8,128)S(1)}) custom-call(s32[53]{0:T(128)S(1)} %concatenate.3.table_ref, bf16[1024,1024]{1,0:T(8,128)(2,1)S(1)} %get-tuple-element.67.grads_ref.rows_ref, bf16[1024,1024]{1,0:T(8,128)(2,1)S(1)} %get-tuple-element.68.rows_ref, ...), custom_call_target="tpu_custom_call" | custom-call | bytes 6291456 | tf_op jit(solution)/shard_map/pallas_call | solution.py:289
  48.7 3.1 %collective-permute-start.16 = (bf16[256,1024]{1,0:T(8,128)(2,1)S(1)}, bf16[256,1024]{1,0:T(8,128)(2,1)S(1)}, u32[]{:S(2)}, u32[]{:S(2)}) collective-permute-start(bf16[256,1024]{1,0:T(8,128)(2,1)S(1)} %get-tuple-element.82), channel_id=1, source_target_pairs={{0,96},{32,0},{64,32},{96,64},{1,97},{33,1},{65,33},{97,65},{2,98}... | collective-permute-start | bytes 1572872 | tf_op jit(solution)/shard_map/ppermute | solution.py:388
  51.8 3.4 %shard_map.115 = (bf16[1024,1024]{1,0:T(8,128)(2,1)S(1)}, bf16[512,1024]{1,0:T(8,128)(2,1)S(1)}, f32[8,128]{1,0:T(8,128)S(1)}) custom-call(bf16[2048,1024]{1,0:T(8,128)(2,1)S(1)} %get-tuple-element.63.act_ref, bf16[1024,1024]{1,0:T(8,128)(2,1)S(1)} %get-tuple-element.67.grads_ref.rows_ref, f32[8,128]{1,0:T(8,128)S(1)} %get-tuple-element.73.refs_0_), custom_call_target="tpu_custom_call" | custom-call | bytes 8388608 | tf_op jit(solution)/shard_map/pallas_call | solution.py:255
  55.2 5.8 %shard_map.116 = (bf16[1024,1024]{1,0:T(8,128)(2,1)S(1)}, bf16[1024,1024]{1,0:T(8,128)(2,1)S(1)}, f32[8,128]{1,0:T(8,128)S(1)}) custom-call(s32[53]{0:T(128)S(1)} %concatenate.3.table_ref, bf16[1024,1024]{1,0:T(8,128)(2,1)S(1)} %get-tuple-element.67.grads_ref.rows_ref, bf16[1024,1024]{1,0:T(8,128)(2,1)S(1)} %get-tuple-element.68.rows_ref, ...), custom_call_target="tpu_custom_call" | custom-call | bytes 10485760 | tf_op jit(solution)/shard_map/pallas_call | solution.py:289
  63.4 2.5 %collective-permute-start.19 = (bf16[512,1024]{1,0:T(8,128)(2,1)}, bf16[512,1024]{1,0:T(8,128)(2,1)}, u32[]{:S(2)}, u32[]{:S(2)}) collective-permute-start(bf16[512,1024]{1,0:T(8,128)(2,1)} %get-tuple-element.88), channel_id=1, source_target_pairs={{0,24},{8,0},{16,8},{24,16},{1,25},{9,1},{17,9},{25,17},{2,26},{10... | collective-permute-start | bytes 3145736 | tf_op jit(solution)/shard_map/ppermute | solution.py:392
  68.7 2.5 %collective-permute-start.21 = (bf16[512,1024]{1,0:T(8,128)(2,1)}, bf16[512,1024]{1,0:T(8,128)(2,1)}, u32[]{:S(2)}, u32[]{:S(2)}) collective-permute-start(bf16[512,1024]{1,0:T(8,128)(2,1)} %get-tuple-element.92), channel_id=1, source_target_pairs={{0,96},{32,0},{64,32},{96,64},{1,97},{33,1},{65,33},{97,65},{2,98}... | collective-permute-start | bytes 3145736 | tf_op jit(solution)/shard_map/ppermute | solution.py:392
  71.2 3.4 %shard_map.121 = (bf16[512,1024]{1,0:T(8,128)(2,1)S(1)}, bf16[512,1024]{1,0:T(8,128)(2,1)S(1)}, f32[8,128]{1,0:T(8,128)}) custom-call(s32[53]{0:T(128)S(1)} %concatenate.3.table_ref, bf16[1024,1024]{1,0:T(8,128)(2,1)S(1)} %get-tuple-element.67.grads_ref.rows_ref, bf16[1024,1024]{1,0:T(8,128)(2,1)S(1)} %get-tuple-element.68.rows_ref, ...), custom_call_target="tpu_custom_call" | custom-call | bytes 6291456 | tf_op jit(solution)/shard_map/pallas_call | solution.py:289
  74.6 7.5 %shard_map.122 = bf16[1024,1024]{1,0:T(8,128)(2,1)} custom-call(s32[53]{0:T(128)S(1)} %concatenate.3.table_ref, bf16[512,1024]{1,0:T(8,128)(2,1)S(1)} %get-tuple-element.72.a_ref, bf16[1024,1024]{1,0:T(8,128)(2,1)S(1)} %get-tuple-element.75.b_ref, bf16[512,1024]{1,0:T(8,128)(2,1)S(1)} %get-tuple-element.85.c_ref, ...), custom_call_target="tpu_custom_call" | custom-call | bytes 12582912 | tf_op jit(solution)/shard_map/pallas_call | solution.py:327
  82.1 4.8 %all-to-all-start = ((bf16[2,512,1024]{2,1,0:T(8,128)(2,1)}), bf16[2,512,1024]{2,1,0:T(8,128)(2,1)}, u32[]{:S(2)}, u32[]{:S(2)}) async-start(bf16[2,512,1024]{2,1,0:T(8,128)(2,1)} %bitcast.6), calls=%async_computation | async-start | bytes 4194304 | tf_op jit(solution)/shard_map/all_to_all | solution.py:433
  90.7 3.0 %collective-permute-start.22 = (bf16[64,1024]{1,0:T(8,128)(2,1)}, bf16[64,1024]{1,0:T(8,128)(2,1)S(1)}, u32[]{:S(2)}, u32[]{:S(2)}) collective-permute-start(bf16[64,1024]{1,0:T(8,128)(2,1)} %get-tuple-element.95), channel_id=1, source_target_pairs={{0,96},{32,0},{64,32},{96,64},{1,97},{33,1},{65,33},{97,65},{2,98}... | collective-permute-start | bytes 393224 | tf_op jit(solution)/shard_map/ppermute | solution.py:388
  93.7 2.3 %shard_map.127 = (bf16[128,1024]{1,0:T(8,128)(2,1)S(1)}, bf16[256,1024]{1,0:T(8,128)(2,1)S(1)}, bf16[64,1024]{1,0:T(8,128)(2,1)}, bf16[64,1024]{1,0:T(8,128)(2,1)}, f32[8,128]{1,0:T(8,128)}) custom-call(bf16[512,1024]{1,0:T(8,128)(2,1)S(1)} %shard_map.126.own_ref, bf16[512,1024]{1,0:T(8,128)(2,1)} %collective-permute-done.20.left, ...), custom_call_target="tpu_custom_call" | custom-call | bytes 4194304 | tf_op jit(solution)/shard_map/pallas_call | solution.py:418
  96.0 3.1 %collective-permute-start.24 = (bf16[64,1024]{1,0:T(8,128)(2,1)}, bf16[64,1024]{1,0:T(8,128)(2,1)S(1)}, u32[]{:S(2)}, u32[]{:S(2)}) collective-permute-start(bf16[64,1024]{1,0:T(8,128)(2,1)} %get-tuple-element.98), channel_id=1, source_target_pairs={{0,24},{8,0},{16,8},{24,16},{1,25},{9,1},{17,9},{25,17},{2,26},{10... | collective-permute-start | bytes 393224 | tf_op jit(solution)/shard_map/ppermute | solution.py:388
  99.0 2.9 %fusion.refs_0_ = bf16[512,1024]{1,0:T(8,128)(2,1)} fusion(bf16[2,512,1024]{2,1,0:T(8,128)(2,1)} %all-to-all-done), kind=kLoop, calls=%fused_computation.1 | loop fusion | flops 2097152 | bytes 3145728 | tf_op jit(solution)/shard_map/convert_element_type | solution.py:435
  101.9 3.6 %all-to-all-start.1 = ((bf16[4,128,1024]{2,1,0:T(8,128)(2,1)}), bf16[4,128,1024]{2,1,0:T(8,128)(2,1)S(1)}, u32[]{:S(2)}, u32[]{:S(2)}) async-start(bf16[4,128,1024]{2,1,0:T(8,128)(2,1)} %bitcast.8), calls=%async_computation.1 | async-start | bytes 2097152 | tf_op jit(solution)/shard_map/all_to_all | solution.py:483
  106.5 3.0 %collective-permute-start.27 = (bf16[128,1024]{1,0:T(8,128)(2,1)S(1)}, bf16[128,1024]{1,0:T(8,128)(2,1)S(1)}, u32[]{:S(2)}, u32[]{:S(2)}) collective-permute-start(bf16[128,1024]{1,0:T(8,128)(2,1)S(1)} %get-tuple-element.101), channel_id=1, source_target_pairs={{0,24},{8,0},{16,8},{24,16},{1,25},{9,1},{17,9},{25,17},{2,26},{10... | collective-permute-start | bytes 786440 | tf_op jit(solution)/shard_map/ppermute | solution.py:392
  110.5 2.3 %collective-permute-start.29 = (bf16[128,1024]{1,0:T(8,128)(2,1)S(1)}, bf16[128,1024]{1,0:T(8,128)(2,1)S(1)}, u32[]{:S(2)}, u32[]{:S(2)}) collective-permute-start(bf16[128,1024]{1,0:T(8,128)(2,1)S(1)} %get-tuple-element.104), channel_id=1, source_target_pairs={{0,96},{32,0},{64,32},{96,64},{1,97},{33,1},{65,33},{97,65},{2,98}... | collective-permute-start | bytes 786440 | tf_op jit(solution)/shard_map/ppermute | solution.py:392
  114.8 2.3 %collective-permute-done.28 = bf16[128,1024]{1,0:T(8,128)(2,1)S(1)} collective-permute-done((bf16[128,1024]{1,0:T(8,128)(2,1)S(1)}, bf16[128,1024]{1,0:T(8,128)(2,1)S(1)}, u32[]{:S(2)}, u32[]{:S(2)}) %collective-permute-start.28) | collective-permute-done | bytes 262176 | tf_op jit(solution)/shard_map/ppermute | solution.py:392
  (89 shorter events, 32.1 us)
Async XLA Ops:
  2.7 15.6 %collective-permute-start = (bf16[128,1024]{1,0:T(8,128)(2,1)}, bf16[128,1024]{1,0:T(8,128)(2,1)S(1)}, u32[]{:S(2)}, u32[]{:S(2)}) collective-permute-start(bf16[128,1024]{1,0:T(8,128)(2,1)} %get-tuple-element.58), channel_id=1, source_target_pairs={{0,1},{1,2},{2,3},{3,0},{4,5},{5,6},{6,7},{7,4},{8,9},{9,10},{10,1... | collective-permute-start | bytes 786440 | tf_op jit(solution)/shard_map/ppermute | solution.py:456
  4.8 16.6 %collective-permute-start.1 = (bf16[128,1024]{1,0:T(8,128)(2,1)S(1)}, bf16[128,1024]{1,0:T(8,128)(2,1)S(1)}, u32[]{:S(2)}, u32[]{:S(2)}) collective-permute-start(bf16[128,1024]{1,0:T(8,128)(2,1)S(1)} %get-tuple-element.59), channel_id=1, source_target_pairs={{0,2},{1,3},{2,0},{3,1},{4,6},{5,7},{6,4},{7,5},{8,10},{9,11},{10,... | collective-permute-start | bytes 786440 | tf_op jit(solution)/shard_map/ppermute | solution.py:456
  8.4 12.3 %collective-permute-start.3 = (bf16[128,1024]{1,0:T(8,128)(2,1)S(1)}, bf16[128,1024]{1,0:T(8,128)(2,1)S(1)}, u32[]{:S(2)}, u32[]{:S(2)}) collective-permute-start(bf16[128,1024]{1,0:T(8,128)(2,1)S(1)} %get-tuple-element.61), channel_id=1, source_target_pairs={{0,3},{1,0},{2,1},{3,2},{4,7},{5,4},{6,5},{7,6},{8,11},{9,8},{10,9... | collective-permute-start | bytes 786440 | tf_op jit(solution)/shard_map/ppermute | solution.py:456
  11.7 14.1 %collective-permute-start.2 = (bf16[128,1024]{1,0:T(8,128)(2,1)S(1)}, bf16[128,1024]{1,0:T(8,128)(2,1)S(1)}, u32[]{:S(2)}, u32[]{:S(2)}) collective-permute-start(bf16[128,1024]{1,0:T(8,128)(2,1)S(1)} %get-tuple-element.60), channel_id=1, source_target_pairs={{0,2},{1,3},{2,0},{3,1},{4,6},{5,7},{6,4},{7,5},{8,10},{9,11},{10,... | collective-permute-start | bytes 786440 | tf_op jit(solution)/shard_map/ppermute | solution.py:456
  18.3 9.0 %collective-permute-start.4 = (bf16[128,1024]{1,0:T(8,128)(2,1)S(1)}, bf16[128,1024]{1,0:T(8,128)(2,1)S(1)}, u32[]{:S(2)}, u32[]{:S(2)}) collective-permute-start(bf16[128,1024]{1,0:T(8,128)(2,1)S(1)} %shard_map.106.refs_0_), channel_id=1, source_target_pairs={{0,4},{4,0},{1,5},{5,1},{2,6},{6,2},{3,7},{7,3},{8,12},{12,8},{9,1... | collective-permute-start | bytes 786440 | tf_op jit(solution)/shard_map/ppermute | solution.py:22
  18.4 10.7 %collective-permute-start.5 = (bf16[128,1024]{1,0:T(8,128)(2,1)S(1)}, bf16[128,1024]{1,0:T(8,128)(2,1)S(1)}, u32[]{:S(2)}, u32[]{:S(2)}) collective-permute-start(bf16[128,1024]{1,0:T(8,128)(2,1)S(1)} %collective-permute-done.refs_1_), channel_id=1, source_target_pairs={{0,4},{4,0},{1,5},{5,1},{2,6},{6,2},{3,7},{7,3},{8,12},{12,8},{9,1... | collective-permute-start | bytes 786440 | tf_op jit(solution)/shard_map/ppermute | solution.py:22
  20.7 8.4 %collective-permute-start.7 = (bf16[128,1024]{1,0:T(8,128)(2,1)S(1)}, bf16[128,1024]{1,0:T(8,128)(2,1)S(1)}, u32[]{:S(2)}, u32[]{:S(2)}) collective-permute-start(bf16[128,1024]{1,0:T(8,128)(2,1)S(1)} %collective-permute-done.3.refs_3_), channel_id=1, source_target_pairs={{0,4},{4,0},{1,5},{5,1},{2,6},{6,2},{3,7},{7,3},{8,12},{12,8},{9,1... | collective-permute-start | bytes 786440 | tf_op jit(solution)/shard_map/ppermute | solution.py:22
  25.9 12.4 %collective-permute-start.8 = (bf16[128,1024]{1,0:T(8,128)(2,1)S(1)}, bf16[128,1024]{1,0:T(8,128)(2,1)S(1)}, u32[]{:S(2)}, u32[]{:S(2)}) collective-permute-start(bf16[128,1024]{1,0:T(8,128)(2,1)S(1)} %get-tuple-element.65), channel_id=1, source_target_pairs={{0,1},{1,2},{2,3},{3,0},{4,5},{5,6},{6,7},{7,4},{8,9},{9,10},{10,1... | collective-permute-start | bytes 786440 | tf_op jit(solution)/shard_map/ppermute | solution.py:456
  27.3 11.6 %collective-permute-start.9 = (bf16[128,1024]{1,0:T(8,128)(2,1)S(1)}, bf16[128,1024]{1,0:T(8,128)(2,1)S(1)}, u32[]{:S(2)}, u32[]{:S(2)}) collective-permute-start(bf16[128,1024]{1,0:T(8,128)(2,1)S(1)} %get-tuple-element.66), channel_id=1, source_target_pairs={{0,3},{1,0},{2,1},{3,2},{4,7},{5,4},{6,5},{7,6},{8,11},{9,8},{10,9... | collective-permute-start | bytes 786440 | tf_op jit(solution)/shard_map/ppermute | solution.py:456
  42.9 18.1 %collective-permute-start.14 = (bf16[256,1024]{1,0:T(8,128)(2,1)S(1)}, bf16[256,1024]{1,0:T(8,128)(2,1)S(1)}, u32[]{:S(2)}, u32[]{:S(2)}) collective-permute-start(bf16[256,1024]{1,0:T(8,128)(2,1)S(1)} %get-tuple-element.79), channel_id=1, source_target_pairs={{0,24},{8,0},{16,8},{24,16},{1,25},{9,1},{17,9},{25,17},{2,26},{10... | collective-permute-start | bytes 1572872 | tf_op jit(solution)/shard_map/ppermute | solution.py:388
  45.7 15.3 %collective-permute-start.15 = (bf16[256,1024]{1,0:T(8,128)(2,1)S(1)}, bf16[256,1024]{1,0:T(8,128)(2,1)S(1)}, u32[]{:S(2)}, u32[]{:S(2)}) collective-permute-start(bf16[256,1024]{1,0:T(8,128)(2,1)S(1)} %get-tuple-element.80), channel_id=1, source_target_pairs={{0,8},{8,16},{16,24},{24,0},{1,9},{9,17},{17,25},{25,1},{2,10},{10... | collective-permute-start | bytes 1572872 | tf_op jit(solution)/shard_map/ppermute | solution.py:388
  48.7 17.2 %collective-permute-start.16 = (bf16[256,1024]{1,0:T(8,128)(2,1)S(1)}, bf16[256,1024]{1,0:T(8,128)(2,1)S(1)}, u32[]{:S(2)}, u32[]{:S(2)}) collective-permute-start(bf16[256,1024]{1,0:T(8,128)(2,1)S(1)} %get-tuple-element.82), channel_id=1, source_target_pairs={{0,96},{32,0},{64,32},{96,64},{1,97},{33,1},{65,33},{97,65},{2,98}... | collective-permute-start | bytes 1572872 | tf_op jit(solution)/shard_map/ppermute | solution.py:388
  51.8 14.6 %collective-permute-start.17 = (bf16[256,1024]{1,0:T(8,128)(2,1)S(1)}, bf16[256,1024]{1,0:T(8,128)(2,1)S(1)}, u32[]{:S(2)}, u32[]{:S(2)}) collective-permute-start(bf16[256,1024]{1,0:T(8,128)(2,1)S(1)} %get-tuple-element.83), channel_id=1, source_target_pairs={{0,32},{32,64},{64,96},{96,0},{1,33},{33,65},{65,97},{97,1},{2,34}... | collective-permute-start | bytes 1572872 | tf_op jit(solution)/shard_map/ppermute | solution.py:388
  62.7 26.1 %collective-permute-start.18 = (bf16[512,1024]{1,0:T(8,128)(2,1)}, bf16[512,1024]{1,0:T(8,128)(2,1)S(1)}, u32[]{:S(2)}, u32[]{:S(2)}) collective-permute-start(bf16[512,1024]{1,0:T(8,128)(2,1)} %get-tuple-element.87), channel_id=1, source_target_pairs={{0,8},{8,16},{16,24},{24,0},{1,9},{9,17},{17,25},{25,1},{2,10},{10... | collective-permute-start | bytes 3145736 | tf_op jit(solution)/shard_map/ppermute | solution.py:392
  63.4 25.3 %collective-permute-start.19 = (bf16[512,1024]{1,0:T(8,128)(2,1)}, bf16[512,1024]{1,0:T(8,128)(2,1)}, u32[]{:S(2)}, u32[]{:S(2)}) collective-permute-start(bf16[512,1024]{1,0:T(8,128)(2,1)} %get-tuple-element.88), channel_id=1, source_target_pairs={{0,24},{8,0},{16,8},{24,16},{1,25},{9,1},{17,9},{25,17},{2,26},{10... | collective-permute-start | bytes 3145736 | tf_op jit(solution)/shard_map/ppermute | solution.py:392
  67.9 25.7 %collective-permute-start.20 = (bf16[512,1024]{1,0:T(8,128)(2,1)}, bf16[512,1024]{1,0:T(8,128)(2,1)}, u32[]{:S(2)}, u32[]{:S(2)}) collective-permute-start(bf16[512,1024]{1,0:T(8,128)(2,1)} %get-tuple-element.91), channel_id=1, source_target_pairs={{0,32},{32,64},{64,96},{96,0},{1,33},{33,65},{65,97},{97,1},{2,34}... | collective-permute-start | bytes 3145736 | tf_op jit(solution)/shard_map/ppermute | solution.py:392
  68.7 25.0 %collective-permute-start.21 = (bf16[512,1024]{1,0:T(8,128)(2,1)}, bf16[512,1024]{1,0:T(8,128)(2,1)}, u32[]{:S(2)}, u32[]{:S(2)}) collective-permute-start(bf16[512,1024]{1,0:T(8,128)(2,1)} %get-tuple-element.92), channel_id=1, source_target_pairs={{0,96},{32,0},{64,32},{96,64},{1,97},{33,1},{65,33},{97,65},{2,98}... | collective-permute-start | bytes 3145736 | tf_op jit(solution)/shard_map/ppermute | solution.py:392
  82.1 16.9 %all-to-all-start = ((bf16[2,512,1024]{2,1,0:T(8,128)(2,1)}), bf16[2,512,1024]{2,1,0:T(8,128)(2,1)}, u32[]{:S(2)}, u32[]{:S(2)}) async-start(bf16[2,512,1024]{2,1,0:T(8,128)(2,1)} %bitcast.6), calls=%async_computation | async-start | bytes 4194304 | tf_op jit(solution)/shard_map/all_to_all | solution.py:433
  90.7 14.9 %collective-permute-start.22 = (bf16[64,1024]{1,0:T(8,128)(2,1)}, bf16[64,1024]{1,0:T(8,128)(2,1)S(1)}, u32[]{:S(2)}, u32[]{:S(2)}) collective-permute-start(bf16[64,1024]{1,0:T(8,128)(2,1)} %get-tuple-element.95), channel_id=1, source_target_pairs={{0,96},{32,0},{64,32},{96,64},{1,97},{33,1},{65,33},{97,65},{2,98}... | collective-permute-start | bytes 393224 | tf_op jit(solution)/shard_map/ppermute | solution.py:388
  93.6 12.0 %collective-permute-start.23 = (bf16[64,1024]{1,0:T(8,128)(2,1)S(1)}, bf16[64,1024]{1,0:T(8,128)(2,1)S(1)}, u32[]{:S(2)}, u32[]{:S(2)}) collective-permute-start(bf16[64,1024]{1,0:T(8,128)(2,1)S(1)} %get-tuple-element.96), channel_id=1, source_target_pairs={{0,32},{32,64},{64,96},{96,0},{1,33},{33,65},{65,97},{97,1},{2,34}... | collective-permute-start | bytes 393224 | tf_op jit(solution)/shard_map/ppermute | solution.py:388
  96.0 9.7 %collective-permute-start.24 = (bf16[64,1024]{1,0:T(8,128)(2,1)}, bf16[64,1024]{1,0:T(8,128)(2,1)S(1)}, u32[]{:S(2)}, u32[]{:S(2)}) collective-permute-start(bf16[64,1024]{1,0:T(8,128)(2,1)} %get-tuple-element.98), channel_id=1, source_target_pairs={{0,24},{8,0},{16,8},{24,16},{1,25},{9,1},{17,9},{25,17},{2,26},{10... | collective-permute-start | bytes 393224 | tf_op jit(solution)/shard_map/ppermute | solution.py:388
  101.9 16.7 %all-to-all-start.1 = ((bf16[4,128,1024]{2,1,0:T(8,128)(2,1)}), bf16[4,128,1024]{2,1,0:T(8,128)(2,1)S(1)}, u32[]{:S(2)}, u32[]{:S(2)}) async-start(bf16[4,128,1024]{2,1,0:T(8,128)(2,1)} %bitcast.8), calls=%async_computation.1 | async-start | bytes 2097152 | tf_op jit(solution)/shard_map/all_to_all | solution.py:483
  106.3 7.6 %collective-permute-start.26 = (bf16[128,1024]{1,0:T(8,128)(2,1)S(1)}, bf16[128,1024]{1,0:T(8,128)(2,1)S(1)}, u32[]{:S(2)}, u32[]{:S(2)}) collective-permute-start(bf16[128,1024]{1,0:T(8,128)(2,1)S(1)} %get-tuple-element.100), channel_id=1, source_target_pairs={{0,8},{8,16},{16,24},{24,0},{1,9},{9,17},{17,25},{25,1},{2,10},{10... | collective-permute-start | bytes 786440 | tf_op jit(solution)/shard_map/ppermute | solution.py:392
  109.6 7.6 %collective-permute-start.28 = (bf16[128,1024]{1,0:T(8,128)(2,1)S(1)}, bf16[128,1024]{1,0:T(8,128)(2,1)S(1)}, u32[]{:S(2)}, u32[]{:S(2)}) collective-permute-start(bf16[128,1024]{1,0:T(8,128)(2,1)S(1)} %get-tuple-element.103), channel_id=1, source_target_pairs={{0,32},{32,64},{64,96},{96,0},{1,33},{33,65},{65,97},{97,1},{2,34}... | collective-permute-start | bytes 786440 | tf_op jit(solution)/shard_map/ppermute | solution.py:392
  (14 other events, 57.8 us)

commit v9 on v8

--- a/solution.py
+++ b/solution.py
@@ -458,7 +458,6 @@
     own_x = to_owner(send_x)
     own_d = to_owner(send_d)
     own_x[0] = after(own_x[0], mark, send_d[0])
-    own_x[2] = after(own_x[2], own_d[2])
     both_x = own_x + [swap_core(p) for p in own_x]
     act, slope, rows_x, mark = forward(table, both_x, weight_in)
     own_d = [after(part, mark) for part in own_d]

time: 120 us -> 117 us (0.975)
  waiting for transfers between devices: 14.9 us -> 10.8 us
    ppermute x6, waiting for transfers between devices: 7 us -> 3.39 us  [to_owner(): lax.ppermute(parts[r], 'expert', ring(r))]
  transfers between devices with their start and end apart: 32 -> 32, of which waited for: 12 -> 10; matrix products, arithmetic and copies ran while one was open for 5% -> 6% of each run, Pallas kernels for 38% -> 39%
where the time goes in v9:
time: 117 us; the launch traced here: 116 us
  Pallas kernels  49.8 us (43%)
  starting transfers between devices  46.6 us (40%)
  waiting for transfers between devices  10.8 us (9%)
  other arithmetic  5.52 us (5%)
  local copies, waits for them, and re-layouts  2.64 us (2%)
    ppermute x8, starting transfers between devices, second_hop(): return (lax.ppermute(up, axis, ring(1)), lax.ppermute(down, axis, ring(3)))  12.9 us
    pallas_call x3, Pallas kernels, backward(): pl.pallas_call(body, grid=(count,), in_specs=[SMEM] + [VMEM] * 4 + [ANY]...  12.2 us
    ppermute x8, starting transfers between devices, first_hop(): return (lax.ppermute(low, axis, ring(3)), lax.ppermute(high, axis, ring(1)))  11.9 us
    ppermute x6, starting transfers between devices, to_owner(): lax.ppermute(parts[r], 'expert', ring(r))  11 us
    pallas_call x1, Pallas kernels, forward(): pl.pallas_call(body, grid=(4,), in_specs=[SMEM] + [VMEM] * (len(parts) +...  9.07 us
    pallas_call x1, Pallas kernels, row_gradients(): pl.pallas_call(body, grid=(4,), in_specs=[SMEM] + [VMEM] * 4, out_specs=V...  7.53 us
    ppermute x8, waiting for transfers between devices, second_hop(): return (lax.ppermute(up, axis, ring(1)), lax.ppermute(down, axis, ring(3)))  5.18 us
    all_to_all x1, starting transfers between devices, sum_cores(): lax.all_to_all(terms, 'core', split_axis=0, concat_axis=0, tiled=True)  4.84 us
  transfers between devices with their start and end apart: 32, of which 10 were waited for; matrix products, arithmetic and copies ran while one was open for 6% of the time, Pallas kernels for 39%

profile of v9, /device:TPU:0, one launch (start us, length us, event | category | flops | bytes accessed | tf_op | source)
XLA Modules:
  0.0 116.3 jit_solution(3043470818929898923)
XLA Ops:
  2.2 2.1 %collective-permute-start = (bf16[128,1024]{1,0:T(8,128)(2,1)S(1)}, bf16[128,1024]{1,0:T(8,128)(2,1)S(1)}, u32[]{:S(2)}, u32[]{:S(2)}) collective-permute-start(bf16[128,1024]{1,0:T(8,128)(2,1)S(1)} %get-tuple-element.58), channel_id=1, source_target_pairs={{0,1},{1,2},{2,3},{3,0},{4,5},{5,6},{6,7},{7,4},{8,9},{9,10},{10,1... | collective-permute-start | bytes 786440 | tf_op jit(solution)/shard_map/ppermute | solution.py:456
  4.3 3.6 %collective-permute-start.1 = (bf16[128,1024]{1,0:T(8,128)(2,1)S(1)}, bf16[128,1024]{1,0:T(8,128)(2,1)S(1)}, u32[]{:S(2)}, u32[]{:S(2)}) collective-permute-start(bf16[128,1024]{1,0:T(8,128)(2,1)S(1)} %get-tuple-element.59), channel_id=1, source_target_pairs={{0,2},{1,3},{2,0},{3,1},{4,6},{5,7},{6,4},{7,5},{8,10},{9,11},{10,... | collective-permute-start | bytes 786440 | tf_op jit(solution)/shard_map/ppermute | solution.py:456
  12.9 4.2 %shard_map.104 = (bf16[2048,1024]{1,0:T(8,128)(2,1)S(1)}, bf16[2048,1024]{1,0:T(8,128)(2,1)S(1)}, f32[8,128]{1,0:T(8,128)S(1)}) custom-call(s32[53]{0:T(128)S(1)} %concatenate.3.table_ref, bf16[4096,1024]{1,0:T(8,128)(2,1)} %bitcast.17, bf16[4096,1024]{1,0:T(8,128)(2,1)} %bitcast.18), custom_call_target="tpu_custom_call" | custom-call | bytes 16777216 | tf_op jit(solution)/shard_map/pallas_call | solution.py:153
  20.7 2.4 %collective-permute-start.8 = (bf16[128,1024]{1,0:T(8,128)(2,1)S(1)}, bf16[128,1024]{1,0:T(8,128)(2,1)S(1)}, u32[]{:S(2)}, u32[]{:S(2)}) collective-permute-start(bf16[128,1024]{1,0:T(8,128)(2,1)S(1)} %get-tuple-element.65), channel_id=1, source_target_pairs={{0,2},{1,3},{2,0},{3,1},{4,6},{5,7},{6,4},{7,5},{8,10},{9,11},{10,... | collective-permute-start | bytes 786440 | tf_op jit(solution)/shard_map/ppermute | solution.py:456
  24.4 9.1 %shard_map.107 = (bf16[2048,1024]{1,0:T(8,128)(2,1)S(1)}, bf16[2048,1024]{1,0:T(8,128)(2,1)S(1)}, bf16[1024,1024]{1,0:T(8,128)(2,1)S(1)}, f32[8,128]{1,0:T(8,128)S(1)}) custom-call(s32[53]{0:T(128)S(1)} %concatenate.3.table_ref, bf16[128,1024]{1,0:T(8,128)(2,1)S(1)} %shard_map.106.refs_0_, bf16[128,1024]{1,0:T(8,128)(2,1)S(1)} %collective-permute-done.refs_1_, ...), custom_call_target="tpu_custom_call" | custom-call | bytes 16777216 | tf_op jit(solution)/shard_map/pallas_call | solution.py:213
  37.3 1.9 %shard_map.112 = (bf16[256,1024]{1,0:T(8,128)(2,1)S(1)}, bf16[256,1024]{1,0:T(8,128)(2,1)S(1)}, bf16[1024,1024]{1,0:T(8,128)(2,1)S(1)}, f32[8,128]{1,0:T(8,128)S(1)}) custom-call(s32[53]{0:T(128)S(1)} %concatenate.3.table_ref, bf16[2048,1024]{1,0:T(8,128)(2,1)S(1)} %get-tuple-element.62.act_ref, bf16[128,1024]{1,0:T(8,128)(2,1)S(1)} %shard_map.108.refs_0_, ...), custom_call_target="tpu_custom_call" | custom-call | bytes 4194304 | tf_op jit(solution)/shard_map/pallas_call | solution.py:235
  39.3 2.8 %collective-permute-start.14 = (bf16[256,1024]{1,0:T(8,128)(2,1)S(1)}, bf16[256,1024]{1,0:T(8,128)(2,1)S(1)}, u32[]{:S(2)}, u32[]{:S(2)}) collective-permute-start(bf16[256,1024]{1,0:T(8,128)(2,1)S(1)} %get-tuple-element.79), channel_id=1, source_target_pairs={{0,24},{8,0},{16,8},{24,16},{1,25},{9,1},{17,9},{25,17},{2,26},{10... | collective-permute-start | bytes 1572872 | tf_op jit(solution)/shard_map/ppermute | solution.py:388
  42.1 2.9 %shard_map.113 = (bf16[512,1024]{1,0:T(8,128)(2,1)S(1)}, bf16[256,1024]{1,0:T(8,128)(2,1)S(1)}, bf16[256,1024]{1,0:T(8,128)(2,1)S(1)}, f32[8,128]{1,0:T(8,128)S(1)}) custom-call(s32[53]{0:T(128)S(1)} %concatenate.3.table_ref, bf16[1024,1024]{1,0:T(8,128)(2,1)S(1)} %get-tuple-element.67.grads_ref.rows_ref, bf16[1024,1024]{1,0:T(8,128)(2,1)S(1)} %get-tuple-element.68.rows_ref, ...), custom_call_target="tpu_custom_call" | custom-call | bytes 6291456 | tf_op jit(solution)/shard_map/pallas_call | solution.py:289
  45.0 3.1 %collective-permute-start.16 = (bf16[256,1024]{1,0:T(8,128)(2,1)S(1)}, bf16[256,1024]{1,0:T(8,128)(2,1)S(1)}, u32[]{:S(2)}, u32[]{:S(2)}) collective-permute-start(bf16[256,1024]{1,0:T(8,128)(2,1)S(1)} %get-tuple-element.82), channel_id=1, source_target_pairs={{0,96},{32,0},{64,32},{96,64},{1,97},{33,1},{65,33},{97,65},{2,98}... | collective-permute-start | bytes 1572872 | tf_op jit(solution)/shard_map/ppermute | solution.py:388
  48.1 3.4 %shard_map.114 = (bf16[1024,1024]{1,0:T(8,128)(2,1)S(1)}, bf16[512,1024]{1,0:T(8,128)(2,1)S(1)}, f32[8,128]{1,0:T(8,128)S(1)}) custom-call(bf16[2048,1024]{1,0:T(8,128)(2,1)S(1)} %get-tuple-element.62.act_ref, bf16[1024,1024]{1,0:T(8,128)(2,1)S(1)} %get-tuple-element.67.grads_ref.rows_ref, f32[8,128]{1,0:T(8,128)S(1)} %get-tuple-element.73.refs_0_), custom_call_target="tpu_custom_call" | custom-call | bytes 8388608 | tf_op jit(solution)/shard_map/pallas_call | solution.py:255
  51.6 5.8 %shard_map.115 = (bf16[1024,1024]{1,0:T(8,128)(2,1)S(1)}, bf16[1024,1024]{1,0:T(8,128)(2,1)S(1)}, f32[8,128]{1,0:T(8,128)S(1)}) custom-call(s32[53]{0:T(128)S(1)} %concatenate.3.table_ref, bf16[1024,1024]{1,0:T(8,128)(2,1)S(1)} %get-tuple-element.67.grads_ref.rows_ref, bf16[1024,1024]{1,0:T(8,128)(2,1)S(1)} %get-tuple-element.68.rows_ref, ...), custom_call_target="tpu_custom_call" | custom-call | bytes 10485760 | tf_op jit(solution)/shard_map/pallas_call | solution.py:289
  59.8 2.5 %collective-permute-start.19 = (bf16[512,1024]{1,0:T(8,128)(2,1)}, bf16[512,1024]{1,0:T(8,128)(2,1)}, u32[]{:S(2)}, u32[]{:S(2)}) collective-permute-start(bf16[512,1024]{1,0:T(8,128)(2,1)} %get-tuple-element.88), channel_id=1, source_target_pairs={{0,24},{8,0},{16,8},{24,16},{1,25},{9,1},{17,9},{25,17},{2,26},{10... | collective-permute-start | bytes 3145736 | tf_op jit(solution)/shard_map/ppermute | solution.py:392
  65.0 2.5 %collective-permute-start.21 = (bf16[512,1024]{1,0:T(8,128)(2,1)}, bf16[512,1024]{1,0:T(8,128)(2,1)}, u32[]{:S(2)}, u32[]{:S(2)}) collective-permute-start(bf16[512,1024]{1,0:T(8,128)(2,1)} %get-tuple-element.92), channel_id=1, source_target_pairs={{0,96},{32,0},{64,32},{96,64},{1,97},{33,1},{65,33},{97,65},{2,98}... | collective-permute-start | bytes 3145736 | tf_op jit(solution)/shard_map/ppermute | solution.py:392
  67.6 3.4 %shard_map.120 = (bf16[512,1024]{1,0:T(8,128)(2,1)S(1)}, bf16[512,1024]{1,0:T(8,128)(2,1)S(1)}, f32[8,128]{1,0:T(8,128)}) custom-call(s32[53]{0:T(128)S(1)} %concatenate.3.table_ref, bf16[1024,1024]{1,0:T(8,128)(2,1)S(1)} %get-tuple-element.67.grads_ref.rows_ref, bf16[1024,1024]{1,0:T(8,128)(2,1)S(1)} %get-tuple-element.68.rows_ref, ...), custom_call_target="tpu_custom_call" | custom-call | bytes 6291456 | tf_op jit(solution)/shard_map/pallas_call | solution.py:289
  71.0 7.5 %shard_map.121 = bf16[1024,1024]{1,0:T(8,128)(2,1)} custom-call(s32[53]{0:T(128)S(1)} %concatenate.3.table_ref, bf16[512,1024]{1,0:T(8,128)(2,1)S(1)} %get-tuple-element.72.a_ref, bf16[1024,1024]{1,0:T(8,128)(2,1)S(1)} %get-tuple-element.75.b_ref, bf16[512,1024]{1,0:T(8,128)(2,1)S(1)} %get-tuple-element.85.c_ref, ...), custom_call_target="tpu_custom_call" | custom-call | bytes 12582912 | tf_op jit(solution)/shard_map/pallas_call | solution.py:327
  78.5 4.8 %all-to-all-start = ((bf16[2,512,1024]{2,1,0:T(8,128)(2,1)}), bf16[2,512,1024]{2,1,0:T(8,128)(2,1)}, u32[]{:S(2)}, u32[]{:S(2)}) async-start(bf16[2,512,1024]{2,1,0:T(8,128)(2,1)} %bitcast.6), calls=%async_computation | async-start | bytes 4194304 | tf_op jit(solution)/shard_map/all_to_all | solution.py:433
  87.0 3.0 %collective-permute-start.22 = (bf16[64,1024]{1,0:T(8,128)(2,1)}, bf16[64,1024]{1,0:T(8,128)(2,1)S(1)}, u32[]{:S(2)}, u32[]{:S(2)}) collective-permute-start(bf16[64,1024]{1,0:T(8,128)(2,1)} %get-tuple-element.95), channel_id=1, source_target_pairs={{0,96},{32,0},{64,32},{96,64},{1,97},{33,1},{65,33},{97,65},{2,98}... | collective-permute-start | bytes 393224 | tf_op jit(solution)/shard_map/ppermute | solution.py:388
  90.0 2.3 %shard_map.126 = (bf16[128,1024]{1,0:T(8,128)(2,1)S(1)}, bf16[256,1024]{1,0:T(8,128)(2,1)S(1)}, bf16[64,1024]{1,0:T(8,128)(2,1)}, bf16[64,1024]{1,0:T(8,128)(2,1)}, f32[8,128]{1,0:T(8,128)}) custom-call(bf16[512,1024]{1,0:T(8,128)(2,1)S(1)} %shard_map.125.own_ref, bf16[512,1024]{1,0:T(8,128)(2,1)} %collective-permute-done.20.left, ...), custom_call_target="tpu_custom_call" | custom-call | bytes 4194304 | tf_op jit(solution)/shard_map/pallas_call | solution.py:418
  92.3 3.1 %collective-permute-start.24 = (bf16[64,1024]{1,0:T(8,128)(2,1)}, bf16[64,1024]{1,0:T(8,128)(2,1)S(1)}, u32[]{:S(2)}, u32[]{:S(2)}) collective-permute-start(bf16[64,1024]{1,0:T(8,128)(2,1)} %get-tuple-element.98), channel_id=1, source_target_pairs={{0,24},{8,0},{16,8},{24,16},{1,25},{9,1},{17,9},{25,17},{2,26},{10... | collective-permute-start | bytes 393224 | tf_op jit(solution)/shard_map/ppermute | solution.py:388
  95.4 2.9 %fusion.refs_0_ = bf16[512,1024]{1,0:T(8,128)(2,1)} fusion(bf16[2,512,1024]{2,1,0:T(8,128)(2,1)} %all-to-all-done), kind=kLoop, calls=%fused_computation.1 | loop fusion | flops 2097152 | bytes 3145728 | tf_op jit(solution)/shard_map/convert_element_type | solution.py:435
  98.3 3.9 %all-to-all-start.1 = ((bf16[4,128,1024]{2,1,0:T(8,128)(2,1)}), bf16[4,128,1024]{2,1,0:T(8,128)(2,1)S(1)}, u32[]{:S(2)}, u32[]{:S(2)}) async-start(bf16[4,128,1024]{2,1,0:T(8,128)(2,1)} %bitcast.8), calls=%async_computation.1 | async-start | bytes 2097152 | tf_op jit(solution)/shard_map/all_to_all | solution.py:482
  103.1 3.0 %collective-permute-start.27 = (bf16[128,1024]{1,0:T(8,128)(2,1)S(1)}, bf16[128,1024]{1,0:T(8,128)(2,1)S(1)}, u32[]{:S(2)}, u32[]{:S(2)}) collective-permute-start(bf16[128,1024]{1,0:T(8,128)(2,1)S(1)} %get-tuple-element.101), channel_id=1, source_target_pairs={{0,24},{8,0},{16,8},{24,16},{1,25},{9,1},{17,9},{25,17},{2,26},{10... | collective-permute-start | bytes 786440 | tf_op jit(solution)/shard_map/ppermute | solution.py:392
  107.1 2.3 %collective-permute-start.29 = (bf16[128,1024]{1,0:T(8,128)(2,1)S(1)}, bf16[128,1024]{1,0:T(8,128)(2,1)S(1)}, u32[]{:S(2)}, u32[]{:S(2)}) collective-permute-start(bf16[128,1024]{1,0:T(8,128)(2,1)S(1)} %get-tuple-element.104), channel_id=1, source_target_pairs={{0,96},{32,0},{64,32},{96,64},{1,97},{33,1},{65,33},{97,65},{2,98}... | collective-permute-start | bytes 786440 | tf_op jit(solution)/shard_map/ppermute | solution.py:392
  111.4 2.3 %collective-permute-done.28 = bf16[128,1024]{1,0:T(8,128)(2,1)S(1)} collective-permute-done((bf16[128,1024]{1,0:T(8,128)(2,1)S(1)}, bf16[128,1024]{1,0:T(8,128)(2,1)S(1)}, u32[]{:S(2)}, u32[]{:S(2)}) %collective-permute-start.28) | collective-permute-done | bytes 262176 | tf_op jit(solution)/shard_map/ppermute | solution.py:392
  (88 shorter events, 30.5 us)
Async XLA Ops:
  2.2 15.0 %collective-permute-start = (bf16[128,1024]{1,0:T(8,128)(2,1)S(1)}, bf16[128,1024]{1,0:T(8,128)(2,1)S(1)}, u32[]{:S(2)}, u32[]{:S(2)}) collective-permute-start(bf16[128,1024]{1,0:T(8,128)(2,1)S(1)} %get-tuple-element.58), channel_id=1, source_target_pairs={{0,1},{1,2},{2,3},{3,0},{4,5},{5,6},{6,7},{7,4},{8,9},{9,10},{10,1... | collective-permute-start | bytes 786440 | tf_op jit(solution)/shard_map/ppermute | solution.py:456
  4.3 15.2 %collective-permute-start.1 = (bf16[128,1024]{1,0:T(8,128)(2,1)S(1)}, bf16[128,1024]{1,0:T(8,128)(2,1)S(1)}, u32[]{:S(2)}, u32[]{:S(2)}) collective-permute-start(bf16[128,1024]{1,0:T(8,128)(2,1)S(1)} %get-tuple-element.59), channel_id=1, source_target_pairs={{0,2},{1,3},{2,0},{3,1},{4,6},{5,7},{6,4},{7,5},{8,10},{9,11},{10,... | collective-permute-start | bytes 786440 | tf_op jit(solution)/shard_map/ppermute | solution.py:456
  7.8 11.6 %collective-permute-start.2 = (bf16[128,1024]{1,0:T(8,128)(2,1)S(1)}, bf16[128,1024]{1,0:T(8,128)(2,1)S(1)}, u32[]{:S(2)}, u32[]{:S(2)}) collective-permute-start(bf16[128,1024]{1,0:T(8,128)(2,1)S(1)} %get-tuple-element.60), channel_id=1, source_target_pairs={{0,3},{1,0},{2,1},{3,2},{4,7},{5,4},{6,5},{7,6},{8,11},{9,8},{10,9... | collective-permute-start | bytes 786440 | tf_op jit(solution)/shard_map/ppermute | solution.py:456
  20.0 13.6 %collective-permute-start.7 = (bf16[128,1024]{1,0:T(8,128)(2,1)S(1)}, bf16[128,1024]{1,0:T(8,128)(2,1)S(1)}, u32[]{:S(2)}, u32[]{:S(2)}) collective-permute-start(bf16[128,1024]{1,0:T(8,128)(2,1)S(1)} %get-tuple-element.64), channel_id=1, source_target_pairs={{0,1},{1,2},{2,3},{3,0},{4,5},{5,6},{6,7},{7,4},{8,9},{9,10},{10,1... | collective-permute-start | bytes 786440 | tf_op jit(solution)/shard_map/ppermute | solution.py:456
  20.7 14.7 %collective-permute-start.8 = (bf16[128,1024]{1,0:T(8,128)(2,1)S(1)}, bf16[128,1024]{1,0:T(8,128)(2,1)S(1)}, u32[]{:S(2)}, u32[]{:S(2)}) collective-permute-start(bf16[128,1024]{1,0:T(8,128)(2,1)S(1)} %get-tuple-element.65), channel_id=1, source_target_pairs={{0,2},{1,3},{2,0},{3,1},{4,6},{5,7},{6,4},{7,5},{8,10},{9,11},{10,... | collective-permute-start | bytes 786440 | tf_op jit(solution)/shard_map/ppermute | solution.py:456
  23.1 12.5 %collective-permute-start.9 = (bf16[128,1024]{1,0:T(8,128)(2,1)S(1)}, bf16[128,1024]{1,0:T(8,128)(2,1)S(1)}, u32[]{:S(2)}, u32[]{:S(2)}) collective-permute-start(bf16[128,1024]{1,0:T(8,128)(2,1)S(1)} %get-tuple-element.66), channel_id=1, source_target_pairs={{0,3},{1,0},{2,1},{3,2},{4,7},{5,4},{6,5},{7,6},{8,11},{9,8},{10,9... | collective-permute-start | bytes 786440 | tf_op jit(solution)/shard_map/ppermute | solution.py:456
  39.3 18.1 %collective-permute-start.14 = (bf16[256,1024]{1,0:T(8,128)(2,1)S(1)}, bf16[256,1024]{1,0:T(8,128)(2,1)S(1)}, u32[]{:S(2)}, u32[]{:S(2)}) collective-permute-start(bf16[256,1024]{1,0:T(8,128)(2,1)S(1)} %get-tuple-element.79), channel_id=1, source_target_pairs={{0,24},{8,0},{16,8},{24,16},{1,25},{9,1},{17,9},{25,17},{2,26},{10... | collective-permute-start | bytes 1572872 | tf_op jit(solution)/shard_map/ppermute | solution.py:388
  42.1 15.3 %collective-permute-start.15 = (bf16[256,1024]{1,0:T(8,128)(2,1)S(1)}, bf16[256,1024]{1,0:T(8,128)(2,1)S(1)}, u32[]{:S(2)}, u32[]{:S(2)}) collective-permute-start(bf16[256,1024]{1,0:T(8,128)(2,1)S(1)} %get-tuple-element.80), channel_id=1, source_target_pairs={{0,8},{8,16},{16,24},{24,0},{1,9},{9,17},{17,25},{25,1},{2,10},{10... | collective-permute-start | bytes 1572872 | tf_op jit(solution)/shard_map/ppermute | solution.py:388
  45.0 17.2 %collective-permute-start.16 = (bf16[256,1024]{1,0:T(8,128)(2,1)S(1)}, bf16[256,1024]{1,0:T(8,128)(2,1)S(1)}, u32[]{:S(2)}, u32[]{:S(2)}) collective-permute-start(bf16[256,1024]{1,0:T(8,128)(2,1)S(1)} %get-tuple-element.82), channel_id=1, source_target_pairs={{0,96},{32,0},{64,32},{96,64},{1,97},{33,1},{65,33},{97,65},{2,98}... | collective-permute-start | bytes 1572872 | tf_op jit(solution)/shard_map/ppermute | solution.py:388
  48.1 14.6 %collective-permute-start.17 = (bf16[256,1024]{1,0:T(8,128)(2,1)S(1)}, bf16[256,1024]{1,0:T(8,128)(2,1)S(1)}, u32[]{:S(2)}, u32[]{:S(2)}) collective-permute-start(bf16[256,1024]{1,0:T(8,128)(2,1)S(1)} %get-tuple-element.83), channel_id=1, source_target_pairs={{0,32},{32,64},{64,96},{96,0},{1,33},{33,65},{65,97},{97,1},{2,34}... | collective-permute-start | bytes 1572872 | tf_op jit(solution)/shard_map/ppermute | solution.py:388
  59.0 26.1 %collective-permute-start.18 = (bf16[512,1024]{1,0:T(8,128)(2,1)}, bf16[512,1024]{1,0:T(8,128)(2,1)S(1)}, u32[]{:S(2)}, u32[]{:S(2)}) collective-permute-start(bf16[512,1024]{1,0:T(8,128)(2,1)} %get-tuple-element.87), channel_id=1, source_target_pairs={{0,8},{8,16},{16,24},{24,0},{1,9},{9,17},{17,25},{25,1},{2,10},{10... | collective-permute-start | bytes 3145736 | tf_op jit(solution)/shard_map/ppermute | solution.py:392
  59.8 25.3 %collective-permute-start.19 = (bf16[512,1024]{1,0:T(8,128)(2,1)}, bf16[512,1024]{1,0:T(8,128)(2,1)}, u32[]{:S(2)}, u32[]{:S(2)}) collective-permute-start(bf16[512,1024]{1,0:T(8,128)(2,1)} %get-tuple-element.88), channel_id=1, source_target_pairs={{0,24},{8,0},{16,8},{24,16},{1,25},{9,1},{17,9},{25,17},{2,26},{10... | collective-permute-start | bytes 3145736 | tf_op jit(solution)/shard_map/ppermute | solution.py:392
  64.3 25.7 %collective-permute-start.20 = (bf16[512,1024]{1,0:T(8,128)(2,1)}, bf16[512,1024]{1,0:T(8,128)(2,1)}, u32[]{:S(2)}, u32[]{:S(2)}) collective-permute-start(bf16[512,1024]{1,0:T(8,128)(2,1)} %get-tuple-element.91), channel_id=1, source_target_pairs={{0,32},{32,64},{64,96},{96,0},{1,33},{33,65},{65,97},{97,1},{2,34}... | collective-permute-start | bytes 3145736 | tf_op jit(solution)/shard_map/ppermute | solution.py:392
  65.0 25.0 %collective-permute-start.21 = (bf16[512,1024]{1,0:T(8,128)(2,1)}, bf16[512,1024]{1,0:T(8,128)(2,1)}, u32[]{:S(2)}, u32[]{:S(2)}) collective-permute-start(bf16[512,1024]{1,0:T(8,128)(2,1)} %get-tuple-element.92), channel_id=1, source_target_pairs={{0,96},{32,0},{64,32},{96,64},{1,97},{33,1},{65,33},{97,65},{2,98}... | collective-permute-start | bytes 3145736 | tf_op jit(solution)/shard_map/ppermute | solution.py:392
  78.5 16.9 %all-to-all-start = ((bf16[2,512,1024]{2,1,0:T(8,128)(2,1)}), bf16[2,512,1024]{2,1,0:T(8,128)(2,1)}, u32[]{:S(2)}, u32[]{:S(2)}) async-start(bf16[2,512,1024]{2,1,0:T(8,128)(2,1)} %bitcast.6), calls=%async_computation | async-start | bytes 4194304 | tf_op jit(solution)/shard_map/all_to_all | solution.py:433
  87.0 15.2 %collective-permute-start.22 = (bf16[64,1024]{1,0:T(8,128)(2,1)}, bf16[64,1024]{1,0:T(8,128)(2,1)S(1)}, u32[]{:S(2)}, u32[]{:S(2)}) collective-permute-start(bf16[64,1024]{1,0:T(8,128)(2,1)} %get-tuple-element.95), channel_id=1, source_target_pairs={{0,96},{32,0},{64,32},{96,64},{1,97},{33,1},{65,33},{97,65},{2,98}... | collective-permute-start | bytes 393224 | tf_op jit(solution)/shard_map/ppermute | solution.py:388
  90.0 12.2 %collective-permute-start.23 = (bf16[64,1024]{1,0:T(8,128)(2,1)S(1)}, bf16[64,1024]{1,0:T(8,128)(2,1)S(1)}, u32[]{:S(2)}, u32[]{:S(2)}) collective-permute-start(bf16[64,1024]{1,0:T(8,128)(2,1)S(1)} %get-tuple-element.96), channel_id=1, source_target_pairs={{0,32},{32,64},{64,96},{96,0},{1,33},{33,65},{65,97},{97,1},{2,34}... | collective-permute-start | bytes 393224 | tf_op jit(solution)/shard_map/ppermute | solution.py:388
  92.3 9.9 %collective-permute-start.24 = (bf16[64,1024]{1,0:T(8,128)(2,1)}, bf16[64,1024]{1,0:T(8,128)(2,1)S(1)}, u32[]{:S(2)}, u32[]{:S(2)}) collective-permute-start(bf16[64,1024]{1,0:T(8,128)(2,1)} %get-tuple-element.98), channel_id=1, source_target_pairs={{0,24},{8,0},{16,8},{24,16},{1,25},{9,1},{17,9},{25,17},{2,26},{10... | collective-permute-start | bytes 393224 | tf_op jit(solution)/shard_map/ppermute | solution.py:388
  95.4 6.8 %collective-permute-start.25 = (bf16[64,1024]{1,0:T(8,128)(2,1)}, bf16[64,1024]{1,0:T(8,128)(2,1)S(1)}, u32[]{:S(2)}, u32[]{:S(2)}) collective-permute-start(bf16[64,1024]{1,0:T(8,128)(2,1)} %get-tuple-element.99), channel_id=1, source_target_pairs={{0,8},{8,16},{16,24},{24,0},{1,9},{9,17},{17,25},{25,1},{2,10},{10... | collective-permute-start | bytes 393224 | tf_op jit(solution)/shard_map/ppermute | solution.py:388
  98.3 16.7 %all-to-all-start.1 = ((bf16[4,128,1024]{2,1,0:T(8,128)(2,1)}), bf16[4,128,1024]{2,1,0:T(8,128)(2,1)S(1)}, u32[]{:S(2)}, u32[]{:S(2)}) async-start(bf16[4,128,1024]{2,1,0:T(8,128)(2,1)} %bitcast.8), calls=%async_computation.1 | async-start | bytes 2097152 | tf_op jit(solution)/shard_map/all_to_all | solution.py:482
  102.9 7.6 %collective-permute-start.26 = (bf16[128,1024]{1,0:T(8,128)(2,1)S(1)}, bf16[128,1024]{1,0:T(8,128)(2,1)S(1)}, u32[]{:S(2)}, u32[]{:S(2)}) collective-permute-start(bf16[128,1024]{1,0:T(8,128)(2,1)S(1)} %get-tuple-element.100), channel_id=1, source_target_pairs={{0,8},{8,16},{16,24},{24,0},{1,9},{9,17},{17,25},{25,1},{2,10},{10... | collective-permute-start | bytes 786440 | tf_op jit(solution)/shard_map/ppermute | solution.py:392
  103.1 7.4 %collective-permute-start.27 = (bf16[128,1024]{1,0:T(8,128)(2,1)S(1)}, bf16[128,1024]{1,0:T(8,128)(2,1)S(1)}, u32[]{:S(2)}, u32[]{:S(2)}) collective-permute-start(bf16[128,1024]{1,0:T(8,128)(2,1)S(1)} %get-tuple-element.101), channel_id=1, source_target_pairs={{0,24},{8,0},{16,8},{24,16},{1,25},{9,1},{17,9},{25,17},{2,26},{10... | collective-permute-start | bytes 786440 | tf_op jit(solution)/shard_map/ppermute | solution.py:392
  106.2 7.6 %collective-permute-start.28 = (bf16[128,1024]{1,0:T(8,128)(2,1)S(1)}, bf16[128,1024]{1,0:T(8,128)(2,1)S(1)}, u32[]{:S(2)}, u32[]{:S(2)}) collective-permute-start(bf16[128,1024]{1,0:T(8,128)(2,1)S(1)} %get-tuple-element.103), channel_id=1, source_target_pairs={{0,32},{32,64},{64,96},{96,0},{1,33},{33,65},{65,97},{97,1},{2,34}... | collective-permute-start | bytes 786440 | tf_op jit(solution)/shard_map/ppermute | solution.py:392
  107.1 6.7 %collective-permute-start.29 = (bf16[128,1024]{1,0:T(8,128)(2,1)S(1)}, bf16[128,1024]{1,0:T(8,128)(2,1)S(1)}, u32[]{:S(2)}, u32[]{:S(2)}) collective-permute-start(bf16[128,1024]{1,0:T(8,128)(2,1)S(1)} %get-tuple-element.104), channel_id=1, source_target_pairs={{0,96},{32,0},{64,32},{96,64},{1,97},{33,1},{65,33},{97,65},{2,98}... | collective-permute-start | bytes 786440 | tf_op jit(solution)/shard_map/ppermute | solution.py:392
  (14 other events, 54.4 us)

commit v10 on v9

--- a/solution.py
+++ b/solution.py
@@ -482,9 +482,10 @@
     back = lax.all_to_all(after(own, mark), "expert", split_axis=0, concat_axis=0, tiled=True)
     in_keep, in_sides, low, high, mark = combine(after(in_own, mark), in_parts)
     in_hop = first_hop(low, high, "x")
-    *pairs, _ = join((out_sides, out_hop), (in_sides, in_hop))
-    out_parts = second_hop(*pairs[:2], "y")
-    in_parts = second_hop(*pairs[2:], "x")
+    *pair, mark = join((out_sides, out_hop))
+    out_parts = second_hop(*pair, "y")
+    *pair, _ = join((in_sides, in_hop))
+    in_parts = second_hop(*pair, "x")
     grad_out = add(out_keep, *out_parts) * scale
     grad_in = add(in_keep, *in_parts) * scale
     token_grad = restore_order(place, back)

time: 117 us -> 127 us (1.085)
  waiting for transfers between devices: 10.8 us -> 16.7 us
  local copies, waits for them, and re-layouts: 2.64 us -> 5.16 us
  Pallas kernels: 49.8 us -> 51.4 us
    ppermute x8, waiting for transfers between devices: 0.5 us -> 6.76 us  [first_hop(): return (lax.ppermute(low, axis, ring(3)), lax.ppermute(high, axis, ring(1)))]
    unnamed x12, local copies, waits for them, and re-layouts: 1.74 us -> 4.26 us
    pallas_call x3 -> x4, Pallas kernels: 3.87 us -> 5.28 us  [join(): pl.pallas_call(body, out_shape=[shape(2 * h, width)] * (2 * len(sums)) +...]
  transfers between devices with their start and end apart: 32 -> 32, of which waited for: 10 -> 10; matrix products, arithmetic and copies ran while one was open for 6% -> 5% of each run, Pallas kernels for 39% -> 37%
where the time goes in v10:
time: 127 us; the launch traced here: 126 us
  Pallas kernels  51.4 us (40%)
  starting transfers between devices  46.3 us (36%)
  waiting for transfers between devices  16.7 us (13%)
  other arithmetic  5.53 us (4%)
  local copies, waits for them, and re-layouts  5.16 us (4%)
    ppermute x8, starting transfers between devices, second_hop(): return (lax.ppermute(up, axis, ring(1)), lax.ppermute(down, axis, ring(3)))  12.9 us
    pallas_call x3, Pallas kernels, backward(): pl.pallas_call(body, grid=(count,), in_specs=[SMEM] + [VMEM] * 4 + [ANY]...  12.2 us
    ppermute x8, starting transfers between devices, first_hop(): return (lax.ppermute(low, axis, ring(3)), lax.ppermute(high, axis, ring(1)))  11.8 us
    ppermute x6, starting transfers between devices, to_owner(): lax.ppermute(parts[r], 'expert', ring(r))  11 us
    pallas_call x1, Pallas kernels, forward(): pl.pallas_call(body, grid=(4,), in_specs=[SMEM] + [VMEM] * (len(parts) +...  9.06 us
    pallas_call x1, Pallas kernels, row_gradients(): pl.pallas_call(body, grid=(4,), in_specs=[SMEM] + [VMEM] * 4, out_specs=V...  7.52 us
    ppermute x8, waiting for transfers between devices, first_hop(): return (lax.ppermute(low, axis, ring(3)), lax.ppermute(high, axis, ring(1)))  6.76 us
    pallas_call x4, Pallas kernels, join(): pl.pallas_call(body, out_shape=[shape(2 * h, width)] * (2 * len(sums)) +...  5.28 us
  transfers between devices with their start and end apart: 32, of which 10 were waited for; matrix products, arithmetic and copies ran while one was open for 5% of the time, Pallas kernels for 37%

profile of v10, /device:TPU:0, one launch (start us, length us, event | category | flops | bytes accessed | tf_op | source)
XLA Modules:
  0.0 126.0 jit_solution(4509770487475375435)
XLA Ops:
  4.3 3.6 %collective-permute-start.1 = (bf16[128,1024]{1,0:T(8,128)(2,1)S(1)}, bf16[128,1024]{1,0:T(8,128)(2,1)S(1)}, u32[]{:S(2)}, u32[]{:S(2)}) collective-permute-start(bf16[128,1024]{1,0:T(8,128)(2,1)S(1)} %get-tuple-element.59), channel_id=1, source_target_pairs={{0,2},{1,3},{2,0},{3,1},{4,6},{5,7},{6,4},{7,5},{8,10},{9,11},{10,... | collective-permute-start | bytes 786440 | tf_op jit(solution)/shard_map/ppermute | solution.py:456
  12.9 4.2 %shard_map.104 = (bf16[2048,1024]{1,0:T(8,128)(2,1)S(1)}, bf16[2048,1024]{1,0:T(8,128)(2,1)S(1)}, f32[8,128]{1,0:T(8,128)S(1)}) custom-call(s32[53]{0:T(128)S(1)} %concatenate.3.table_ref, bf16[4096,1024]{1,0:T(8,128)(2,1)} %bitcast.17, bf16[4096,1024]{1,0:T(8,128)(2,1)} %bitcast.18), custom_call_target="tpu_custom_call" | custom-call | bytes 16777216 | tf_op jit(solution)/shard_map/pallas_call | solution.py:153
  20.7 2.4 %collective-permute-start.8 = (bf16[128,1024]{1,0:T(8,128)(2,1)S(1)}, bf16[128,1024]{1,0:T(8,128)(2,1)S(1)}, u32[]{:S(2)}, u32[]{:S(2)}) collective-permute-start(bf16[128,1024]{1,0:T(8,128)(2,1)S(1)} %get-tuple-element.65), channel_id=1, source_target_pairs={{0,2},{1,3},{2,0},{3,1},{4,6},{5,7},{6,4},{7,5},{8,10},{9,11},{10,... | collective-permute-start | bytes 786440 | tf_op jit(solution)/shard_map/ppermute | solution.py:456
  24.4 9.1 %shard_map.107 = (bf16[2048,1024]{1,0:T(8,128)(2,1)S(1)}, bf16[2048,1024]{1,0:T(8,128)(2,1)S(1)}, bf16[1024,1024]{1,0:T(8,128)(2,1)S(1)}, f32[8,128]{1,0:T(8,128)S(1)}) custom-call(s32[53]{0:T(128)S(1)} %concatenate.3.table_ref, bf16[128,1024]{1,0:T(8,128)(2,1)S(1)} %shard_map.106.refs_0_, bf16[128,1024]{1,0:T(8,128)(2,1)S(1)} %collective-permute-done.refs_1_, ...), custom_call_target="tpu_custom_call" | custom-call | bytes 16777216 | tf_op jit(solution)/shard_map/pallas_call | solution.py:213
  39.3 2.8 %collective-permute-start.14 = (bf16[256,1024]{1,0:T(8,128)(2,1)S(1)}, bf16[256,1024]{1,0:T(8,128)(2,1)S(1)}, u32[]{:S(2)}, u32[]{:S(2)}) collective-permute-start(bf16[256,1024]{1,0:T(8,128)(2,1)S(1)} %get-tuple-element.79), channel_id=1, source_target_pairs={{0,24},{8,0},{16,8},{24,16},{1,25},{9,1},{17,9},{25,17},{2,26},{10... | collective-permute-start | bytes 1572872 | tf_op jit(solution)/shard_map/ppermute | solution.py:388
  42.1 2.9 %shard_map.113 = (bf16[512,1024]{1,0:T(8,128)(2,1)S(1)}, bf16[256,1024]{1,0:T(8,128)(2,1)S(1)}, bf16[256,1024]{1,0:T(8,128)(2,1)S(1)}, f32[8,128]{1,0:T(8,128)S(1)}) custom-call(s32[53]{0:T(128)S(1)} %concatenate.3.table_ref, bf16[1024,1024]{1,0:T(8,128)(2,1)S(1)} %get-tuple-element.67.grads_ref.rows_ref, bf16[1024,1024]{1,0:T(8,128)(2,1)S(1)} %get-tuple-element.68.rows_ref, ...), custom_call_target="tpu_custom_call" | custom-call | bytes 6291456 | tf_op jit(solution)/shard_map/pallas_call | solution.py:289
  45.0 3.1 %collective-permute-start.16 = (bf16[256,1024]{1,0:T(8,128)(2,1)S(1)}, bf16[256,1024]{1,0:T(8,128)(2,1)S(1)}, u32[]{:S(2)}, u32[]{:S(2)}) collective-permute-start(bf16[256,1024]{1,0:T(8,128)(2,1)S(1)} %get-tuple-element.82), channel_id=1, source_target_pairs={{0,96},{32,0},{64,32},{96,64},{1,97},{33,1},{65,33},{97,65},{2,98}... | collective-permute-start | bytes 1572872 | tf_op jit(solution)/shard_map/ppermute | solution.py:388
  48.1 3.4 %shard_map.114 = (bf16[1024,1024]{1,0:T(8,128)(2,1)S(1)}, bf16[512,1024]{1,0:T(8,128)(2,1)S(1)}, f32[8,128]{1,0:T(8,128)S(1)}) custom-call(bf16[2048,1024]{1,0:T(8,128)(2,1)S(1)} %get-tuple-element.62.act_ref, bf16[1024,1024]{1,0:T(8,128)(2,1)S(1)} %get-tuple-element.67.grads_ref.rows_ref, f32[8,128]{1,0:T(8,128)S(1)} %get-tuple-element.73.refs_0_), custom_call_target="tpu_custom_call" | custom-call | bytes 8388608 | tf_op jit(solution)/shard_map/pallas_call | solution.py:255
  51.6 5.8 %shard_map.115 = (bf16[1024,1024]{1,0:T(8,128)(2,1)S(1)}, bf16[1024,1024]{1,0:T(8,128)(2,1)S(1)}, f32[8,128]{1,0:T(8,128)S(1)}) custom-call(s32[53]{0:T(128)S(1)} %concatenate.3.table_ref, bf16[1024,1024]{1,0:T(8,128)(2,1)S(1)} %get-tuple-element.67.grads_ref.rows_ref, bf16[1024,1024]{1,0:T(8,128)(2,1)S(1)} %get-tuple-element.68.rows_ref, ...), custom_call_target="tpu_custom_call" | custom-call | bytes 10485760 | tf_op jit(solution)/shard_map/pallas_call | solution.py:289
  59.7 2.5 %collective-permute-start.19 = (bf16[512,1024]{1,0:T(8,128)(2,1)}, bf16[512,1024]{1,0:T(8,128)(2,1)}, u32[]{:S(2)}, u32[]{:S(2)}) collective-permute-start(bf16[512,1024]{1,0:T(8,128)(2,1)} %get-tuple-element.88), channel_id=1, source_target_pairs={{0,24},{8,0},{16,8},{24,16},{1,25},{9,1},{17,9},{25,17},{2,26},{10... | collective-permute-start | bytes 3145736 | tf_op jit(solution)/shard_map/ppermute | solution.py:392
  65.0 2.6 %collective-permute-start.21 = (bf16[512,1024]{1,0:T(8,128)(2,1)}, bf16[512,1024]{1,0:T(8,128)(2,1)}, u32[]{:S(2)}, u32[]{:S(2)}) collective-permute-start(bf16[512,1024]{1,0:T(8,128)(2,1)} %get-tuple-element.92), channel_id=1, source_target_pairs={{0,96},{32,0},{64,32},{96,64},{1,97},{33,1},{65,33},{97,65},{2,98}... | collective-permute-start | bytes 3145736 | tf_op jit(solution)/shard_map/ppermute | solution.py:392
  67.6 3.4 %shard_map.120 = (bf16[512,1024]{1,0:T(8,128)(2,1)S(1)}, bf16[512,1024]{1,0:T(8,128)(2,1)S(1)}, f32[8,128]{1,0:T(8,128)}) custom-call(s32[53]{0:T(128)S(1)} %concatenate.3.table_ref, bf16[1024,1024]{1,0:T(8,128)(2,1)S(1)} %get-tuple-element.67.grads_ref.rows_ref, bf16[1024,1024]{1,0:T(8,128)(2,1)S(1)} %get-tuple-element.68.rows_ref, ...), custom_call_target="tpu_custom_call" | custom-call | bytes 6291456 | tf_op jit(solution)/shard_map/pallas_call | solution.py:289
  71.0 7.5 %shard_map.121 = bf16[1024,1024]{1,0:T(8,128)(2,1)} custom-call(s32[53]{0:T(128)S(1)} %concatenate.3.table_ref, bf16[512,1024]{1,0:T(8,128)(2,1)S(1)} %get-tuple-element.72.a_ref, bf16[1024,1024]{1,0:T(8,128)(2,1)S(1)} %get-tuple-element.75.b_ref, bf16[512,1024]{1,0:T(8,128)(2,1)S(1)} %get-tuple-element.85.c_ref, ...), custom_call_target="tpu_custom_call" | custom-call | bytes 12582912 | tf_op jit(solution)/shard_map/pallas_call | solution.py:327
  78.5 4.8 %all-to-all-start = ((bf16[2,512,1024]{2,1,0:T(8,128)(2,1)}), bf16[2,512,1024]{2,1,0:T(8,128)(2,1)}, u32[]{:S(2)}, u32[]{:S(2)}) async-start(bf16[2,512,1024]{2,1,0:T(8,128)(2,1)} %bitcast.6), calls=%async_computation | async-start | bytes 4194304 | tf_op jit(solution)/shard_map/all_to_all | solution.py:433
  85.1 2.3 %shard_map.122 = (bf16[128,1024]{1,0:T(8,128)(2,1)S(1)}, bf16[256,1024]{1,0:T(8,128)(2,1)S(1)}, bf16[64,1024]{1,0:T(8,128)(2,1)}, bf16[64,1024]{1,0:T(8,128)(2,1)}, f32[8,128]{1,0:T(8,128)S(1)}) custom-call(bf16[512,1024]{1,0:T(8,128)(2,1)S(1)} %get-tuple-element.86.own_ref, bf16[512,1024]{1,0:T(8,128)(2,1)} %collective-permute-done.18.left, ...), custom_call_target="tpu_custom_call" | custom-call | bytes 4194304 | tf_op jit(solution)/shard_map/pallas_call | solution.py:418
  88.9 3.0 %collective-permute-start.26 = (bf16[64,1024]{1,0:T(8,128)(2,1)}, bf16[64,1024]{1,0:T(8,128)(2,1)S(1)}, u32[]{:S(2)}, u32[]{:S(2)}) collective-permute-start(bf16[64,1024]{1,0:T(8,128)(2,1)} %get-tuple-element.101), channel_id=1, source_target_pairs={{0,96},{32,0},{64,32},{96,64},{1,97},{33,1},{65,33},{97,65},{2,98}... | collective-permute-start | bytes 393224 | tf_op jit(solution)/shard_map/ppermute | solution.py:388
  91.9 2.9 %fusion.refs_0_ = bf16[512,1024]{1,0:T(8,128)(2,1)} fusion(bf16[2,512,1024]{2,1,0:T(8,128)(2,1)} %all-to-all-done), kind=kLoop, calls=%fused_computation.1 | loop fusion | flops 2097152 | bytes 3145728 | tf_op jit(solution)/shard_map/convert_element_type | solution.py:435
  94.8 3.8 %all-to-all-start.1 = ((bf16[4,128,1024]{2,1,0:T(8,128)(2,1)}), bf16[4,128,1024]{2,1,0:T(8,128)(2,1)S(1)}, u32[]{:S(2)}, u32[]{:S(2)}) async-start(bf16[4,128,1024]{2,1,0:T(8,128)(2,1)} %bitcast.8), calls=%async_computation.1 | async-start | bytes 2097152 | tf_op jit(solution)/shard_map/all_to_all | solution.py:482
  101.1 3.2 %collective-permute-start.29 = (bf16[128,1024]{1,0:T(8,128)(2,1)S(1)}, bf16[128,1024]{1,0:T(8,128)(2,1)S(1)}, u32[]{:S(2)}, u32[]{:S(2)}) collective-permute-start(bf16[128,1024]{1,0:T(8,128)(2,1)S(1)} %get-tuple-element.104), channel_id=1, source_target_pairs={{0,96},{32,0},{64,32},{96,64},{1,97},{33,1},{65,33},{97,65},{2,98}... | collective-permute-start | bytes 786440 | tf_op jit(solution)/shard_map/ppermute | solution.py:392
  106.4 3.0 %collective-permute-start.22 = (bf16[64,1024]{1,0:T(8,128)(2,1)S(1)}, bf16[64,1024]{1,0:T(8,128)(2,1)S(1)}, u32[]{:S(2)}, u32[]{:S(2)}) collective-permute-start(bf16[64,1024]{1,0:T(8,128)(2,1)S(1)} %get-tuple-element.95), channel_id=1, source_target_pairs={{0,24},{8,0},{16,8},{24,16},{1,25},{9,1},{17,9},{25,17},{2,26},{10... | collective-permute-start | bytes 393224 | tf_op jit(solution)/shard_map/ppermute | solution.py:388
  109.4 2.5 %collective-permute-done.22.refs_1_ = bf16[64,1024]{1,0:T(8,128)(2,1)S(1)} collective-permute-done((bf16[64,1024]{1,0:T(8,128)(2,1)S(1)}, bf16[64,1024]{1,0:T(8,128)(2,1)S(1)}, u32[]{:S(2)}, u32[]{:S(2)}) %collective-permute-start.22) | collective-permute-done | bytes 131104 | tf_op jit(solution)/shard_map/ppermute | solution.py:388
  111.9 3.7 %collective-permute-done.23.refs_2_ = bf16[64,1024]{1,0:T(8,128)(2,1)S(1)} collective-permute-done((bf16[64,1024]{1,0:T(8,128)(2,1)S(1)}, bf16[64,1024]{1,0:T(8,128)(2,1)S(1)}, u32[]{:S(2)}, u32[]{:S(2)}) %collective-permute-start.23) | collective-permute-done | bytes 131104 | tf_op jit(solution)/shard_map/ppermute | solution.py:388
  116.2 3.2 %collective-permute-start.25 = (bf16[128,1024]{1,0:T(8,128)(2,1)S(1)}, bf16[128,1024]{1,0:T(8,128)(2,1)S(1)}, u32[]{:S(2)}, u32[]{:S(2)}) collective-permute-start(bf16[128,1024]{1,0:T(8,128)(2,1)S(1)} %get-tuple-element.98), channel_id=1, source_target_pairs={{0,24},{8,0},{16,8},{24,16},{1,25},{9,1},{17,9},{25,17},{2,26},{10... | collective-permute-start | bytes 786440 | tf_op jit(solution)/shard_map/ppermute | solution.py:392
  120.4 3.4 %collective-permute-done.24 = bf16[128,1024]{1,0:T(8,128)(2,1)S(1)} collective-permute-done((bf16[128,1024]{1,0:T(8,128)(2,1)S(1)}, bf16[128,1024]{1,0:T(8,128)(2,1)S(1)}, u32[]{:S(2)}, u32[]{:S(2)}) %collective-permute-start.24) | collective-permute-done | bytes 262176 | tf_op jit(solution)/shard_map/ppermute | solution.py:392
  (89 shorter events, 36.0 us)
Async XLA Ops:
  2.2 15.0 %collective-permute-start = (bf16[128,1024]{1,0:T(8,128)(2,1)S(1)}, bf16[128,1024]{1,0:T(8,128)(2,1)S(1)}, u32[]{:S(2)}, u32[]{:S(2)}) collective-permute-start(bf16[128,1024]{1,0:T(8,128)(2,1)S(1)} %get-tuple-element.58), channel_id=1, source_target_pairs={{0,1},{1,2},{2,3},{3,0},{4,5},{5,6},{6,7},{7,4},{8,9},{9,10},{10,1... | collective-permute-start | bytes 786440 | tf_op jit(solution)/shard_map/ppermute | solution.py:456
  4.3 15.2 %collective-permute-start.1 = (bf16[128,1024]{1,0:T(8,128)(2,1)S(1)}, bf16[128,1024]{1,0:T(8,128)(2,1)S(1)}, u32[]{:S(2)}, u32[]{:S(2)}) collective-permute-start(bf16[128,1024]{1,0:T(8,128)(2,1)S(1)} %get-tuple-element.59), channel_id=1, source_target_pairs={{0,2},{1,3},{2,0},{3,1},{4,6},{5,7},{6,4},{7,5},{8,10},{9,11},{10,... | collective-permute-start | bytes 786440 | tf_op jit(solution)/shard_map/ppermute | solution.py:456
  7.8 11.6 %collective-permute-start.2 = (bf16[128,1024]{1,0:T(8,128)(2,1)S(1)}, bf16[128,1024]{1,0:T(8,128)(2,1)S(1)}, u32[]{:S(2)}, u32[]{:S(2)}) collective-permute-start(bf16[128,1024]{1,0:T(8,128)(2,1)S(1)} %get-tuple-element.60), channel_id=1, source_target_pairs={{0,3},{1,0},{2,1},{3,2},{4,7},{5,4},{6,5},{7,6},{8,11},{9,8},{10,9... | collective-permute-start | bytes 786440 | tf_op jit(solution)/shard_map/ppermute | solution.py:456
  17.2 5.9 %collective-permute-start.4 = (bf16[128,1024]{1,0:T(8,128)(2,1)S(1)}, bf16[128,1024]{1,0:T(8,128)(2,1)S(1)}, u32[]{:S(2)}, u32[]{:S(2)}) collective-permute-start(bf16[128,1024]{1,0:T(8,128)(2,1)S(1)} %collective-permute-done.refs_1_), channel_id=1, source_target_pairs={{0,4},{4,0},{1,5},{5,1},{2,6},{6,2},{3,7},{7,3},{8,12},{12,8},{9,1... | collective-permute-start | bytes 786440 | tf_op jit(solution)/shard_map/ppermute | solution.py:22
  20.0 13.6 %collective-permute-start.7 = (bf16[128,1024]{1,0:T(8,128)(2,1)S(1)}, bf16[128,1024]{1,0:T(8,128)(2,1)S(1)}, u32[]{:S(2)}, u32[]{:S(2)}) collective-permute-start(bf16[128,1024]{1,0:T(8,128)(2,1)S(1)} %get-tuple-element.64), channel_id=1, source_target_pairs={{0,1},{1,2},{2,3},{3,0},{4,5},{5,6},{6,7},{7,4},{8,9},{9,10},{10,1... | collective-permute-start | bytes 786440 | tf_op jit(solution)/shard_map/ppermute | solution.py:456
  20.7 14.7 %collective-permute-start.8 = (bf16[128,1024]{1,0:T(8,128)(2,1)S(1)}, bf16[128,1024]{1,0:T(8,128)(2,1)S(1)}, u32[]{:S(2)}, u32[]{:S(2)}) collective-permute-start(bf16[128,1024]{1,0:T(8,128)(2,1)S(1)} %get-tuple-element.65), channel_id=1, source_target_pairs={{0,2},{1,3},{2,0},{3,1},{4,6},{5,7},{6,4},{7,5},{8,10},{9,11},{10,... | collective-permute-start | bytes 786440 | tf_op jit(solution)/shard_map/ppermute | solution.py:456
  23.1 12.5 %collective-permute-start.9 = (bf16[128,1024]{1,0:T(8,128)(2,1)S(1)}, bf16[128,1024]{1,0:T(8,128)(2,1)S(1)}, u32[]{:S(2)}, u32[]{:S(2)}) collective-permute-start(bf16[128,1024]{1,0:T(8,128)(2,1)S(1)} %get-tuple-element.66), channel_id=1, source_target_pairs={{0,3},{1,0},{2,1},{3,2},{4,7},{5,4},{6,5},{7,6},{8,11},{9,8},{10,9... | collective-permute-start | bytes 786440 | tf_op jit(solution)/shard_map/ppermute | solution.py:456
  39.3 18.1 %collective-permute-start.14 = (bf16[256,1024]{1,0:T(8,128)(2,1)S(1)}, bf16[256,1024]{1,0:T(8,128)(2,1)S(1)}, u32[]{:S(2)}, u32[]{:S(2)}) collective-permute-start(bf16[256,1024]{1,0:T(8,128)(2,1)S(1)} %get-tuple-element.79), channel_id=1, source_target_pairs={{0,24},{8,0},{16,8},{24,16},{1,25},{9,1},{17,9},{25,17},{2,26},{10... | collective-permute-start | bytes 1572872 | tf_op jit(solution)/shard_map/ppermute | solution.py:388
  42.1 15.3 %collective-permute-start.15 = (bf16[256,1024]{1,0:T(8,128)(2,1)S(1)}, bf16[256,1024]{1,0:T(8,128)(2,1)S(1)}, u32[]{:S(2)}, u32[]{:S(2)}) collective-permute-start(bf16[256,1024]{1,0:T(8,128)(2,1)S(1)} %get-tuple-element.80), channel_id=1, source_target_pairs={{0,8},{8,16},{16,24},{24,0},{1,9},{9,17},{17,25},{25,1},{2,10},{10... | collective-permute-start | bytes 1572872 | tf_op jit(solution)/shard_map/ppermute | solution.py:388
  45.0 17.1 %collective-permute-start.16 = (bf16[256,1024]{1,0:T(8,128)(2,1)S(1)}, bf16[256,1024]{1,0:T(8,128)(2,1)S(1)}, u32[]{:S(2)}, u32[]{:S(2)}) collective-permute-start(bf16[256,1024]{1,0:T(8,128)(2,1)S(1)} %get-tuple-element.82), channel_id=1, source_target_pairs={{0,96},{32,0},{64,32},{96,64},{1,97},{33,1},{65,33},{97,65},{2,98}... | collective-permute-start | bytes 1572872 | tf_op jit(solution)/shard_map/ppermute | solution.py:388
  48.1 14.6 %collective-permute-start.17 = (bf16[256,1024]{1,0:T(8,128)(2,1)S(1)}, bf16[256,1024]{1,0:T(8,128)(2,1)S(1)}, u32[]{:S(2)}, u32[]{:S(2)}) collective-permute-start(bf16[256,1024]{1,0:T(8,128)(2,1)S(1)} %get-tuple-element.83), channel_id=1, source_target_pairs={{0,32},{32,64},{64,96},{96,0},{1,33},{33,65},{65,97},{97,1},{2,34}... | collective-permute-start | bytes 1572872 | tf_op jit(solution)/shard_map/ppermute | solution.py:388
  58.9 26.2 %collective-permute-start.18 = (bf16[512,1024]{1,0:T(8,128)(2,1)}, bf16[512,1024]{1,0:T(8,128)(2,1)}, u32[]{:S(2)}, u32[]{:S(2)}) collective-permute-start(bf16[512,1024]{1,0:T(8,128)(2,1)} %get-tuple-element.87), channel_id=1, source_target_pairs={{0,8},{8,16},{16,24},{24,0},{1,9},{9,17},{17,25},{25,1},{2,10},{10... | collective-permute-start | bytes 3145736 | tf_op jit(solution)/shard_map/ppermute | solution.py:392
  59.7 25.4 %collective-permute-start.19 = (bf16[512,1024]{1,0:T(8,128)(2,1)}, bf16[512,1024]{1,0:T(8,128)(2,1)}, u32[]{:S(2)}, u32[]{:S(2)}) collective-permute-start(bf16[512,1024]{1,0:T(8,128)(2,1)} %get-tuple-element.88), channel_id=1, source_target_pairs={{0,24},{8,0},{16,8},{24,16},{1,25},{9,1},{17,9},{25,17},{2,26},{10... | collective-permute-start | bytes 3145736 | tf_op jit(solution)/shard_map/ppermute | solution.py:392
  64.4 40.0 %collective-permute-start.20 = (bf16[512,1024]{1,0:T(8,128)(2,1)}, bf16[512,1024]{1,0:T(8,128)(2,1)S(1)}, u32[]{:S(2)}, u32[]{:S(2)}) collective-permute-start(bf16[512,1024]{1,0:T(8,128)(2,1)} %get-tuple-element.91), channel_id=1, source_target_pairs={{0,32},{32,64},{64,96},{96,0},{1,33},{33,65},{65,97},{97,1},{2,34}... | collective-permute-start | bytes 3145736 | tf_op jit(solution)/shard_map/ppermute | solution.py:392
  65.0 39.4 %collective-permute-start.21 = (bf16[512,1024]{1,0:T(8,128)(2,1)}, bf16[512,1024]{1,0:T(8,128)(2,1)}, u32[]{:S(2)}, u32[]{:S(2)}) collective-permute-start(bf16[512,1024]{1,0:T(8,128)(2,1)} %get-tuple-element.92), channel_id=1, source_target_pairs={{0,96},{32,0},{64,32},{96,64},{1,97},{33,1},{65,33},{97,65},{2,98}... | collective-permute-start | bytes 3145736 | tf_op jit(solution)/shard_map/ppermute | solution.py:392
  78.5 13.3 %all-to-all-start = ((bf16[2,512,1024]{2,1,0:T(8,128)(2,1)}), bf16[2,512,1024]{2,1,0:T(8,128)(2,1)}, u32[]{:S(2)}, u32[]{:S(2)}) async-start(bf16[2,512,1024]{2,1,0:T(8,128)(2,1)} %bitcast.6), calls=%async_computation | async-start | bytes 4194304 | tf_op jit(solution)/shard_map/all_to_all | solution.py:433
  88.9 9.7 %collective-permute-start.26 = (bf16[64,1024]{1,0:T(8,128)(2,1)}, bf16[64,1024]{1,0:T(8,128)(2,1)S(1)}, u32[]{:S(2)}, u32[]{:S(2)}) collective-permute-start(bf16[64,1024]{1,0:T(8,128)(2,1)} %get-tuple-element.101), channel_id=1, source_target_pairs={{0,96},{32,0},{64,32},{96,64},{1,97},{33,1},{65,33},{97,65},{2,98}... | collective-permute-start | bytes 393224 | tf_op jit(solution)/shard_map/ppermute | solution.py:388
  91.9 6.7 %collective-permute-start.27 = (bf16[64,1024]{1,0:T(8,128)(2,1)}, bf16[64,1024]{1,0:T(8,128)(2,1)}, u32[]{:S(2)}, u32[]{:S(2)}) collective-permute-start(bf16[64,1024]{1,0:T(8,128)(2,1)} %get-tuple-element.102), channel_id=1, source_target_pairs={{0,32},{32,64},{64,96},{96,0},{1,33},{33,65},{65,97},{97,1},{2,34}... | collective-permute-start | bytes 393224 | tf_op jit(solution)/shard_map/ppermute | solution.py:388
  94.8 29.9 %all-to-all-start.1 = ((bf16[4,128,1024]{2,1,0:T(8,128)(2,1)}), bf16[4,128,1024]{2,1,0:T(8,128)(2,1)S(1)}, u32[]{:S(2)}, u32[]{:S(2)}) async-start(bf16[4,128,1024]{2,1,0:T(8,128)(2,1)} %bitcast.8), calls=%async_computation.1 | async-start | bytes 2097152 | tf_op jit(solution)/shard_map/all_to_all | solution.py:482
  101.1 18.4 %collective-permute-start.28 = (bf16[128,1024]{1,0:T(8,128)(2,1)S(1)}, bf16[128,1024]{1,0:T(8,128)(2,1)S(1)}, u32[]{:S(2)}, u32[]{:S(2)}) collective-permute-start(bf16[128,1024]{1,0:T(8,128)(2,1)S(1)} %get-tuple-element.103), channel_id=1, source_target_pairs={{0,32},{32,64},{64,96},{96,0},{1,33},{33,65},{65,97},{97,1},{2,34}... | collective-permute-start | bytes 786440 | tf_op jit(solution)/shard_map/ppermute | solution.py:392
  101.1 18.4 %collective-permute-start.29 = (bf16[128,1024]{1,0:T(8,128)(2,1)S(1)}, bf16[128,1024]{1,0:T(8,128)(2,1)S(1)}, u32[]{:S(2)}, u32[]{:S(2)}) collective-permute-start(bf16[128,1024]{1,0:T(8,128)(2,1)S(1)} %get-tuple-element.104), channel_id=1, source_target_pairs={{0,96},{32,0},{64,32},{96,64},{1,97},{33,1},{65,33},{97,65},{2,98}... | collective-permute-start | bytes 786440 | tf_op jit(solution)/shard_map/ppermute | solution.py:392
  109.4 6.2 %collective-permute-start.23 = (bf16[64,1024]{1,0:T(8,128)(2,1)S(1)}, bf16[64,1024]{1,0:T(8,128)(2,1)S(1)}, u32[]{:S(2)}, u32[]{:S(2)}) collective-permute-start(bf16[64,1024]{1,0:T(8,128)(2,1)S(1)} %get-tuple-element.96), channel_id=1, source_target_pairs={{0,8},{8,16},{16,24},{24,0},{1,9},{9,17},{17,25},{25,1},{2,10},{10... | collective-permute-start | bytes 393224 | tf_op jit(solution)/shard_map/ppermute | solution.py:388
  116.2 7.6 %collective-permute-start.24 = (bf16[128,1024]{1,0:T(8,128)(2,1)S(1)}, bf16[128,1024]{1,0:T(8,128)(2,1)S(1)}, u32[]{:S(2)}, u32[]{:S(2)}) collective-permute-start(bf16[128,1024]{1,0:T(8,128)(2,1)S(1)} %get-tuple-element.97), channel_id=1, source_target_pairs={{0,8},{8,16},{16,24},{24,0},{1,9},{9,17},{17,25},{25,1},{2,10},{10... | collective-permute-start | bytes 786440 | tf_op jit(solution)/shard_map/ppermute | solution.py:392
  116.2 7.6 %collective-permute-start.25 = (bf16[128,1024]{1,0:T(8,128)(2,1)S(1)}, bf16[128,1024]{1,0:T(8,128)(2,1)S(1)}, u32[]{:S(2)}, u32[]{:S(2)}) collective-permute-start(bf16[128,1024]{1,0:T(8,128)(2,1)S(1)} %get-tuple-element.98), channel_id=1, source_target_pairs={{0,24},{8,0},{16,8},{24,16},{1,25},{9,1},{17,9},{25,17},{2,26},{10... | collective-permute-start | bytes 786440 | tf_op jit(solution)/shard_map/ppermute | solution.py:392
  (14 other events, 46.3 us)
